TPU v7x, 32 devices: a whole 2x2x4 slice. The times are simulated.
32 devices in a mesh: groups: 2 (over y), ctx: 16 (over z, x, core).
Axes of the slice: x: 2, y: 2, z: 4, core: 2. Of those that a mesh axis runs over, the one named last changes fastest.
Arguments:
- queries: bfloat16 [4096, 4096], P(('groups', 'ctx')), parts along dimension 0, may hold values from -12 to 12
- context_keys: bfloat16 [32, 2048, 512], P('groups', 'ctx'), parts along dimension 0, may hold values from -6 to 6
- context_values: bfloat16 [32, 2048, 512], P('groups', 'ctx'), parts along dimension 0, may hold values from -6 to 6
- forward_output: bfloat16 [4096, 4096], P(('groups', 'ctx')), parts along dimension 0, may hold values from -6 to 6
- output_cotangent: bfloat16 [4096, 4096], P(('groups', 'ctx')), parts along dimension 0, may hold values from -48 to 48
- verticals: int32 [8, 8], P('groups'), parts along dimension 0, may hold values from 0 to 511, as said below
- offsets: int32 [8, 3], P('groups'), parts along dimension 0, may hold values from 1 to 10, as said below
- slab_index: int32 [2], P('groups'), parts along dimension 0, may hold values from 1 to 15
Outputs:
- query_grad: bfloat16 [4096, 4096], P(('groups', 'ctx')), parts along dimension 0
- key_gradient: bfloat16 [32, 2048, 512], P('groups', 'ctx'), parts along dimension 0
- value_gradient: bfloat16 [32, 2048, 512], P('groups', 'ctx'), parts along dimension 0
There are 2 independent parts, one for each index of `groups`. A program takes and returns all parts, laid end to end along the dimension named above; each array names one. Nothing has to cross between parts.
Inputs may be any that keep to these rules, and one draw needn't show every extreme that they name: `verticals`: each row holds 8 distinct block numbers; the first of every row is 0, and some row names the last block. Each row holds 3 distinct offsets; some row names 10.
All inputs are finite; a program needn't handle non-finite values.
Results may differ from a plain program's by a relative error of at most 0.0051.
Values may be sent and summed in bfloat16 or wider, within the bound.
No kernel may reach another device: no remote copies, remote signals or barrier semaphores. Data moves between devices by JAX's collectives and lax.ppermute only.
A program may use at most 128 MiB of HBM per device.

v0:
```python
import math

import jax
import jax.numpy as jnp
from jax import lax
from jax.sharding import PartitionSpec as P

MASK_BLOCK_SIZE = 64
WDEV = 5
NV = 8
SLASH_COUNT = 3


def from_behind(shard, axis, by):
    peers = lax.axis_size(axis)
    return lax.ppermute(shard, axis, [(i, (i + by) % peers) for i in range(peers)])


def pick_region(stack, which_region):
    return lax.dynamic_index_in_dim(stack, which_region, 0, keepdims=False)


def head_pass(inputs):
    q_head, grad_head, delta_head, keys_cand, values_cand, visible = inputs
    scaling = 1.0 / math.sqrt(q_head.shape[-1])
    scores = (
        jnp.einsum("jrgd,jkd->jrgk", q_head, keys_cand, preferred_element_type=jnp.float32)
        * scaling
    )
    masked = jnp.where(visible[:, :, None, :], scores, -jnp.inf)
    row_max = jnp.max(masked, axis=-1, keepdims=True)
    row_sum = jnp.sum(jnp.exp(masked - row_max), axis=-1, keepdims=True)
    weights = jnp.exp(masked - (row_max + jnp.log(row_sum)))
    weight_grad = jnp.einsum(
        "jrgd,jkd->jrgk", grad_head, values_cand, preferred_element_type=jnp.float32
    )
    score_grad = weights * (weight_grad - delta_head[..., None])
    weights_low = weights.astype(jnp.bfloat16)
    score_low = score_grad.astype(jnp.bfloat16)
    value_part = jnp.einsum(
        "jrgk,jrgd->jkd", weights_low, grad_head, preferred_element_type=jnp.float32
    )
    key_part = (
        jnp.einsum("jrgk,jrgd->jkd", score_low, q_head, preferred_element_type=jnp.float32)
        * scaling
    )
    query_part = (
        jnp.einsum("jrgk,jkd->jrgd", score_low, keys_cand, preferred_element_type=jnp.float32)
        * scaling
    )
    return (query_part, key_part, value_part)


def shards(
    queries,
    context_keys,
    context_values,
    forward_output,
    output_cotangent,
    verticals,
    offsets,
    slab_index,
):
    devices = lax.axis_size("ctx")
    my_index = lax.axis_index("ctx")
    row_count = queries.shape[0]
    regions = context_keys.shape[0]
    heads_kv = verticals.shape[0]
    features = context_keys.shape[2]
    head_dim = features // heads_kv
    query_per_key_head = queries.shape[1] // features
    per_device = row_count // MASK_BLOCK_SIZE
    blocks_per_slab = per_device * devices
    local_blocks = regions * per_device
    window_blocks = (WDEV + 1) * per_device
    cand_count = 1 + NV + SLASH_COUNT
    present_slab = slab_index[0]
    first_block = present_slab * blocks_per_slab + my_index * per_device
    slab_local_keys = pick_region(context_keys, present_slab)
    own_values = pick_region(context_values, present_slab)
    prior_keys = pick_region(context_keys, present_slab - 1)
    prior_values = pick_region(context_values, present_slab - 1)
    head_numbers = jnp.arange(heads_kv, dtype=jnp.int32)[:, None]
    arrived = []
    for distance in range(1, WDEV + 1):
        wrapped = my_index + distance >= devices
        send_keys = jnp.where(wrapped, prior_keys, slab_local_keys)
        send_values = jnp.where(wrapped, prior_values, own_values)
        arrived.append(from_behind((send_keys, send_values), "ctx", distance))
    window_keys = jnp.concatenate(
        [received[0] for received in reversed(arrived)] + [slab_local_keys], axis=0
    )
    window_values = jnp.concatenate(
        [received[1] for received in reversed(arrived)] + [own_values], axis=0
    )
    window_keys = window_keys.reshape(window_blocks, MASK_BLOCK_SIZE, heads_kv, head_dim)
    window_values = window_values.reshape(window_blocks, MASK_BLOCK_SIZE, heads_kv, head_dim)
    vert_region = verticals // blocks_per_slab
    vert_inner = verticals % blocks_per_slab
    vert_owner = vert_inner // per_device
    vert_local = vert_region * per_device + vert_inner % per_device
    owned_view = (vert_owner == my_index)[:, :, None, None]
    local_keys = context_keys.reshape(local_blocks, MASK_BLOCK_SIZE, heads_kv, head_dim)
    local_values = context_values.reshape(local_blocks, MASK_BLOCK_SIZE, heads_kv, head_dim)
    picked_keys = jnp.where(
        owned_view, local_keys[vert_local, :, head_numbers].astype(jnp.float32), 0.0
    )
    picked_values = jnp.where(
        owned_view, local_values[vert_local, :, head_numbers].astype(jnp.float32), 0.0
    )
    vert_keys, vert_values = lax.psum((picked_keys, picked_values), "ctx")
    vert_keys = vert_keys.astype(jnp.bfloat16)
    vert_values = vert_values.astype(jnp.bfloat16)
    query_blocks = first_block + jnp.arange(per_device, dtype=jnp.int32)
    slash_blocks = query_blocks[None, :, None] - offsets[:, None, :]
    collide = jnp.any(slash_blocks[..., None] == verticals[:, None, None, :], axis=-1)
    slash_valid = (offsets[:, None, :] > 0) & jnp.logical_not(collide)
    vertical_valid = verticals[:, None, :] < query_blocks[None, :, None]
    window_at = WDEV * per_device + jnp.arange(per_device, dtype=jnp.int32)
    local_at = jnp.concatenate(
        [
            jnp.broadcast_to(window_at[None, :, None], (heads_kv, per_device, 1)),
            window_at[None, :, None] - offsets[:, None, :],
        ],
        axis=-1,
    )
    head_grid = head_numbers[:, :, None]
    near_keys = window_keys[local_at, :, head_grid]
    near_values = window_values[local_at, :, head_grid]
    vert_shape = (heads_kv, per_device, NV, MASK_BLOCK_SIZE, head_dim)
    cand_keys = jnp.concatenate(
        [
            near_keys[:, :, :1],
            jnp.broadcast_to(vert_keys[:, None], vert_shape),
            near_keys[:, :, 1:],
        ],
        axis=2,
    )
    cand_values = jnp.concatenate(
        [
            near_values[:, :, :1],
            jnp.broadcast_to(vert_values[:, None], vert_shape),
            near_values[:, :, 1:],
        ],
        axis=2,
    )
    cand_blocks = jnp.concatenate(
        [
            jnp.broadcast_to(query_blocks[None, :, None], (heads_kv, per_device, 1)),
            jnp.broadcast_to(verticals[:, None, :], (heads_kv, per_device, NV)),
            slash_blocks,
        ],
        axis=-1,
    )
    candidate_valid = jnp.concatenate(
        [jnp.ones((heads_kv, per_device, 1), jnp.bool_), vertical_valid, slash_valid], axis=-1
    )
    lower_tri = jnp.arange(MASK_BLOCK_SIZE)[:, None] >= jnp.arange(MASK_BLOCK_SIZE)[None, :]
    causal = (cand_blocks < query_blocks[None, :, None])[..., None, None] | lower_tri[
        None, None, None
    ]
    visible = (
        (candidate_valid[..., None, None] & causal)
        .transpose(0, 1, 3, 2, 4)
        .reshape(heads_kv, per_device, MASK_BLOCK_SIZE, cand_count * MASK_BLOCK_SIZE)
    )
    q_heads = queries.reshape(
        per_device, MASK_BLOCK_SIZE, heads_kv, query_per_key_head, head_dim
    ).transpose(2, 0, 1, 3, 4)
    grad_heads = output_cotangent.reshape(
        per_device, MASK_BLOCK_SIZE, heads_kv, query_per_key_head, head_dim
    ).transpose(2, 0, 1, 3, 4)
    products = output_cotangent.astype(jnp.float32) * forward_output.astype(jnp.float32)
    delta_rows = jnp.sum(
        products.reshape(per_device, MASK_BLOCK_SIZE, heads_kv, query_per_key_head, head_dim),
        axis=-1,
    )
    delta_heads = delta_rows.transpose(2, 0, 1, 3)
    flat_keys = cand_keys.reshape(heads_kv, per_device, cand_count * MASK_BLOCK_SIZE, head_dim)
    flat_values = cand_values.reshape(heads_kv, per_device, cand_count * MASK_BLOCK_SIZE, head_dim)
    query_part, key_part, value_part = lax.map(
        head_pass, (q_heads, grad_heads, delta_heads, flat_keys, flat_values, visible)
    )
    query_grad = (
        query_part.transpose(1, 2, 0, 3, 4)
        .reshape(row_count, heads_kv * query_per_key_head * head_dim)
        .astype(jnp.bfloat16)
    )
    key_part = key_part.reshape(heads_kv, per_device, cand_count, MASK_BLOCK_SIZE, head_dim)
    value_part = value_part.reshape(heads_kv, per_device, cand_count, MASK_BLOCK_SIZE, head_dim)
    near_key_part = jnp.concatenate([key_part[:, :, :1], key_part[:, :, 1 + NV :]], axis=2)
    near_value_part = jnp.concatenate([value_part[:, :, :1], value_part[:, :, 1 + NV :]], axis=2)
    blank_window = jnp.zeros((window_blocks, MASK_BLOCK_SIZE, heads_kv, head_dim), jnp.float32)
    near_key_flat = (
        blank_window.at[local_at, :, head_grid]
        .add(near_key_part)
        .reshape(window_blocks * MASK_BLOCK_SIZE, features)
    )
    near_value_flat = (
        blank_window.at[local_at, :, head_grid]
        .add(near_value_part)
        .reshape(window_blocks * MASK_BLOCK_SIZE, features)
    )

    def portion(flat_rows, distance):
        lower_row = (WDEV - distance) * row_count
        return flat_rows[lower_row : lower_row + row_count]

    home_keys = near_key_flat[WDEV * row_count :]
    home_values = near_value_flat[WDEV * row_count :]
    prior_key_sum = jnp.zeros((row_count, features), jnp.float32)
    prior_value_sum = jnp.zeros((row_count, features), jnp.float32)
    for distance in range(1, WDEV + 1):
        back_keys, back_values = from_behind(
            (portion(near_key_flat, distance), portion(near_value_flat, distance)), "ctx", -distance
        )
        wrapped = my_index + distance >= devices
        home_keys = home_keys + jnp.where(wrapped, 0.0, back_keys)
        home_values = home_values + jnp.where(wrapped, 0.0, back_values)
        prior_key_sum = prior_key_sum + jnp.where(wrapped, back_keys, 0.0)
        prior_value_sum = prior_value_sum + jnp.where(wrapped, back_values, 0.0)
    vert_key_grad, vert_value_grad = lax.psum(
        (
            jnp.sum(key_part[:, :, 1 : 1 + NV], axis=1),
            jnp.sum(value_part[:, :, 1 : 1 + NV], axis=1),
        ),
        "ctx",
    )
    blank_local = jnp.zeros((local_blocks, MASK_BLOCK_SIZE, heads_kv, head_dim), jnp.float32)
    owned_keys = (
        blank_local.at[vert_local, :, head_numbers]
        .add(jnp.where(owned_view, vert_key_grad, 0.0))
        .reshape(regions, row_count, features)
    )
    owned_values = (
        blank_local.at[vert_local, :, head_numbers]
        .add(jnp.where(owned_view, vert_value_grad, 0.0))
        .reshape(regions, row_count, features)
    )
    region_ids = jnp.arange(regions)[:, None, None]
    key_total = (
        owned_keys
        + jnp.where(region_ids == present_slab, home_keys[None], 0.0)
        + jnp.where(region_ids == present_slab - 1, prior_key_sum[None], 0.0)
    )
    value_total = (
        owned_values
        + jnp.where(region_ids == present_slab, home_values[None], 0.0)
        + jnp.where(region_ids == present_slab - 1, prior_value_sum[None], 0.0)
    )
    return (query_grad, key_total.astype(jnp.bfloat16), value_total.astype(jnp.bfloat16))


def solution(mesh):
    in_specs = (
        P(("groups", "ctx"), None),
        P("groups", "ctx", None),
        P("groups", "ctx", None),
        P(("groups", "ctx"), None),
        P(("groups", "ctx"), None),
        P("groups", None),
        P("groups", None),
        P("groups"),
    )
    out_specs = (P(("groups", "ctx"), None), P("groups", "ctx", None), P("groups", "ctx", None))
    return jax.shard_map(shards, mesh=mesh, in_specs=in_specs, out_specs=out_specs, check_vma=False)
```

profile of v0, /device:TPU:0, one launch (start us, length us, event | category | flops | bytes accessed | tf_op | source)
XLA Modules:
  0.0 414.9 jit_solution(1168465586102998522)
XLA Ops:
  22.3 4.0 reshape.188
  28.7 3.5 copy.119
  34.1 3.0 gather_fusion.1
  37.1 3.1 gather_fusion.3
  45.5 76.4 %all-reduce.6 = (bf16[4,8,64,128]{3,2,1,0:T(8,128)(2,1)}, bf16[4,8,64,128]{3,2,1,0:T(8,128)(2,1)}) all-reduce(f32[4,8,64,128]{3,2,1,0:T(8,128)S(1)} %get-tuple-element.163, f32[4,8,64,128]{3,2,1,0:T(8,128)S(1)} %get-tuple-element.162), channel_id=1, replica_groups=mesh['groups'=2,'ctx'=16] {'ctx'}, use_global_device_ids=true, to_apply=%region_1.2 | all-reduce | flops 524288 | bytes 3145728 | tf_op jit(solution)/shard_map/psum | solution.py:111
  140.9 7.8 %collective-permute-done = bf16[128,512]{1,0:T(8,128)(2,1)S(1)} collective-permute-done((bf16[128,512]{1,0:T(8,128)(2,1)}, bf16[128,512]{1,0:T(8,128)(2,1)S(1)}, u32[]{:S(2)}, u32[]{:S(2)}) %collective-permute-start) | collective-permute-done | bytes 131104 | tf_op jit(solution)/shard_map/ppermute | solution.py:16
  164.9 42.9 %while.14 = (s32[]{:T(128)}, bf16[4,2,64,8,128]{4,3,2,1,0:T(8,128)(2,1)}, f32[4,2,768,128]{3,2,1,0:T(8,128)}, f32[4,2,768,128]{3,2,1,0:T(8,128)}, pred[4,2,64,76...) while((s32[]{:T(128)}, ...), condition=%wide.region_7.8_spmd, body=%wide.region_4.7_spmd.sunk | while | flops 1020328960 | bytes 26645648 | solution.py:181
  233.4 3.9 collective-permute-start.15
  237.3 3.4 collective-permute-done.11
  240.7 5.2 %collective-permute-start.16 = (f32[128,512]{1,0:T(8,128)S(1)}, f32[128,512]{1,0:T(8,128)S(1)}, u32[]{:S(2)}, u32[]{:S(2)}) collective-permute-start(f32[128,512]{1,0:T(8,128)S(1)} %bitcast.291), channel_id=1, source_target_pairs={{0,14},{1,15},{2,0},{3,1},{4,2},{5,3},{6,4},{7,5},{8,6},{9,7},{10,... | collective-permute-start | bytes 786440 | tf_op jit(solution)/shard_map/ppermute | solution.py:16
  248.3 3.8 collective-permute-start.17
  254.8 4.2 %collective-permute-start.18 = (f32[128,512]{1,0:T(8,128)S(1)}, f32[128,512]{1,0:T(8,128)S(1)}, u32[]{:S(2)}, u32[]{:S(2)}) collective-permute-start(f32[128,512]{1,0:T(8,128)S(1)} %bitcast.293), channel_id=1, source_target_pairs={{0,12},{1,13},{2,14},{3,15},{4,0},{5,1},{6,2},{7,3},{8,4},{9,5},{1... | collective-permute-start | bytes 786440 | tf_op jit(solution)/shard_map/ppermute | solution.py:16
  260.2 3.9 collective-permute-start.19
  265.7 5.6 %collective-permute-done.16 = f32[128,512]{1,0:T(8,128)S(1)} collective-permute-done((f32[128,512]{1,0:T(8,128)S(1)}, f32[128,512]{1,0:T(8,128)S(1)}, u32[]{:S(2)}, u32[]{:S(2)}) %collective-permute-start.16) | collective-permute-done | bytes 262176 | tf_op jit(solution)/shard_map/ppermute | solution.py:16
  271.4 5.6 %collective-permute-done.17 = f32[128,512]{1,0:T(8,128)S(1)} collective-permute-done((f32[128,512]{1,0:T(8,128)S(1)}, f32[128,512]{1,0:T(8,128)S(1)}, u32[]{:S(2)}, u32[]{:S(2)}) %collective-permute-start.17) | collective-permute-done | bytes 262176 | tf_op jit(solution)/shard_map/ppermute | solution.py:16
  277.0 3.2 collective-permute-done.18
  283.3 73.9 %all-reduce.5.cloned.1.call-done = (f32[4,8,64,128]{3,2,1,0:T(8,128)}, f32[4,8,64,128]{3,2,1,0:T(8,128)}) async-done(((f32[4,8,64,128]{3,2,1,0:T(8,128)}, f32[4,8,64,128]{3,2,1,0:T(8,128)}), (f32[4,8,64,128]{3,2,1,0:T(8,128)}, f32[4,8,64,128]{3,2,1,0:T(8,128)})) %all-reduce.5.cloned.1.call-update) | async-done | bytes 2097168 | tf_op jit(solution)/shard_map/psum | solution.py:222
  361.5 5.2 %scatter_fusion = f32[32,64,4,128]{3,1,2,0:T(8,128)} fusion(f32[32,64,4,128]{3,1,2,0:T(8,128)} %broadcast_in_dim.233.clone.1, s32[32]{0:T(128)S(1)} %reshape.223, f32[32,64,128]{2,1,0:T(8,128)S(1)} %bitcast.260), kind=kCustom, calls=%fused_computation.4 | custom fusion | flops 262144 | bytes 3145984 | tf_op jit(solution)/shard_map/scatter-add | solution.py:232
  366.7 7.8 %copy.126 = f32[32,64,4,128]{3,2,1,0:T(4,128)} copy(f32[32,64,4,128]{3,1,2,0:T(8,128)} %scatter_fusion) | data formatting | bytes 8388608 | tf_op jit(solution)/shard_map/scatter-add | solution.py:232
  374.5 5.5 %reshape.196 = f32[16,128,512]{2,1,0:T(8,128)} reshape(f32[32,64,4,128]{3,2,1,0:T(4,128)} %copy.126) | data formatting | bytes 8388608 | tf_op jit(solution)/shard_map/reshape | solution.py:233
  382.4 5.1 %scatter_fusion.2 = f32[32,64,4,128]{3,1,2,0:T(8,128)} fusion(f32[32,64,4,128]{3,1,2,0:T(8,128)} %broadcast_in_dim.233.clone, s32[32]{0:T(128)S(1)} %reshape.223, f32[32,64,128]{2,1,0:T(8,128)S(1)} %bitcast.259), kind=kCustom, calls=%fused_computation.6 | custom fusion | flops 262144 | bytes 3145984 | tf_op jit(solution)/shard_map/scatter-add | solution.py:237
  387.6 7.8 %copy.134 = f32[32,64,4,128]{3,2,1,0:T(4,128)} copy(f32[32,64,4,128]{3,1,2,0:T(8,128)} %scatter_fusion.2) | data formatting | bytes 8388608 | tf_op jit(solution)/shard_map/scatter-add | solution.py:237
  395.3 5.5 %reshape.198 = f32[16,128,512]{2,1,0:T(8,128)} reshape(f32[32,64,4,128]{3,2,1,0:T(4,128)} %copy.134) | data formatting | bytes 8388608 | tf_op jit(solution)/shard_map/reshape | solution.py:238
  400.9 7.2 %add_convert_fusion = (bf16[16,128,512]{2,1,0:T(8,128)(2,1)}, bf16[16,128,512]{2,1,0:T(8,128)(2,1)}) fusion(f32[16,128,512]{2,1,0:T(8,128)} %reshape.198, f32[128,512]{1,0:T(8,128)S(1)} %get-tuple-element.153, f32[128,512]{1,0:T(8,128)S(1)} %get-tuple-element.152, pred[16]{0:T(512)(128)(4,1)S(1)} %copy-done.13, pred[16]{0:T(512)(128)(4,1)S(1)} %copy-done.14, ...), kind=kLoop, calls=%fused_computation.53 | loop fusion | flops 10485760 | bytes 13631520 | tf_op jit(solution)/shard_map/convert_element_type | solution.py:251
  (225 shorter events, 144.9 us)
Async XLA Ops:
  7.2 350.1 %all-reduce.5.cloned.1.call-start = ((), (), s32[]{:S(2)}) async-start(), calls=%async_computation | async-start | bytes 4194304 | tf_op jit(solution)/shard_map/psum | solution.py:222
  9.8 123.7 %collective-permute-start.5 = (bf16[128,512]{1,0:T(8,128)(2,1)}, bf16[128,512]{1,0:T(8,128)(2,1)}, u32[]{:S(2)}, u32[]{:S(2)}) collective-permute-start(bf16[128,512]{1,0:T(8,128)(2,1)} %get-tuple-element.134), channel_id=1, source_target_pairs={{0,5},{1,6},{2,7},{3,8},{4,9},{5,10},{6,11},{7,12},{8,13},{9,14},{... | collective-permute-start | bytes 393224 | tf_op jit(solution)/shard_map/ppermute | solution.py:16
  12.2 122.1 %collective-permute-start.6 = (bf16[128,512]{1,0:T(8,128)(2,1)}, bf16[128,512]{1,0:T(8,128)(2,1)}, u32[]{:S(2)}, u32[]{:S(2)}) collective-permute-start(bf16[128,512]{1,0:T(8,128)(2,1)} %get-tuple-element.133), channel_id=1, source_target_pairs={{0,4},{1,5},{2,6},{3,7},{4,8},{5,9},{6,10},{7,11},{8,12},{9,13},{1... | collective-permute-start | bytes 393224 | tf_op jit(solution)/shard_map/ppermute | solution.py:16
  13.8 121.6 %collective-permute-start.7 = (bf16[128,512]{1,0:T(8,128)(2,1)}, bf16[128,512]{1,0:T(8,128)(2,1)}, u32[]{:S(2)}, u32[]{:S(2)}) collective-permute-start(bf16[128,512]{1,0:T(8,128)(2,1)} %get-tuple-element.132), channel_id=1, source_target_pairs={{0,3},{1,4},{2,5},{3,6},{4,7},{5,8},{6,9},{7,10},{8,11},{9,12},{10... | collective-permute-start | bytes 393224 | tf_op jit(solution)/shard_map/ppermute | solution.py:16
  16.3 120.1 %collective-permute-start.8 = (bf16[128,512]{1,0:T(8,128)(2,1)}, bf16[128,512]{1,0:T(8,128)(2,1)}, u32[]{:S(2)}, u32[]{:S(2)}) collective-permute-start(bf16[128,512]{1,0:T(8,128)(2,1)} %get-tuple-element.131), channel_id=1, source_target_pairs={{0,2},{1,3},{2,4},{3,5},{4,6},{5,7},{6,8},{7,9},{8,10},{9,11},{10,... | collective-permute-start | bytes 393224 | tf_op jit(solution)/shard_map/ppermute | solution.py:16
  17.8 121.1 %collective-permute-start.9 = (bf16[128,512]{1,0:T(8,128)(2,1)}, bf16[128,512]{1,0:T(8,128)(2,1)}, u32[]{:S(2)}, u32[]{:S(2)}) collective-permute-start(bf16[128,512]{1,0:T(8,128)(2,1)} %get-tuple-element.130), channel_id=1, source_target_pairs={{0,1},{1,2},{2,3},{3,4},{4,5},{5,6},{6,7},{7,8},{8,9},{9,10},{10,1... | collective-permute-start | bytes 393224 | tf_op jit(solution)/shard_map/ppermute | solution.py:16
  37.1 84.8 %copy-start = (bf16[128,4096]{1,0:T(8,128)(2,1)S(1)}, bf16[128,4096]{1,0:T(8,128)(2,1)}, u32[]{:S(2)}) copy-start(bf16[128,4096]{1,0:T(8,128)(2,1)} %param.14) | copy-start | bytes 3145732
  45.5 79.2 %copy-start.7 = (pred[4,2,768]{2,1,0:T(4,128)(4,1)S(1)}, pred[4,2,768]{2,1,0:T(4,128)(4,1)}, u32[]{:S(2)}) copy-start(pred[4,2,768]{2,1,0:T(4,128)(4,1)} %copy.116) | copy-start | bytes 18436
  133.4 15.3 %collective-permute-start = (bf16[128,512]{1,0:T(8,128)(2,1)}, bf16[128,512]{1,0:T(8,128)(2,1)S(1)}, u32[]{:S(2)}, u32[]{:S(2)}) collective-permute-start(bf16[128,512]{1,0:T(8,128)(2,1)} %get-tuple-element.139), channel_id=1, source_target_pairs={{0,5},{1,6},{2,7},{3,8},{4,9},{5,10},{6,11},{7,12},{8,13},{9,14},{... | collective-permute-start | bytes 393224 | tf_op jit(solution)/shard_map/ppermute | solution.py:16
  134.4 15.0 %collective-permute-start.1 = (bf16[128,512]{1,0:T(8,128)(2,1)}, bf16[128,512]{1,0:T(8,128)(2,1)S(1)}, u32[]{:S(2)}, u32[]{:S(2)}) collective-permute-start(bf16[128,512]{1,0:T(8,128)(2,1)} %get-tuple-element.138), channel_id=1, source_target_pairs={{0,4},{1,5},{2,6},{3,7},{4,8},{5,9},{6,10},{7,11},{8,12},{9,13},{1... | collective-permute-start | bytes 393224 | tf_op jit(solution)/shard_map/ppermute | solution.py:16
  135.4 14.7 %collective-permute-start.2 = (bf16[128,512]{1,0:T(8,128)(2,1)}, bf16[128,512]{1,0:T(8,128)(2,1)S(1)}, u32[]{:S(2)}, u32[]{:S(2)}) collective-permute-start(bf16[128,512]{1,0:T(8,128)(2,1)} %get-tuple-element.137), channel_id=1, source_target_pairs={{0,3},{1,4},{2,5},{3,6},{4,7},{5,8},{6,9},{7,10},{8,11},{9,12},{10... | collective-permute-start | bytes 393224 | tf_op jit(solution)/shard_map/ppermute | solution.py:16
  136.4 16.9 %collective-permute-start.3 = (bf16[128,512]{1,0:T(8,128)(2,1)}, bf16[128,512]{1,0:T(8,128)(2,1)}, u32[]{:S(2)}, u32[]{:S(2)}) collective-permute-start(bf16[128,512]{1,0:T(8,128)(2,1)} %get-tuple-element.136), channel_id=1, source_target_pairs={{0,2},{1,3},{2,4},{3,5},{4,6},{5,7},{6,8},{7,9},{8,10},{9,11},{10,... | collective-permute-start | bytes 393224 | tf_op jit(solution)/shard_map/ppermute | solution.py:16
  138.8 16.0 %collective-permute-start.4 = (bf16[128,512]{1,0:T(8,128)(2,1)}, bf16[128,512]{1,0:T(8,128)(2,1)}, u32[]{:S(2)}, u32[]{:S(2)}) collective-permute-start(bf16[128,512]{1,0:T(8,128)(2,1)} %get-tuple-element.135), channel_id=1, source_target_pairs={{0,1},{1,2},{2,3},{3,4},{4,5},{5,6},{6,7},{7,8},{8,9},{9,10},{10,1... | collective-permute-start | bytes 393224 | tf_op jit(solution)/shard_map/ppermute | solution.py:16
  220.1 13.4 %collective-permute-start.10 = (f32[128,512]{1,0:T(8,128)}, f32[128,512]{1,0:T(8,128)}, u32[]{:S(2)}, u32[]{:S(2)}) collective-permute-start(f32[128,512]{1,0:T(8,128)} %bitcast.218), channel_id=1, source_target_pairs={{0,15},{1,0},{2,1},{3,2},{4,3},{5,4},{6,5},{7,6},{8,7},{9,8},{10,9... | collective-permute-start | bytes 786440 | tf_op jit(solution)/shard_map/ppermute | solution.py:16
  220.9 19.8 %collective-permute-start.11 = (f32[128,512]{1,0:T(8,128)}, f32[128,512]{1,0:T(8,128)}, u32[]{:S(2)}, u32[]{:S(2)}) collective-permute-start(f32[128,512]{1,0:T(8,128)} %bitcast.217), channel_id=1, source_target_pairs={{0,14},{1,15},{2,0},{3,1},{4,2},{5,3},{6,4},{7,5},{8,6},{9,7},{10,... | collective-permute-start | bytes 786440 | tf_op jit(solution)/shard_map/ppermute | solution.py:16
  221.9 26.4 %collective-permute-start.12 = (f32[128,512]{1,0:T(8,128)}, f32[128,512]{1,0:T(8,128)}, u32[]{:S(2)}, u32[]{:S(2)}) collective-permute-start(f32[128,512]{1,0:T(8,128)} %bitcast.216), channel_id=1, source_target_pairs={{0,13},{1,14},{2,15},{3,0},{4,1},{5,2},{6,3},{7,4},{8,5},{9,6},{10... | collective-permute-start | bytes 786440 | tf_op jit(solution)/shard_map/ppermute | solution.py:16
  223.3 31.5 %collective-permute-start.13 = (f32[128,512]{1,0:T(8,128)}, f32[128,512]{1,0:T(8,128)}, u32[]{:S(2)}, u32[]{:S(2)}) collective-permute-start(f32[128,512]{1,0:T(8,128)} %bitcast.215), channel_id=1, source_target_pairs={{0,12},{1,13},{2,14},{3,15},{4,0},{5,1},{6,2},{7,3},{8,4},{9,5},{1... | collective-permute-start | bytes 786440 | tf_op jit(solution)/shard_map/ppermute | solution.py:16
  224.5 35.7 %collective-permute-start.14 = (f32[128,512]{1,0:T(8,128)}, f32[128,512]{1,0:T(8,128)}, u32[]{:S(2)}, u32[]{:S(2)}) collective-permute-start(f32[128,512]{1,0:T(8,128)} %bitcast.214), channel_id=1, source_target_pairs={{0,11},{1,12},{2,13},{3,14},{4,15},{5,0},{6,1},{7,2},{8,3},{9,4},{... | collective-permute-start | bytes 786440 | tf_op jit(solution)/shard_map/ppermute | solution.py:16
  232.1 125.1 %copy-start.12 = (pred[4,8]{1,0:T(4,128)(4,1)S(1)}, pred[4,8]{1,0:T(4,128)(4,1)}, u32[]{:S(2)}) copy-start(pred[4,8]{1,0:T(4,128)(4,1)} %copy-done.11) | copy-start | bytes 100
  233.4 32.3 %collective-permute-start.15 = (f32[128,512]{1,0:T(8,128)S(1)}, f32[128,512]{1,0:T(8,128)S(1)}, u32[]{:S(2)}, u32[]{:S(2)}) collective-permute-start(f32[128,512]{1,0:T(8,128)S(1)} %bitcast.290), channel_id=1, source_target_pairs={{0,15},{1,0},{2,1},{3,2},{4,3},{5,4},{6,5},{7,6},{8,7},{9,8},{10,9... | collective-permute-start | bytes 786440 | tf_op jit(solution)/shard_map/ppermute | solution.py:16
  240.7 30.6 %collective-permute-start.16 = (f32[128,512]{1,0:T(8,128)S(1)}, f32[128,512]{1,0:T(8,128)S(1)}, u32[]{:S(2)}, u32[]{:S(2)}) collective-permute-start(f32[128,512]{1,0:T(8,128)S(1)} %bitcast.291), channel_id=1, source_target_pairs={{0,14},{1,15},{2,0},{3,1},{4,2},{5,3},{6,4},{7,5},{8,6},{9,7},{10,... | collective-permute-start | bytes 786440 | tf_op jit(solution)/shard_map/ppermute | solution.py:16
  248.3 28.7 %collective-permute-start.17 = (f32[128,512]{1,0:T(8,128)S(1)}, f32[128,512]{1,0:T(8,128)S(1)}, u32[]{:S(2)}, u32[]{:S(2)}) collective-permute-start(f32[128,512]{1,0:T(8,128)S(1)} %bitcast.292), channel_id=1, source_target_pairs={{0,13},{1,14},{2,15},{3,0},{4,1},{5,2},{6,3},{7,4},{8,5},{9,6},{10... | collective-permute-start | bytes 786440 | tf_op jit(solution)/shard_map/ppermute | solution.py:16
  254.8 25.4 %collective-permute-start.18 = (f32[128,512]{1,0:T(8,128)S(1)}, f32[128,512]{1,0:T(8,128)S(1)}, u32[]{:S(2)}, u32[]{:S(2)}) collective-permute-start(f32[128,512]{1,0:T(8,128)S(1)} %bitcast.293), channel_id=1, source_target_pairs={{0,12},{1,13},{2,14},{3,15},{4,0},{5,1},{6,2},{7,3},{8,4},{9,5},{1... | collective-permute-start | bytes 786440 | tf_op jit(solution)/shard_map/ppermute | solution.py:16
  260.2 22.9 %collective-permute-start.19 = (f32[128,512]{1,0:T(8,128)}, f32[128,512]{1,0:T(8,128)S(1)}, u32[]{:S(2)}, u32[]{:S(2)}) collective-permute-start(f32[128,512]{1,0:T(8,128)} %bitcast.209), channel_id=1, source_target_pairs={{0,11},{1,12},{2,13},{3,14},{4,15},{5,0},{6,1},{7,2},{8,3},{9,4},{... | collective-permute-start | bytes 786440 | tf_op jit(solution)/shard_map/ppermute | solution.py:16
  (15 other events, 75.4 us)
Sparse Core Ops, SparseCore 0:
  214.3 142.8 all-reduce.4
where the time goes:
time: 417 us; the launch traced here: 415 us
  waiting for transfers between devices  109 us (26%)
  local copies, waits for them, and re-layouts  96 us (23%)
  blocking collectives  76.4 us (18%)
  other arithmetic  50.8 us (12%)
  matrix products  34.3 us (8%)
  starting transfers between devices  32.9 us (8%)
  between operations  15.2 us (4%)
    psum x1, blocking collectives, shards(): vert_keys, vert_values = lax.psum((picked_keys, picked_values), 'ctx')  76.4 us
    psum x1, waiting for transfers between devices, shards(): lax.psum((jnp.sum(key_part[:, :, 1:1 + NV], axis=1), jnp.sum(value_part[:...  73.9 us
    ppermute x20, waiting for transfers between devices, from_behind(): lax.ppermute(shard, axis, [(i, (i + by) % peers) for i in range(peers)])  35.2 us
    ppermute x20, starting transfers between devices, from_behind(): lax.ppermute(shard, axis, [(i, (i + by) % peers) for i in range(peers)])  32.9 us
    unnamed x52, local copies, waits for them, and re-layouts  19 us
    dot_general x4, matrix products, head_pass(): jnp.einsum('jrgd,jkd->jrgk', grad_head, values_cand, preferred_element_ty...  9.6 us
    dot_general x4, matrix products, head_pass(): jnp.einsum('jrgk,jrgd->jkd', weights_low, grad_head, preferred_element_ty...  9.26 us
  transfers between devices with their start and end apart: 21, of which 11 were waited for; matrix products, arithmetic and copies ran while one was open for 17% of the time, Pallas kernels for 0%

commit v1 on v0

v1 whole, which is shorter than its diff:
```python
import functools
import math

import jax
import jax.numpy as jnp
from jax import lax
from jax.experimental import pallas as pl
from jax.experimental.pallas import tpu as pltpu
from jax.sharding import PartitionSpec as P

BLOCK = 64
WDEV = 5
VMEM_LIMIT = 40 * 1024 * 1024
BF16 = jnp.bfloat16
F32 = jnp.float32


def from_behind(shard, by):
    peers = lax.axis_size("ctx")
    return lax.ppermute(shard, "ctx", [(i, (i + by) % peers) for i in range(peers)])


def pack_kernel(place, verts, keys, values, *rest, devices, heads, nv, per_device):
    sends, picked, sems, pick_sems = rest[:WDEV], rest[WDEV], rest[WDEV + 1], rest[WDEV + 2]
    slab, me = place[0], place[1]
    head_dim = picked.shape[2]
    copies = []
    for distance in range(1, WDEV + 1):
        region = slab - (me + distance >= devices).astype(jnp.int32)
        for kv, source in enumerate((keys, values)):
            copy = pltpu.make_async_copy(
                source.at[region], sends[distance - 1].at[kv], sems.at[distance - 1, kv]
            )
            copy.start()
            copies.append(copy)
    picked[...] = jnp.zeros_like(picked)
    slab_blocks = per_device * devices

    def unit_copy(h, m, kv, source):
        inner = verts[h, m] % slab_blocks
        region = verts[h, m] // slab_blocks
        row = pl.multiple_of((inner % per_device) * BLOCK, BLOCK)
        unit = h * nv + m
        return pltpu.make_async_copy(
            source.at[region, pl.ds(row, BLOCK), pl.ds(h * head_dim, head_dim)],
            picked.at[kv, pl.ds(unit * BLOCK, BLOCK), :],
            pick_sems.at[kv, unit],
        )

    def owned(h, m):
        return (verts[h, m] % slab_blocks) // per_device == me

    for h in range(heads):
        for m in range(nv):

            @pl.when(owned(h, m))
            def _():
                unit_copy(h, m, 0, keys).start()
                unit_copy(h, m, 1, values).start()

    for h in range(heads):
        for m in range(nv):

            @pl.when(owned(h, m))
            def _():
                unit_copy(h, m, 0, keys).wait()
                unit_copy(h, m, 1, values).wait()

    for copy in copies:
        copy.wait()


def pack(place, verticals, keys, values, devices):
    regions, rows, features = keys.shape
    heads, nv = verticals.shape
    head_dim = features // heads
    smem = pl.BlockSpec(memory_space=pltpu.SMEM)
    hbm = pl.BlockSpec(memory_space=pl.ANY)
    return pl.pallas_call(
        functools.partial(
            pack_kernel, devices=devices, heads=heads, nv=nv, per_device=rows // BLOCK
        ),
        in_specs=[smem, smem, hbm, hbm],
        out_specs=[hbm] * WDEV + [pl.BlockSpec(memory_space=pltpu.VMEM)],
        out_shape=[jax.ShapeDtypeStruct((2, rows, features), BF16)] * WDEV
        + [jax.ShapeDtypeStruct((2, heads * nv * BLOCK, head_dim), BF16)],
        scratch_shapes=[
            pltpu.SemaphoreType.DMA((WDEV, 2)),
            pltpu.SemaphoreType.DMA((2, heads * nv)),
        ],
        compiler_params=pltpu.CompilerParams(vmem_limit_bytes=VMEM_LIMIT),
    )(place, verticals, keys, values)


def attend_kernel(
    place, verts, offs, q, grad, out, keys, values, vert, *rest,
    devices, heads, nv, ns, per_device,
):
    recv = rest[:WDEV]
    dq, near, home, vgrad = rest[WDEV : WDEV + 4]
    (win, vkv, kc, vc, qs, gs, s_ref, dp_ref, w_ref, ds_ref, nacc, vacc, sems) = rest[WDEV + 4 :]
    h, j = pl.program_id(0), pl.program_id(1)
    slab, me = place[0], place[1]
    head_dim = kc.shape[1]
    group = q.shape[1] // head_dim
    cand = 1 + nv + ns
    scaling = 1.0 / math.sqrt(head_dim)
    rows = per_device * BLOCK
    block = slab * (per_device * devices) + me * per_device + j
    lanes = pl.ds(pl.multiple_of(h * head_dim, head_dim), head_dim)

    @pl.when((h == 0) & (j == 0))
    def _():
        copies = [
            pltpu.make_async_copy(
                recv[d - 1], win.at[:, pl.ds((WDEV - d) * rows, rows), :], sems.at[d - 1]
            )
            for d in range(1, WDEV + 1)
        ]
        own_rows = pl.ds(WDEV * rows, rows)
        copies.append(pltpu.make_async_copy(keys.at[slab], win.at[0, own_rows, :], sems.at[WDEV]))
        copies.append(
            pltpu.make_async_copy(values.at[slab], win.at[1, own_rows, :], sems.at[WDEV + 1])
        )
        copies.append(pltpu.make_async_copy(vert, vkv, sems.at[WDEV + 2]))
        for copy in copies:
            copy.start()
        nacc[...] = jnp.zeros_like(nacc)
        for copy in copies:
            copy.wait()

    own_at = pl.multiple_of((WDEV * per_device + j) * BLOCK, BLOCK)
    slash_at = [
        pl.multiple_of((WDEV * per_device + j - offs[h, s]) * BLOCK, BLOCK) for s in range(ns)
    ]
    vert_at = pl.multiple_of(h * (nv * BLOCK), nv * BLOCK)
    valid = [None]
    for m in range(nv):
        valid.append(verts[h, m] < block)
    for s in range(ns):
        collide = verts[h, 0] == block - offs[h, s]
        for m in range(1, nv):
            collide = collide | (verts[h, m] == block - offs[h, s])
        valid.append((offs[h, s] > 0) & jnp.logical_not(collide))
    for kv, to in enumerate((kc, vc)):
        to[0:BLOCK, :] = win[kv, pl.ds(own_at, BLOCK), lanes]
        to[BLOCK : (1 + nv) * BLOCK, :] = vkv[kv, pl.ds(vert_at, nv * BLOCK), :]
        for s in range(ns):
            to[(1 + nv + s) * BLOCK : (2 + nv + s) * BLOCK, :] = win[
                kv, pl.ds(slash_at[s], BLOCK), lanes
            ]
    products = []
    for g in range(group):
        cols = slice(g * head_dim, (g + 1) * head_dim)
        qs[g * BLOCK : (g + 1) * BLOCK, :] = q[:, cols]
        gs[g * BLOCK : (g + 1) * BLOCK, :] = grad[:, cols]
        products.append(grad[:, cols].astype(F32) * out[:, cols].astype(F32))
    width = group * BLOCK
    delta = jnp.sum(jnp.transpose(jnp.concatenate(products, axis=0)), axis=0, keepdims=True)

    nt = (((1,), (1,)), ((), ()))
    s_ref[...] = lax.dot_general(kc[...], qs[...], nt, preferred_element_type=F32)
    dp_ref[...] = lax.dot_general(vc[...], gs[...], nt, preferred_element_type=F32)

    log2_scale = scaling * math.log2(math.e)
    neg = jnp.float32(-jnp.inf)
    key_at = lax.broadcasted_iota(jnp.int32, (BLOCK, width), 0)
    row_at = lax.broadcasted_iota(jnp.int32, (BLOCK, width), 1) % BLOCK
    s_ref[0:BLOCK, :] = jnp.where(key_at <= row_at, s_ref[0:BLOCK, :], neg)

    def scaled(c):
        t = s_ref[c * BLOCK : (c + 1) * BLOCK, :] * log2_scale
        if c > 0:
            t = t + jnp.where(valid[c], jnp.float32(0), neg)
        return t

    def fold(x, op):
        y = x[0:8, :]
        for r in range(1, BLOCK // 8):
            y = op(y, x[r * 8 : (r + 1) * 8, :])
        return y

    top = fold(scaled(0), jnp.maximum)
    for c in range(1, cand):
        top = jnp.maximum(top, fold(scaled(c), jnp.maximum))
    top = jnp.max(top, axis=0, keepdims=True)
    total = jnp.zeros((8, width), F32)
    for c in range(cand):
        p = jnp.exp2(scaled(c) - top)
        s_ref[c * BLOCK : (c + 1) * BLOCK, :] = p
        total = total + fold(p, jnp.add)
    inverse = 1.0 / jnp.sum(total, axis=0, keepdims=True)
    for c in range(cand):
        span = slice(c * BLOCK, (c + 1) * BLOCK)
        w = s_ref[span, :] * inverse
        w_ref[span, :] = w.astype(BF16)
        ds_ref[span, :] = (w * (dp_ref[span, :] - delta)).astype(BF16)

    dv = jnp.dot(w_ref[...], gs[...], preferred_element_type=F32)
    dk = jnp.dot(ds_ref[...], qs[...], preferred_element_type=F32) * scaling
    dqt = lax.dot_general(
        kc[...], ds_ref[...], (((0,), (0,)), ((), ())), preferred_element_type=F32
    )
    dqr = (jnp.transpose(dqt) * scaling).astype(BF16)
    for g in range(group):
        dq[:, g * head_dim : (g + 1) * head_dim] = dqr[g * BLOCK : (g + 1) * BLOCK, :]

    for kv, part in enumerate((dk, dv)):
        nacc[kv, pl.ds(own_at, BLOCK), lanes] += part[0:BLOCK]
        for s in range(ns):
            nacc[kv, pl.ds(slash_at[s], BLOCK), lanes] += part[
                (1 + nv + s) * BLOCK : (2 + nv + s) * BLOCK
            ]
        verticals_part = part[BLOCK : (1 + nv) * BLOCK]

        @pl.when(j == 0)
        def _():
            vacc[kv] = verticals_part

        @pl.when(j > 0)
        def _():
            vacc[kv] += verticals_part

    @pl.when(j == per_device - 1)
    def _():
        for kv in range(2):
            vgrad[kv, pl.ds(vert_at, nv * BLOCK), :] = vacc[kv].astype(BF16)
            home[kv, :, lanes] = nacc[kv, WDEV * rows :, lanes]
            for d in range(1, WDEV + 1):
                near[d - 1, kv, :, lanes] = nacc[
                    kv, (WDEV - d) * rows : (WDEV - d + 1) * rows, lanes
                ].astype(BF16)


def attend(place, verticals, offsets, queries, cotangent, output, keys, values, vert, recv, devices):
    rows, width = queries.shape
    features = keys.shape[2]
    heads, nv = verticals.shape
    ns = offsets.shape[1]
    head_dim = features // heads
    group = width // features
    per_device = rows // BLOCK
    cand = 1 + nv + ns
    smem = pl.BlockSpec(memory_space=pltpu.SMEM)
    hbm = pl.BlockSpec(memory_space=pl.ANY)
    tile = pl.BlockSpec((BLOCK, group * head_dim), lambda h, j: (j, h))

    def whole(shape):
        return pl.BlockSpec(shape, lambda h, j: (0,) * len(shape))

    near_shape = (WDEV, 2, rows, features)
    home_shape = (2, rows, features)
    vert_shape = (2, heads * nv * BLOCK, head_dim)
    return pl.pallas_call(
        functools.partial(
            attend_kernel, devices=devices, heads=heads, nv=nv, ns=ns, per_device=per_device
        ),
        grid=(heads, per_device),
        in_specs=[smem] * 3 + [tile] * 3 + [hbm] * (3 + WDEV),
        out_specs=[tile, whole(near_shape), whole(home_shape), whole(vert_shape)],
        out_shape=[
            jax.ShapeDtypeStruct((rows, width), BF16),
            jax.ShapeDtypeStruct(near_shape, BF16),
            jax.ShapeDtypeStruct(home_shape, F32),
            jax.ShapeDtypeStruct(vert_shape, BF16),
        ],
        scratch_shapes=[
            pltpu.VMEM((2, (WDEV + 1) * rows, features), BF16),
            pltpu.VMEM(vert_shape, BF16),
            pltpu.VMEM((cand * BLOCK, head_dim), BF16),
            pltpu.VMEM((cand * BLOCK, head_dim), BF16),
            pltpu.VMEM((group * BLOCK, head_dim), BF16),
            pltpu.VMEM((group * BLOCK, head_dim), BF16),
            pltpu.VMEM((cand * BLOCK, group * BLOCK), F32),
            pltpu.VMEM((cand * BLOCK, group * BLOCK), F32),
            pltpu.VMEM((cand * BLOCK, group * BLOCK), BF16),
            pltpu.VMEM((cand * BLOCK, group * BLOCK), BF16),
            pltpu.VMEM((2, (WDEV + 1) * rows, features), F32),
            pltpu.VMEM((2, nv * BLOCK, head_dim), F32),
            pltpu.SemaphoreType.DMA((WDEV + 3,)),
        ],
        compiler_params=pltpu.CompilerParams(vmem_limit_bytes=VMEM_LIMIT),
    )(place, verticals, offsets, queries, cotangent, output, keys, values, vert, *recv)


def assemble_kernel(place, verts, home, *rest, devices, heads, nv, per_device):
    back = rest[:WDEV]
    vert, key_out, value_out, acc = rest[WDEV:]
    slab, me = place[0], place[1]
    head_dim = vert.shape[2]
    slab_blocks = per_device * devices
    acc[0] = home[...]
    acc[1] = jnp.zeros_like(home)
    for d in range(1, WDEV + 1):
        slot = (me + d >= devices).astype(jnp.int32)
        acc[slot] += back[d - 1][...].astype(F32)
    key_out[...] = jnp.zeros_like(key_out)
    value_out[...] = jnp.zeros_like(value_out)
    outs = (key_out, value_out)
    for h in range(heads):
        lanes = slice(h * head_dim, (h + 1) * head_dim)
        for m in range(nv):
            inner = verts[h, m] % slab_blocks
            region = verts[h, m] // slab_blocks
            row = pl.multiple_of((inner % per_device) * BLOCK, BLOCK)
            at = (h * nv + m) * BLOCK

            @pl.when(inner // per_device == me)
            def _():
                close = (region == slab) | (region == slab - 1)

                @pl.when(close)
                def _():
                    for kv in range(2):
                        acc[slab - region, kv, pl.ds(row, BLOCK), lanes] += vert[
                            kv, at : at + BLOCK, :
                        ].astype(F32)

                @pl.when(jnp.logical_not(close))
                def _():
                    for kv in range(2):
                        outs[kv][region, pl.ds(row, BLOCK), lanes] = vert[kv, at : at + BLOCK, :]

    for kv in range(2):
        outs[kv][slab] = acc[0, kv].astype(BF16)
        outs[kv][slab - 1] = acc[1, kv].astype(BF16)


def assemble(place, verticals, home, back, vert, regions, devices):
    _, rows, features = home.shape
    heads, nv = verticals.shape
    smem = pl.BlockSpec(memory_space=pltpu.SMEM)
    vmem = pl.BlockSpec(memory_space=pltpu.VMEM)
    return pl.pallas_call(
        functools.partial(
            assemble_kernel, devices=devices, heads=heads, nv=nv, per_device=rows // BLOCK
        ),
        in_specs=[smem] * 2 + [vmem] * (2 + WDEV),
        out_specs=[vmem] * 2,
        out_shape=[jax.ShapeDtypeStruct((regions, rows, features), BF16)] * 2,
        scratch_shapes=[pltpu.VMEM((2, 2, rows, features), F32)],
        compiler_params=pltpu.CompilerParams(vmem_limit_bytes=VMEM_LIMIT),
    )(place, verticals, home, *back, vert)


def shards(
    queries,
    context_keys,
    context_values,
    forward_output,
    output_cotangent,
    verticals,
    offsets,
    slab_index,
):
    devices = lax.axis_size("ctx")
    me = lax.axis_index("ctx")
    regions = context_keys.shape[0]
    place = jnp.stack([slab_index[0], me.astype(jnp.int32)])
    *sends, picked = pack(place, verticals, context_keys, context_values, devices)
    vert = lax.psum(picked, "ctx")
    recv = [from_behind(sends[d - 1], d) for d in range(1, WDEV + 1)]
    query_grad, near, home, vgrad = attend(
        place, verticals, offsets, queries, output_cotangent, forward_output,
        context_keys, context_values, vert, recv, devices,
    )
    flat = vgrad.reshape(devices, -1, vgrad.shape[-1])
    shares = lax.all_to_all(flat, "ctx", 0, 0, tiled=True)
    summed = jnp.sum(shares.astype(F32), axis=0).astype(BF16)
    vert_sum = lax.all_gather(summed, "ctx", axis=0, tiled=True).reshape(vgrad.shape)
    back = [from_behind(near[d - 1], -d) for d in range(1, WDEV + 1)]
    key_gradient, value_gradient = assemble(
        place, verticals, home, back, vert_sum, regions, devices
    )
    return query_grad, key_gradient, value_gradient


def solution(mesh):
    in_specs = (
        P(("groups", "ctx"), None),
        P("groups", "ctx", None),
        P("groups", "ctx", None),
        P(("groups", "ctx"), None),
        P(("groups", "ctx"), None),
        P("groups", None),
        P("groups", None),
        P("groups"),
    )
    out_specs = (P(("groups", "ctx"), None), P("groups", "ctx", None), P("groups", "ctx", None))
    return jax.shard_map(shards, mesh=mesh, in_specs=in_specs, out_specs=out_specs, check_vma=False)
```

time: 417 us -> 252 us (0.60)
  local copies, waits for them, and re-layouts: 96 us -> 20.7 us
  other arithmetic: 50.8 us -> 0.85 us
  blocking collectives: 76.4 us -> 28.6 us
  waiting for transfers between devices: 109 us -> 147 us
  matrix products: 34.3 us -> 0 us
  Pallas kernels: 0 us -> 25.1 us
  starting transfers between devices: 32.9 us -> 14.4 us
    psum x1 -> x0, blocking collectives: 76.4 us -> none  [shards(): vert_keys, vert_values = lax.psum((picked_keys, picked_values), 'ctx')]
    dot_general x20 -> x0, matrix products: 34.3 us -> none  [the longest x4 9.6 us: head_pass(): jnp.einsum('jrgd,jkd->jrgk', grad_head, values_cand, preferred_element_ty...]
    all_to_all x0 -> x1, blocking collectives: none -> 28.6 us  [shards(): shares = lax.all_to_all(flat, 'ctx', 0, 0, tiled=True)]
    reshape x10 -> x0, local copies, waits for them, and re-layouts: 25.2 us -> none  [the longest x2 7.44 us: shards(): context_keys.reshape(local_blocks, MASK_BLOCK_SIZE, heads_kv, head_dim)]
    pallas_call x0 -> x3, Pallas kernels: none -> 25.1 us  [the longest x1 15.9 us: attend(): pl.pallas_call(functools.partial(attend_kernel, devices=devices, heads=he...]
    all_gather x0 -> x1, waiting for transfers between devices: none -> 23.2 us  [shards(): lax.all_gather(summed, 'ctx', axis=0, tiled=True).reshape(vgrad.shape)]
    ppermute x20 -> x10, starting transfers between devices: 32.9 us -> 14.3 us  [from_behind(): lax.ppermute(shard, 'ctx', [(i, (i + by) % peers) for i in range(peers)])]
    ppermute x20 -> x10, waiting for transfers between devices: 35.2 us -> 53 us  [from_behind(): lax.ppermute(shard, 'ctx', [(i, (i + by) % peers) for i in range(peers)])]
  transfers between devices with their start and end apart: 21 -> 12, of which waited for: 11 -> 12; matrix products, arithmetic and copies ran while one was open for 17% -> 0% of each run, Pallas kernels for 0% -> 0%
where the time goes in v1:
time: 252 us; the launch traced here: 251 us
  waiting for transfers between devices  147 us (58%)
  blocking collectives  28.6 us (11%)
  Pallas kernels  25.1 us (10%)
  local copies, waits for them, and re-layouts  20.7 us (8%)
  between operations  14.8 us (6%)
  starting transfers between devices  14.4 us (6%)
    psum x1, waiting for transfers between devices, shards(): vert = lax.psum(picked, 'ctx')  70.6 us
    ppermute x10, waiting for transfers between devices, from_behind(): lax.ppermute(shard, 'ctx', [(i, (i + by) % peers) for i in range(peers)])  53 us
    all_to_all x1, blocking collectives, shards(): shares = lax.all_to_all(flat, 'ctx', 0, 0, tiled=True)  28.6 us
    all_gather x1, waiting for transfers between devices, shards(): lax.all_gather(summed, 'ctx', axis=0, tiled=True).reshape(vgrad.shape)  23.2 us
    unnamed x48, local copies, waits for them, and re-layouts  20.6 us
    pallas_call x1, Pallas kernels, attend(): pl.pallas_call(functools.partial(attend_kernel, devices=devices, heads=he...  15.9 us
    ppermute x10, starting transfers between devices, from_behind(): lax.ppermute(shard, 'ctx', [(i, (i + by) % peers) for i in range(peers)])  14.3 us
    pallas_call x1, Pallas kernels, pack(): pl.pallas_call(functools.partial(pack_kernel, devices=devices, heads=head...  5.27 us
  transfers between devices with their start and end apart: 12, of which 12 were waited for; matrix products, arithmetic and copies ran while one was open for 0% of the time, Pallas kernels for 0%

profile of v1, /device:TPU:0, one launch (start us, length us, event | category | flops | bytes accessed | tf_op | source)
XLA Modules:
  0.0 251.2 jit_solution(17080743595278078659)
XLA Ops:
  7.9 1.6 copy-done
  9.5 1.6 copy-done.2
  11.8 5.3 %shard_map.103 = (bf16[2,128,512]{2,1,0:T(8,128)(2,1)S(1)}, bf16[2,128,512]{2,1,0:T(8,128)(2,1)S(1)}, bf16[2,128,512]{2,1,0:T(8,128)(2,1)S(1)}, bf16[2,128,512]{...) custom-call(s32[2]{0:T(128)S(1)} %pad_add_fusion.place, s32[4,8]{1,0:T(4,128)S(1)} %copy-done.21, ...), custom_call_target="tpu_custom_call" | custom-call | tf_op jit(solution)/shard_map/pallas_call | solution.py:79
  17.6 2.5 %collective-permute-start.1 = (bf16[2,128,512]{2,1,0:T(8,128)(2,1)S(1)}, bf16[2,128,512]{2,1,0:T(8,128)(2,1)S(1)}, u32[]{:S(2)}, u32[]{:S(2)}) collective-permute-start(bf16[2,128,512]{2,1,0:T(8,128)(2,1)S(1)} %get-tuple-element.17), channel_id=1, source_target_pairs={{0,2},{1,3},{2,4},{3,5},{4,6},{5,7},{6,8},{7,9},{8,10},{9,11},{10,... | collective-permute-start | bytes 786440 | tf_op jit(solution)/shard_map/ppermute | solution.py:20
  20.1 2.5 collective-permute-start.2
  22.6 1.5 collective-permute-start.3
  24.3 4.6 %collective-permute-done.rest_0_ = bf16[2,128,512]{2,1,0:T(8,128)(2,1)S(1)} collective-permute-done((bf16[2,128,512]{2,1,0:T(8,128)(2,1)S(1)}, bf16[2,128,512]{2,1,0:T(8,128)(2,1)S(1)}, u32[]{:S(2)}, u32[]{:S(2)}) %collective-permute-start) | collective-permute-done | bytes 262176 | tf_op jit(solution)/shard_map/ppermute | solution.py:20
  31.2 1.9 collective-permute-done.2.rest_2_
  33.7 2.1 collective-permute-done.3.rest_3_
  36.5 20.6 %collective-permute-done.4.rest_4_ = bf16[2,128,512]{2,1,0:T(8,128)(2,1)S(1)} collective-permute-done((bf16[2,128,512]{2,1,0:T(8,128)(2,1)S(1)}, bf16[2,128,512]{2,1,0:T(8,128)(2,1)S(1)}, u32[]{:S(2)}, u32[]{:S(2)}) %collective-permute-start.4) | collective-permute-done | bytes 262176 | tf_op jit(solution)/shard_map/ppermute | solution.py:20
  57.8 70.6 %all-reduce.2.cloned.1.call-done.vert = bf16[2,2048,128]{2,1,0:T(8,128)(2,1)} async-done(((bf16[2,2048,128]{2,1,0:T(8,128)(2,1)}), bf16[2,2048,128]{2,1,0:T(8,128)(2,1)}) %all-reduce.2.cloned.1.call-update) | async-done | bytes 1048592 | tf_op jit(solution)/shard_map/psum | solution.py:361
  128.4 1.6 copy-done.3
  139.6 15.9 %shard_map.104 = (bf16[128,4096]{1,0:T(8,128)(2,1)}, bf16[5,2,128,512]{3,2,1,0:T(8,128)(2,1)S(1)}, f32[2,128,512]{2,1,0:T(8,128)S(1)}, bf16[2,2048,128]{2,1,0:T(8,128)(2,1)S(1)}) custom-call(s32[2]{0:T(128)S(1)} %pad_add_fusion.place, s32[4,8]{1,0:T(4,128)S(1)} %copy-done.22, s32[4,3]{1,0:T(4,128)S(1)} %copy-done.23, bf16[128,4096]{1,0:T(8,128)(2,1)S(1)} %copy-done.4, ...), custom_call_target="tpu_custom_call" | custom-call | tf_op jit(solution)/shard_map/pallas_call | solution.py:254
  156.3 28.6 %all_to_all.5 = bf16[16,256,128]{2,1,0:T(8,128)(2,1)S(1)} all-to-all(bf16[16,256,128]{2,1,0:T(8,128)(2,1)S(1)} %bitcast.13), channel_id=1, replica_groups=mesh['groups'=2,'ctx'=16] {'ctx'}, dimensions={0} | all-to-all | bytes 2097152 | tf_op jit(solution)/shard_map/all_to_all | solution.py:368
  185.8 1.7 collective-permute-start.9
  187.6 3.3 %collective-permute-start.8 = (bf16[2,128,512]{2,1,0:T(8,128)(2,1)S(1)}, bf16[2,128,512]{2,1,0:T(8,128)(2,1)S(1)}, u32[]{:S(2)}, u32[]{:S(2)}) collective-permute-start(bf16[2,128,512]{2,1,0:T(8,128)(2,1)S(1)} %get-tuple-element.28), channel_id=1, source_target_pairs={{0,12},{1,13},{2,14},{3,15},{4,0},{5,1},{6,2},{7,3},{8,4},{9,5},{1... | collective-permute-start | bytes 786440 | tf_op jit(solution)/shard_map/ppermute | solution.py:20
  193.0 1.3 collective-permute-done.9.rest_4_
  194.3 7.0 %collective-permute-done.8.rest_3_ = bf16[2,128,512]{2,1,0:T(8,128)(2,1)S(1)} collective-permute-done((bf16[2,128,512]{2,1,0:T(8,128)(2,1)S(1)}, bf16[2,128,512]{2,1,0:T(8,128)(2,1)S(1)}, u32[]{:S(2)}, u32[]{:S(2)}) %collective-permute-start.8) | collective-permute-done | bytes 262176 | tf_op jit(solution)/shard_map/ppermute | solution.py:20
  201.3 6.3 %collective-permute-done.7.rest_2_ = bf16[2,128,512]{2,1,0:T(8,128)(2,1)S(1)} collective-permute-done((bf16[2,128,512]{2,1,0:T(8,128)(2,1)S(1)}, bf16[2,128,512]{2,1,0:T(8,128)(2,1)S(1)}, u32[]{:S(2)}, u32[]{:S(2)}) %collective-permute-start.7) | collective-permute-done | bytes 262176 | tf_op jit(solution)/shard_map/ppermute | solution.py:20
  207.6 5.6 %collective-permute-done.6.rest_1_ = bf16[2,128,512]{2,1,0:T(8,128)(2,1)S(1)} collective-permute-done((bf16[2,128,512]{2,1,0:T(8,128)(2,1)S(1)}, bf16[2,128,512]{2,1,0:T(8,128)(2,1)S(1)}, u32[]{:S(2)}, u32[]{:S(2)}) %collective-permute-start.6) | collective-permute-done | bytes 262176 | tf_op jit(solution)/shard_map/ppermute | solution.py:20
  213.3 2.8 %collective-permute-done.5.rest_0_ = bf16[2,128,512]{2,1,0:T(8,128)(2,1)S(1)} collective-permute-done((bf16[2,128,512]{2,1,0:T(8,128)(2,1)S(1)}, bf16[2,128,512]{2,1,0:T(8,128)(2,1)S(1)}, u32[]{:S(2)}, u32[]{:S(2)}) %collective-permute-start.5) | collective-permute-done | bytes 262176 | tf_op jit(solution)/shard_map/ppermute | solution.py:20
  216.0 23.2 %all-gather.2.cloned.1.call-done = bf16[4096,128]{1,0:T(8,128)(2,1)} async-done(((bf16[256,128]{1,0:T(8,128)(2,1)}), bf16[4096,128]{1,0:T(8,128)(2,1)}) %all-gather.2.cloned.1.call-update) | async-done | bytes 1048592 | tf_op jit(solution)/shard_map/all_gather | solution.py:370
  239.2 1.2 copy-done.8
  240.4 3.9 %shard_map.105 = (bf16[16,128,512]{2,1,0:T(8,128)(2,1)}, bf16[16,128,512]{2,1,0:T(8,128)(2,1)}) custom-call(s32[2]{0:T(128)S(1)} %pad_add_fusion.place, s32[4,8]{1,0:T(4,128)S(1)} %copy-done.22, f32[2,128,512]{2,1,0:T(8,128)S(1)} %copy-done.10, bf16[2,128,512]{2,1,0:T(8,128)(2,1)S(1)} %collective-permute-done.5.rest_0_, ...), custom_call_target="tpu_custom_call" | custom-call | tf_op jit(solution)/shard_map/pallas_call | solution.py:334
  (57 shorter events, 19.3 us)
Async XLA Ops:
  7.2 121.2 %all-reduce.2.cloned.1.call-start = ((), (), s32[]{:S(2)}) async-start(), calls=%async_computation.1 | async-start | bytes 2097152 | tf_op jit(solution)/shard_map/psum | solution.py:361
  7.9 1.6 copy-start
  9.5 1.6 copy-start.2
  11.8 116.5 %copy-start.1 = (bf16[16,128,512]{2,1,0:T(8,128)(2,1)S(1)}, bf16[16,128,512]{2,1,0:T(8,128)(2,1)}, u32[]{:S(2)}) copy-start(bf16[16,128,512]{2,1,0:T(8,128)(2,1)} %keys.3) | copy-start | bytes 6291460
  11.8 116.5 %copy-start.22 = (s32[4,8]{1,0:T(4,128)S(1)}, s32[4,8]{1,0:T(4,128)}, u32[]{:S(2)}) copy-start(s32[4,8]{1,0:T(4,128)} %verts.5) | copy-start | bytes 388
  11.8 116.5 %copy-start.23 = (s32[4,3]{1,0:T(4,128)S(1)}, s32[4,3]{1,0:T(4,128)}, u32[]{:S(2)}) copy-start(s32[4,3]{1,0:T(4,128)} %offs.1) | copy-start | bytes 148
  17.1 222.1 %all-gather.2.cloned.1.call-start = ((), (), s32[]{:S(2)}) async-start(), calls=%async_computation.2 | async-start | bytes 1114112 | tf_op jit(solution)/shard_map/all_gather | solution.py:370
  17.2 11.8 %collective-permute-start = (bf16[2,128,512]{2,1,0:T(8,128)(2,1)S(1)}, bf16[2,128,512]{2,1,0:T(8,128)(2,1)S(1)}, u32[]{:S(2)}, u32[]{:S(2)}) collective-permute-start(bf16[2,128,512]{2,1,0:T(8,128)(2,1)S(1)} %get-tuple-element.16), channel_id=1, source_target_pairs={{0,1},{1,2},{2,3},{3,4},{4,5},{5,6},{6,7},{7,8},{8,9},{9,10},{10,1... | collective-permute-start | bytes 786440 | tf_op jit(solution)/shard_map/ppermute | solution.py:20
  17.6 12.9 %collective-permute-start.1 = (bf16[2,128,512]{2,1,0:T(8,128)(2,1)S(1)}, bf16[2,128,512]{2,1,0:T(8,128)(2,1)S(1)}, u32[]{:S(2)}, u32[]{:S(2)}) collective-permute-start(bf16[2,128,512]{2,1,0:T(8,128)(2,1)S(1)} %get-tuple-element.17), channel_id=1, source_target_pairs={{0,2},{1,3},{2,4},{3,5},{4,6},{5,7},{6,8},{7,9},{8,10},{9,11},{10,... | collective-permute-start | bytes 786440 | tf_op jit(solution)/shard_map/ppermute | solution.py:20
  20.1 12.9 %collective-permute-start.2 = (bf16[2,128,512]{2,1,0:T(8,128)(2,1)S(1)}, bf16[2,128,512]{2,1,0:T(8,128)(2,1)S(1)}, u32[]{:S(2)}, u32[]{:S(2)}) collective-permute-start(bf16[2,128,512]{2,1,0:T(8,128)(2,1)S(1)} %get-tuple-element.18), channel_id=1, source_target_pairs={{0,3},{1,4},{2,5},{3,6},{4,7},{5,8},{6,9},{7,10},{8,11},{9,12},{10... | collective-permute-start | bytes 786440 | tf_op jit(solution)/shard_map/ppermute | solution.py:20
  22.6 13.2 %collective-permute-start.3 = (bf16[2,128,512]{2,1,0:T(8,128)(2,1)S(1)}, bf16[2,128,512]{2,1,0:T(8,128)(2,1)S(1)}, u32[]{:S(2)}, u32[]{:S(2)}) collective-permute-start(bf16[2,128,512]{2,1,0:T(8,128)(2,1)S(1)} %get-tuple-element.19), channel_id=1, source_target_pairs={{0,4},{1,5},{2,6},{3,7},{4,8},{5,9},{6,10},{7,11},{8,12},{9,13},{1... | collective-permute-start | bytes 786440 | tf_op jit(solution)/shard_map/ppermute | solution.py:20
  24.1 32.9 %collective-permute-start.4 = (bf16[2,128,512]{2,1,0:T(8,128)(2,1)S(1)}, bf16[2,128,512]{2,1,0:T(8,128)(2,1)S(1)}, u32[]{:S(2)}, u32[]{:S(2)}) collective-permute-start(bf16[2,128,512]{2,1,0:T(8,128)(2,1)S(1)} %get-tuple-element.20), channel_id=1, source_target_pairs={{0,5},{1,6},{2,7},{3,8},{4,9},{5,10},{6,11},{7,12},{8,13},{9,14},{... | collective-permute-start | bytes 786440 | tf_op jit(solution)/shard_map/ppermute | solution.py:20
  128.3 1.6 copy-start.3
  129.9 1.2 copy-start.4
  131.2 1.2 copy-start.5
  132.4 1.2 copy-start.6
  133.6 1.2 copy-start.7
  184.9 54.3 %copy-start.10 = (f32[2,128,512]{2,1,0:T(8,128)S(1)}, f32[2,128,512]{2,1,0:T(8,128)}, u32[]{:S(2)}) copy-start(f32[2,128,512]{2,1,0:T(8,128)} %copy-done.9) | copy-start | bytes 1572868
  185.8 8.5 %collective-permute-start.9 = (bf16[2,128,512]{2,1,0:T(8,128)(2,1)S(1)}, bf16[2,128,512]{2,1,0:T(8,128)(2,1)S(1)}, u32[]{:S(2)}, u32[]{:S(2)}) collective-permute-start(bf16[2,128,512]{2,1,0:T(8,128)(2,1)S(1)} %get-tuple-element.27), channel_id=1, source_target_pairs={{0,11},{1,12},{2,13},{3,14},{4,15},{5,0},{6,1},{7,2},{8,3},{9,4},{... | collective-permute-start | bytes 786440 | tf_op jit(solution)/shard_map/ppermute | solution.py:20
  187.6 13.8 %collective-permute-start.8 = (bf16[2,128,512]{2,1,0:T(8,128)(2,1)S(1)}, bf16[2,128,512]{2,1,0:T(8,128)(2,1)S(1)}, u32[]{:S(2)}, u32[]{:S(2)}) collective-permute-start(bf16[2,128,512]{2,1,0:T(8,128)(2,1)S(1)} %get-tuple-element.28), channel_id=1, source_target_pairs={{0,12},{1,13},{2,14},{3,15},{4,0},{5,1},{6,2},{7,3},{8,4},{9,5},{1... | collective-permute-start | bytes 786440 | tf_op jit(solution)/shard_map/ppermute | solution.py:20
  190.8 16.8 %collective-permute-start.7 = (bf16[2,128,512]{2,1,0:T(8,128)(2,1)S(1)}, bf16[2,128,512]{2,1,0:T(8,128)(2,1)S(1)}, u32[]{:S(2)}, u32[]{:S(2)}) collective-permute-start(bf16[2,128,512]{2,1,0:T(8,128)(2,1)S(1)} %get-tuple-element.29), channel_id=1, source_target_pairs={{0,13},{1,14},{2,15},{3,0},{4,1},{5,2},{6,3},{7,4},{8,5},{9,6},{10... | collective-permute-start | bytes 786440 | tf_op jit(solution)/shard_map/ppermute | solution.py:20
  190.8 22.4 %collective-permute-start.6 = (bf16[2,128,512]{2,1,0:T(8,128)(2,1)S(1)}, bf16[2,128,512]{2,1,0:T(8,128)(2,1)S(1)}, u32[]{:S(2)}, u32[]{:S(2)}) collective-permute-start(bf16[2,128,512]{2,1,0:T(8,128)(2,1)S(1)} %get-tuple-element.30), channel_id=1, source_target_pairs={{0,14},{1,15},{2,0},{3,1},{4,2},{5,3},{6,4},{7,5},{8,6},{9,7},{10,... | collective-permute-start | bytes 786440 | tf_op jit(solution)/shard_map/ppermute | solution.py:20
  192.0 24.1 %collective-permute-start.5 = (bf16[2,128,512]{2,1,0:T(8,128)(2,1)S(1)}, bf16[2,128,512]{2,1,0:T(8,128)(2,1)S(1)}, u32[]{:S(2)}, u32[]{:S(2)}) collective-permute-start(bf16[2,128,512]{2,1,0:T(8,128)(2,1)S(1)} %get-tuple-element.31), channel_id=1, source_target_pairs={{0,15},{1,0},{2,1},{3,2},{4,3},{5,4},{6,5},{7,6},{8,7},{9,8},{10,9... | collective-permute-start | bytes 786440 | tf_op jit(solution)/shard_map/ppermute | solution.py:20
  239.2 1.2 copy-start.8
  (12 other events, 9.7 us)
Sparse Core Ops, SparseCore 0:
  17.2 111.0 all-reduce.1
  185.9 53.3 all-gather.1

commit v2 on v1

--- a/solution.py
+++ b/solution.py
@@ -10,7 +10,7 @@
 
 BLOCK = 64
 WDEV = 5
-VMEM_LIMIT = 40 * 1024 * 1024
+VMEM_LIMIT = 60 * 1024 * 1024
 BF16 = jnp.bfloat16
 F32 = jnp.float32
 
@@ -20,9 +20,33 @@
     return lax.ppermute(shard, "ctx", [(i, (i + by) % peers) for i in range(peers)])
 
 
+def other_core(shard):
+    peers = lax.axis_size("ctx")
+    return lax.ppermute(shard, "ctx", [(i, i ^ 1) for i in range(peers)])
+
+
+def same_core_groups():
+    peers = lax.axis_size("ctx")
+    return [list(range(core, peers, 2)) for core in range(2)]
+
+
+def sum_over_chips(half):
+    chips = lax.axis_size("ctx") // 2
+    groups = same_core_groups()
+    shares = lax.all_to_all(
+        half.reshape(chips, -1, half.shape[-1]), "ctx", 0, 0, axis_index_groups=groups, tiled=True
+    )
+    summed = jnp.sum(shares.astype(F32), axis=0).astype(BF16)
+    spread = jnp.broadcast_to(summed[None], shares.shape)
+    every = lax.all_to_all(spread, "ctx", 0, 0, axis_index_groups=groups, tiled=True)
+    return every.reshape(half.shape)
+
+
 def pack_kernel(place, verts, keys, values, *rest, devices, heads, nv, per_device):
-    sends, picked, sems, pick_sems = rest[:WDEV], rest[WDEV], rest[WDEV + 1], rest[WDEV + 2]
+    sends = rest[:WDEV]
+    keep, give, picked, sems, pick_sems = rest[WDEV:]
     slab, me = place[0], place[1]
+    core = me % 2
     head_dim = picked.shape[2]
     copies = []
     for distance in range(1, WDEV + 1):
@@ -43,7 +67,7 @@
         unit = h * nv + m
         return pltpu.make_async_copy(
             source.at[region, pl.ds(row, BLOCK), pl.ds(h * head_dim, head_dim)],
-            picked.at[kv, pl.ds(unit * BLOCK, BLOCK), :],
+            picked.at[(kv + core) % 2, pl.ds(unit * BLOCK, BLOCK), :],
             pick_sems.at[kv, unit],
         )
 
@@ -66,6 +90,8 @@
                 unit_copy(h, m, 0, keys).wait()
                 unit_copy(h, m, 1, values).wait()
 
+    keep[...] = picked[0]
+    give[...] = picked[1]
     for copy in copies:
         copy.wait()
 
@@ -81,10 +107,11 @@
             pack_kernel, devices=devices, heads=heads, nv=nv, per_device=rows // BLOCK
         ),
         in_specs=[smem, smem, hbm, hbm],
-        out_specs=[hbm] * WDEV + [pl.BlockSpec(memory_space=pltpu.VMEM)],
+        out_specs=[hbm] * WDEV + [pl.BlockSpec(memory_space=pltpu.VMEM)] * 2,
         out_shape=[jax.ShapeDtypeStruct((2, rows, features), BF16)] * WDEV
-        + [jax.ShapeDtypeStruct((2, heads * nv * BLOCK, head_dim), BF16)],
+        + [jax.ShapeDtypeStruct((heads * nv * BLOCK, head_dim), BF16)] * 2,
         scratch_shapes=[
+            pltpu.VMEM((2, heads * nv * BLOCK, head_dim), BF16),
             pltpu.SemaphoreType.DMA((WDEV, 2)),
             pltpu.SemaphoreType.DMA((2, heads * nv)),
         ],
@@ -93,14 +120,15 @@
 
 
 def attend_kernel(
-    place, verts, offs, q, grad, out, keys, values, vert, *rest,
+    place, verts, offs, q, grad, out, keys, values, vert_mine, vert_other, *rest,
     devices, heads, nv, ns, per_device,
 ):
     recv = rest[:WDEV]
-    dq, near, home, vgrad = rest[WDEV : WDEV + 4]
-    (win, vkv, kc, vc, qs, gs, s_ref, dp_ref, w_ref, ds_ref, nacc, vacc, sems) = rest[WDEV + 4 :]
+    dq, near, home, vkeep, vgive = rest[WDEV : WDEV + 5]
+    (win, vkv, kc, vc, qs, gs, s_ref, dp_ref, w_ref, ds_ref, nacc, vacc, sems) = rest[WDEV + 5 :]
     h, j = pl.program_id(0), pl.program_id(1)
     slab, me = place[0], place[1]
+    core = me % 2
     head_dim = kc.shape[1]
     group = q.shape[1] // head_dim
     cand = 1 + nv + ns
@@ -122,7 +150,8 @@
         copies.append(
             pltpu.make_async_copy(values.at[slab], win.at[1, own_rows, :], sems.at[WDEV + 1])
         )
-        copies.append(pltpu.make_async_copy(vert, vkv, sems.at[WDEV + 2]))
+        copies.append(pltpu.make_async_copy(vert_mine, vkv.at[core], sems.at[WDEV + 2]))
+        copies.append(pltpu.make_async_copy(vert_other, vkv.at[1 - core], sems.at[WDEV + 3]))
         for copy in copies:
             copy.start()
         nacc[...] = jnp.zeros_like(nacc)
@@ -223,8 +252,9 @@
 
     @pl.when(j == per_device - 1)
     def _():
+        vkeep[pl.ds(vert_at, nv * BLOCK), :] = vacc[core]
+        vgive[pl.ds(vert_at, nv * BLOCK), :] = vacc[1 - core].astype(BF16)
         for kv in range(2):
-            vgrad[kv, pl.ds(vert_at, nv * BLOCK), :] = vacc[kv].astype(BF16)
             home[kv, :, lanes] = nacc[kv, WDEV * rows :, lanes]
             for d in range(1, WDEV + 1):
                 near[d - 1, kv, :, lanes] = nacc[
@@ -232,7 +262,8 @@
                 ].astype(BF16)
 
 
-def attend(place, verticals, offsets, queries, cotangent, output, keys, values, vert, recv, devices):
+def attend(place, verticals, offsets, queries, cotangent, output, keys, values, vert_mine,
+           vert_other, recv, devices):
     rows, width = queries.shape
     features = keys.shape[2]
     heads, nv = verticals.shape
@@ -250,23 +281,24 @@
 
     near_shape = (WDEV, 2, rows, features)
     home_shape = (2, rows, features)
-    vert_shape = (2, heads * nv * BLOCK, head_dim)
+    vert_shape = (heads * nv * BLOCK, head_dim)
     return pl.pallas_call(
         functools.partial(
             attend_kernel, devices=devices, heads=heads, nv=nv, ns=ns, per_device=per_device
         ),
         grid=(heads, per_device),
-        in_specs=[smem] * 3 + [tile] * 3 + [hbm] * (3 + WDEV),
-        out_specs=[tile, whole(near_shape), whole(home_shape), whole(vert_shape)],
+        in_specs=[smem] * 3 + [tile] * 3 + [hbm] * (4 + WDEV),
+        out_specs=[tile, whole(near_shape), whole(home_shape), whole(vert_shape), whole(vert_shape)],
         out_shape=[
             jax.ShapeDtypeStruct((rows, width), BF16),
             jax.ShapeDtypeStruct(near_shape, BF16),
             jax.ShapeDtypeStruct(home_shape, F32),
+            jax.ShapeDtypeStruct(vert_shape, F32),
             jax.ShapeDtypeStruct(vert_shape, BF16),
         ],
         scratch_shapes=[
             pltpu.VMEM((2, (WDEV + 1) * rows, features), BF16),
-            pltpu.VMEM(vert_shape, BF16),
+            pltpu.VMEM((2,) + vert_shape, BF16),
             pltpu.VMEM((cand * BLOCK, head_dim), BF16),
             pltpu.VMEM((cand * BLOCK, head_dim), BF16),
             pltpu.VMEM((group * BLOCK, head_dim), BF16),
@@ -277,16 +309,22 @@
             pltpu.VMEM((cand * BLOCK, group * BLOCK), BF16),
             pltpu.VMEM((2, (WDEV + 1) * rows, features), F32),
             pltpu.VMEM((2, nv * BLOCK, head_dim), F32),
-            pltpu.SemaphoreType.DMA((WDEV + 3,)),
+            pltpu.SemaphoreType.DMA((WDEV + 4,)),
         ],
         compiler_params=pltpu.CompilerParams(vmem_limit_bytes=VMEM_LIMIT),
-    )(place, verticals, offsets, queries, cotangent, output, keys, values, vert, *recv)
+    )(
+        place, verticals, offsets, queries, cotangent, output, keys, values, vert_mine, vert_other,
+        *recv,
+    )
 
 
 def assemble_kernel(place, verts, home, *rest, devices, heads, nv, per_device):
     back = rest[:WDEV]
-    vert, key_out, value_out, acc = rest[WDEV:]
+    vert_mine, vert_other, key_out, value_out, vert, acc = rest[WDEV:]
     slab, me = place[0], place[1]
+    core = me % 2
+    vert[core] = vert_mine[...]
+    vert[1 - core] = vert_other[...]
     head_dim = vert.shape[2]
     slab_blocks = per_device * devices
     acc[0] = home[...]
@@ -326,7 +364,7 @@
         outs[kv][slab - 1] = acc[1, kv].astype(BF16)
 
 
-def assemble(place, verticals, home, back, vert, regions, devices):
+def assemble(place, verticals, home, back, vert_mine, vert_other, regions, devices):
     _, rows, features = home.shape
     heads, nv = verticals.shape
     smem = pl.BlockSpec(memory_space=pltpu.SMEM)
@@ -335,12 +373,15 @@
         functools.partial(
             assemble_kernel, devices=devices, heads=heads, nv=nv, per_device=rows // BLOCK
         ),
-        in_specs=[smem] * 2 + [vmem] * (2 + WDEV),
+        in_specs=[smem] * 2 + [vmem] * (3 + WDEV),
         out_specs=[vmem] * 2,
         out_shape=[jax.ShapeDtypeStruct((regions, rows, features), BF16)] * 2,
-        scratch_shapes=[pltpu.VMEM((2, 2, rows, features), F32)],
+        scratch_shapes=[
+            pltpu.VMEM((2,) + vert_mine.shape, BF16),
+            pltpu.VMEM((2, 2, rows, features), F32),
+        ],
         compiler_params=pltpu.CompilerParams(vmem_limit_bytes=VMEM_LIMIT),
-    )(place, verticals, home, *back, vert)
+    )(place, verticals, home, *back, vert_mine, vert_other)
 
 
 def shards(
@@ -357,20 +398,20 @@
     me = lax.axis_index("ctx")
     regions = context_keys.shape[0]
     place = jnp.stack([slab_index[0], me.astype(jnp.int32)])
-    *sends, picked = pack(place, verticals, context_keys, context_values, devices)
-    vert = lax.psum(picked, "ctx")
+    *sends, keep, give = pack(place, verticals, context_keys, context_values, devices)
     recv = [from_behind(sends[d - 1], d) for d in range(1, WDEV + 1)]
-    query_grad, near, home, vgrad = attend(
+    vert_mine = sum_over_chips(keep + other_core(give))
+    vert_other = other_core(vert_mine)
+    query_grad, near, home, vkeep, vgive = attend(
         place, verticals, offsets, queries, output_cotangent, forward_output,
-        context_keys, context_values, vert, recv, devices,
-    )
-    flat = vgrad.reshape(devices, -1, vgrad.shape[-1])
-    shares = lax.all_to_all(flat, "ctx", 0, 0, tiled=True)
-    summed = jnp.sum(shares.astype(F32), axis=0).astype(BF16)
-    vert_sum = lax.all_gather(summed, "ctx", axis=0, tiled=True).reshape(vgrad.shape)
+        context_keys, context_values, vert_mine, vert_other, recv, devices,
+    )
     back = [from_behind(near[d - 1], -d) for d in range(1, WDEV + 1)]
+    half = (vkeep + other_core(vgive).astype(F32)).astype(BF16)
+    total_mine = sum_over_chips(half)
+    total_other = other_core(total_mine)
     key_gradient, value_gradient = assemble(
-        place, verticals, home, back, vert_sum, regions, devices
+        place, verticals, home, back, total_mine, total_other, regions, devices
     )
     return query_grad, key_gradient, value_gradient
 

time: 252 us -> 214 us (0.85)
  waiting for transfers between devices: 147 us -> 77 us
  Pallas kernels: 25.1 us -> 66.7 us
  local copies, waits for them, and re-layouts: 20.7 us -> 4.13 us
  between operations: 14.8 us -> 1.48 us
  blocking collectives: 28.6 us -> 39.4 us
  starting transfers between devices: 14.4 us -> 21.5 us
  other arithmetic: 0.85 us -> 3.4 us
    psum x1 -> x0, waiting for transfers between devices: 70.6 us -> none  [shards(): vert = lax.psum(picked, 'ctx')]
    pallas_call x1, Pallas kernels: 5.27 us -> 43.1 us  [pack(): pl.pallas_call(functools.partial(pack_kernel, devices=devices, heads=head...]
    all_to_all x0 -> x2, waiting for transfers between devices: none -> 29.9 us  [sum_over_chips(): lax.all_to_all(spread, 'ctx', 0, 0, axis_index_groups=groups, tiled=True)]
    all_gather x1 -> x0, waiting for transfers between devices: 23.2 us -> none  [shards(): lax.all_gather(summed, 'ctx', axis=0, tiled=True).reshape(vgrad.shape)]
    unnamed x48 -> x40, local copies, waits for them, and re-layouts: 20.6 us -> 2.32 us
    all_to_all x1 -> x2, blocking collectives: 28.6 us -> 39.4 us  [sum_over_chips(): lax.all_to_all(half.reshape(chips, -1, half.shape[-1]), 'ctx', 0, 0, axis...]
    ppermute x10, waiting for transfers between devices: 53 us -> 43.3 us  [from_behind(): lax.ppermute(shard, 'ctx', [(i, (i + by) % peers) for i in range(peers)])]
    all_to_all x0 -> x2, starting transfers between devices: none -> 7.27 us  [sum_over_chips(): lax.all_to_all(spread, 'ctx', 0, 0, axis_index_groups=groups, tiled=True)]
  transfers between devices with their start and end apart: 12 -> 16, of which waited for: 12 -> 12; matrix products, arithmetic and copies ran while one was open for 0% -> 0% of each run, Pallas kernels for 0% -> 0%
where the time goes in v2:
time: 214 us
  waiting for transfers between devices  77 us (36%)
  Pallas kernels  66.7 us (31%)
  blocking collectives  39.4 us (18%)
  starting transfers between devices  21.5 us (10%)
  local copies, waits for them, and re-layouts  4.13 us (2%)
  other arithmetic  3.4 us (2%)
    ppermute x10, waiting for transfers between devices, from_behind(): lax.ppermute(shard, 'ctx', [(i, (i + by) % peers) for i in range(peers)])  43.3 us
    pallas_call x1, Pallas kernels, pack(): pl.pallas_call(functools.partial(pack_kernel, devices=devices, heads=head...  43.1 us
    all_to_all x2, blocking collectives, sum_over_chips(): lax.all_to_all(half.reshape(chips, -1, half.shape[-1]), 'ctx', 0, 0, axis...  39.4 us
    all_to_all x2, waiting for transfers between devices, sum_over_chips(): lax.all_to_all(spread, 'ctx', 0, 0, axis_index_groups=groups, tiled=True)  29.9 us
    pallas_call x1, Pallas kernels, attend(): pl.pallas_call(functools.partial(attend_kernel, devices=devices, heads=he...  18.4 us
    ppermute x10, starting transfers between devices, from_behind(): lax.ppermute(shard, 'ctx', [(i, (i + by) % peers) for i in range(peers)])  13.6 us
    all_to_all x2, starting transfers between devices, sum_over_chips(): lax.all_to_all(spread, 'ctx', 0, 0, axis_index_groups=groups, tiled=True)  7.27 us
    pallas_call x1, Pallas kernels, assemble(): pl.pallas_call(functools.partial(assemble_kernel, devices=devices, heads=...  5.14 us
  transfers between devices with their start and end apart: 16, of which 12 were waited for; matrix products, arithmetic and copies ran while one was open for 0% of the time, Pallas kernels for 0%

profile of v2, /device:TPU:0, one launch (start us, length us, event | category | flops | bytes accessed | tf_op | source)
XLA Modules:
  0.0 213.5 jit_solution(3553642790716160117)
XLA Ops:
  1.9 43.1 %shard_map.103 = (bf16[2,128,512]{2,1,0:T(8,128)(2,1)}, bf16[2,128,512]{2,1,0:T(8,128)(2,1)}, bf16[2,128,512]{2,1,0:T(8,128)(2,1)}, bf16[2,128,512]{2,1,0:T(8,12...) custom-call(s32[2]{0:T(128)} %pad_add_fusion.place, s32[4,8]{1,0:T(4,128)} %verts.5, ...), custom_call_target="tpu_custom_call" | custom-call | tf_op jit(solution)/shard_map/pallas_call | solution.py:105
  45.6 1.7 collective-permute-done
  48.6 21.8 %all_to_all.20 = bf16[8,256,128]{2,1,0:T(8,128)(2,1)S(1)} all-to-all(bf16[8,256,128]{2,1,0:T(8,128)(2,1)S(1)} %bitcast.17), channel_id=1, replica_groups={{0,2,4,6,8,10,12,14},{1,3,5,7,9,11,13,15},{16,18,20,22,24,26,28,30},{17..., dimensions={0} | all-to-all | bytes 1048576 | tf_op jit(solution)/shard_map/all_to_all | solution.py:36
  71.3 3.6 %all-to-all-start.1 = ((bf16[8,256,128]{2,1,0:T(8,128)(2,1)}), bf16[8,256,128]{2,1,0:T(8,128)(2,1)S(1)}, u32[]{:S(2)}, u32[]{:S(2)}) async-start(bf16[8,256,128]{2,1,0:T(8,128)(2,1)} %broadcast_in_dim.4), calls=%async_computation.1 | async-start | bytes 1048576 | tf_op jit(solution)/shard_map/all_to_all | solution.py:41
  75.0 14.1 %all-to-all-done.1 = bf16[8,256,128]{2,1,0:T(8,128)(2,1)S(1)} async-done(((bf16[8,256,128]{2,1,0:T(8,128)(2,1)}), bf16[8,256,128]{2,1,0:T(8,128)(2,1)S(1)}, u32[]{:S(2)}, u32[]{:S(2)}) %all-to-all-start.1) | async-done | bytes 524320 | tf_op jit(solution)/shard_map/all_to_all | solution.py:41
  89.2 4.3 %collective-permute-start.3 = (bf16[2,128,512]{2,1,0:T(8,128)(2,1)S(1)}, bf16[2,128,512]{2,1,0:T(8,128)(2,1)S(1)}, u32[]{:S(2)}, u32[]{:S(2)}) collective-permute-start(bf16[2,128,512]{2,1,0:T(8,128)(2,1)S(1)} %copy-done.18), channel_id=1, source_target_pairs={{0,2},{1,3},{2,4},{3,5},{4,6},{5,7},{6,8},{7,9},{8,10},{9,11},{10,... | collective-permute-start | bytes 786440 | tf_op jit(solution)/shard_map/ppermute | solution.py:20
  94.1 7.0 %collective-permute-done.3.rest_1_ = bf16[2,128,512]{2,1,0:T(8,128)(2,1)S(1)} collective-permute-done((bf16[2,128,512]{2,1,0:T(8,128)(2,1)S(1)}, bf16[2,128,512]{2,1,0:T(8,128)(2,1)S(1)}, u32[]{:S(2)}, u32[]{:S(2)}) %collective-permute-start.3) | collective-permute-done | bytes 262176 | tf_op jit(solution)/shard_map/ppermute | solution.py:20
  101.1 1.6 collective-permute-done.4.rest_2_
  102.7 2.3 %collective-permute-done.5.rest_3_ = bf16[2,128,512]{2,1,0:T(8,128)(2,1)S(1)} collective-permute-done((bf16[2,128,512]{2,1,0:T(8,128)(2,1)S(1)}, bf16[2,128,512]{2,1,0:T(8,128)(2,1)S(1)}, u32[]{:S(2)}, u32[]{:S(2)}) %collective-permute-start.5) | collective-permute-done | bytes 262176 | tf_op jit(solution)/shard_map/ppermute | solution.py:20
  105.0 15.3 %collective-permute-done.6.rest_4_ = bf16[2,128,512]{2,1,0:T(8,128)(2,1)S(1)} collective-permute-done((bf16[2,128,512]{2,1,0:T(8,128)(2,1)S(1)}, bf16[2,128,512]{2,1,0:T(8,128)(2,1)S(1)}, u32[]{:S(2)}, u32[]{:S(2)}) %collective-permute-start.6) | collective-permute-done | bytes 262176 | tf_op jit(solution)/shard_map/ppermute | solution.py:20
  121.7 18.4 %shard_map.104 = (bf16[128,4096]{1,0:T(8,128)(2,1)}, bf16[5,2,128,512]{3,2,1,0:T(8,128)(2,1)}, f32[2,128,512]{2,1,0:T(8,128)}, f32[2048,128]{1,0:T(8,128)}, bf16[2048,128]{1,0:T(8,128)(2,1)}) custom-call(s32[2]{0:T(128)} %pad_add_fusion.place, s32[4,8]{1,0:T(4,128)} %verts.5, s32[4,3]{1,0:T(4,128)} %offs.1, bf16[128,4096]{1,0:T(8,128)(2,1)} %q.1, ...), custom_call_target="tpu_custom_call" | custom-call | tf_op jit(solution)/shard_map/pallas_call | solution.py:285
  140.2 2.1 collective-permute-done.12
  142.3 1.3 add_convert_fusion
  143.6 17.6 %all_to_all.21 = bf16[8,256,128]{2,1,0:T(8,128)(2,1)S(1)} all-to-all(bf16[8,256,128]{2,1,0:T(8,128)(2,1)S(1)} %bitcast.20), channel_id=1, replica_groups={{0,2,4,6,8,10,12,14},{1,3,5,7,9,11,13,15},{16,18,20,22,24,26,28,30},{17..., dimensions={0} | all-to-all | bytes 1048576 | tf_op jit(solution)/shard_map/all_to_all | solution.py:36
  162.2 3.6 %all-to-all-start.3 = ((bf16[8,256,128]{2,1,0:T(8,128)(2,1)}), bf16[8,256,128]{2,1,0:T(8,128)(2,1)S(1)}, u32[]{:S(2)}, u32[]{:S(2)}) async-start(bf16[8,256,128]{2,1,0:T(8,128)(2,1)} %broadcast_in_dim.5), calls=%async_computation.3 | async-start | bytes 1048576 | tf_op jit(solution)/shard_map/all_to_all | solution.py:41
  165.9 2.9 %collective-permute-start.11 = (bf16[2,128,512]{2,1,0:T(8,128)(2,1)S(1)}, bf16[2,128,512]{2,1,0:T(8,128)(2,1)S(1)}, u32[]{:S(2)}, u32[]{:S(2)}) collective-permute-start(bf16[2,128,512]{2,1,0:T(8,128)(2,1)S(1)} %get-tuple-element.31), channel_id=1, source_target_pairs={{0,11},{1,12},{2,13},{3,14},{4,15},{5,0},{6,1},{7,2},{8,3},{9,4},{... | collective-permute-start | bytes 786440 | tf_op jit(solution)/shard_map/ppermute | solution.py:20
  168.8 15.7 %all-to-all-done.3 = bf16[8,256,128]{2,1,0:T(8,128)(2,1)S(1)} async-done(((bf16[8,256,128]{2,1,0:T(8,128)(2,1)}), bf16[8,256,128]{2,1,0:T(8,128)(2,1)S(1)}, u32[]{:S(2)}, u32[]{:S(2)}) %all-to-all-start.3) | async-done | bytes 524320 | tf_op jit(solution)/shard_map/all_to_all | solution.py:41
  184.6 2.7 %collective-permute-start.10 = (bf16[2,128,512]{2,1,0:T(8,128)(2,1)S(1)}, bf16[2,128,512]{2,1,0:T(8,128)(2,1)S(1)}, u32[]{:S(2)}, u32[]{:S(2)}) collective-permute-start(bf16[2,128,512]{2,1,0:T(8,128)(2,1)S(1)} %get-tuple-element.32), channel_id=1, source_target_pairs={{0,12},{1,13},{2,14},{3,15},{4,0},{5,1},{6,2},{7,3},{8,4},{9,5},{1... | collective-permute-start | bytes 786440 | tf_op jit(solution)/shard_map/ppermute | solution.py:20
  188.8 1.6 collective-permute-start.7
  190.4 4.1 %collective-permute-done.10.rest_3_ = bf16[2,128,512]{2,1,0:T(8,128)(2,1)S(1)} collective-permute-done((bf16[2,128,512]{2,1,0:T(8,128)(2,1)S(1)}, bf16[2,128,512]{2,1,0:T(8,128)(2,1)S(1)}, u32[]{:S(2)}, u32[]{:S(2)}) %collective-permute-start.10) | collective-permute-done | bytes 262176 | tf_op jit(solution)/shard_map/ppermute | solution.py:20
  194.5 5.0 %collective-permute-done.9.rest_2_ = bf16[2,128,512]{2,1,0:T(8,128)(2,1)S(1)} collective-permute-done((bf16[2,128,512]{2,1,0:T(8,128)(2,1)S(1)}, bf16[2,128,512]{2,1,0:T(8,128)(2,1)S(1)}, u32[]{:S(2)}, u32[]{:S(2)}) %collective-permute-start.9) | collective-permute-done | bytes 262176 | tf_op jit(solution)/shard_map/ppermute | solution.py:20
  199.5 5.2 %collective-permute-done.8.rest_1_ = bf16[2,128,512]{2,1,0:T(8,128)(2,1)S(1)} collective-permute-done((bf16[2,128,512]{2,1,0:T(8,128)(2,1)S(1)}, bf16[2,128,512]{2,1,0:T(8,128)(2,1)S(1)}, u32[]{:S(2)}, u32[]{:S(2)}) %collective-permute-start.8) | collective-permute-done | bytes 262176 | tf_op jit(solution)/shard_map/ppermute | solution.py:20
  204.7 2.8 %collective-permute-done.7.rest_0_ = bf16[2,128,512]{2,1,0:T(8,128)(2,1)S(1)} collective-permute-done((bf16[2,128,512]{2,1,0:T(8,128)(2,1)S(1)}, bf16[2,128,512]{2,1,0:T(8,128)(2,1)S(1)}, u32[]{:S(2)}, u32[]{:S(2)}) %collective-permute-start.7) | collective-permute-done | bytes 262176 | tf_op jit(solution)/shard_map/ppermute | solution.py:20
  208.4 5.1 %shard_map.105 = (bf16[16,128,512]{2,1,0:T(8,128)(2,1)}, bf16[16,128,512]{2,1,0:T(8,128)(2,1)}) custom-call(s32[2]{0:T(128)} %pad_add_fusion.place, s32[4,8]{1,0:T(4,128)} %verts.5, f32[2,128,512]{2,1,0:T(8,128)} %get-tuple-element.25.home, bf16[2,128,512]{2,1,0:T(8,128)(2,1)} %copy-done.14, bf16[2,128,512]{2,1,0:T(8,128)(2,1)} %copy-done.13, ...), custom_call_target="tpu_custom_call" | custom-call | tf_op jit(solution)/shard_map/pallas_call | solution.py:372
  (61 shorter events, 9.0 us)
Async XLA Ops:
  45.1 2.3 %collective-permute-start = (bf16[2048,128]{1,0:T(8,128)(2,1)}, bf16[2048,128]{1,0:T(8,128)(2,1)S(1)}, u32[]{:S(2)}, u32[]{:S(2)}) collective-permute-start(bf16[2048,128]{1,0:T(8,128)(2,1)} %get-tuple-element.18), channel_id=1, source_target_pairs={{0,1},{1,0},{2,3},{3,2},{4,5},{5,4},{6,7},{7,6},{8,9},{9,8},{10,11... | collective-permute-start | bytes 1572872 | tf_op jit(solution)/shard_map/ppermute | solution.py:25
  47.3 27.6 %copy-start.19 = (bf16[2,128,512]{2,1,0:T(8,128)(2,1)S(1)}, bf16[2,128,512]{2,1,0:T(8,128)(2,1)}, u32[]{:S(2)}) copy-start(bf16[2,128,512]{2,1,0:T(8,128)(2,1)} %get-tuple-element.19) | copy-start | bytes 786436
  47.3 41.8 %copy-start.18 = (bf16[2,128,512]{2,1,0:T(8,128)(2,1)S(1)}, bf16[2,128,512]{2,1,0:T(8,128)(2,1)}, u32[]{:S(2)}) copy-start(bf16[2,128,512]{2,1,0:T(8,128)(2,1)} %get-tuple-element.20) | copy-start | bytes 786436
  47.3 46.1 %copy-start.17 = (bf16[2,128,512]{2,1,0:T(8,128)(2,1)S(1)}, bf16[2,128,512]{2,1,0:T(8,128)(2,1)}, u32[]{:S(2)}) copy-start(bf16[2,128,512]{2,1,0:T(8,128)(2,1)} %get-tuple-element.21) | copy-start | bytes 786436
  47.3 46.6 %copy-start.16 = (bf16[2,128,512]{2,1,0:T(8,128)(2,1)S(1)}, bf16[2,128,512]{2,1,0:T(8,128)(2,1)}, u32[]{:S(2)}) copy-start(bf16[2,128,512]{2,1,0:T(8,128)(2,1)} %get-tuple-element.22) | copy-start | bytes 786436
  47.3 46.7 %copy-start.15 = (bf16[2,128,512]{2,1,0:T(8,128)(2,1)S(1)}, bf16[2,128,512]{2,1,0:T(8,128)(2,1)}, u32[]{:S(2)}) copy-start(bf16[2,128,512]{2,1,0:T(8,128)(2,1)} %get-tuple-element.23) | copy-start | bytes 786436
  71.3 17.8 %all-to-all-start.1 = ((bf16[8,256,128]{2,1,0:T(8,128)(2,1)}), bf16[8,256,128]{2,1,0:T(8,128)(2,1)S(1)}, u32[]{:S(2)}, u32[]{:S(2)}) async-start(bf16[8,256,128]{2,1,0:T(8,128)(2,1)} %broadcast_in_dim.4), calls=%async_computation.1 | async-start | bytes 1048576 | tf_op jit(solution)/shard_map/all_to_all | solution.py:41
  75.0 19.0 %collective-permute-start.2 = (bf16[2,128,512]{2,1,0:T(8,128)(2,1)S(1)}, bf16[2,128,512]{2,1,0:T(8,128)(2,1)S(1)}, u32[]{:S(2)}, u32[]{:S(2)}) collective-permute-start(bf16[2,128,512]{2,1,0:T(8,128)(2,1)S(1)} %copy-done.19), channel_id=1, source_target_pairs={{0,1},{1,2},{2,3},{3,4},{4,5},{5,6},{6,7},{7,8},{8,9},{9,10},{10,1... | collective-permute-start | bytes 786440 | tf_op jit(solution)/shard_map/ppermute | solution.py:20
  89.1 31.1 %copy-start = (bf16[8,256,128]{2,1,0:T(8,128)(2,1)}, bf16[8,256,128]{2,1,0:T(8,128)(2,1)S(1)}, u32[]{:S(2)}) copy-start(bf16[8,256,128]{2,1,0:T(8,128)(2,1)S(1)} %all-to-all-done.1) | copy-start | bytes 1572868
  89.2 31.1 %collective-permute-start.1 = (bf16[2048,128]{1,0:T(8,128)(2,1)S(1)}, bf16[2048,128]{1,0:T(8,128)(2,1)S(1)}, u32[]{:S(2)}, u32[]{:S(2)}) collective-permute-start(bf16[2048,128]{1,0:T(8,128)(2,1)S(1)} %bitcast.15), channel_id=1, source_target_pairs={{0,1},{1,0},{2,3},{3,2},{4,5},{5,4},{6,7},{7,6},{8,9},{9,8},{10,11... | collective-permute-start | bytes 1572872 | tf_op jit(solution)/shard_map/ppermute | solution.py:25
  89.2 12.0 %collective-permute-start.3 = (bf16[2,128,512]{2,1,0:T(8,128)(2,1)S(1)}, bf16[2,128,512]{2,1,0:T(8,128)(2,1)S(1)}, u32[]{:S(2)}, u32[]{:S(2)}) collective-permute-start(bf16[2,128,512]{2,1,0:T(8,128)(2,1)S(1)} %copy-done.18), channel_id=1, source_target_pairs={{0,2},{1,3},{2,4},{3,5},{4,6},{5,7},{6,8},{7,9},{8,10},{9,11},{10,... | collective-permute-start | bytes 786440 | tf_op jit(solution)/shard_map/ppermute | solution.py:20
  93.4 9.3 %collective-permute-start.4 = (bf16[2,128,512]{2,1,0:T(8,128)(2,1)S(1)}, bf16[2,128,512]{2,1,0:T(8,128)(2,1)S(1)}, u32[]{:S(2)}, u32[]{:S(2)}) collective-permute-start(bf16[2,128,512]{2,1,0:T(8,128)(2,1)S(1)} %copy-done.17), channel_id=1, source_target_pairs={{0,3},{1,4},{2,5},{3,6},{4,7},{5,8},{6,9},{7,10},{8,11},{9,12},{10... | collective-permute-start | bytes 786440 | tf_op jit(solution)/shard_map/ppermute | solution.py:20
  94.0 11.0 %collective-permute-start.5 = (bf16[2,128,512]{2,1,0:T(8,128)(2,1)S(1)}, bf16[2,128,512]{2,1,0:T(8,128)(2,1)S(1)}, u32[]{:S(2)}, u32[]{:S(2)}) collective-permute-start(bf16[2,128,512]{2,1,0:T(8,128)(2,1)S(1)} %copy-done.16), channel_id=1, source_target_pairs={{0,4},{1,5},{2,6},{3,7},{4,8},{5,9},{6,10},{7,11},{8,12},{9,13},{1... | collective-permute-start | bytes 786440 | tf_op jit(solution)/shard_map/ppermute | solution.py:20
  94.0 26.3 %copy-start.5 = (bf16[2,128,512]{2,1,0:T(8,128)(2,1)}, bf16[2,128,512]{2,1,0:T(8,128)(2,1)S(1)}, u32[]{:S(2)}) copy-start(bf16[2,128,512]{2,1,0:T(8,128)(2,1)S(1)} %collective-permute-done.2.rest_0_) | copy-start | bytes 786436
  94.0 26.2 %collective-permute-start.6 = (bf16[2,128,512]{2,1,0:T(8,128)(2,1)S(1)}, bf16[2,128,512]{2,1,0:T(8,128)(2,1)S(1)}, u32[]{:S(2)}, u32[]{:S(2)}) collective-permute-start(bf16[2,128,512]{2,1,0:T(8,128)(2,1)S(1)} %copy-done.15), channel_id=1, source_target_pairs={{0,5},{1,6},{2,7},{3,8},{4,9},{5,10},{6,11},{7,12},{8,13},{9,14},{... | collective-permute-start | bytes 786440 | tf_op jit(solution)/shard_map/ppermute | solution.py:20
  140.1 2.2 %collective-permute-start.12 = (bf16[2048,128]{1,0:T(8,128)(2,1)}, bf16[2048,128]{1,0:T(8,128)(2,1)S(1)}, u32[]{:S(2)}, u32[]{:S(2)}) collective-permute-start(bf16[2048,128]{1,0:T(8,128)(2,1)} %get-tuple-element.28), channel_id=1, source_target_pairs={{0,1},{1,0},{2,3},{3,2},{4,5},{5,4},{6,7},{7,6},{8,9},{9,8},{10,11... | collective-permute-start | bytes 1572872 | tf_op jit(solution)/shard_map/ppermute | solution.py:25
  162.2 22.4 %all-to-all-start.3 = ((bf16[8,256,128]{2,1,0:T(8,128)(2,1)}), bf16[8,256,128]{2,1,0:T(8,128)(2,1)S(1)}, u32[]{:S(2)}, u32[]{:S(2)}) async-start(bf16[8,256,128]{2,1,0:T(8,128)(2,1)} %broadcast_in_dim.5), calls=%async_computation.3 | async-start | bytes 1048576 | tf_op jit(solution)/shard_map/all_to_all | solution.py:41
  165.9 22.9 %collective-permute-start.11 = (bf16[2,128,512]{2,1,0:T(8,128)(2,1)S(1)}, bf16[2,128,512]{2,1,0:T(8,128)(2,1)S(1)}, u32[]{:S(2)}, u32[]{:S(2)}) collective-permute-start(bf16[2,128,512]{2,1,0:T(8,128)(2,1)S(1)} %get-tuple-element.31), channel_id=1, source_target_pairs={{0,11},{1,12},{2,13},{3,14},{4,15},{5,0},{6,1},{7,2},{8,3},{9,4},{... | collective-permute-start | bytes 786440 | tf_op jit(solution)/shard_map/ppermute | solution.py:20
  184.6 23.0 %copy-start.1 = (bf16[8,256,128]{2,1,0:T(8,128)(2,1)}, bf16[8,256,128]{2,1,0:T(8,128)(2,1)S(1)}, u32[]{:S(2)}) copy-start(bf16[8,256,128]{2,1,0:T(8,128)(2,1)S(1)} %all-to-all-done.3) | copy-start | bytes 1572868
  184.6 23.0 %collective-permute-start.13 = (bf16[2048,128]{1,0:T(8,128)(2,1)S(1)}, bf16[2048,128]{1,0:T(8,128)(2,1)S(1)}, u32[]{:S(2)}, u32[]{:S(2)}) collective-permute-start(bf16[2048,128]{1,0:T(8,128)(2,1)S(1)} %bitcast.18), channel_id=1, source_target_pairs={{0,1},{1,0},{2,3},{3,2},{4,5},{5,4},{6,7},{7,6},{8,9},{9,8},{10,11... | collective-permute-start | bytes 1572872 | tf_op jit(solution)/shard_map/ppermute | solution.py:25
  184.6 10.0 %collective-permute-start.10 = (bf16[2,128,512]{2,1,0:T(8,128)(2,1)S(1)}, bf16[2,128,512]{2,1,0:T(8,128)(2,1)S(1)}, u32[]{:S(2)}, u32[]{:S(2)}) collective-permute-start(bf16[2,128,512]{2,1,0:T(8,128)(2,1)S(1)} %get-tuple-element.32), channel_id=1, source_target_pairs={{0,12},{1,13},{2,14},{3,15},{4,0},{5,1},{6,2},{7,3},{8,4},{9,5},{1... | collective-permute-start | bytes 786440 | tf_op jit(solution)/shard_map/ppermute | solution.py:20
  187.3 12.2 %collective-permute-start.9 = (bf16[2,128,512]{2,1,0:T(8,128)(2,1)S(1)}, bf16[2,128,512]{2,1,0:T(8,128)(2,1)S(1)}, u32[]{:S(2)}, u32[]{:S(2)}) collective-permute-start(bf16[2,128,512]{2,1,0:T(8,128)(2,1)S(1)} %get-tuple-element.33), channel_id=1, source_target_pairs={{0,13},{1,14},{2,15},{3,0},{4,1},{5,2},{6,3},{7,4},{8,5},{9,6},{10... | collective-permute-start | bytes 786440 | tf_op jit(solution)/shard_map/ppermute | solution.py:20
  188.3 16.4 %collective-permute-start.8 = (bf16[2,128,512]{2,1,0:T(8,128)(2,1)S(1)}, bf16[2,128,512]{2,1,0:T(8,128)(2,1)S(1)}, u32[]{:S(2)}, u32[]{:S(2)}) collective-permute-start(bf16[2,128,512]{2,1,0:T(8,128)(2,1)S(1)} %get-tuple-element.34), channel_id=1, source_target_pairs={{0,14},{1,15},{2,0},{3,1},{4,2},{5,3},{6,4},{7,5},{8,6},{9,7},{10,... | collective-permute-start | bytes 786440 | tf_op jit(solution)/shard_map/ppermute | solution.py:20
  188.8 18.7 %collective-permute-start.7 = (bf16[2,128,512]{2,1,0:T(8,128)(2,1)S(1)}, bf16[2,128,512]{2,1,0:T(8,128)(2,1)S(1)}, u32[]{:S(2)}, u32[]{:S(2)}) collective-permute-start(bf16[2,128,512]{2,1,0:T(8,128)(2,1)S(1)} %get-tuple-element.35), channel_id=1, source_target_pairs={{0,15},{1,0},{2,1},{3,2},{4,3},{5,4},{6,5},{7,6},{8,7},{9,8},{10,9... | collective-permute-start | bytes 786440 | tf_op jit(solution)/shard_map/ppermute | solution.py:20
  (12 other events, 120.0 us)

commit v3 on v1

--- a/solution.py
+++ b/solution.py
@@ -10,42 +10,102 @@
 
 BLOCK = 64
 WDEV = 5
-VMEM_LIMIT = 40 * 1024 * 1024
+VMEM_LIMIT = 60 * 1024 * 1024
 BF16 = jnp.bfloat16
 F32 = jnp.float32
 
 
-def from_behind(shard, by):
-    peers = lax.axis_size("ctx")
-    return lax.ppermute(shard, "ctx", [(i, (i + by) % peers) for i in range(peers)])
-
-
-def pack_kernel(place, verts, keys, values, *rest, devices, heads, nv, per_device):
-    sends, picked, sems, pick_sems = rest[:WDEV], rest[WDEV], rest[WDEV + 1], rest[WDEV + 2]
+class Lines:
+    def __init__(self, devices):
+        self.devices = devices
+        self.far = devices // 4
+
+    def place(self, me):
+        return me // 4, (me // 2) % 2, me % 2
+
+    def core_pairs(self):
+        return [(i, i ^ 1) for i in range(self.devices)]
+
+    def near_pairs(self):
+        return [(i, i ^ 2) for i in range(self.devices)]
+
+    def far_pairs(self, by):
+        return [(i, (i + 4 * by) % self.devices) for i in range(self.devices)]
+
+    def shift_pairs(self, by):
+        return [(i, (i + by) % self.devices) for i in range(self.devices)]
+
+    def mixed_pairs(self):
+        return [(i, (i + (5 if i % 2 else 1)) % self.devices) for i in range(self.devices)]
+
+
+def back(pairs):
+    return [(b, a) for a, b in pairs]
+
+
+def move(array, pairs):
+    return lax.ppermute(array, "ctx", pairs)
+
+
+def gather_verticals(lines, own):
+    parts = [own] + [move(own, lines.far_pairs(by)) for by in range(1, lines.far)]
+    mine = jnp.stack(parts)
+    across = move(mine, lines.near_pairs())
+    core_mine = move(mine, lines.core_pairs())
+    core_across = move(across, lines.core_pairs())
+    return mine, across, core_mine, core_across
+
+
+def sum_verticals(lines, keep, give, wide):
+    half = keep.astype(wide) + move(give, lines.core_pairs()).astype(wide)
+    quarter = half[0] + move(half[1].astype(BF16), lines.near_pairs()).astype(wide)
+    share = quarter[0]
+    for by in range(1, lines.far):
+        share = share + move(quarter[by].astype(BF16), lines.far_pairs(by)).astype(wide)
+    return share.astype(BF16)
+
+
+def wraps(me, devices):
+    return [me + 2 >= devices, me + 4 >= devices, (me % 2 == 1) & (me + 5 >= devices)]
+
+
+def pack_kernel(place, verts, keys, values, *rest, lines, heads, nv, per_device):
+    sends = rest[:3]
+    keep, give, picked, sems, pick_sems = rest[3:]
     slab, me = place[0], place[1]
-    head_dim = picked.shape[2]
+    far, near, core = lines.place(me)
+    _, _, chunk, head_dim = keep.shape
     copies = []
-    for distance in range(1, WDEV + 1):
-        region = slab - (me + distance >= devices).astype(jnp.int32)
+    for n, wrapped in enumerate(wraps(me, lines.devices)):
+        region = slab - wrapped.astype(jnp.int32)
         for kv, source in enumerate((keys, values)):
-            copy = pltpu.make_async_copy(
-                source.at[region], sends[distance - 1].at[kv], sems.at[distance - 1, kv]
-            )
+            copy = pltpu.make_async_copy(source.at[region], sends[n].at[kv], sems.at[n, kv])
             copy.start()
             copies.append(copy)
     picked[...] = jnp.zeros_like(picked)
-    slab_blocks = per_device * devices
-
-    def unit_copy(h, m, kv, source):
+    slab_blocks = per_device * lines.devices
+    piece = min(BLOCK, chunk)
+
+    def unit_copies(h, m):
         inner = verts[h, m] % slab_blocks
         region = verts[h, m] // slab_blocks
-        row = pl.multiple_of((inner % per_device) * BLOCK, BLOCK)
-        unit = h * nv + m
-        return pltpu.make_async_copy(
-            source.at[region, pl.ds(row, BLOCK), pl.ds(h * head_dim, head_dim)],
-            picked.at[kv, pl.ds(unit * BLOCK, BLOCK), :],
-            pick_sems.at[kv, unit],
-        )
+        row = (inner % per_device) * BLOCK
+        for p in range(BLOCK // piece):
+            at = (h * nv + m) * BLOCK + p * piece
+            line, at = at // (lines.far * chunk), at % (lines.far * chunk)
+            slot, at = at // chunk, at % chunk
+            line = lax.rem(line + near, 2)
+            slot = lax.rem(slot - far + lines.far, lines.far)
+            for kv, source in enumerate((keys, values)):
+                yield pltpu.make_async_copy(
+                    source.at[
+                        region,
+                        pl.ds(pl.multiple_of(row + p * piece, piece), piece),
+                        pl.ds(h * head_dim, head_dim),
+                    ],
+                    picked.at[lax.rem(kv + core, 2), line, slot, pl.ds(at, piece), :],
+                    pick_sems.at[kv, (h * nv + m) * (BLOCK // piece) + p],
+                )
 
     def owned(h, m):
         return (verts[h, m] % slab_blocks) // per_device == me
@@ -55,52 +115,78 @@
 
             @pl.when(owned(h, m))
             def _():
-                unit_copy(h, m, 0, keys).start()
-                unit_copy(h, m, 1, values).start()
+                for copy in unit_copies(h, m):
+                    copy.start()
 
     for h in range(heads):
         for m in range(nv):
 
             @pl.when(owned(h, m))
             def _():
-                unit_copy(h, m, 0, keys).wait()
-                unit_copy(h, m, 1, values).wait()
-
+                for copy in unit_copies(h, m):
+                    copy.wait()
+
+    keep[...] = picked[0]
+    give[...] = picked[1]
     for copy in copies:
         copy.wait()
 
 
-def pack(place, verticals, keys, values, devices):
+def pack(place, verticals, keys, values, lines):
     regions, rows, features = keys.shape
     heads, nv = verticals.shape
     head_dim = features // heads
+    chunk = heads * nv * BLOCK // (2 * lines.far)
     smem = pl.BlockSpec(memory_space=pltpu.SMEM)
     hbm = pl.BlockSpec(memory_space=pl.ANY)
+    share = (2, lines.far, chunk, head_dim)
     return pl.pallas_call(
-        functools.partial(
-            pack_kernel, devices=devices, heads=heads, nv=nv, per_device=rows // BLOCK
-        ),
+        functools.partial(pack_kernel, lines=lines, heads=heads, nv=nv, per_device=rows // BLOCK),
         in_specs=[smem, smem, hbm, hbm],
-        out_specs=[hbm] * WDEV + [pl.BlockSpec(memory_space=pltpu.VMEM)],
-        out_shape=[jax.ShapeDtypeStruct((2, rows, features), BF16)] * WDEV
-        + [jax.ShapeDtypeStruct((2, heads * nv * BLOCK, head_dim), BF16)],
+        out_specs=[pl.BlockSpec(memory_space=pltpu.VMEM)] * 5,
+        out_shape=[jax.ShapeDtypeStruct((2, rows, features), BF16)] * 3
+        + [jax.ShapeDtypeStruct(share, BF16)] * 2,
         scratch_shapes=[
-            pltpu.SemaphoreType.DMA((WDEV, 2)),
-            pltpu.SemaphoreType.DMA((2, heads * nv)),
+            pltpu.VMEM((2,) + share, BF16),
+            pltpu.SemaphoreType.DMA((3, 2)),
+            pltpu.SemaphoreType.DMA((2, heads * nv * max(1, BLOCK // chunk))),
         ],
         compiler_params=pltpu.CompilerParams(vmem_limit_bytes=VMEM_LIMIT),
     )(place, verticals, keys, values)
 
 
+def distances(core):
+    return [2, 4, 5 - 4 * core, 1 + 2 * core, 3 + 2 * core]
+
+
+def vertical_copies(lines, me, chunk, gathered, to, sems, first):
+    far, near, core = lines.place(me)
+    copies = []
+    for n, source in enumerate(gathered):
+        kv = core if n < 2 else 1 - core
+        line = near if n % 2 == 0 else 1 - near
+        for s in range(lines.far):
+            slot = lax.rem(far - s + lines.far, lines.far)
+            row = pl.multiple_of((line * lines.far + slot) * chunk, chunk)
+            copies.append(
+                pltpu.make_async_copy(
+                    source.at[s], to.at[kv, pl.ds(row, chunk), :], sems.at[first + len(copies)]
+                )
+            )
+    return copies
+
+
 def attend_kernel(
-    place, verts, offs, q, grad, out, keys, values, vert, *rest,
-    devices, heads, nv, ns, per_device,
+    place, verts, offs, q, grad, out, keys, values, *rest, lines, heads, nv, ns, per_device,
 ):
-    recv = rest[:WDEV]
-    dq, near, home, vgrad = rest[WDEV : WDEV + 4]
-    (win, vkv, kc, vc, qs, gs, s_ref, dp_ref, w_ref, ds_ref, nacc, vacc, sems) = rest[WDEV + 4 :]
+    gathered, recv, rest = rest[:4], rest[4 : 4 + WDEV], rest[4 + WDEV :]
+    dq, home, near_parts, vkeep, vgive = rest[0], rest[1], rest[2 : 2 + WDEV], rest[-15], rest[-14]
+    (win, vkv, kc, vc, qs, gs, s_ref, dp_ref, w_ref, ds_ref, nacc, vacc, sems) = rest[-13:]
     h, j = pl.program_id(0), pl.program_id(1)
     slab, me = place[0], place[1]
+    far, near, core = lines.place(me)
+    devices = lines.devices
+    _, _, chunk, _ = vkeep.shape
     head_dim = kc.shape[1]
     group = q.shape[1] // head_dim
     cand = 1 + nv + ns
@@ -109,20 +195,23 @@
     block = slab * (per_device * devices) + me * per_device + j
     lanes = pl.ds(pl.multiple_of(h * head_dim, head_dim), head_dim)
 
+    def window_row(d):
+        return pl.multiple_of((WDEV - d) * rows, rows)
+
     @pl.when((h == 0) & (j == 0))
     def _():
         copies = [
             pltpu.make_async_copy(
-                recv[d - 1], win.at[:, pl.ds((WDEV - d) * rows, rows), :], sems.at[d - 1]
+                recv[n], win.at[:, pl.ds(window_row(d), rows), :], sems.at[n]
             )
-            for d in range(1, WDEV + 1)
+            for n, d in enumerate(distances(core))
         ]
         own_rows = pl.ds(WDEV * rows, rows)
         copies.append(pltpu.make_async_copy(keys.at[slab], win.at[0, own_rows, :], sems.at[WDEV]))
         copies.append(
             pltpu.make_async_copy(values.at[slab], win.at[1, own_rows, :], sems.at[WDEV + 1])
         )
-        copies.append(pltpu.make_async_copy(vert, vkv, sems.at[WDEV + 2]))
+        copies += vertical_copies(lines, me, chunk, gathered, vkv, sems, WDEV + 2)
         for copy in copies:
             copy.start()
         nacc[...] = jnp.zeros_like(nacc)
@@ -223,16 +312,21 @@
 
     @pl.when(j == per_device - 1)
     def _():
+        per_line = heads // 2
+        for c in range(nv * BLOCK // chunk):
+            line = lax.rem(h // per_line + near, 2)
+            slot = (h % per_line) * (nv * BLOCK // chunk) + c
+            slot = lax.rem(slot - far + lines.far, lines.far)
+            span = slice(c * chunk, (c + 1) * chunk)
+            vkeep[line, slot] = vacc[core, span, :]
+            vgive[line, slot] = vacc[1 - core, span, :].astype(BF16)
         for kv in range(2):
-            vgrad[kv, pl.ds(vert_at, nv * BLOCK), :] = vacc[kv].astype(BF16)
             home[kv, :, lanes] = nacc[kv, WDEV * rows :, lanes]
-            for d in range(1, WDEV + 1):
-                near[d - 1, kv, :, lanes] = nacc[
-                    kv, (WDEV - d) * rows : (WDEV - d + 1) * rows, lanes
-                ].astype(BF16)
-
-
-def attend(place, verticals, offsets, queries, cotangent, output, keys, values, vert, recv, devices):
+            for part, d in zip(near_parts, distances(core)):
+                part[kv, :, lanes] = nacc[kv, pl.ds(window_row(d), rows), lanes].astype(part.dtype)
+
+
+def attend(place, verticals, offsets, queries, cotangent, output, keys, values, gathered, recv, lines):
     rows, width = queries.shape
     features = keys.shape[2]
     heads, nv = verticals.shape
@@ -248,21 +342,26 @@
     def whole(shape):
         return pl.BlockSpec(shape, lambda h, j: (0,) * len(shape))
 
-    near_shape = (WDEV, 2, rows, features)
-    home_shape = (2, rows, features)
+    shard = (2, rows, features)
     vert_shape = (2, heads * nv * BLOCK, head_dim)
+    share = (2, lines.far, heads * nv * BLOCK // (2 * lines.far), head_dim)
     return pl.pallas_call(
         functools.partial(
-            attend_kernel, devices=devices, heads=heads, nv=nv, ns=ns, per_device=per_device
+            attend_kernel, lines=lines, heads=heads, nv=nv, ns=ns, per_device=per_device
         ),
         grid=(heads, per_device),
-        in_specs=[smem] * 3 + [tile] * 3 + [hbm] * (3 + WDEV),
-        out_specs=[tile, whole(near_shape), whole(home_shape), whole(vert_shape)],
+        in_specs=[smem] * 3 + [tile] * 3 + [hbm] * (6 + WDEV),
+        out_specs=[tile] + [whole(shard)] * (1 + WDEV) + [whole(share)] * 2,
         out_shape=[
             jax.ShapeDtypeStruct((rows, width), BF16),
-            jax.ShapeDtypeStruct(near_shape, BF16),
-            jax.ShapeDtypeStruct(home_shape, F32),
-            jax.ShapeDtypeStruct(vert_shape, BF16),
+            jax.ShapeDtypeStruct(shard, F32),
+            jax.ShapeDtypeStruct(shard, F32),
+            jax.ShapeDtypeStruct(shard, F32),
+            jax.ShapeDtypeStruct(shard, BF16),
+            jax.ShapeDtypeStruct(shard, BF16),
+            jax.ShapeDtypeStruct(shard, BF16),
+            jax.ShapeDtypeStruct(share, F32),
+            jax.ShapeDtypeStruct(share, BF16),
         ],
         scratch_shapes=[
             pltpu.VMEM((2, (WDEV + 1) * rows, features), BF16),
@@ -277,26 +376,34 @@
             pltpu.VMEM((cand * BLOCK, group * BLOCK), BF16),
             pltpu.VMEM((2, (WDEV + 1) * rows, features), F32),
             pltpu.VMEM((2, nv * BLOCK, head_dim), F32),
-            pltpu.SemaphoreType.DMA((WDEV + 3,)),
+            pltpu.SemaphoreType.DMA((WDEV + 2 + 4 * lines.far,)),
         ],
         compiler_params=pltpu.CompilerParams(vmem_limit_bytes=VMEM_LIMIT),
-    )(place, verticals, offsets, queries, cotangent, output, keys, values, vert, *recv)
-
-
-def assemble_kernel(place, verts, home, *rest, devices, heads, nv, per_device):
-    back = rest[:WDEV]
-    vert, key_out, value_out, acc = rest[WDEV:]
+    )(
+        place, verticals, offsets, queries, cotangent, output, keys, values, *gathered, *recv,
+    )
+
+
+def assemble_kernel(place, verts, home, *rest, lines, heads, nv, per_device):
+    arrived, gathered = rest[:3], rest[3:7]
+    key_out, value_out, vert, acc, sems = rest[7:]
     slab, me = place[0], place[1]
+    devices = lines.devices
+    chunk = gathered[0].shape[1]
+    copies = vertical_copies(lines, me, chunk, gathered, vert, sems, 0)
+    for copy in copies:
+        copy.start()
     head_dim = vert.shape[2]
     slab_blocks = per_device * devices
     acc[0] = home[...]
     acc[1] = jnp.zeros_like(home)
-    for d in range(1, WDEV + 1):
-        slot = (me + d >= devices).astype(jnp.int32)
-        acc[slot] += back[d - 1][...].astype(F32)
+    for part, wrapped in zip(arrived, wraps(me, devices)):
+        acc[wrapped.astype(jnp.int32)] += part[...].astype(F32)
     key_out[...] = jnp.zeros_like(key_out)
     value_out[...] = jnp.zeros_like(value_out)
     outs = (key_out, value_out)
+    for copy in copies:
+        copy.wait()
     for h in range(heads):
         lanes = slice(h * head_dim, (h + 1) * head_dim)
         for m in range(nv):
@@ -326,21 +433,26 @@
         outs[kv][slab - 1] = acc[1, kv].astype(BF16)
 
 
-def assemble(place, verticals, home, back, vert, regions, devices):
+def assemble(place, verticals, home, arrived, gathered, regions, lines):
     _, rows, features = home.shape
     heads, nv = verticals.shape
     smem = pl.BlockSpec(memory_space=pltpu.SMEM)
     vmem = pl.BlockSpec(memory_space=pltpu.VMEM)
+    hbm = pl.BlockSpec(memory_space=pl.ANY)
     return pl.pallas_call(
         functools.partial(
-            assemble_kernel, devices=devices, heads=heads, nv=nv, per_device=rows // BLOCK
+            assemble_kernel, lines=lines, heads=heads, nv=nv, per_device=rows // BLOCK
         ),
-        in_specs=[smem] * 2 + [vmem] * (2 + WDEV),
+        in_specs=[smem] * 2 + [vmem] * 4 + [hbm] * 4,
         out_specs=[vmem] * 2,
         out_shape=[jax.ShapeDtypeStruct((regions, rows, features), BF16)] * 2,
-        scratch_shapes=[pltpu.VMEM((2, 2, rows, features), F32)],
+        scratch_shapes=[
+            pltpu.VMEM((2, heads * nv * BLOCK, features // heads), BF16),
+            pltpu.VMEM((2, 2, rows, features), F32),
+            pltpu.SemaphoreType.DMA((4 * lines.far,)),
+        ],
         compiler_params=pltpu.CompilerParams(vmem_limit_bytes=VMEM_LIMIT),
-    )(place, verticals, home, *back, vert)
+    )(place, verticals, home, *arrived, *gathered)
 
 
 def shards(
@@ -353,24 +465,34 @@
     offsets,
     slab_index,
 ):
-    devices = lax.axis_size("ctx")
-    me = lax.axis_index("ctx")
+    lines = Lines(lax.axis_size("ctx"))
+    me = lax.axis_index("ctx").astype(jnp.int32)
     regions = context_keys.shape[0]
-    place = jnp.stack([slab_index[0], me.astype(jnp.int32)])
-    *sends, picked = pack(place, verticals, context_keys, context_values, devices)
-    vert = lax.psum(picked, "ctx")
-    recv = [from_behind(sends[d - 1], d) for d in range(1, WDEV + 1)]
-    query_grad, near, home, vgrad = attend(
+    place = jnp.stack([slab_index[0], me])
+
+    send2, send4, mixed, keep, give = pack(place, verticals, context_keys, context_values, lines)
+    recv2 = move(send2, lines.shift_pairs(2))
+    recv4 = move(send4, lines.shift_pairs(4))
+    recv_mixed = move(mixed, lines.mixed_pairs())
+    other2 = move(recv2, lines.core_pairs())
+    other4 = move(recv4, lines.core_pairs())
+    gathered = gather_verticals(lines, sum_verticals(lines, keep, give, BF16))
+
+    query_grad, home, part2, part4, mixed, give2, give4, vkeep, vgive = attend(
         place, verticals, offsets, queries, output_cotangent, forward_output,
-        context_keys, context_values, vert, recv, devices,
+        context_keys, context_values, gathered, [recv2, recv4, recv_mixed, other2, other4], lines,
     )
-    flat = vgrad.reshape(devices, -1, vgrad.shape[-1])
-    shares = lax.all_to_all(flat, "ctx", 0, 0, tiled=True)
-    summed = jnp.sum(shares.astype(F32), axis=0).astype(BF16)
-    vert_sum = lax.all_gather(summed, "ctx", axis=0, tiled=True).reshape(vgrad.shape)
-    back = [from_behind(near[d - 1], -d) for d in range(1, WDEV + 1)]
+
+    sum2 = (part2 + move(give2, lines.core_pairs()).astype(F32)).astype(BF16)
+    sum4 = (part4 + move(give4, lines.core_pairs()).astype(F32)).astype(BF16)
+    arrived = [
+        move(sum2, back(lines.shift_pairs(2))),
+        move(sum4, back(lines.shift_pairs(4))),
+        move(mixed, back(lines.mixed_pairs())),
+    ]
+    totals = gather_verticals(lines, sum_verticals(lines, vkeep, vgive, F32))
     key_gradient, value_gradient = assemble(
-        place, verticals, home, back, vert_sum, regions, devices
+        place, verticals, home, arrived, totals, regions, lines
     )
     return query_grad, key_gradient, value_gradient
 

time: 252 us -> 134 us (0.53)
  waiting for transfers between devices: 147 us -> 56.3 us
  blocking collectives: 28.6 us -> 0 us
  starting transfers between devices: 14.4 us -> 41.3 us
  local copies, waits for them, and re-layouts: 20.7 us -> 1.86 us
  between operations: 14.8 us -> 1.59 us
  Pallas kernels: 25.1 us -> 28.5 us
  other arithmetic: 0.85 us -> 3.51 us
    psum x1 -> x0, waiting for transfers between devices: 70.6 us -> none  [shards(): vert = lax.psum(picked, 'ctx')]
    all_to_all x1 -> x0, blocking collectives: 28.6 us -> none  [shards(): shares = lax.all_to_all(flat, 'ctx', 0, 0, tiled=True)]
    ppermute x10 -> x32, starting transfers between devices: 14.3 us -> 41.3 us  [move(): return lax.ppermute(array, 'ctx', pairs)]
    all_gather x1 -> x0, waiting for transfers between devices: 23.2 us -> none  [shards(): lax.all_gather(summed, 'ctx', axis=0, tiled=True).reshape(vgrad.shape)]
    unnamed x48, local copies, waits for them, and re-layouts: 20.6 us -> 1.78 us
    pallas_call x3, Pallas kernels: 25.1 us -> 28.5 us  [the longest x1 18.8 us: attend(): pl.pallas_call(functools.partial(attend_kernel, lines=lines, heads=heads,...]
    ppermute x10 -> x32, waiting for transfers between devices: 53 us -> 56.3 us  [move(): return lax.ppermute(array, 'ctx', pairs)]
    add x0 -> x4, other arithmetic: none -> 2.59 us  [the longest x2 2.54 us: sum_verticals(): half = keep.astype(wide) + move(give, lines.core_pairs()).astype(wide)]
  transfers between devices with their start and end apart: 12 -> 32, of which waited for: 12 -> 20; matrix products, arithmetic and copies ran while one was open for 0% -> 0% of each run, Pallas kernels for 0% -> 0%
where the time goes in v3:
time: 134 us; the launch traced here: 133 us
  waiting for transfers between devices  56.3 us (42%)
  starting transfers between devices  41.3 us (31%)
  Pallas kernels  28.5 us (21%)
  other arithmetic  3.51 us (3%)
  local copies, waits for them, and re-layouts  1.86 us (1%)
  between operations  1.59 us (1%)
    ppermute x32, waiting for transfers between devices, move(): return lax.ppermute(array, 'ctx', pairs)  56.3 us
    ppermute x32, starting transfers between devices, move(): return lax.ppermute(array, 'ctx', pairs)  41.3 us
    pallas_call x1, Pallas kernels, attend(): pl.pallas_call(functools.partial(attend_kernel, lines=lines, heads=heads,...  18.8 us
    pallas_call x1, Pallas kernels, assemble(): pl.pallas_call(functools.partial(assemble_kernel, lines=lines, heads=head...  5.36 us
    pallas_call x1, Pallas kernels, pack(): pl.pallas_call(functools.partial(pack_kernel, lines=lines, heads=heads, n...  4.33 us
  transfers between devices with their start and end apart: 32, of which 20 were waited for; matrix products, arithmetic and copies ran while one was open for 0% of the time, Pallas kernels for 0%

profile of v3, /device:TPU:0, one launch (start us, length us, event | category | flops | bytes accessed | tf_op | source)
XLA Modules:
  0.0 133.1 jit_solution(5025927309365151412)
XLA Ops:
  1.9 4.3 %shard_map.103 = (bf16[2,128,512]{2,1,0:T(8,128)(2,1)}, bf16[2,128,512]{2,1,0:T(8,128)(2,1)}, bf16[2,128,512]{2,1,0:T(8,128)(2,1)}, bf16[2,4,256,128]{3,2,1,0:T(8,128)(2,1)}, bf16[2,4,256,128]{3,2,1,0:T(8,128)(2,1)}) custom-call(s32[2]{0:T(128)} %pad_add_fusion.place, s32[4,8]{1,0:T(4,128)} %verts.5, bf16[16,128,512]{2,1,0:T(8,128)(2,1)} %keys.3, ...), custom_call_target="tpu_custom_call" | custom-call | tf_op jit(solution)/shard_map/pallas_call | solution.py:143
  9.7 2.9 %collective-permute-start.1 = (bf16[4,256,128]{2,1,0:T(8,128)(2,1)S(1)}, bf16[4,256,128]{2,1,0:T(8,128)(2,1)S(1)}, u32[]{:S(2)}, u32[]{:S(2)}) collective-permute-start(bf16[4,256,128]{2,1,0:T(8,128)(2,1)S(1)} %slice_bitcast_fusion.1), channel_id=1, source_target_pairs={{0,2},{1,3},{2,0},{3,1},{4,6},{5,7},{6,4},{7,5},{8,10},{9,11},{10,... | collective-permute-start | bytes 786440 | tf_op jit(solution)/shard_map/ppermute | solution.py:47
  12.7 6.6 %collective-permute-done.1 = bf16[4,256,128]{2,1,0:T(8,128)(2,1)S(1)} collective-permute-done((bf16[4,256,128]{2,1,0:T(8,128)(2,1)S(1)}, bf16[4,256,128]{2,1,0:T(8,128)(2,1)S(1)}, u32[]{:S(2)}, u32[]{:S(2)}) %collective-permute-start.1) | collective-permute-done | bytes 262176 | tf_op jit(solution)/shard_map/ppermute | solution.py:47
  19.3 1.9 %collective-permute-start.2 = (bf16[256,128]{1,0:T(8,128)(2,1)S(1)}, bf16[256,128]{1,0:T(8,128)(2,1)S(1)}, u32[]{:S(2)}, u32[]{:S(2)}) collective-permute-start(bf16[256,128]{1,0:T(8,128)(2,1)S(1)} %get-tuple-element.40), channel_id=1, source_target_pairs={{0,4},{1,5},{2,6},{3,7},{4,8},{5,9},{6,10},{7,11},{8,12},{9,13},{1... | collective-permute-start | bytes 196616 | tf_op jit(solution)/shard_map/ppermute | solution.py:47
  21.2 2.1 %collective-permute-start.4 = (bf16[256,128]{1,0:T(8,128)(2,1)S(1)}, bf16[256,128]{1,0:T(8,128)(2,1)S(1)}, u32[]{:S(2)}, u32[]{:S(2)}) collective-permute-start(bf16[256,128]{1,0:T(8,128)(2,1)S(1)} %get-tuple-element.41), channel_id=1, source_target_pairs={{0,12},{1,13},{2,14},{3,15},{4,0},{5,1},{6,2},{7,3},{8,4},{9,5},{1... | collective-permute-start | bytes 196616 | tf_op jit(solution)/shard_map/ppermute | solution.py:47
  24.2 1.8 %collective-permute-done.2 = bf16[256,128]{1,0:T(8,128)(2,1)S(1)} collective-permute-done((bf16[256,128]{1,0:T(8,128)(2,1)S(1)}, bf16[256,128]{1,0:T(8,128)(2,1)S(1)}, u32[]{:S(2)}, u32[]{:S(2)}) %collective-permute-start.2) | collective-permute-done | bytes 65568 | tf_op jit(solution)/shard_map/ppermute | solution.py:47
  26.3 3.2 %collective-permute-done.3 = bf16[256,128]{1,0:T(8,128)(2,1)S(1)} collective-permute-done((bf16[256,128]{1,0:T(8,128)(2,1)S(1)}, bf16[256,128]{1,0:T(8,128)(2,1)S(1)}, u32[]{:S(2)}, u32[]{:S(2)}) %collective-permute-start.3) | collective-permute-done | bytes 65568 | tf_op jit(solution)/shard_map/ppermute | solution.py:47
  29.5 2.2 %collective-permute-start.7 = (bf16[256,128]{1,0:T(8,128)(2,1)S(1)}, bf16[256,128]{1,0:T(8,128)(2,1)S(1)}, u32[]{:S(2)}, u32[]{:S(2)}) collective-permute-start(bf16[256,128]{1,0:T(8,128)(2,1)S(1)} %fusion.9), channel_id=1, source_target_pairs={{0,12},{1,13},{2,14},{3,15},{4,0},{5,1},{6,2},{7,3},{8,4},{9,5},{1... | collective-permute-start | bytes 196616 | tf_op jit(solution)/shard_map/ppermute | solution.py:47
  33.8 2.8 %collective-permute-start.12 = (bf16[2,128,512]{2,1,0:T(8,128)(2,1)S(1)}, bf16[2,128,512]{2,1,0:T(8,128)(2,1)S(1)}, u32[]{:S(2)}, u32[]{:S(2)}) collective-permute-start(bf16[2,128,512]{2,1,0:T(8,128)(2,1)S(1)} %copy-done.22), channel_id=1, source_target_pairs={{0,4},{1,5},{2,6},{3,7},{4,8},{5,9},{6,10},{7,11},{8,12},{9,13},{1... | collective-permute-start | bytes 786440 | tf_op jit(solution)/shard_map/ppermute | solution.py:47
  36.7 7.2 %collective-permute-done.6 = bf16[256,128]{1,0:T(8,128)(2,1)S(1)} collective-permute-done((bf16[256,128]{1,0:T(8,128)(2,1)S(1)}, bf16[256,128]{1,0:T(8,128)(2,1)S(1)}, u32[]{:S(2)}, u32[]{:S(2)}) %collective-permute-start.6) | collective-permute-done | bytes 65568 | tf_op jit(solution)/shard_map/ppermute | solution.py:47
  44.0 10.1 %collective-permute-start.8 = (bf16[4,256,128]{2,1,0:T(8,128)(2,1)S(1)}, bf16[4,256,128]{2,1,0:T(8,128)(2,1)S(1)}, u32[]{:S(2)}, u32[]{:S(2)}) collective-permute-start(bf16[4,256,128]{2,1,0:T(8,128)(2,1)S(1)} %pad_maximum_fusion.rest_0_), channel_id=1, source_target_pairs={{0,2},{1,3},{2,0},{3,1},{4,6},{5,7},{6,4},{7,5},{8,10},{9,11},{10,... | collective-permute-start | bytes 786440 | tf_op jit(solution)/shard_map/ppermute | solution.py:47
  54.8 6.0 %collective-permute-done.8.rest_1_ = bf16[4,256,128]{2,1,0:T(8,128)(2,1)S(1)} collective-permute-done((bf16[4,256,128]{2,1,0:T(8,128)(2,1)S(1)}, bf16[4,256,128]{2,1,0:T(8,128)(2,1)S(1)}, u32[]{:S(2)}, u32[]{:S(2)}) %collective-permute-start.8) | collective-permute-done | bytes 262176 | tf_op jit(solution)/shard_map/ppermute | solution.py:47
  63.4 18.8 %shard_map.104 = (bf16[128,4096]{1,0:T(8,128)(2,1)}, f32[2,128,512]{2,1,0:T(8,128)}, f32[2,128,512]{2,1,0:T(8,128)}, f32[2,128,512]{2,1,0:T(8,128)}, bf16[2,128,...) custom-call(s32[2]{0:T(128)} %pad_add_fusion.place, ...), custom_call_target="tpu_custom_call" | custom-call | tf_op jit(solution)/shard_map/pallas_call | solution.py:348
  82.3 2.1 %collective-permute-done.21 = bf16[2,4,256,128]{3,2,1,0:T(8,128)(2,1)S(1)} collective-permute-done((bf16[2,4,256,128]{3,2,1,0:T(8,128)(2,1)}, bf16[2,4,256,128]{3,2,1,0:T(8,128)(2,1)S(1)}, u32[]{:S(2)}, u32[]{:S(2)}) %collective-permute-start.21) | collective-permute-done | bytes 524320 | tf_op jit(solution)/shard_map/ppermute | solution.py:47
  85.8 2.2 %collective-permute-start.22 = (bf16[4,256,128]{2,1,0:T(8,128)(2,1)S(1)}, bf16[4,256,128]{2,1,0:T(8,128)(2,1)S(1)}, u32[]{:S(2)}, u32[]{:S(2)}) collective-permute-start(bf16[4,256,128]{2,1,0:T(8,128)(2,1)S(1)} %fusion.1), channel_id=1, source_target_pairs={{0,2},{1,3},{2,0},{3,1},{4,6},{5,7},{6,4},{7,5},{8,10},{9,11},{10,... | collective-permute-start | bytes 786440 | tf_op jit(solution)/shard_map/ppermute | solution.py:47
  88.1 6.6 %collective-permute-done.22 = bf16[4,256,128]{2,1,0:T(8,128)(2,1)S(1)} collective-permute-done((bf16[4,256,128]{2,1,0:T(8,128)(2,1)S(1)}, bf16[4,256,128]{2,1,0:T(8,128)(2,1)S(1)}, u32[]{:S(2)}, u32[]{:S(2)}) %collective-permute-start.22) | collective-permute-done | bytes 262176 | tf_op jit(solution)/shard_map/ppermute | solution.py:47
  94.9 3.8 %collective-permute-start.25 = (bf16[256,128]{1,0:T(8,128)(2,1)S(1)}, bf16[256,128]{1,0:T(8,128)(2,1)S(1)}, u32[]{:S(2)}, u32[]{:S(2)}) collective-permute-start(bf16[256,128]{1,0:T(8,128)(2,1)S(1)} %get-tuple-element.38), channel_id=1, source_target_pairs={{0,12},{1,13},{2,14},{3,15},{4,0},{5,1},{6,2},{7,3},{8,4},{9,5},{1... | collective-permute-start | bytes 196616 | tf_op jit(solution)/shard_map/ppermute | solution.py:47
  98.7 3.0 %collective-permute-done.23 = bf16[256,128]{1,0:T(8,128)(2,1)S(1)} collective-permute-done((bf16[256,128]{1,0:T(8,128)(2,1)S(1)}, bf16[256,128]{1,0:T(8,128)(2,1)S(1)}, u32[]{:S(2)}, u32[]{:S(2)}) %collective-permute-start.23) | collective-permute-done | bytes 65568 | tf_op jit(solution)/shard_map/ppermute | solution.py:47
  101.7 2.1 %collective-permute-done.24 = bf16[256,128]{1,0:T(8,128)(2,1)S(1)} collective-permute-done((bf16[256,128]{1,0:T(8,128)(2,1)S(1)}, bf16[256,128]{1,0:T(8,128)(2,1)S(1)}, u32[]{:S(2)}, u32[]{:S(2)}) %collective-permute-start.24) | collective-permute-done | bytes 65568 | tf_op jit(solution)/shard_map/ppermute | solution.py:47
  103.9 2.1 %collective-permute-start.28 = (bf16[256,128]{1,0:T(8,128)(2,1)S(1)}, bf16[256,128]{1,0:T(8,128)(2,1)S(1)}, u32[]{:S(2)}, u32[]{:S(2)}) collective-permute-start(bf16[256,128]{1,0:T(8,128)(2,1)S(1)} %fusion.6), channel_id=1, source_target_pairs={{0,12},{1,13},{2,14},{3,15},{4,0},{5,1},{6,2},{7,3},{8,4},{9,5},{1... | collective-permute-start | bytes 196616 | tf_op jit(solution)/shard_map/ppermute | solution.py:47
  106.7 2.1 %collective-permute-done.28 = bf16[256,128]{1,0:T(8,128)(2,1)S(1)} collective-permute-done((bf16[256,128]{1,0:T(8,128)(2,1)S(1)}, bf16[256,128]{1,0:T(8,128)(2,1)S(1)}, u32[]{:S(2)}, u32[]{:S(2)}) %collective-permute-start.28) | collective-permute-done | bytes 65568 | tf_op jit(solution)/shard_map/ppermute | solution.py:47
  112.1 2.1 %collective-permute-start.29 = (bf16[4,256,128]{2,1,0:T(8,128)(2,1)S(1)}, bf16[4,256,128]{2,1,0:T(8,128)(2,1)S(1)}, u32[]{:S(2)}, u32[]{:S(2)}) collective-permute-start(bf16[4,256,128]{2,1,0:T(8,128)(2,1)S(1)} %pad_maximum_fusion.1.rest_3_), channel_id=1, source_target_pairs={{0,2},{1,3},{2,0},{3,1},{4,6},{5,7},{6,4},{7,5},{8,10},{9,11},{10,... | collective-permute-start | bytes 786440 | tf_op jit(solution)/shard_map/ppermute | solution.py:47
  116.5 9.0 %collective-permute-done.29.rest_4_ = bf16[4,256,128]{2,1,0:T(8,128)(2,1)S(1)} collective-permute-done((bf16[4,256,128]{2,1,0:T(8,128)(2,1)S(1)}, bf16[4,256,128]{2,1,0:T(8,128)(2,1)S(1)}, u32[]{:S(2)}, u32[]{:S(2)}) %collective-permute-start.29) | collective-permute-done | bytes 262176 | tf_op jit(solution)/shard_map/ppermute | solution.py:47
  127.7 5.4 %shard_map.105 = (bf16[16,128,512]{2,1,0:T(8,128)(2,1)}, bf16[16,128,512]{2,1,0:T(8,128)(2,1)}) custom-call(s32[2]{0:T(128)} %pad_add_fusion.place, s32[4,8]{1,0:T(4,128)} %verts.5, f32[2,128,512]{2,1,0:T(8,128)} %get-tuple-element.25.home, bf16[2,128,512]{2,1,0:T(8,128)(2,1)} %copy-done.11, bf16[2,128,512]{2,1,0:T(8,128)(2,1)} %copy-done.14, ...), custom_call_target="tpu_custom_call" | custom-call | tf_op jit(solution)/shard_map/pallas_call | solution.py:442
  (106 shorter events, 20.8 us)
Async XLA Ops:
  9.7 9.5 %collective-permute-start.1 = (bf16[4,256,128]{2,1,0:T(8,128)(2,1)S(1)}, bf16[4,256,128]{2,1,0:T(8,128)(2,1)S(1)}, u32[]{:S(2)}, u32[]{:S(2)}) collective-permute-start(bf16[4,256,128]{2,1,0:T(8,128)(2,1)S(1)} %slice_bitcast_fusion.1), channel_id=1, source_target_pairs={{0,2},{1,3},{2,0},{3,1},{4,6},{5,7},{6,4},{7,5},{8,10},{9,11},{10,... | collective-permute-start | bytes 786440 | tf_op jit(solution)/shard_map/ppermute | solution.py:47
  19.3 6.8 %collective-permute-start.2 = (bf16[256,128]{1,0:T(8,128)(2,1)S(1)}, bf16[256,128]{1,0:T(8,128)(2,1)S(1)}, u32[]{:S(2)}, u32[]{:S(2)}) collective-permute-start(bf16[256,128]{1,0:T(8,128)(2,1)S(1)} %get-tuple-element.40), channel_id=1, source_target_pairs={{0,4},{1,5},{2,6},{3,7},{4,8},{5,9},{6,10},{7,11},{8,12},{9,13},{1... | collective-permute-start | bytes 196616 | tf_op jit(solution)/shard_map/ppermute | solution.py:47
  23.3 6.2 %collective-permute-start.3 = (bf16[256,128]{1,0:T(8,128)(2,1)S(1)}, bf16[256,128]{1,0:T(8,128)(2,1)S(1)}, u32[]{:S(2)}, u32[]{:S(2)}) collective-permute-start(bf16[256,128]{1,0:T(8,128)(2,1)S(1)} %get-tuple-element.42), channel_id=1, source_target_pairs={{0,8},{1,9},{2,10},{3,11},{4,12},{5,13},{6,14},{7,15},{8,0},{9,1},... | collective-permute-start | bytes 196616 | tf_op jit(solution)/shard_map/ppermute | solution.py:47
  29.5 7.2 %collective-permute-start.7 = (bf16[256,128]{1,0:T(8,128)(2,1)S(1)}, bf16[256,128]{1,0:T(8,128)(2,1)S(1)}, u32[]{:S(2)}, u32[]{:S(2)}) collective-permute-start(bf16[256,128]{1,0:T(8,128)(2,1)S(1)} %fusion.9), channel_id=1, source_target_pairs={{0,12},{1,13},{2,14},{3,15},{4,0},{5,1},{6,2},{7,3},{8,4},{9,5},{1... | collective-permute-start | bytes 196616 | tf_op jit(solution)/shard_map/ppermute | solution.py:47
  31.7 12.2 %collective-permute-start.6 = (bf16[256,128]{1,0:T(8,128)(2,1)S(1)}, bf16[256,128]{1,0:T(8,128)(2,1)S(1)}, u32[]{:S(2)}, u32[]{:S(2)}) collective-permute-start(bf16[256,128]{1,0:T(8,128)(2,1)S(1)} %fusion.9), channel_id=1, source_target_pairs={{0,8},{1,9},{2,10},{3,11},{4,12},{5,13},{6,14},{7,15},{8,0},{9,1},... | collective-permute-start | bytes 196616 | tf_op jit(solution)/shard_map/ppermute | solution.py:47
  31.7 12.2 %collective-permute-start.5 = (bf16[256,128]{1,0:T(8,128)(2,1)S(1)}, bf16[256,128]{1,0:T(8,128)(2,1)S(1)}, u32[]{:S(2)}, u32[]{:S(2)}) collective-permute-start(bf16[256,128]{1,0:T(8,128)(2,1)S(1)} %fusion.9), channel_id=1, source_target_pairs={{0,4},{1,5},{2,6},{3,7},{4,8},{5,9},{6,10},{7,11},{8,12},{9,13},{1... | collective-permute-start | bytes 196616 | tf_op jit(solution)/shard_map/ppermute | solution.py:47
  32.3 21.8 %collective-permute-start.11 = (bf16[2,128,512]{2,1,0:T(8,128)(2,1)S(1)}, bf16[2,128,512]{2,1,0:T(8,128)(2,1)S(1)}, u32[]{:S(2)}, u32[]{:S(2)}) collective-permute-start(bf16[2,128,512]{2,1,0:T(8,128)(2,1)S(1)} %copy-done.23), channel_id=1, source_target_pairs={{0,2},{1,3},{2,4},{3,5},{4,6},{5,7},{6,8},{7,9},{8,10},{9,11},{10,... | collective-permute-start | bytes 786440 | tf_op jit(solution)/shard_map/ppermute | solution.py:47
  33.8 20.4 %collective-permute-start.12 = (bf16[2,128,512]{2,1,0:T(8,128)(2,1)S(1)}, bf16[2,128,512]{2,1,0:T(8,128)(2,1)S(1)}, u32[]{:S(2)}, u32[]{:S(2)}) collective-permute-start(bf16[2,128,512]{2,1,0:T(8,128)(2,1)S(1)} %copy-done.22), channel_id=1, source_target_pairs={{0,4},{1,5},{2,6},{3,7},{4,8},{5,9},{6,10},{7,11},{8,12},{9,13},{1... | collective-permute-start | bytes 786440 | tf_op jit(solution)/shard_map/ppermute | solution.py:47
  44.0 16.8 %collective-permute-start.8 = (bf16[4,256,128]{2,1,0:T(8,128)(2,1)S(1)}, bf16[4,256,128]{2,1,0:T(8,128)(2,1)S(1)}, u32[]{:S(2)}, u32[]{:S(2)}) collective-permute-start(bf16[4,256,128]{2,1,0:T(8,128)(2,1)S(1)} %pad_maximum_fusion.rest_0_), channel_id=1, source_target_pairs={{0,2},{1,3},{2,0},{3,1},{4,6},{5,7},{6,4},{7,5},{8,10},{9,11},{10,... | collective-permute-start | bytes 786440 | tf_op jit(solution)/shard_map/ppermute | solution.py:47
  54.1 7.6 %collective-permute-start.13 = (bf16[2,128,512]{2,1,0:T(8,128)(2,1)S(1)}, bf16[2,128,512]{2,1,0:T(8,128)(2,1)S(1)}, u32[]{:S(2)}, u32[]{:S(2)}) collective-permute-start(bf16[2,128,512]{2,1,0:T(8,128)(2,1)S(1)} %copy-done.20), channel_id=1, source_target_pairs={{0,1},{1,6},{2,3},{3,8},{4,5},{5,10},{6,7},{7,12},{8,9},{9,14},{10... | collective-permute-start | bytes 786440 | tf_op jit(solution)/shard_map/ppermute | solution.py:47
  54.1 7.6 %collective-permute-start.14 = (bf16[2,128,512]{2,1,0:T(8,128)(2,1)S(1)}, bf16[2,128,512]{2,1,0:T(8,128)(2,1)S(1)}, u32[]{:S(2)}, u32[]{:S(2)}) collective-permute-start(bf16[2,128,512]{2,1,0:T(8,128)(2,1)S(1)} %collective-permute-done.11.rest_4_), channel_id=1, source_target_pairs={{0,1},{1,0},{2,3},{3,2},{4,5},{5,4},{6,7},{7,6},{8,9},{9,8},{10,11... | collective-permute-start | bytes 786440 | tf_op jit(solution)/shard_map/ppermute | solution.py:47
  54.2 7.5 %collective-permute-start.15 = (bf16[2,128,512]{2,1,0:T(8,128)(2,1)S(1)}, bf16[2,128,512]{2,1,0:T(8,128)(2,1)S(1)}, u32[]{:S(2)}, u32[]{:S(2)}) collective-permute-start(bf16[2,128,512]{2,1,0:T(8,128)(2,1)S(1)} %collective-permute-done.12.rest_5_), channel_id=1, source_target_pairs={{0,1},{1,0},{2,3},{3,2},{4,5},{5,4},{6,7},{7,6},{8,9},{9,8},{10,11... | collective-permute-start | bytes 786440 | tf_op jit(solution)/shard_map/ppermute | solution.py:47
  54.7 7.0 %collective-permute-start.9 = (bf16[4,256,128]{2,1,0:T(8,128)(2,1)S(1)}, bf16[4,256,128]{2,1,0:T(8,128)(2,1)S(1)}, u32[]{:S(2)}, u32[]{:S(2)}) collective-permute-start(bf16[4,256,128]{2,1,0:T(8,128)(2,1)S(1)} %pad_maximum_fusion.rest_0_), channel_id=1, source_target_pairs={{0,1},{1,0},{2,3},{3,2},{4,5},{5,4},{6,7},{7,6},{8,9},{9,8},{10,11... | collective-permute-start | bytes 786440 | tf_op jit(solution)/shard_map/ppermute | solution.py:47
  85.8 8.9 %collective-permute-start.22 = (bf16[4,256,128]{2,1,0:T(8,128)(2,1)S(1)}, bf16[4,256,128]{2,1,0:T(8,128)(2,1)S(1)}, u32[]{:S(2)}, u32[]{:S(2)}) collective-permute-start(bf16[4,256,128]{2,1,0:T(8,128)(2,1)S(1)} %fusion.1), channel_id=1, source_target_pairs={{0,2},{1,3},{2,0},{3,1},{4,6},{5,7},{6,4},{7,5},{8,10},{9,11},{10,... | collective-permute-start | bytes 786440 | tf_op jit(solution)/shard_map/ppermute | solution.py:47
  94.8 6.9 %collective-permute-start.23 = (bf16[256,128]{1,0:T(8,128)(2,1)S(1)}, bf16[256,128]{1,0:T(8,128)(2,1)S(1)}, u32[]{:S(2)}, u32[]{:S(2)}) collective-permute-start(bf16[256,128]{1,0:T(8,128)(2,1)S(1)} %get-tuple-element.37), channel_id=1, source_target_pairs={{0,4},{1,5},{2,6},{3,7},{4,8},{5,9},{6,10},{7,11},{8,12},{9,13},{1... | collective-permute-start | bytes 196616 | tf_op jit(solution)/shard_map/ppermute | solution.py:47
  94.9 6.8 %collective-permute-start.25 = (bf16[256,128]{1,0:T(8,128)(2,1)S(1)}, bf16[256,128]{1,0:T(8,128)(2,1)S(1)}, u32[]{:S(2)}, u32[]{:S(2)}) collective-permute-start(bf16[256,128]{1,0:T(8,128)(2,1)S(1)} %get-tuple-element.38), channel_id=1, source_target_pairs={{0,12},{1,13},{2,14},{3,15},{4,0},{5,1},{6,2},{7,3},{8,4},{9,5},{1... | collective-permute-start | bytes 196616 | tf_op jit(solution)/shard_map/ppermute | solution.py:47
  98.7 15.5 %collective-permute-start.16 = (bf16[2,128,512]{2,1,0:T(8,128)(2,1)S(1)}, bf16[2,128,512]{2,1,0:T(8,128)(2,1)S(1)}, u32[]{:S(2)}, u32[]{:S(2)}) collective-permute-start(bf16[2,128,512]{2,1,0:T(8,128)(2,1)S(1)} %copy-done.21), channel_id=1, source_target_pairs={{0,1},{1,0},{2,3},{3,2},{4,5},{5,4},{6,7},{7,6},{8,9},{9,8},{10,11... | collective-permute-start | bytes 786440 | tf_op jit(solution)/shard_map/ppermute | solution.py:47
  106.0 6.1 %collective-permute-start.26 = (bf16[256,128]{1,0:T(8,128)(2,1)S(1)}, bf16[256,128]{1,0:T(8,128)(2,1)S(1)}, u32[]{:S(2)}, u32[]{:S(2)}) collective-permute-start(bf16[256,128]{1,0:T(8,128)(2,1)S(1)} %fusion.6), channel_id=1, source_target_pairs={{0,4},{1,5},{2,6},{3,7},{4,8},{5,9},{6,10},{7,11},{8,12},{9,13},{1... | collective-permute-start | bytes 196616 | tf_op jit(solution)/shard_map/ppermute | solution.py:47
  106.7 7.9 %collective-permute-start.18 = (bf16[2,128,512]{2,1,0:T(8,128)(2,1)S(1)}, bf16[2,128,512]{2,1,0:T(8,128)(2,1)S(1)}, u32[]{:S(2)}, u32[]{:S(2)}) collective-permute-start(bf16[2,128,512]{2,1,0:T(8,128)(2,1)S(1)} %copy-done.19), channel_id=1, source_target_pairs={{0,1},{1,0},{2,3},{3,2},{4,5},{5,4},{6,7},{7,6},{8,9},{9,8},{10,11... | collective-permute-start | bytes 786440 | tf_op jit(solution)/shard_map/ppermute | solution.py:47
  108.8 16.7 %collective-permute-start.20 = (bf16[2,128,512]{2,1,0:T(8,128)(2,1)S(1)}, bf16[2,128,512]{2,1,0:T(8,128)(2,1)S(1)}, u32[]{:S(2)}, u32[]{:S(2)}) collective-permute-start(bf16[2,128,512]{2,1,0:T(8,128)(2,1)S(1)} %copy-done.18), channel_id=1, source_target_pairs={{1,0},{6,1},{3,2},{8,3},{5,4},{10,5},{7,6},{12,7},{9,8},{14,9},{11... | collective-permute-start | bytes 786440 | tf_op jit(solution)/shard_map/ppermute | solution.py:47
  112.1 13.3 %collective-permute-start.29 = (bf16[4,256,128]{2,1,0:T(8,128)(2,1)S(1)}, bf16[4,256,128]{2,1,0:T(8,128)(2,1)S(1)}, u32[]{:S(2)}, u32[]{:S(2)}) collective-permute-start(bf16[4,256,128]{2,1,0:T(8,128)(2,1)S(1)} %pad_maximum_fusion.1.rest_3_), channel_id=1, source_target_pairs={{0,2},{1,3},{2,0},{3,1},{4,6},{5,7},{6,4},{7,5},{8,10},{9,11},{10,... | collective-permute-start | bytes 786440 | tf_op jit(solution)/shard_map/ppermute | solution.py:47
  114.3 11.8 %collective-permute-start.17 = (bf16[2,128,512]{2,1,0:T(8,128)(2,1)S(1)}, bf16[2,128,512]{2,1,0:T(8,128)(2,1)S(1)}, u32[]{:S(2)}, u32[]{:S(2)}) collective-permute-start(bf16[2,128,512]{2,1,0:T(8,128)(2,1)S(1)} %add_convert_fusion.1), channel_id=1, source_target_pairs={{2,0},{3,1},{4,2},{5,3},{6,4},{7,5},{8,6},{9,7},{10,8},{11,9},{12,... | collective-permute-start | bytes 786440 | tf_op jit(solution)/shard_map/ppermute | solution.py:47
  114.7 11.9 %collective-permute-start.19 = (bf16[2,128,512]{2,1,0:T(8,128)(2,1)S(1)}, bf16[2,128,512]{2,1,0:T(8,128)(2,1)S(1)}, u32[]{:S(2)}, u32[]{:S(2)}) collective-permute-start(bf16[2,128,512]{2,1,0:T(8,128)(2,1)S(1)} %add_convert_fusion), channel_id=1, source_target_pairs={{4,0},{5,1},{6,2},{7,3},{8,4},{9,5},{10,6},{11,7},{12,8},{13,9},{1... | collective-permute-start | bytes 786440 | tf_op jit(solution)/shard_map/ppermute | solution.py:47
  116.5 10.1 %collective-permute-start.30 = (bf16[4,256,128]{2,1,0:T(8,128)(2,1)S(1)}, bf16[4,256,128]{2,1,0:T(8,128)(2,1)S(1)}, u32[]{:S(2)}, u32[]{:S(2)}) collective-permute-start(bf16[4,256,128]{2,1,0:T(8,128)(2,1)S(1)} %pad_maximum_fusion.1.rest_3_), channel_id=1, source_target_pairs={{0,1},{1,0},{2,3},{3,2},{4,5},{5,4},{6,7},{7,6},{8,9},{9,8},{10,11... | collective-permute-start | bytes 786440 | tf_op jit(solution)/shard_map/ppermute | solution.py:47
  (32 other events, 306.5 us)

commit v4 on v3

v4 whole, which is shorter than its diff:
```python
import functools
import math

import jax
import jax.numpy as jnp
from jax import lax
from jax.experimental import pallas as pl
from jax.experimental.pallas import tpu as pltpu
from jax.sharding import PartitionSpec as P

BLOCK = 64
WDEV = 5
VMEM_LIMIT = 60 * 1024 * 1024
BF16 = jnp.bfloat16
F32 = jnp.float32


class Lines:
    def __init__(self, devices):
        self.devices = devices
        self.far = devices // 4

    def place(self, me):
        return lax.div(me, 4), lax.rem(lax.div(me, 2), 2), lax.rem(me, 2)

    def core_pairs(self):
        return [(i, i ^ 1) for i in range(self.devices)]

    def near_pairs(self):
        return [(i, i ^ 2) for i in range(self.devices)]

    def far_pairs(self, by):
        return [(i, (i + 4 * by) % self.devices) for i in range(self.devices)]

    def shift_pairs(self, by):
        return [(i, (i + by) % self.devices) for i in range(self.devices)]

    def mixed_pairs(self):
        return [(i, (i + (5 if i % 2 else 1)) % self.devices) for i in range(self.devices)]


def back(pairs):
    return [(b, a) for a, b in pairs]


def move(array, pairs):
    return lax.ppermute(array, "ctx", pairs)


def gather_verticals(lines, own):
    parts = [own] + [move(own, lines.far_pairs(by)) for by in range(1, lines.far)]
    mine = jnp.stack(parts)
    across = move(mine, lines.near_pairs())
    core_mine = move(mine, lines.core_pairs())
    core_across = move(across, lines.core_pairs())
    return mine, across, core_mine, core_across


def after(array, *others):
    return lax.optimization_barrier((array, *others))[0]


def sum_verticals(lines, keep, give, wide, ahead_of_far, ahead_of_share):
    half = keep.astype(wide) + move(give, lines.core_pairs()).astype(wide)
    quarter = half[0] + move(half[1].astype(BF16), lines.near_pairs()).astype(wide)
    quarter = after(quarter, *ahead_of_far)
    share = quarter[0]
    for by in range(1, lines.far):
        share = share + move(quarter[by].astype(BF16), lines.far_pairs(by)).astype(wide)
    return after(share.astype(BF16), *ahead_of_share)


def wraps(me, devices):
    return [me + 2 >= devices, me + 4 >= devices, (lax.rem(me, 2) == 1) & (me + 5 >= devices)]


def pack_kernel(slab_index, verts, keys, values, *rest, lines, heads, nv, per_device):
    sends = rest[:3]
    keep, give, picked, sems, pick_sems = rest[3:]
    slab, me = slab_index[0], lax.axis_index("ctx")
    far, near, core = lines.place(me)
    _, _, chunk, head_dim = keep.shape
    copies = []
    _, wrapped4, wrapped_mixed = wraps(me, lines.devices)
    for n, region in enumerate(
        (slab, slab - wrapped4.astype(jnp.int32), slab - wrapped_mixed.astype(jnp.int32))
    ):
        for kv, source in enumerate((keys, values)):
            copy = pltpu.make_async_copy(source.at[region], sends[n].at[kv], sems.at[n, kv])
            copy.start()
            copies.append(copy)
    picked[...] = jnp.zeros_like(picked)
    slab_blocks = per_device * lines.devices
    piece = min(BLOCK, chunk)

    def unit_copies(h, m):
        inner = lax.rem(verts[h, m], slab_blocks)
        region = lax.div(verts[h, m], slab_blocks)
        row = lax.rem(inner, per_device) * BLOCK
        for p in range(BLOCK // piece):
            at = (h * nv + m) * BLOCK + p * piece
            line, at = at // (lines.far * chunk), at % (lines.far * chunk)
            slot, at = at // chunk, at % chunk
            line = lax.rem(line + near, 2)
            slot = lax.rem(slot - far + lines.far, lines.far)
            for kv, source in enumerate((keys, values)):
                yield pltpu.make_async_copy(
                    source.at[
                        region,
                        pl.ds(pl.multiple_of(row + p * piece, piece), piece),
                        pl.ds(h * head_dim, head_dim),
                    ],
                    picked.at[lax.rem(kv + core, 2), line, slot, pl.ds(at, piece), :],
                    pick_sems.at[kv, (h * nv + m) * (BLOCK // piece) + p],
                )

    def owned(h, m):
        return lax.div(lax.rem(verts[h, m], slab_blocks), per_device) == me

    for h in range(heads):
        for m in range(nv):

            @pl.when(owned(h, m))
            def _():
                for copy in unit_copies(h, m):
                    copy.start()

    for h in range(heads):
        for m in range(nv):

            @pl.when(owned(h, m))
            def _():
                for copy in unit_copies(h, m):
                    copy.wait()

    keep[...] = picked[0]
    give[...] = picked[1]
    for copy in copies:
        copy.wait()


def pack(slab_index, verticals, keys, values, lines):
    regions, rows, features = keys.shape
    heads, nv = verticals.shape
    head_dim = features // heads
    chunk = heads * nv * BLOCK // (2 * lines.far)
    smem = pl.BlockSpec(memory_space=pltpu.SMEM)
    hbm = pl.BlockSpec(memory_space=pl.ANY)
    share = (2, lines.far, chunk, head_dim)
    return pl.pallas_call(
        functools.partial(pack_kernel, lines=lines, heads=heads, nv=nv, per_device=rows // BLOCK),
        in_specs=[smem, smem, hbm, hbm],
        out_specs=[pl.BlockSpec(memory_space=pltpu.VMEM)] * 5,
        out_shape=[jax.ShapeDtypeStruct((2, rows, features), BF16)] * 3
        + [jax.ShapeDtypeStruct(share, BF16)] * 2,
        scratch_shapes=[
            pltpu.VMEM((2,) + share, BF16),
            pltpu.SemaphoreType.DMA((3, 2)),
            pltpu.SemaphoreType.DMA((2, heads * nv * max(1, BLOCK // chunk))),
        ],
        compiler_params=pltpu.CompilerParams(vmem_limit_bytes=VMEM_LIMIT),
    )(slab_index, verticals, keys, values)


def distances(core):
    return [2, 4, 5 - 4 * core, 1 + 2 * core, 3 + 2 * core]


def vertical_copies(lines, me, chunk, gathered, to, sems, first):
    far, near, core = lines.place(me)
    copies = []
    for n, source in enumerate(gathered):
        kv = core if n < 2 else 1 - core
        line = near if n % 2 == 0 else 1 - near
        for s in range(lines.far):
            slot = lax.rem(far - s + lines.far, lines.far)
            row = pl.multiple_of((line * lines.far + slot) * chunk, chunk)
            copies.append(
                pltpu.make_async_copy(
                    source.at[s], to.at[kv, pl.ds(row, chunk), :], sems.at[first + len(copies)]
                )
            )
    return copies


def attend_kernel(
    slab_index, verts, offs, q, grad, out, keys, values, *rest, lines, heads, nv, ns, per_device,
):
    gathered, recv, rest = rest[:4], rest[4 : 4 + WDEV], rest[4 + WDEV :]
    dq, home, near_parts, vkeep, vgive = rest[0], rest[1], rest[2 : 2 + WDEV], rest[7], rest[8]
    (win, vkv, kc, vc, qs, gs, s_ref, dp_ref, w_ref, ds_ref, nacc, sems) = rest[9:]
    h = pl.program_id(0)
    slab, me = slab_index[0], lax.axis_index("ctx")
    far, near, core = lines.place(me)
    _, _, chunk, head_dim = vkeep.shape
    group = q.shape[1] // head_dim
    cand = 1 + nv + ns
    scaling = 1.0 / math.sqrt(head_dim)
    rows = per_device * BLOCK
    width = group * BLOCK
    first_block = slab * (per_device * lines.devices) + me * per_device
    lanes = pl.ds(pl.multiple_of(h * head_dim, head_dim), head_dim)

    def window_row(d):
        return pl.multiple_of((WDEV - d) * rows, rows)

    @pl.when(h == 0)
    def _():
        own_rows = pl.ds(WDEV * rows, rows)
        copies = [
            pltpu.make_async_copy(
                recv[n], win.at[:, pl.ds(window_row(d), rows), :], sems.at[n]
            )
            for n, d in enumerate(distances(core))
        ]
        copies.append(pltpu.make_async_copy(keys.at[slab], win.at[0, own_rows, :], sems.at[WDEV]))
        copies.append(
            pltpu.make_async_copy(values.at[slab], win.at[1, own_rows, :], sems.at[WDEV + 1])
        )
        copies += vertical_copies(lines, me, chunk, gathered, vkv, sems, WDEV + 2)
        for copy in copies:
            copy.start()
        nacc[...] = jnp.zeros_like(nacc)
        for copy in copies:
            copy.wait()

    vert_rows = pl.ds(pl.multiple_of(h * (nv * BLOCK), nv * BLOCK), nv * BLOCK)
    neg, posinf = jnp.float32(-jnp.inf), jnp.float32(jnp.inf)
    log2_scale = scaling * math.log2(math.e)
    key_at = lax.broadcasted_iota(jnp.int32, (BLOCK, width), 0)
    row_at = lax.broadcasted_iota(jnp.int32, (BLOCK, width), 1) % BLOCK
    nt = (((1,), (1,)), ((), ()))

    def fold(x, op):
        y = x[0:8, :]
        for r in range(1, BLOCK // 8):
            y = op(y, x[r * 8 : (r + 1) * 8, :])
        return y

    vertical_sum = [None, None]
    for j in range(per_device):
        block = first_block + j
        own_at = (WDEV * per_device + j) * BLOCK
        slash_at = [
            pl.multiple_of((WDEV * per_device + j - offs[h, s]) * BLOCK, BLOCK) for s in range(ns)
        ]
        valid = [None]
        for m in range(nv):
            valid.append(verts[h, m] < block)
        for s in range(ns):
            collide = verts[h, 0] == block - offs[h, s]
            for m in range(1, nv):
                collide = collide | (verts[h, m] == block - offs[h, s])
            valid.append((offs[h, s] > 0) & jnp.logical_not(collide))
        for kv, to in enumerate((kc, vc)):
            to[j, 0:BLOCK, :] = win[kv, own_at : own_at + BLOCK, lanes]
            to[j, BLOCK : (1 + nv) * BLOCK, :] = vkv[kv, vert_rows, :]
            for s in range(ns):
                to[j, (1 + nv + s) * BLOCK : (2 + nv + s) * BLOCK, :] = win[
                    kv, pl.ds(slash_at[s], BLOCK), lanes
                ]
        products = []
        block_rows = slice(j * BLOCK, (j + 1) * BLOCK)
        for g in range(group):
            cols = slice(g * head_dim, (g + 1) * head_dim)
            qs[j, g * BLOCK : (g + 1) * BLOCK, :] = q[block_rows, cols]
            gs[j, g * BLOCK : (g + 1) * BLOCK, :] = grad[block_rows, cols]
            products.append(grad[block_rows, cols].astype(F32) * out[block_rows, cols].astype(F32))
        delta = jnp.sum(jnp.transpose(jnp.concatenate(products, axis=0)), axis=0, keepdims=True)

        s_ref[j] = lax.dot_general(kc[j], qs[j], nt, preferred_element_type=F32)
        dp_ref[j] = lax.dot_general(vc[j], gs[j], nt, preferred_element_type=F32)

        own = jnp.where(key_at <= row_at, s_ref[j, 0:BLOCK, :], neg)
        s_ref[j, 0:BLOCK, :] = own
        top = fold(own, jnp.maximum)
        for c in range(1, cand):
            best = fold(s_ref[j, c * BLOCK : (c + 1) * BLOCK, :], jnp.maximum)
            top = jnp.maximum(top, best + jnp.where(valid[c], jnp.float32(0), neg))
        top = jnp.max(top, axis=0, keepdims=True) * log2_scale
        total = jnp.zeros((8, width), F32)
        for c in range(cand):
            span = slice(c * BLOCK, (c + 1) * BLOCK)
            less = top if c == 0 else top + jnp.where(valid[c], jnp.float32(0), posinf)
            p = jnp.exp2(s_ref[j, span, :] * log2_scale - less)
            s_ref[j, span, :] = p
            total = total + fold(p, jnp.add)
        inverse = 1.0 / jnp.sum(total, axis=0, keepdims=True)
        for c in range(cand):
            span = slice(c * BLOCK, (c + 1) * BLOCK)
            w = s_ref[j, span, :] * inverse
            w_ref[j, span, :] = w.astype(BF16)
            ds_ref[j, span, :] = (w * (dp_ref[j, span, :] - delta)).astype(BF16)

        dv = jnp.dot(w_ref[j], gs[j], preferred_element_type=F32)
        dk = jnp.dot(ds_ref[j], qs[j], preferred_element_type=F32) * scaling
        dqt = lax.dot_general(
            kc[j], ds_ref[j], (((0,), (0,)), ((), ())), preferred_element_type=F32
        )
        dqr = (jnp.transpose(dqt) * scaling).astype(BF16)
        for g in range(group):
            dq[block_rows, g * head_dim : (g + 1) * head_dim] = dqr[g * BLOCK : (g + 1) * BLOCK, :]

        for kv, part in enumerate((dk, dv)):
            nacc[kv, own_at : own_at + BLOCK, lanes] += part[0:BLOCK]
            for s in range(ns):
                nacc[kv, pl.ds(slash_at[s], BLOCK), lanes] += part[
                    (1 + nv + s) * BLOCK : (2 + nv + s) * BLOCK
                ]
            of_verticals = part[BLOCK : (1 + nv) * BLOCK]
            vertical_sum[kv] = of_verticals if j == 0 else vertical_sum[kv] + of_verticals

    first = core == 0
    keep = jnp.where(first, vertical_sum[0], vertical_sum[1])
    give = jnp.where(first, vertical_sum[1], vertical_sum[0]).astype(BF16)
    per_line = heads // 2
    for c in range(nv * BLOCK // chunk):
        line = lax.rem(lax.div(h, per_line) + near, 2)
        slot = lax.rem(h, per_line) * (nv * BLOCK // chunk) + c
        slot = lax.rem(slot - far + lines.far, lines.far)
        span = slice(c * chunk, (c + 1) * chunk)
        vkeep[line, slot] = keep[span, :]
        vgive[line, slot] = give[span, :]
    for kv in range(2):
        home[kv, :, lanes] = nacc[kv, WDEV * rows :, lanes]
        for part, d in zip(near_parts, distances(core)):
            part[kv, :, lanes] = nacc[kv, pl.ds(window_row(d), rows), lanes].astype(part.dtype)


def attend(
    slab_index, verticals, offsets, queries, cotangent, output, keys, values, gathered, recv, lines
):
    rows, width = queries.shape
    features = keys.shape[2]
    heads, nv = verticals.shape
    ns = offsets.shape[1]
    head_dim = features // heads
    group = width // features
    per_device = rows // BLOCK
    cand = 1 + nv + ns
    smem = pl.BlockSpec(memory_space=pltpu.SMEM)
    hbm = pl.BlockSpec(memory_space=pl.ANY)
    tile = pl.BlockSpec((rows, group * head_dim), lambda h: (0, h))

    def whole(shape):
        return pl.BlockSpec(shape, lambda h: (0,) * len(shape))

    shard = (2, rows, features)
    vert_shape = (2, heads * nv * BLOCK, head_dim)
    share = (2, lines.far, heads * nv * BLOCK // (2 * lines.far), head_dim)
    return pl.pallas_call(
        functools.partial(
            attend_kernel, lines=lines, heads=heads, nv=nv, ns=ns, per_device=per_device
        ),
        grid=(heads,),
        in_specs=[smem] * 3 + [tile] * 3 + [hbm] * (6 + WDEV),
        out_specs=[tile] + [whole(shard)] * (1 + WDEV) + [whole(share)] * 2,
        out_shape=[
            jax.ShapeDtypeStruct((rows, width), BF16),
            jax.ShapeDtypeStruct(shard, F32),
            jax.ShapeDtypeStruct(shard, F32),
            jax.ShapeDtypeStruct(shard, F32),
            jax.ShapeDtypeStruct(shard, BF16),
            jax.ShapeDtypeStruct(shard, BF16),
            jax.ShapeDtypeStruct(shard, BF16),
            jax.ShapeDtypeStruct(share, F32),
            jax.ShapeDtypeStruct(share, BF16),
        ],
        scratch_shapes=[
            pltpu.VMEM((2, (WDEV + 1) * rows, features), BF16),
            pltpu.VMEM(vert_shape, BF16),
            pltpu.VMEM((per_device, cand * BLOCK, head_dim), BF16),
            pltpu.VMEM((per_device, cand * BLOCK, head_dim), BF16),
            pltpu.VMEM((per_device, group * BLOCK, head_dim), BF16),
            pltpu.VMEM((per_device, group * BLOCK, head_dim), BF16),
            pltpu.VMEM((per_device, cand * BLOCK, group * BLOCK), F32),
            pltpu.VMEM((per_device, cand * BLOCK, group * BLOCK), F32),
            pltpu.VMEM((per_device, cand * BLOCK, group * BLOCK), BF16),
            pltpu.VMEM((per_device, cand * BLOCK, group * BLOCK), BF16),
            pltpu.VMEM((2, (WDEV + 1) * rows, features), F32),
            pltpu.SemaphoreType.DMA((WDEV + 2 + 4 * lines.far,)),
        ],
        compiler_params=pltpu.CompilerParams(vmem_limit_bytes=VMEM_LIMIT),
    )(
        slab_index, verticals, offsets, queries, cotangent, output, keys, values, *gathered, *recv,
    )


def assemble_kernel(slab_index, verts, home, *rest, lines, heads, nv, per_device):
    arrived, gathered = rest[:3], rest[3:7]
    key_out, value_out, vert, acc, sems = rest[7:]
    slab, me = slab_index[0], lax.axis_index("ctx")
    devices = lines.devices
    chunk = gathered[0].shape[1]
    copies = vertical_copies(lines, me, chunk, gathered, vert, sems, 0)
    for copy in copies:
        copy.start()
    head_dim = vert.shape[2]
    slab_blocks = per_device * devices
    acc[0] = home[...]
    acc[1] = jnp.zeros_like(home)
    for part, wrapped in zip(arrived, wraps(me, devices)):
        acc[wrapped.astype(jnp.int32)] += part[...].astype(F32)
    key_out[...] = jnp.zeros_like(key_out)
    value_out[...] = jnp.zeros_like(value_out)
    outs = (key_out, value_out)
    for copy in copies:
        copy.wait()
    for h in range(heads):
        lanes = slice(h * head_dim, (h + 1) * head_dim)
        for m in range(nv):
            inner = lax.rem(verts[h, m], slab_blocks)
            region = lax.div(verts[h, m], slab_blocks)
            row = pl.multiple_of(lax.rem(inner, per_device) * BLOCK, BLOCK)
            at = (h * nv + m) * BLOCK

            @pl.when(lax.div(inner, per_device) == me)
            def _():
                close = (region == slab) | (region == slab - 1)

                @pl.when(close)
                def _():
                    for kv in range(2):
                        acc[slab - region, kv, pl.ds(row, BLOCK), lanes] += vert[
                            kv, at : at + BLOCK, :
                        ].astype(F32)

                @pl.when(jnp.logical_not(close))
                def _():
                    for kv in range(2):
                        outs[kv][region, pl.ds(row, BLOCK), lanes] = vert[kv, at : at + BLOCK, :]

    for kv in range(2):
        outs[kv][slab] = acc[0, kv].astype(BF16)
        outs[kv][slab - 1] = acc[1, kv].astype(BF16)


def assemble(slab_index, verticals, home, arrived, gathered, regions, lines):
    _, rows, features = home.shape
    heads, nv = verticals.shape
    smem = pl.BlockSpec(memory_space=pltpu.SMEM)
    vmem = pl.BlockSpec(memory_space=pltpu.VMEM)
    hbm = pl.BlockSpec(memory_space=pl.ANY)
    return pl.pallas_call(
        functools.partial(
            assemble_kernel, lines=lines, heads=heads, nv=nv, per_device=rows // BLOCK
        ),
        in_specs=[smem] * 2 + [vmem] * 4 + [hbm] * 4,
        out_specs=[vmem] * 2,
        out_shape=[jax.ShapeDtypeStruct((regions, rows, features), BF16)] * 2,
        scratch_shapes=[
            pltpu.VMEM((2, heads * nv * BLOCK, features // heads), BF16),
            pltpu.VMEM((2, 2, rows, features), F32),
            pltpu.SemaphoreType.DMA((4 * lines.far,)),
        ],
        compiler_params=pltpu.CompilerParams(vmem_limit_bytes=VMEM_LIMIT),
    )(slab_index, verticals, home, *arrived, *gathered)


def shards(
    queries,
    context_keys,
    context_values,
    forward_output,
    output_cotangent,
    verticals,
    offsets,
    slab_index,
):
    lines = Lines(lax.axis_size("ctx"))
    regions = context_keys.shape[0]
    _, near, _ = lines.place(lax.axis_index("ctx"))

    own, send4, mixed, keep, give = pack(
        slab_index, verticals, context_keys, context_values, lines
    )
    recv4 = move(send4, lines.shift_pairs(4))
    recv_mixed = move(mixed, lines.mixed_pairs())
    recv2 = move(jnp.where(near == 1, recv4, own), lines.near_pairs())
    other2 = move(recv2, lines.core_pairs())
    other4 = move(recv4, lines.core_pairs())
    share = sum_verticals(lines, keep, give, BF16, (recv4, recv_mixed), ())
    gathered = gather_verticals(lines, share)

    query_grad, home, part2, part4, mixed, give2, give4, vkeep, vgive = attend(
        slab_index, verticals, offsets, queries, output_cotangent, forward_output,
        context_keys, context_values, gathered, [recv2, recv4, recv_mixed, other2, other4], lines,
    )

    sum2 = (part2 + move(give2, lines.core_pairs()).astype(F32)).astype(BF16)
    sum4 = (part4 + move(give4, lines.core_pairs()).astype(F32)).astype(BF16)
    arrived2 = move(sum2, back(lines.shift_pairs(2)))
    arrived4 = move(sum4, back(lines.shift_pairs(4)))
    arrived_mixed = move(mixed, back(lines.mixed_pairs()))
    share = sum_verticals(lines, vkeep, vgive, F32, (arrived4, arrived_mixed), (arrived2,))
    totals = gather_verticals(lines, share)
    key_gradient, value_gradient = assemble(
        slab_index, verticals, home, (arrived2, arrived4, arrived_mixed), totals, regions, lines
    )
    return query_grad, key_gradient, value_gradient


def solution(mesh):
    in_specs = (
        P(("groups", "ctx"), None),
        P("groups", "ctx", None),
        P("groups", "ctx", None),
        P(("groups", "ctx"), None),
        P(("groups", "ctx"), None),
        P("groups", None),
        P("groups", None),
        P("groups"),
    )
    out_specs = (P(("groups", "ctx"), None), P("groups", "ctx", None), P("groups", "ctx", None))
    return jax.shard_map(shards, mesh=mesh, in_specs=in_specs, out_specs=out_specs, check_vma=False)
```

time: 134 us -> 127 us (0.948)
  starting transfers between devices: 41.3 us -> 28.7 us
  waiting for transfers between devices: 56.3 us -> 66 us
  Pallas kernels: 28.5 us -> 26.2 us
    ppermute x32, starting transfers between devices: 41.3 us -> 28.7 us  [move(): return lax.ppermute(array, 'ctx', pairs)]
    ppermute x32, waiting for transfers between devices: 56.3 us -> 66 us  [move(): return lax.ppermute(array, 'ctx', pairs)]
    pallas_call x1, Pallas kernels: 18.8 us -> 16.8 us  [attend(): pl.pallas_call(functools.partial(attend_kernel, lines=lines, heads=heads,...]
  transfers between devices with their start and end apart: 32 -> 32, of which waited for: 20 -> 24; matrix products, arithmetic and copies ran while one was open for 0% -> 1% of each run, Pallas kernels for 0% -> 0%
where the time goes in v4:
time: 127 us
  waiting for transfers between devices  66 us (52%)
  starting transfers between devices  28.7 us (23%)
  Pallas kernels  26.2 us (21%)
  other arithmetic  2.96 us (2%)
  between operations  1.64 us (1%)
  local copies, waits for them, and re-layouts  1.56 us (1%)
    ppermute x32, waiting for transfers between devices, move(): return lax.ppermute(array, 'ctx', pairs)  66 us
    ppermute x32, starting transfers between devices, move(): return lax.ppermute(array, 'ctx', pairs)  28.7 us
    pallas_call x1, Pallas kernels, attend(): pl.pallas_call(functools.partial(attend_kernel, lines=lines, heads=heads,...  16.8 us
    pallas_call x1, Pallas kernels, assemble(): pl.pallas_call(functools.partial(assemble_kernel, lines=lines, heads=head...  5.16 us
    pallas_call x1, Pallas kernels, pack(): pl.pallas_call(functools.partial(pack_kernel, lines=lines, heads=heads, n...  4.21 us
  transfers between devices with their start and end apart: 32, of which 24 were waited for; matrix products, arithmetic and copies ran while one was open for 1% of the time, Pallas kernels for 0%

profile of v4, /device:TPU:0, one launch (start us, length us, event | category | flops | bytes accessed | tf_op | source)
XLA Modules:
  0.0 127.0 jit_solution(10422898319343910380)
XLA Ops:
  1.3 4.2 %shard_map.103 = (bf16[2,128,512]{2,1,0:T(8,128)(2,1)}, bf16[2,128,512]{2,1,0:T(8,128)(2,1)}, bf16[2,128,512]{2,1,0:T(8,128)(2,1)}, bf16[2,4,256,128]{3,2,1,0:T(8,128)(2,1)}, bf16[2,4,256,128]{3,2,1,0:T(8,128)(2,1)}) custom-call(s32[1]{0:T(128)S(6)} %copy.11.slab_index, s32[4,8]{1,0:T(4,128)} %verts.5, bf16[16,128,512]{2,1,0:T(8,128)(2,1)} %keys.3, ...), custom_call_target="tpu_custom_call" | custom-call | tf_op jit(solution)/shard_map/pallas_call | solution.py:150
  6.0 1.7 %collective-permute-done = bf16[2,4,256,128]{3,2,1,0:T(8,128)(2,1)S(1)} collective-permute-done((bf16[2,4,256,128]{3,2,1,0:T(8,128)(2,1)}, bf16[2,4,256,128]{3,2,1,0:T(8,128)(2,1)S(1)}, u32[]{:S(2)}, u32[]{:S(2)}) %collective-permute-start) | collective-permute-done | bytes 524320 | tf_op jit(solution)/shard_map/ppermute | solution.py:47
  9.0 2.9 %collective-permute-start.1 = (bf16[4,256,128]{2,1,0:T(8,128)(2,1)S(1)}, bf16[4,256,128]{2,1,0:T(8,128)(2,1)S(1)}, u32[]{:S(2)}, u32[]{:S(2)}) collective-permute-start(bf16[4,256,128]{2,1,0:T(8,128)(2,1)S(1)} %slice_bitcast_fusion.1), channel_id=1, source_target_pairs={{0,2},{1,3},{2,0},{3,1},{4,6},{5,7},{6,4},{7,5},{8,10},{9,11},{10,... | collective-permute-start | bytes 786440 | tf_op jit(solution)/shard_map/ppermute | solution.py:47
  11.9 1.6 %collective-permute-start.2 = (bf16[2,128,512]{2,1,0:T(8,128)(2,1)S(1)}, bf16[2,128,512]{2,1,0:T(8,128)(2,1)S(1)}, u32[]{:S(2)}, u32[]{:S(2)}) collective-permute-start(bf16[2,128,512]{2,1,0:T(8,128)(2,1)S(1)} %copy-done.22), channel_id=1, source_target_pairs={{0,4},{1,5},{2,6},{3,7},{4,8},{5,9},{6,10},{7,11},{8,12},{9,13},{1... | collective-permute-start | bytes 786440 | tf_op jit(solution)/shard_map/ppermute | solution.py:47
  13.5 5.0 %collective-permute-done.1 = bf16[4,256,128]{2,1,0:T(8,128)(2,1)S(1)} collective-permute-done((bf16[4,256,128]{2,1,0:T(8,128)(2,1)S(1)}, bf16[4,256,128]{2,1,0:T(8,128)(2,1)S(1)}, u32[]{:S(2)}, u32[]{:S(2)}) %collective-permute-start.1) | collective-permute-done | bytes 262176 | tf_op jit(solution)/shard_map/ppermute | solution.py:47
  18.6 4.3 %collective-permute-done.2.rest_5_ = bf16[2,128,512]{2,1,0:T(8,128)(2,1)S(1)} collective-permute-done((bf16[2,128,512]{2,1,0:T(8,128)(2,1)S(1)}, bf16[2,128,512]{2,1,0:T(8,128)(2,1)S(1)}, u32[]{:S(2)}, u32[]{:S(2)}) %collective-permute-start.2) | collective-permute-done | bytes 262176 | tf_op jit(solution)/shard_map/ppermute | solution.py:47
  22.9 5.2 %collective-permute-done.3.rest_6_ = bf16[2,128,512]{2,1,0:T(8,128)(2,1)S(1)} collective-permute-done((bf16[2,128,512]{2,1,0:T(8,128)(2,1)S(1)}, bf16[2,128,512]{2,1,0:T(8,128)(2,1)S(1)}, u32[]{:S(2)}, u32[]{:S(2)}) %collective-permute-start.3) | collective-permute-done | bytes 262176 | tf_op jit(solution)/shard_map/ppermute | solution.py:47
  28.2 3.8 %collective-permute-start.6 = (bf16[256,128]{1,0:T(8,128)(2,1)S(1)}, bf16[256,128]{1,0:T(8,128)(2,1)S(1)}, u32[]{:S(2)}, u32[]{:S(2)}) collective-permute-start(bf16[256,128]{1,0:T(8,128)(2,1)S(1)} %get-tuple-element.45), channel_id=1, source_target_pairs={{0,12},{1,13},{2,14},{3,15},{4,0},{5,1},{6,2},{7,3},{8,4},{9,5},{1... | collective-permute-start | bytes 196616 | tf_op jit(solution)/shard_map/ppermute | solution.py:47
  32.0 2.5 %collective-permute-done.4 = bf16[256,128]{1,0:T(8,128)(2,1)S(1)} collective-permute-done((bf16[256,128]{1,0:T(8,128)(2,1)S(1)}, bf16[256,128]{1,0:T(8,128)(2,1)S(1)}, u32[]{:S(2)}, u32[]{:S(2)}) %collective-permute-start.4) | collective-permute-done | bytes 65568 | tf_op jit(solution)/shard_map/ppermute | solution.py:47
  34.6 3.4 %collective-permute-done.5 = bf16[256,128]{1,0:T(8,128)(2,1)S(1)} collective-permute-done((bf16[256,128]{1,0:T(8,128)(2,1)S(1)}, bf16[256,128]{1,0:T(8,128)(2,1)S(1)}, u32[]{:S(2)}, u32[]{:S(2)}) %collective-permute-start.5) | collective-permute-done | bytes 65568 | tf_op jit(solution)/shard_map/ppermute | solution.py:47
  38.0 2.3 %collective-permute-start.9 = (bf16[256,128]{1,0:T(8,128)(2,1)S(1)}, bf16[256,128]{1,0:T(8,128)(2,1)S(1)}, u32[]{:S(2)}, u32[]{:S(2)}) collective-permute-start(bf16[256,128]{1,0:T(8,128)(2,1)S(1)} %fusion.7), channel_id=1, source_target_pairs={{0,12},{1,13},{2,14},{3,15},{4,0},{5,1},{6,2},{7,3},{8,4},{9,5},{1... | collective-permute-start | bytes 196616 | tf_op jit(solution)/shard_map/ppermute | solution.py:47
  42.3 3.1 %collective-permute-done.8 = bf16[256,128]{1,0:T(8,128)(2,1)S(1)} collective-permute-done((bf16[256,128]{1,0:T(8,128)(2,1)S(1)}, bf16[256,128]{1,0:T(8,128)(2,1)S(1)}, u32[]{:S(2)}, u32[]{:S(2)}) %collective-permute-start.8) | collective-permute-done | bytes 65568 | tf_op jit(solution)/shard_map/ppermute | solution.py:47
  48.4 4.4 %collective-permute-done.10.rest_1_ = bf16[4,256,128]{2,1,0:T(8,128)(2,1)S(1)} collective-permute-done((bf16[4,256,128]{2,1,0:T(8,128)(2,1)S(1)}, bf16[4,256,128]{2,1,0:T(8,128)(2,1)S(1)}, u32[]{:S(2)}, u32[]{:S(2)}) %collective-permute-start.10) | collective-permute-done | bytes 262176 | tf_op jit(solution)/shard_map/ppermute | solution.py:47
  55.1 16.8 %shard_map.104 = (bf16[128,4096]{1,0:T(8,128)(2,1)}, f32[2,128,512]{2,1,0:T(8,128)}, f32[2,128,512]{2,1,0:T(8,128)}, f32[2,128,512]{2,1,0:T(8,128)}, bf16[2,128,...) custom-call(s32[1]{0:T(128)S(6)} %copy.11.slab_index, ...), custom_call_target="tpu_custom_call" | custom-call | tf_op jit(solution)/shard_map/pallas_call | solution.py:351
  72.5 1.6 %collective-permute-done.21 = bf16[2,4,256,128]{3,2,1,0:T(8,128)(2,1)S(1)} collective-permute-done((bf16[2,4,256,128]{3,2,1,0:T(8,128)(2,1)}, bf16[2,4,256,128]{3,2,1,0:T(8,128)(2,1)S(1)}, u32[]{:S(2)}, u32[]{:S(2)}) %collective-permute-start.21) | collective-permute-done | bytes 524320 | tf_op jit(solution)/shard_map/ppermute | solution.py:47
  75.7 2.0 %collective-permute-start.20 = (bf16[2,128,512]{2,1,0:T(8,128)(2,1)S(1)}, bf16[2,128,512]{2,1,0:T(8,128)(2,1)S(1)}, u32[]{:S(2)}, u32[]{:S(2)}) collective-permute-start(bf16[2,128,512]{2,1,0:T(8,128)(2,1)S(1)} %copy-done.20), channel_id=1, source_target_pairs={{1,0},{6,1},{3,2},{8,3},{5,4},{10,5},{7,6},{12,7},{9,8},{14,9},{11... | collective-permute-start | bytes 786440 | tf_op jit(solution)/shard_map/ppermute | solution.py:47
  79.3 7.5 %collective-permute-done.22 = bf16[4,256,128]{2,1,0:T(8,128)(2,1)S(1)} collective-permute-done((bf16[4,256,128]{2,1,0:T(8,128)(2,1)S(1)}, bf16[4,256,128]{2,1,0:T(8,128)(2,1)S(1)}, u32[]{:S(2)}, u32[]{:S(2)}) %collective-permute-start.22) | collective-permute-done | bytes 262176 | tf_op jit(solution)/shard_map/ppermute | solution.py:47
  87.3 5.0 %collective-permute-start.23 = (bf16[256,128]{1,0:T(8,128)(2,1)S(1)}, bf16[256,128]{1,0:T(8,128)(2,1)S(1)}, u32[]{:S(2)}, u32[]{:S(2)}) collective-permute-start(bf16[256,128]{1,0:T(8,128)(2,1)S(1)} %get-tuple-element.41), channel_id=1, source_target_pairs={{0,4},{1,5},{2,6},{3,7},{4,8},{5,9},{6,10},{7,11},{8,12},{9,13},{1... | collective-permute-start | bytes 196616 | tf_op jit(solution)/shard_map/ppermute | solution.py:47
  94.2 2.3 %collective-permute-done.25 = bf16[256,128]{1,0:T(8,128)(2,1)S(1)} collective-permute-done((bf16[256,128]{1,0:T(8,128)(2,1)S(1)}, bf16[256,128]{1,0:T(8,128)(2,1)S(1)}, u32[]{:S(2)}, u32[]{:S(2)}) %collective-permute-start.25) | collective-permute-done | bytes 65568 | tf_op jit(solution)/shard_map/ppermute | solution.py:47
  97.6 4.8 %collective-permute-done.17.rest_0_ = bf16[2,128,512]{2,1,0:T(8,128)(2,1)S(1)} collective-permute-done((bf16[2,128,512]{2,1,0:T(8,128)(2,1)S(1)}, bf16[2,128,512]{2,1,0:T(8,128)(2,1)S(1)}, u32[]{:S(2)}, u32[]{:S(2)}) %collective-permute-start.17) | collective-permute-done | bytes 262176 | tf_op jit(solution)/shard_map/ppermute | solution.py:47
  102.4 3.7 %collective-permute-start.28 = (bf16[256,128]{1,0:T(8,128)(2,1)S(1)}, bf16[256,128]{1,0:T(8,128)(2,1)S(1)}, u32[]{:S(2)}, u32[]{:S(2)}) collective-permute-start(bf16[256,128]{1,0:T(8,128)(2,1)S(1)} %fusion.5), channel_id=1, source_target_pairs={{0,12},{1,13},{2,14},{3,15},{4,0},{5,1},{6,2},{7,3},{8,4},{9,5},{1... | collective-permute-start | bytes 196616 | tf_op jit(solution)/shard_map/ppermute | solution.py:47
  108.0 3.5 %collective-permute-done.27 = bf16[256,128]{1,0:T(8,128)(2,1)S(1)} collective-permute-done((bf16[256,128]{1,0:T(8,128)(2,1)S(1)}, bf16[256,128]{1,0:T(8,128)(2,1)S(1)}, u32[]{:S(2)}, u32[]{:S(2)}) %collective-permute-start.27) | collective-permute-done | bytes 65568 | tf_op jit(solution)/shard_map/ppermute | solution.py:47
  113.0 6.6 %collective-permute-done.29.rest_4_ = bf16[4,256,128]{2,1,0:T(8,128)(2,1)S(1)} collective-permute-done((bf16[4,256,128]{2,1,0:T(8,128)(2,1)S(1)}, bf16[4,256,128]{2,1,0:T(8,128)(2,1)S(1)}, u32[]{:S(2)}, u32[]{:S(2)}) %collective-permute-start.29) | collective-permute-done | bytes 262176 | tf_op jit(solution)/shard_map/ppermute | solution.py:47
  121.9 5.2 %shard_map.105 = (bf16[16,128,512]{2,1,0:T(8,128)(2,1)}, bf16[16,128,512]{2,1,0:T(8,128)(2,1)}) custom-call(s32[1]{0:T(128)S(6)} %copy.11.slab_index, s32[4,8]{1,0:T(4,128)} %verts.5, f32[2,128,512]{2,1,0:T(8,128)} %get-tuple-element.29.home, bf16[2,128,512]{2,1,0:T(8,128)(2,1)} %copy-done.8, bf16[2,128,512]{2,1,0:T(8,128)(2,1)} %copy-done.7, ...), custom_call_target="tpu_custom_call" | custom-call | tf_op jit(solution)/shard_map/pallas_call | solution.py:444
  (105 shorter events, 22.0 us)
Async XLA Ops:
  9.0 9.5 %collective-permute-start.1 = (bf16[4,256,128]{2,1,0:T(8,128)(2,1)S(1)}, bf16[4,256,128]{2,1,0:T(8,128)(2,1)S(1)}, u32[]{:S(2)}, u32[]{:S(2)}) collective-permute-start(bf16[4,256,128]{2,1,0:T(8,128)(2,1)S(1)} %slice_bitcast_fusion.1), channel_id=1, source_target_pairs={{0,2},{1,3},{2,0},{3,1},{4,6},{5,7},{6,4},{7,5},{8,10},{9,11},{10,... | collective-permute-start | bytes 786440 | tf_op jit(solution)/shard_map/ppermute | solution.py:47
  11.9 11.0 %collective-permute-start.2 = (bf16[2,128,512]{2,1,0:T(8,128)(2,1)S(1)}, bf16[2,128,512]{2,1,0:T(8,128)(2,1)S(1)}, u32[]{:S(2)}, u32[]{:S(2)}) collective-permute-start(bf16[2,128,512]{2,1,0:T(8,128)(2,1)S(1)} %copy-done.22), channel_id=1, source_target_pairs={{0,4},{1,5},{2,6},{3,7},{4,8},{5,9},{6,10},{7,11},{8,12},{9,13},{1... | collective-permute-start | bytes 786440 | tf_op jit(solution)/shard_map/ppermute | solution.py:47
  13.5 14.6 %collective-permute-start.3 = (bf16[2,128,512]{2,1,0:T(8,128)(2,1)S(1)}, bf16[2,128,512]{2,1,0:T(8,128)(2,1)S(1)}, u32[]{:S(2)}, u32[]{:S(2)}) collective-permute-start(bf16[2,128,512]{2,1,0:T(8,128)(2,1)S(1)} %copy-done.21), channel_id=1, source_target_pairs={{0,1},{1,6},{2,3},{3,8},{4,5},{5,10},{6,7},{7,12},{8,9},{9,14},{10... | collective-permute-start | bytes 786440 | tf_op jit(solution)/shard_map/ppermute | solution.py:47
  28.2 6.3 %collective-permute-start.4 = (bf16[256,128]{1,0:T(8,128)(2,1)S(1)}, bf16[256,128]{1,0:T(8,128)(2,1)S(1)}, u32[]{:S(2)}, u32[]{:S(2)}) collective-permute-start(bf16[256,128]{1,0:T(8,128)(2,1)S(1)} %get-tuple-element.44), channel_id=1, source_target_pairs={{0,4},{1,5},{2,6},{3,7},{4,8},{5,9},{6,10},{7,11},{8,12},{9,13},{1... | collective-permute-start | bytes 196616 | tf_op jit(solution)/shard_map/ppermute | solution.py:47
  28.2 6.3 %collective-permute-start.6 = (bf16[256,128]{1,0:T(8,128)(2,1)S(1)}, bf16[256,128]{1,0:T(8,128)(2,1)S(1)}, u32[]{:S(2)}, u32[]{:S(2)}) collective-permute-start(bf16[256,128]{1,0:T(8,128)(2,1)S(1)} %get-tuple-element.45), channel_id=1, source_target_pairs={{0,12},{1,13},{2,14},{3,15},{4,0},{5,1},{6,2},{7,3},{8,4},{9,5},{1... | collective-permute-start | bytes 196616 | tf_op jit(solution)/shard_map/ppermute | solution.py:47
  32.0 5.9 %collective-permute-start.5 = (bf16[256,128]{1,0:T(8,128)(2,1)S(1)}, bf16[256,128]{1,0:T(8,128)(2,1)S(1)}, u32[]{:S(2)}, u32[]{:S(2)}) collective-permute-start(bf16[256,128]{1,0:T(8,128)(2,1)S(1)} %get-tuple-element.46), channel_id=1, source_target_pairs={{0,8},{1,9},{2,10},{3,11},{4,12},{5,13},{6,14},{7,15},{8,0},{9,1},... | collective-permute-start | bytes 196616 | tf_op jit(solution)/shard_map/ppermute | solution.py:47
  40.3 5.2 %collective-permute-start.8 = (bf16[256,128]{1,0:T(8,128)(2,1)S(1)}, bf16[256,128]{1,0:T(8,128)(2,1)S(1)}, u32[]{:S(2)}, u32[]{:S(2)}) collective-permute-start(bf16[256,128]{1,0:T(8,128)(2,1)S(1)} %fusion.7), channel_id=1, source_target_pairs={{0,8},{1,9},{2,10},{3,11},{4,12},{5,13},{6,14},{7,15},{8,0},{9,1},... | collective-permute-start | bytes 196616 | tf_op jit(solution)/shard_map/ppermute | solution.py:47
  40.3 6.1 %collective-permute-start.7 = (bf16[256,128]{1,0:T(8,128)(2,1)S(1)}, bf16[256,128]{1,0:T(8,128)(2,1)S(1)}, u32[]{:S(2)}, u32[]{:S(2)}) collective-permute-start(bf16[256,128]{1,0:T(8,128)(2,1)S(1)} %fusion.7), channel_id=1, source_target_pairs={{0,4},{1,5},{2,6},{3,7},{4,8},{5,9},{6,10},{7,11},{8,12},{9,13},{1... | collective-permute-start | bytes 196616 | tf_op jit(solution)/shard_map/ppermute | solution.py:47
  40.9 7.0 %collective-permute-start.13 = (bf16[2,128,512]{2,1,0:T(8,128)(2,1)S(1)}, bf16[2,128,512]{2,1,0:T(8,128)(2,1)S(1)}, u32[]{:S(2)}, u32[]{:S(2)}) collective-permute-start(bf16[2,128,512]{2,1,0:T(8,128)(2,1)S(1)} %broadcast_select_fusion), channel_id=1, source_target_pairs={{0,2},{1,3},{2,0},{3,1},{4,6},{5,7},{6,4},{7,5},{8,10},{9,11},{10,... | collective-permute-start | bytes 786440 | tf_op jit(solution)/shard_map/ppermute | solution.py:47
  46.4 6.4 %collective-permute-start.10 = (bf16[4,256,128]{2,1,0:T(8,128)(2,1)S(1)}, bf16[4,256,128]{2,1,0:T(8,128)(2,1)S(1)}, u32[]{:S(2)}, u32[]{:S(2)}) collective-permute-start(bf16[4,256,128]{2,1,0:T(8,128)(2,1)S(1)} %pad_maximum_fusion.rest_0_), channel_id=1, source_target_pairs={{0,2},{1,3},{2,0},{3,1},{4,6},{5,7},{6,4},{7,5},{8,10},{9,11},{10,... | collective-permute-start | bytes 786440 | tf_op jit(solution)/shard_map/ppermute | solution.py:47
  46.4 6.4 %collective-permute-start.15 = (bf16[2,128,512]{2,1,0:T(8,128)(2,1)S(1)}, bf16[2,128,512]{2,1,0:T(8,128)(2,1)S(1)}, u32[]{:S(2)}, u32[]{:S(2)}) collective-permute-start(bf16[2,128,512]{2,1,0:T(8,128)(2,1)S(1)} %collective-permute-done.2.rest_5_), channel_id=1, source_target_pairs={{0,1},{1,0},{2,3},{3,2},{4,5},{5,4},{6,7},{7,6},{8,9},{9,8},{10,11... | collective-permute-start | bytes 786440 | tf_op jit(solution)/shard_map/ppermute | solution.py:47
  72.2 5.5 %collective-permute-start.18 = (bf16[2,128,512]{2,1,0:T(8,128)(2,1)}, bf16[2,128,512]{2,1,0:T(8,128)(2,1)S(1)}, u32[]{:S(2)}, u32[]{:S(2)}) collective-permute-start(bf16[2,128,512]{2,1,0:T(8,128)(2,1)} %get-tuple-element.33), channel_id=1, source_target_pairs={{0,1},{1,0},{2,3},{3,2},{4,5},{5,4},{6,7},{7,6},{8,9},{9,8},{10,11... | collective-permute-start | bytes 786440 | tf_op jit(solution)/shard_map/ppermute | solution.py:47
  75.6 11.2 %collective-permute-start.22 = (bf16[4,256,128]{2,1,0:T(8,128)(2,1)S(1)}, bf16[4,256,128]{2,1,0:T(8,128)(2,1)S(1)}, u32[]{:S(2)}, u32[]{:S(2)}) collective-permute-start(bf16[4,256,128]{2,1,0:T(8,128)(2,1)S(1)} %fusion.1), channel_id=1, source_target_pairs={{0,2},{1,3},{2,0},{3,1},{4,6},{5,7},{6,4},{7,5},{8,10},{9,11},{10,... | collective-permute-start | bytes 786440 | tf_op jit(solution)/shard_map/ppermute | solution.py:47
  75.7 11.2 %collective-permute-start.20 = (bf16[2,128,512]{2,1,0:T(8,128)(2,1)S(1)}, bf16[2,128,512]{2,1,0:T(8,128)(2,1)S(1)}, u32[]{:S(2)}, u32[]{:S(2)}) collective-permute-start(bf16[2,128,512]{2,1,0:T(8,128)(2,1)S(1)} %copy-done.20), channel_id=1, source_target_pairs={{1,0},{6,1},{3,2},{8,3},{5,4},{10,5},{7,6},{12,7},{9,8},{14,9},{11... | collective-permute-start | bytes 786440 | tf_op jit(solution)/shard_map/ppermute | solution.py:47
  77.8 9.5 %collective-permute-start.19 = (bf16[2,128,512]{2,1,0:T(8,128)(2,1)S(1)}, bf16[2,128,512]{2,1,0:T(8,128)(2,1)S(1)}, u32[]{:S(2)}, u32[]{:S(2)}) collective-permute-start(bf16[2,128,512]{2,1,0:T(8,128)(2,1)S(1)} %add_convert_fusion), channel_id=1, source_target_pairs={{4,0},{5,1},{6,2},{7,3},{8,4},{9,5},{10,6},{11,7},{12,8},{13,9},{1... | collective-permute-start | bytes 786440 | tf_op jit(solution)/shard_map/ppermute | solution.py:47
  79.3 14.5 %collective-permute-start.16 = (bf16[2,128,512]{2,1,0:T(8,128)(2,1)S(1)}, bf16[2,128,512]{2,1,0:T(8,128)(2,1)S(1)}, u32[]{:S(2)}, u32[]{:S(2)}) collective-permute-start(bf16[2,128,512]{2,1,0:T(8,128)(2,1)S(1)} %copy-done.19), channel_id=1, source_target_pairs={{0,1},{1,0},{2,3},{3,2},{4,5},{5,4},{6,7},{7,6},{8,9},{9,8},{10,11... | collective-permute-start | bytes 786440 | tf_op jit(solution)/shard_map/ppermute | solution.py:47
  87.3 6.9 %collective-permute-start.23 = (bf16[256,128]{1,0:T(8,128)(2,1)S(1)}, bf16[256,128]{1,0:T(8,128)(2,1)S(1)}, u32[]{:S(2)}, u32[]{:S(2)}) collective-permute-start(bf16[256,128]{1,0:T(8,128)(2,1)S(1)} %get-tuple-element.41), channel_id=1, source_target_pairs={{0,4},{1,5},{2,6},{3,7},{4,8},{5,9},{6,10},{7,11},{8,12},{9,13},{1... | collective-permute-start | bytes 196616 | tf_op jit(solution)/shard_map/ppermute | solution.py:47
  92.3 5.3 %collective-permute-start.24 = (bf16[256,128]{1,0:T(8,128)(2,1)S(1)}, bf16[256,128]{1,0:T(8,128)(2,1)S(1)}, u32[]{:S(2)}, u32[]{:S(2)}) collective-permute-start(bf16[256,128]{1,0:T(8,128)(2,1)S(1)} %get-tuple-element.43), channel_id=1, source_target_pairs={{0,8},{1,9},{2,10},{3,11},{4,12},{5,13},{6,14},{7,15},{8,0},{9,1},... | collective-permute-start | bytes 196616 | tf_op jit(solution)/shard_map/ppermute | solution.py:47
  93.9 8.5 %collective-permute-start.17 = (bf16[2,128,512]{2,1,0:T(8,128)(2,1)S(1)}, bf16[2,128,512]{2,1,0:T(8,128)(2,1)S(1)}, u32[]{:S(2)}, u32[]{:S(2)}) collective-permute-start(bf16[2,128,512]{2,1,0:T(8,128)(2,1)S(1)} %add_convert_fusion.1), channel_id=1, source_target_pairs={{2,0},{3,1},{4,2},{5,3},{6,4},{7,5},{8,6},{9,7},{10,8},{11,9},{12,... | collective-permute-start | bytes 786440 | tf_op jit(solution)/shard_map/ppermute | solution.py:47
  102.4 5.6 %collective-permute-start.28 = (bf16[256,128]{1,0:T(8,128)(2,1)S(1)}, bf16[256,128]{1,0:T(8,128)(2,1)S(1)}, u32[]{:S(2)}, u32[]{:S(2)}) collective-permute-start(bf16[256,128]{1,0:T(8,128)(2,1)S(1)} %fusion.5), channel_id=1, source_target_pairs={{0,12},{1,13},{2,14},{3,15},{4,0},{5,1},{6,2},{7,3},{8,4},{9,5},{1... | collective-permute-start | bytes 196616 | tf_op jit(solution)/shard_map/ppermute | solution.py:47
  106.1 5.4 %collective-permute-start.27 = (bf16[256,128]{1,0:T(8,128)(2,1)S(1)}, bf16[256,128]{1,0:T(8,128)(2,1)S(1)}, u32[]{:S(2)}, u32[]{:S(2)}) collective-permute-start(bf16[256,128]{1,0:T(8,128)(2,1)S(1)} %fusion.5), channel_id=1, source_target_pairs={{0,8},{1,9},{2,10},{3,11},{4,12},{5,13},{6,14},{7,15},{8,0},{9,1},... | collective-permute-start | bytes 196616 | tf_op jit(solution)/shard_map/ppermute | solution.py:47
  106.1 6.1 %collective-permute-start.26 = (bf16[256,128]{1,0:T(8,128)(2,1)S(1)}, bf16[256,128]{1,0:T(8,128)(2,1)S(1)}, u32[]{:S(2)}, u32[]{:S(2)}) collective-permute-start(bf16[256,128]{1,0:T(8,128)(2,1)S(1)} %fusion.5), channel_id=1, source_target_pairs={{0,4},{1,5},{2,6},{3,7},{4,8},{5,9},{6,10},{7,11},{8,12},{9,13},{1... | collective-permute-start | bytes 196616 | tf_op jit(solution)/shard_map/ppermute | solution.py:47
  112.2 7.4 %collective-permute-start.29 = (bf16[4,256,128]{2,1,0:T(8,128)(2,1)S(1)}, bf16[4,256,128]{2,1,0:T(8,128)(2,1)S(1)}, u32[]{:S(2)}, u32[]{:S(2)}) collective-permute-start(bf16[4,256,128]{2,1,0:T(8,128)(2,1)S(1)} %pad_maximum_fusion.1.rest_3_), channel_id=1, source_target_pairs={{0,2},{1,3},{2,0},{3,1},{4,6},{5,7},{6,4},{7,5},{8,10},{9,11},{10,... | collective-permute-start | bytes 786440 | tf_op jit(solution)/shard_map/ppermute | solution.py:47
  113.0 6.6 %collective-permute-start.30 = (bf16[4,256,128]{2,1,0:T(8,128)(2,1)S(1)}, bf16[4,256,128]{2,1,0:T(8,128)(2,1)S(1)}, u32[]{:S(2)}, u32[]{:S(2)}) collective-permute-start(bf16[4,256,128]{2,1,0:T(8,128)(2,1)S(1)} %pad_maximum_fusion.1.rest_3_), channel_id=1, source_target_pairs={{0,1},{1,0},{2,3},{3,2},{4,5},{5,4},{6,7},{7,6},{8,9},{9,8},{10,11... | collective-permute-start | bytes 786440 | tf_op jit(solution)/shard_map/ppermute | solution.py:47
  (31 other events, 287.5 us)

commit v5 on v4

--- a/solution.py
+++ b/solution.py
@@ -28,6 +28,9 @@
 
     def near_pairs(self):
         return [(i, i ^ 2) for i in range(self.devices)]
+
+    def both_pairs(self):
+        return [(i, i ^ 3) for i in range(self.devices)]
 
     def far_pairs(self, by):
         return [(i, (i + 4 * by) % self.devices) for i in range(self.devices)]
@@ -60,13 +63,17 @@
     return lax.optimization_barrier((array, *others))[0]
 
 
-def sum_verticals(lines, keep, give, wide, ahead_of_far, ahead_of_share):
-    half = keep.astype(wide) + move(give, lines.core_pairs()).astype(wide)
-    quarter = half[0] + move(half[1].astype(BF16), lines.near_pairs()).astype(wide)
+def sum_verticals(lines, mine, to_core, to_near, to_both, ahead_of_far, ahead_of_share):
+    quarter = (
+        mine.astype(F32)
+        + move(to_core, lines.core_pairs()).astype(F32)
+        + move(to_near, lines.near_pairs()).astype(F32)
+        + move(to_both, lines.both_pairs()).astype(F32)
+    )
     quarter = after(quarter, *ahead_of_far)
     share = quarter[0]
     for by in range(1, lines.far):
-        share = share + move(quarter[by].astype(BF16), lines.far_pairs(by)).astype(wide)
+        share = share + move(quarter[by].astype(BF16), lines.far_pairs(by)).astype(F32)
     return after(share.astype(BF16), *ahead_of_share)
 
 
@@ -76,10 +83,11 @@
 
 def pack_kernel(slab_index, verts, keys, values, *rest, lines, heads, nv, per_device):
     sends = rest[:3]
-    keep, give, picked, sems, pick_sems = rest[3:]
+    shares = rest[3:7]
+    picked, sems, pick_sems = rest[7:]
     slab, me = slab_index[0], lax.axis_index("ctx")
     far, near, core = lines.place(me)
-    _, _, chunk, head_dim = keep.shape
+    _, chunk, head_dim = shares[0].shape
     copies = []
     _, wrapped4, wrapped_mixed = wraps(me, lines.devices)
     for n, region in enumerate(
@@ -133,8 +141,8 @@
                 for copy in unit_copies(h, m):
                     copy.wait()
 
-    keep[...] = picked[0]
-    give[...] = picked[1]
+    for n, share in enumerate(shares):
+        share[...] = picked[n // 2, n % 2]
     for copy in copies:
         copy.wait()
 
@@ -146,15 +154,15 @@
     chunk = heads * nv * BLOCK // (2 * lines.far)
     smem = pl.BlockSpec(memory_space=pltpu.SMEM)
     hbm = pl.BlockSpec(memory_space=pl.ANY)
-    share = (2, lines.far, chunk, head_dim)
+    share = (lines.far, chunk, head_dim)
     return pl.pallas_call(
         functools.partial(pack_kernel, lines=lines, heads=heads, nv=nv, per_device=rows // BLOCK),
         in_specs=[smem, smem, hbm, hbm],
-        out_specs=[pl.BlockSpec(memory_space=pltpu.VMEM)] * 5,
+        out_specs=[pl.BlockSpec(memory_space=pltpu.VMEM)] * 7,
         out_shape=[jax.ShapeDtypeStruct((2, rows, features), BF16)] * 3
-        + [jax.ShapeDtypeStruct(share, BF16)] * 2,
+        + [jax.ShapeDtypeStruct(share, BF16)] * 4,
         scratch_shapes=[
-            pltpu.VMEM((2,) + share, BF16),
+            pltpu.VMEM((2, 2) + share, BF16),
             pltpu.SemaphoreType.DMA((3, 2)),
             pltpu.SemaphoreType.DMA((2, heads * nv * max(1, BLOCK // chunk))),
         ],
@@ -187,12 +195,12 @@
     slab_index, verts, offs, q, grad, out, keys, values, *rest, lines, heads, nv, ns, per_device,
 ):
     gathered, recv, rest = rest[:4], rest[4 : 4 + WDEV], rest[4 + WDEV :]
-    dq, home, near_parts, vkeep, vgive = rest[0], rest[1], rest[2 : 2 + WDEV], rest[7], rest[8]
-    (win, vkv, kc, vc, qs, gs, s_ref, dp_ref, w_ref, ds_ref, nacc, sems) = rest[9:]
+    dq, home, near_parts, shares = rest[0], rest[1], rest[2 : 2 + WDEV], rest[7:11]
+    (win, vkv, kc, vc, qs, gs, s_ref, dp_ref, w_ref, ds_ref, nacc, sems) = rest[11:]
     h = pl.program_id(0)
     slab, me = slab_index[0], lax.axis_index("ctx")
     far, near, core = lines.place(me)
-    _, _, chunk, head_dim = vkeep.shape
+    _, chunk, head_dim = shares[0].shape
     group = q.shape[1] // head_dim
     cand = 1 + nv + ns
     scaling = 1.0 / math.sqrt(head_dim)
@@ -312,15 +320,19 @@
 
     first = core == 0
     keep = jnp.where(first, vertical_sum[0], vertical_sum[1])
-    give = jnp.where(first, vertical_sum[1], vertical_sum[0]).astype(BF16)
+    give = jnp.where(first, vertical_sum[1], vertical_sum[0])
     per_line = heads // 2
-    for c in range(nv * BLOCK // chunk):
-        line = lax.rem(lax.div(h, per_line) + near, 2)
-        slot = lax.rem(h, per_line) * (nv * BLOCK // chunk) + c
-        slot = lax.rem(slot - far + lines.far, lines.far)
-        span = slice(c * chunk, (c + 1) * chunk)
-        vkeep[line, slot] = keep[span, :]
-        vgive[line, slot] = give[span, :]
+    for line in range(2):
+
+        @pl.when(lax.rem(lax.div(h, per_line) + near, 2) == line)
+        def _():
+            for c in range(nv * BLOCK // chunk):
+                slot = lax.rem(h, per_line) * (nv * BLOCK // chunk) + c
+                slot = lax.rem(slot - far + lines.far, lines.far)
+                span = slice(c * chunk, (c + 1) * chunk)
+                shares[line][slot] = keep[span, :].astype(shares[line].dtype)
+                shares[2 + line][slot] = give[span, :].astype(BF16)
+
     for kv in range(2):
         home[kv, :, lanes] = nacc[kv, WDEV * rows :, lanes]
         for part, d in zip(near_parts, distances(core)):
@@ -347,14 +359,14 @@
 
     shard = (2, rows, features)
     vert_shape = (2, heads * nv * BLOCK, head_dim)
-    share = (2, lines.far, heads * nv * BLOCK // (2 * lines.far), head_dim)
+    share = (lines.far, heads * nv * BLOCK // (2 * lines.far), head_dim)
     return pl.pallas_call(
         functools.partial(
             attend_kernel, lines=lines, heads=heads, nv=nv, ns=ns, per_device=per_device
         ),
         grid=(heads,),
         in_specs=[smem] * 3 + [tile] * 3 + [hbm] * (6 + WDEV),
-        out_specs=[tile] + [whole(shard)] * (1 + WDEV) + [whole(share)] * 2,
+        out_specs=[tile] + [whole(shard)] * (1 + WDEV) + [whole(share)] * 4,
         out_shape=[
             jax.ShapeDtypeStruct((rows, width), BF16),
             jax.ShapeDtypeStruct(shard, F32),
@@ -364,6 +376,8 @@
             jax.ShapeDtypeStruct(shard, BF16),
             jax.ShapeDtypeStruct(shard, BF16),
             jax.ShapeDtypeStruct(share, F32),
+            jax.ShapeDtypeStruct(share, BF16),
+            jax.ShapeDtypeStruct(share, BF16),
             jax.ShapeDtypeStruct(share, BF16),
         ],
         scratch_shapes=[
@@ -471,7 +485,7 @@
     regions = context_keys.shape[0]
     _, near, _ = lines.place(lax.axis_index("ctx"))
 
-    own, send4, mixed, keep, give = pack(
+    own, send4, mixed, mine, to_near, to_core, to_both = pack(
         slab_index, verticals, context_keys, context_values, lines
     )
     recv4 = move(send4, lines.shift_pairs(4))
@@ -479,10 +493,12 @@
     recv2 = move(jnp.where(near == 1, recv4, own), lines.near_pairs())
     other2 = move(recv2, lines.core_pairs())
     other4 = move(recv4, lines.core_pairs())
-    share = sum_verticals(lines, keep, give, BF16, (recv4, recv_mixed), ())
+    share = sum_verticals(
+        lines, mine, to_core, to_near, to_both, (recv4, recv_mixed), ()
+    )
     gathered = gather_verticals(lines, share)
 
-    query_grad, home, part2, part4, mixed, give2, give4, vkeep, vgive = attend(
+    query_grad, home, part2, part4, mixed, give2, give4, *shares = attend(
         slab_index, verticals, offsets, queries, output_cotangent, forward_output,
         context_keys, context_values, gathered, [recv2, recv4, recv_mixed, other2, other4], lines,
     )
@@ -492,7 +508,10 @@
     arrived2 = move(sum2, back(lines.shift_pairs(2)))
     arrived4 = move(sum4, back(lines.shift_pairs(4)))
     arrived_mixed = move(mixed, back(lines.mixed_pairs()))
-    share = sum_verticals(lines, vkeep, vgive, F32, (arrived4, arrived_mixed), (arrived2,))
+    mine, to_near, to_core, to_both = shares
+    share = sum_verticals(
+        lines, mine, to_core, to_near, to_both, (arrived4, arrived_mixed), (arrived2,)
+    )
     totals = gather_verticals(lines, share)
     key_gradient, value_gradient = assemble(
         slab_index, verticals, home, (arrived2, arrived4, arrived_mixed), totals, regions, lines

time: 127 us -> 129 us (1.016)
  starting transfers between devices: 28.7 us -> 38.2 us
  waiting for transfers between devices: 66 us -> 57.1 us
    ppermute x32 -> x34, starting transfers between devices: 28.7 us -> 38.2 us  [move(): return lax.ppermute(array, 'ctx', pairs)]
    ppermute x32 -> x34, waiting for transfers between devices: 66 us -> 57.1 us  [move(): return lax.ppermute(array, 'ctx', pairs)]
    add x5 -> x2, other arithmetic: 2.65 us -> 2.23 us  [sum_verticals(): mine.astype(F32) + move(to_core, lines.core_pairs()).astype(F32)]
  transfers between devices with their start and end apart: 32 -> 34, of which waited for: 24 -> 19; matrix products, arithmetic and copies ran while one was open for 1% -> 3% of each run, Pallas kernels for 0% -> 0%
where the time goes in v5:
time: 129 us
  waiting for transfers between devices  57.1 us (44%)
  starting transfers between devices  38.2 us (30%)
  Pallas kernels  26.7 us (21%)
  other arithmetic  3.66 us (3%)
  between operations  1.61 us (1%)
  local copies, waits for them, and re-layouts  1.48 us (1%)
    ppermute x34, waiting for transfers between devices, move(): return lax.ppermute(array, 'ctx', pairs)  57.1 us
    ppermute x34, starting transfers between devices, move(): return lax.ppermute(array, 'ctx', pairs)  38.2 us
    pallas_call x1, Pallas kernels, attend(): pl.pallas_call(functools.partial(attend_kernel, lines=lines, heads=heads,...  17.3 us
    pallas_call x1, Pallas kernels, assemble(): pl.pallas_call(functools.partial(assemble_kernel, lines=lines, heads=head...  5.15 us
    pallas_call x1, Pallas kernels, pack(): pl.pallas_call(functools.partial(pack_kernel, lines=lines, heads=heads, n...  4.18 us
  transfers between devices with their start and end apart: 34, of which 19 were waited for; matrix products, arithmetic and copies ran while one was open for 3% of the time, Pallas kernels for 0%

profile of v5, /device:TPU:0, one launch (start us, length us, event | category | flops | bytes accessed | tf_op | source)
XLA Modules:
  0.0 128.7 jit_solution(3035265312817548592)
XLA Ops:
  1.3 4.2 %shard_map.103 = (bf16[2,128,512]{2,1,0:T(8,128)(2,1)}, bf16[2,128,512]{2,1,0:T(8,128)(2,1)}, bf16[2,128,512]{2,1,0:T(8,128)(2,1)}, bf16[4,256,128]{2,1,0:T(8,12...) custom-call(s32[1]{0:T(128)S(6)} %copy.11.slab_index, ...), custom_call_target="tpu_custom_call" | custom-call | tf_op jit(solution)/shard_map/pallas_call | solution.py:158
  6.0 2.6 %collective-permute-start.1 = (bf16[4,256,128]{2,1,0:T(8,128)(2,1)}, bf16[4,256,128]{2,1,0:T(8,128)(2,1)S(1)}, u32[]{:S(2)}, u32[]{:S(2)}) collective-permute-start(bf16[4,256,128]{2,1,0:T(8,128)(2,1)} %get-tuple-element.28), channel_id=1, source_target_pairs={{0,2},{1,3},{2,0},{3,1},{4,6},{5,7},{6,4},{7,5},{8,10},{9,11},{10,... | collective-permute-start | bytes 786440 | tf_op jit(solution)/shard_map/ppermute | solution.py:50
  8.6 1.8 %collective-permute-start.3 = (bf16[2,128,512]{2,1,0:T(8,128)(2,1)}, bf16[2,128,512]{2,1,0:T(8,128)(2,1)S(1)}, u32[]{:S(2)}, u32[]{:S(2)}) collective-permute-start(bf16[2,128,512]{2,1,0:T(8,128)(2,1)} %get-tuple-element.30), channel_id=1, source_target_pairs={{0,4},{1,5},{2,6},{3,7},{4,8},{5,9},{6,10},{7,11},{8,12},{9,13},{1... | collective-permute-start | bytes 786440 | tf_op jit(solution)/shard_map/ppermute | solution.py:50
  10.5 5.5 %collective-permute-done.1 = bf16[4,256,128]{2,1,0:T(8,128)(2,1)S(1)} collective-permute-done((bf16[4,256,128]{2,1,0:T(8,128)(2,1)}, bf16[4,256,128]{2,1,0:T(8,128)(2,1)S(1)}, u32[]{:S(2)}, u32[]{:S(2)}) %collective-permute-start.1) | collective-permute-done | bytes 262176 | tf_op jit(solution)/shard_map/ppermute | solution.py:50
  16.0 7.5 %collective-permute-done.2 = bf16[4,256,128]{2,1,0:T(8,128)(2,1)S(1)} collective-permute-done((bf16[4,256,128]{2,1,0:T(8,128)(2,1)}, bf16[4,256,128]{2,1,0:T(8,128)(2,1)S(1)}, u32[]{:S(2)}, u32[]{:S(2)}) %collective-permute-start.2) | collective-permute-done | bytes 262176 | tf_op jit(solution)/shard_map/ppermute | solution.py:50
  26.7 3.3 %collective-permute-start.7 = (bf16[256,128]{1,0:T(8,128)(2,1)S(1)}, bf16[256,128]{1,0:T(8,128)(2,1)S(1)}, u32[]{:S(2)}, u32[]{:S(2)}) collective-permute-start(bf16[256,128]{1,0:T(8,128)(2,1)S(1)} %get-tuple-element.53), channel_id=1, source_target_pairs={{0,12},{1,13},{2,14},{3,15},{4,0},{5,1},{6,2},{7,3},{8,4},{9,5},{1... | collective-permute-start | bytes 196616 | tf_op jit(solution)/shard_map/ppermute | solution.py:50
  30.0 3.0 %collective-permute-done.5 = bf16[256,128]{1,0:T(8,128)(2,1)S(1)} collective-permute-done((bf16[256,128]{1,0:T(8,128)(2,1)S(1)}, bf16[256,128]{1,0:T(8,128)(2,1)S(1)}, u32[]{:S(2)}, u32[]{:S(2)}) %collective-permute-start.5) | collective-permute-done | bytes 65568 | tf_op jit(solution)/shard_map/ppermute | solution.py:50
  33.0 2.5 %collective-permute-done.6 = bf16[256,128]{1,0:T(8,128)(2,1)S(1)} collective-permute-done((bf16[256,128]{1,0:T(8,128)(2,1)S(1)}, bf16[256,128]{1,0:T(8,128)(2,1)S(1)}, u32[]{:S(2)}, u32[]{:S(2)}) %collective-permute-start.6) | collective-permute-done | bytes 65568 | tf_op jit(solution)/shard_map/ppermute | solution.py:50
  35.6 2.2 %collective-permute-start.10 = (bf16[256,128]{1,0:T(8,128)(2,1)S(1)}, bf16[256,128]{1,0:T(8,128)(2,1)S(1)}, u32[]{:S(2)}, u32[]{:S(2)}) collective-permute-start(bf16[256,128]{1,0:T(8,128)(2,1)S(1)} %fusion.5), channel_id=1, source_target_pairs={{0,12},{1,13},{2,14},{3,15},{4,0},{5,1},{6,2},{7,3},{8,4},{9,5},{1... | collective-permute-start | bytes 196616 | tf_op jit(solution)/shard_map/ppermute | solution.py:50
  40.3 4.3 %collective-permute-done.9 = bf16[256,128]{1,0:T(8,128)(2,1)S(1)} collective-permute-done((bf16[256,128]{1,0:T(8,128)(2,1)S(1)}, bf16[256,128]{1,0:T(8,128)(2,1)S(1)}, u32[]{:S(2)}, u32[]{:S(2)}) %collective-permute-start.9) | collective-permute-done | bytes 65568 | tf_op jit(solution)/shard_map/ppermute | solution.py:50
  46.8 5.6 %collective-permute-done.11.rest_1_ = bf16[4,256,128]{2,1,0:T(8,128)(2,1)S(1)} collective-permute-done((bf16[4,256,128]{2,1,0:T(8,128)(2,1)S(1)}, bf16[4,256,128]{2,1,0:T(8,128)(2,1)S(1)}, u32[]{:S(2)}, u32[]{:S(2)}) %collective-permute-start.11) | collective-permute-done | bytes 262176 | tf_op jit(solution)/shard_map/ppermute | solution.py:50
  54.6 17.3 %shard_map.104 = (bf16[128,4096]{1,0:T(8,128)(2,1)}, f32[2,128,512]{2,1,0:T(8,128)}, f32[2,128,512]{2,1,0:T(8,128)}, f32[2,128,512]{2,1,0:T(8,128)}, bf16[2,128,...) custom-call(s32[1]{0:T(128)S(6)} %copy.11.slab_index, ...), custom_call_target="tpu_custom_call" | custom-call | tf_op jit(solution)/shard_map/pallas_call | solution.py:363
  74.7 2.3 %collective-permute-start.21 = (bf16[2,128,512]{2,1,0:T(8,128)(2,1)}, bf16[2,128,512]{2,1,0:T(8,128)(2,1)S(1)}, u32[]{:S(2)}, u32[]{:S(2)}) collective-permute-start(bf16[2,128,512]{2,1,0:T(8,128)(2,1)} %get-tuple-element.40), channel_id=1, source_target_pairs={{1,0},{6,1},{3,2},{8,3},{5,4},{10,5},{7,6},{12,7},{9,8},{14,9},{11... | collective-permute-start | bytes 786440 | tf_op jit(solution)/shard_map/ppermute | solution.py:50
  78.2 2.7 %collective-permute-start.20 = (bf16[2,128,512]{2,1,0:T(8,128)(2,1)S(1)}, bf16[2,128,512]{2,1,0:T(8,128)(2,1)S(1)}, u32[]{:S(2)}, u32[]{:S(2)}) collective-permute-start(bf16[2,128,512]{2,1,0:T(8,128)(2,1)S(1)} %add_convert_fusion), channel_id=1, source_target_pairs={{4,0},{5,1},{6,2},{7,3},{8,4},{9,5},{10,6},{11,7},{12,8},{13,9},{1... | collective-permute-start | bytes 786440 | tf_op jit(solution)/shard_map/ppermute | solution.py:50
  80.8 3.9 %collective-permute-done.23 = bf16[4,256,128]{2,1,0:T(8,128)(2,1)S(1)} collective-permute-done((bf16[4,256,128]{2,1,0:T(8,128)(2,1)}, bf16[4,256,128]{2,1,0:T(8,128)(2,1)S(1)}, u32[]{:S(2)}, u32[]{:S(2)}) %collective-permute-start.23) | collective-permute-done | bytes 262176 | tf_op jit(solution)/shard_map/ppermute | solution.py:50
  84.7 4.0 %collective-permute-done.24 = bf16[4,256,128]{2,1,0:T(8,128)(2,1)S(1)} collective-permute-done((bf16[4,256,128]{2,1,0:T(8,128)(2,1)}, bf16[4,256,128]{2,1,0:T(8,128)(2,1)S(1)}, u32[]{:S(2)}, u32[]{:S(2)}) %collective-permute-start.24) | collective-permute-done | bytes 262176 | tf_op jit(solution)/shard_map/ppermute | solution.py:50
  90.0 2.2 %collective-permute-start.25 = (bf16[256,128]{1,0:T(8,128)(2,1)S(1)}, bf16[256,128]{1,0:T(8,128)(2,1)S(1)}, u32[]{:S(2)}, u32[]{:S(2)}) collective-permute-start(bf16[256,128]{1,0:T(8,128)(2,1)S(1)} %get-tuple-element.49), channel_id=1, source_target_pairs={{0,4},{1,5},{2,6},{3,7},{4,8},{5,9},{6,10},{7,11},{8,12},{9,13},{1... | collective-permute-start | bytes 196616 | tf_op jit(solution)/shard_map/ppermute | solution.py:50
  93.9 3.6 %collective-permute-start.18 = (bf16[2,128,512]{2,1,0:T(8,128)(2,1)S(1)}, bf16[2,128,512]{2,1,0:T(8,128)(2,1)S(1)}, u32[]{:S(2)}, u32[]{:S(2)}) collective-permute-start(bf16[2,128,512]{2,1,0:T(8,128)(2,1)S(1)} %add_convert_fusion.1), channel_id=1, source_target_pairs={{2,0},{3,1},{4,2},{5,3},{6,4},{7,5},{8,6},{9,7},{10,8},{11,9},{12,... | collective-permute-start | bytes 786440 | tf_op jit(solution)/shard_map/ppermute | solution.py:50
  98.0 2.9 %collective-permute-done.26 = bf16[256,128]{1,0:T(8,128)(2,1)S(1)} collective-permute-done((bf16[256,128]{1,0:T(8,128)(2,1)S(1)}, bf16[256,128]{1,0:T(8,128)(2,1)S(1)}, u32[]{:S(2)}, u32[]{:S(2)}) %collective-permute-start.26) | collective-permute-done | bytes 65568 | tf_op jit(solution)/shard_map/ppermute | solution.py:50
  100.9 2.2 %collective-permute-done.18.rest_0_ = bf16[2,128,512]{2,1,0:T(8,128)(2,1)S(1)} collective-permute-done((bf16[2,128,512]{2,1,0:T(8,128)(2,1)S(1)}, bf16[2,128,512]{2,1,0:T(8,128)(2,1)S(1)}, u32[]{:S(2)}, u32[]{:S(2)}) %collective-permute-start.18) | collective-permute-done | bytes 262176 | tf_op jit(solution)/shard_map/ppermute | solution.py:50
  103.1 5.2 %collective-permute-start.30 = (bf16[256,128]{1,0:T(8,128)(2,1)S(1)}, bf16[256,128]{1,0:T(8,128)(2,1)S(1)}, u32[]{:S(2)}, u32[]{:S(2)}) collective-permute-start(bf16[256,128]{1,0:T(8,128)(2,1)S(1)} %fusion.2), channel_id=1, source_target_pairs={{0,12},{1,13},{2,14},{3,15},{4,0},{5,1},{6,2},{7,3},{8,4},{9,5},{1... | collective-permute-start | bytes 196616 | tf_op jit(solution)/shard_map/ppermute | solution.py:50
  110.7 2.8 %collective-permute-done.29 = bf16[256,128]{1,0:T(8,128)(2,1)S(1)} collective-permute-done((bf16[256,128]{1,0:T(8,128)(2,1)S(1)}, bf16[256,128]{1,0:T(8,128)(2,1)S(1)}, u32[]{:S(2)}, u32[]{:S(2)}) %collective-permute-start.29) | collective-permute-done | bytes 65568 | tf_op jit(solution)/shard_map/ppermute | solution.py:50
  116.1 5.3 %collective-permute-done.31.rest_4_ = bf16[4,256,128]{2,1,0:T(8,128)(2,1)S(1)} collective-permute-done((bf16[4,256,128]{2,1,0:T(8,128)(2,1)S(1)}, bf16[4,256,128]{2,1,0:T(8,128)(2,1)S(1)}, u32[]{:S(2)}, u32[]{:S(2)}) %collective-permute-start.31) | collective-permute-done | bytes 262176 | tf_op jit(solution)/shard_map/ppermute | solution.py:50
  123.6 5.1 %shard_map.105 = (bf16[16,128,512]{2,1,0:T(8,128)(2,1)}, bf16[16,128,512]{2,1,0:T(8,128)(2,1)}) custom-call(s32[1]{0:T(128)S(6)} %copy.11.slab_index, s32[4,8]{1,0:T(4,128)} %verts.5, f32[2,128,512]{2,1,0:T(8,128)} %get-tuple-element.35.home, bf16[2,128,512]{2,1,0:T(8,128)(2,1)} %copy-done.7, bf16[2,128,512]{2,1,0:T(8,128)(2,1)} %copy-done.6, ...), custom_call_target="tpu_custom_call" | custom-call | tf_op jit(solution)/shard_map/pallas_call | solution.py:458
  (96 shorter events, 25.3 us)
Async XLA Ops:
  6.0 10.0 %collective-permute-start.1 = (bf16[4,256,128]{2,1,0:T(8,128)(2,1)}, bf16[4,256,128]{2,1,0:T(8,128)(2,1)S(1)}, u32[]{:S(2)}, u32[]{:S(2)}) collective-permute-start(bf16[4,256,128]{2,1,0:T(8,128)(2,1)} %get-tuple-element.28), channel_id=1, source_target_pairs={{0,2},{1,3},{2,0},{3,1},{4,6},{5,7},{6,4},{7,5},{8,10},{9,11},{10,... | collective-permute-start | bytes 786440 | tf_op jit(solution)/shard_map/ppermute | solution.py:50
  8.6 14.9 %collective-permute-start.2 = (bf16[4,256,128]{2,1,0:T(8,128)(2,1)}, bf16[4,256,128]{2,1,0:T(8,128)(2,1)S(1)}, u32[]{:S(2)}, u32[]{:S(2)}) collective-permute-start(bf16[4,256,128]{2,1,0:T(8,128)(2,1)} %get-tuple-element.29), channel_id=1, source_target_pairs={{0,3},{1,2},{2,1},{3,0},{4,7},{5,6},{6,5},{7,4},{8,11},{9,10},{10,... | collective-permute-start | bytes 786440 | tf_op jit(solution)/shard_map/ppermute | solution.py:50
  8.6 15.9 %collective-permute-start.3 = (bf16[2,128,512]{2,1,0:T(8,128)(2,1)}, bf16[2,128,512]{2,1,0:T(8,128)(2,1)S(1)}, u32[]{:S(2)}, u32[]{:S(2)}) collective-permute-start(bf16[2,128,512]{2,1,0:T(8,128)(2,1)} %get-tuple-element.30), channel_id=1, source_target_pairs={{0,4},{1,5},{2,6},{3,7},{4,8},{5,9},{6,10},{7,11},{8,12},{9,13},{1... | collective-permute-start | bytes 786440 | tf_op jit(solution)/shard_map/ppermute | solution.py:50
  10.4 15.6 %collective-permute-start.4 = (bf16[2,128,512]{2,1,0:T(8,128)(2,1)}, bf16[2,128,512]{2,1,0:T(8,128)(2,1)S(1)}, u32[]{:S(2)}, u32[]{:S(2)}) collective-permute-start(bf16[2,128,512]{2,1,0:T(8,128)(2,1)} %get-tuple-element.31), channel_id=1, source_target_pairs={{0,1},{1,6},{2,3},{3,8},{4,5},{5,10},{6,7},{7,12},{8,9},{9,14},{10... | collective-permute-start | bytes 786440 | tf_op jit(solution)/shard_map/ppermute | solution.py:50
  26.1 6.9 %collective-permute-start.5 = (bf16[256,128]{1,0:T(8,128)(2,1)S(1)}, bf16[256,128]{1,0:T(8,128)(2,1)S(1)}, u32[]{:S(2)}, u32[]{:S(2)}) collective-permute-start(bf16[256,128]{1,0:T(8,128)(2,1)S(1)} %get-tuple-element.52), channel_id=1, source_target_pairs={{0,4},{1,5},{2,6},{3,7},{4,8},{5,9},{6,10},{7,11},{8,12},{9,13},{1... | collective-permute-start | bytes 196616 | tf_op jit(solution)/shard_map/ppermute | solution.py:50
  26.7 6.3 %collective-permute-start.7 = (bf16[256,128]{1,0:T(8,128)(2,1)S(1)}, bf16[256,128]{1,0:T(8,128)(2,1)S(1)}, u32[]{:S(2)}, u32[]{:S(2)}) collective-permute-start(bf16[256,128]{1,0:T(8,128)(2,1)S(1)} %get-tuple-element.53), channel_id=1, source_target_pairs={{0,12},{1,13},{2,14},{3,15},{4,0},{5,1},{6,2},{7,3},{8,4},{9,5},{1... | collective-permute-start | bytes 196616 | tf_op jit(solution)/shard_map/ppermute | solution.py:50
  37.8 6.8 %collective-permute-start.9 = (bf16[256,128]{1,0:T(8,128)(2,1)S(1)}, bf16[256,128]{1,0:T(8,128)(2,1)S(1)}, u32[]{:S(2)}, u32[]{:S(2)}) collective-permute-start(bf16[256,128]{1,0:T(8,128)(2,1)S(1)} %fusion.5), channel_id=1, source_target_pairs={{0,8},{1,9},{2,10},{3,11},{4,12},{5,13},{6,14},{7,15},{8,0},{9,1},... | collective-permute-start | bytes 196616 | tf_op jit(solution)/shard_map/ppermute | solution.py:50
  37.8 6.8 %collective-permute-start.8 = (bf16[256,128]{1,0:T(8,128)(2,1)S(1)}, bf16[256,128]{1,0:T(8,128)(2,1)S(1)}, u32[]{:S(2)}, u32[]{:S(2)}) collective-permute-start(bf16[256,128]{1,0:T(8,128)(2,1)S(1)} %fusion.5), channel_id=1, source_target_pairs={{0,4},{1,5},{2,6},{3,7},{4,8},{5,9},{6,10},{7,11},{8,12},{9,13},{1... | collective-permute-start | bytes 196616 | tf_op jit(solution)/shard_map/ppermute | solution.py:50
  38.5 8.2 %collective-permute-start.14 = (bf16[2,128,512]{2,1,0:T(8,128)(2,1)S(1)}, bf16[2,128,512]{2,1,0:T(8,128)(2,1)S(1)}, u32[]{:S(2)}, u32[]{:S(2)}) collective-permute-start(bf16[2,128,512]{2,1,0:T(8,128)(2,1)S(1)} %broadcast_select_fusion), channel_id=1, source_target_pairs={{0,2},{1,3},{2,0},{3,1},{4,6},{5,7},{6,4},{7,5},{8,10},{9,11},{10,... | collective-permute-start | bytes 786440 | tf_op jit(solution)/shard_map/ppermute | solution.py:50
  44.6 7.7 %collective-permute-start.11 = (bf16[4,256,128]{2,1,0:T(8,128)(2,1)S(1)}, bf16[4,256,128]{2,1,0:T(8,128)(2,1)S(1)}, u32[]{:S(2)}, u32[]{:S(2)}) collective-permute-start(bf16[4,256,128]{2,1,0:T(8,128)(2,1)S(1)} %pad_maximum_fusion.rest_0_), channel_id=1, source_target_pairs={{0,2},{1,3},{2,0},{3,1},{4,6},{5,7},{6,4},{7,5},{8,10},{9,11},{10,... | collective-permute-start | bytes 786440 | tf_op jit(solution)/shard_map/ppermute | solution.py:50
  46.2 6.2 %collective-permute-start.16 = (bf16[2,128,512]{2,1,0:T(8,128)(2,1)S(1)}, bf16[2,128,512]{2,1,0:T(8,128)(2,1)S(1)}, u32[]{:S(2)}, u32[]{:S(2)}) collective-permute-start(bf16[2,128,512]{2,1,0:T(8,128)(2,1)S(1)} %collective-permute-done.3.rest_5_), channel_id=1, source_target_pairs={{0,1},{1,0},{2,3},{3,2},{4,5},{5,4},{6,7},{7,6},{8,9},{9,8},{10,11... | collective-permute-start | bytes 786440 | tf_op jit(solution)/shard_map/ppermute | solution.py:50
  46.2 6.2 %collective-permute-start.12 = (bf16[4,256,128]{2,1,0:T(8,128)(2,1)S(1)}, bf16[4,256,128]{2,1,0:T(8,128)(2,1)S(1)}, u32[]{:S(2)}, u32[]{:S(2)}) collective-permute-start(bf16[4,256,128]{2,1,0:T(8,128)(2,1)S(1)} %pad_maximum_fusion.rest_0_), channel_id=1, source_target_pairs={{0,1},{1,0},{2,3},{3,2},{4,5},{5,4},{6,7},{7,6},{8,9},{9,8},{10,11... | collective-permute-start | bytes 786440 | tf_op jit(solution)/shard_map/ppermute | solution.py:50
  72.2 6.0 %collective-permute-start.22 = (bf16[4,256,128]{2,1,0:T(8,128)(2,1)}, bf16[4,256,128]{2,1,0:T(8,128)(2,1)S(1)}, u32[]{:S(2)}, u32[]{:S(2)}) collective-permute-start(bf16[4,256,128]{2,1,0:T(8,128)(2,1)} %get-tuple-element.42), channel_id=1, source_target_pairs={{0,1},{1,0},{2,3},{3,2},{4,5},{5,4},{6,7},{7,6},{8,9},{9,8},{10,11... | collective-permute-start | bytes 786440 | tf_op jit(solution)/shard_map/ppermute | solution.py:50
  72.6 12.2 %collective-permute-start.23 = (bf16[4,256,128]{2,1,0:T(8,128)(2,1)}, bf16[4,256,128]{2,1,0:T(8,128)(2,1)S(1)}, u32[]{:S(2)}, u32[]{:S(2)}) collective-permute-start(bf16[4,256,128]{2,1,0:T(8,128)(2,1)} %get-tuple-element.43), channel_id=1, source_target_pairs={{0,2},{1,3},{2,0},{3,1},{4,6},{5,7},{6,4},{7,5},{8,10},{9,11},{10,... | collective-permute-start | bytes 786440 | tf_op jit(solution)/shard_map/ppermute | solution.py:50
  74.1 14.6 %collective-permute-start.24 = (bf16[4,256,128]{2,1,0:T(8,128)(2,1)}, bf16[4,256,128]{2,1,0:T(8,128)(2,1)S(1)}, u32[]{:S(2)}, u32[]{:S(2)}) collective-permute-start(bf16[4,256,128]{2,1,0:T(8,128)(2,1)} %get-tuple-element.44), channel_id=1, source_target_pairs={{0,3},{1,2},{2,1},{3,0},{4,7},{5,6},{6,5},{7,4},{8,11},{9,10},{10,... | collective-permute-start | bytes 786440 | tf_op jit(solution)/shard_map/ppermute | solution.py:50
  74.1 19.8 %collective-permute-start.17 = (bf16[2,128,512]{2,1,0:T(8,128)(2,1)}, bf16[2,128,512]{2,1,0:T(8,128)(2,1)S(1)}, u32[]{:S(2)}, u32[]{:S(2)}) collective-permute-start(bf16[2,128,512]{2,1,0:T(8,128)(2,1)} %get-tuple-element.37), channel_id=1, source_target_pairs={{0,1},{1,0},{2,3},{3,2},{4,5},{5,4},{6,7},{7,6},{8,9},{9,8},{10,11... | collective-permute-start | bytes 786440 | tf_op jit(solution)/shard_map/ppermute | solution.py:50
  74.7 15.2 %collective-permute-start.21 = (bf16[2,128,512]{2,1,0:T(8,128)(2,1)}, bf16[2,128,512]{2,1,0:T(8,128)(2,1)S(1)}, u32[]{:S(2)}, u32[]{:S(2)}) collective-permute-start(bf16[2,128,512]{2,1,0:T(8,128)(2,1)} %get-tuple-element.40), channel_id=1, source_target_pairs={{1,0},{6,1},{3,2},{8,3},{5,4},{10,5},{7,6},{12,7},{9,8},{14,9},{11... | collective-permute-start | bytes 786440 | tf_op jit(solution)/shard_map/ppermute | solution.py:50
  78.2 11.7 %collective-permute-start.20 = (bf16[2,128,512]{2,1,0:T(8,128)(2,1)S(1)}, bf16[2,128,512]{2,1,0:T(8,128)(2,1)S(1)}, u32[]{:S(2)}, u32[]{:S(2)}) collective-permute-start(bf16[2,128,512]{2,1,0:T(8,128)(2,1)S(1)} %add_convert_fusion), channel_id=1, source_target_pairs={{4,0},{5,1},{6,2},{7,3},{8,4},{9,5},{10,6},{11,7},{12,8},{13,9},{1... | collective-permute-start | bytes 786440 | tf_op jit(solution)/shard_map/ppermute | solution.py:50
  90.0 7.6 %collective-permute-start.25 = (bf16[256,128]{1,0:T(8,128)(2,1)S(1)}, bf16[256,128]{1,0:T(8,128)(2,1)S(1)}, u32[]{:S(2)}, u32[]{:S(2)}) collective-permute-start(bf16[256,128]{1,0:T(8,128)(2,1)S(1)} %get-tuple-element.49), channel_id=1, source_target_pairs={{0,4},{1,5},{2,6},{3,7},{4,8},{5,9},{6,10},{7,11},{8,12},{9,13},{1... | collective-permute-start | bytes 196616 | tf_op jit(solution)/shard_map/ppermute | solution.py:50
  93.9 7.0 %collective-permute-start.26 = (bf16[256,128]{1,0:T(8,128)(2,1)S(1)}, bf16[256,128]{1,0:T(8,128)(2,1)S(1)}, u32[]{:S(2)}, u32[]{:S(2)}) collective-permute-start(bf16[256,128]{1,0:T(8,128)(2,1)S(1)} %get-tuple-element.51), channel_id=1, source_target_pairs={{0,8},{1,9},{2,10},{3,11},{4,12},{5,13},{6,14},{7,15},{8,0},{9,1},... | collective-permute-start | bytes 196616 | tf_op jit(solution)/shard_map/ppermute | solution.py:50
  93.9 9.1 %collective-permute-start.18 = (bf16[2,128,512]{2,1,0:T(8,128)(2,1)S(1)}, bf16[2,128,512]{2,1,0:T(8,128)(2,1)S(1)}, u32[]{:S(2)}, u32[]{:S(2)}) collective-permute-start(bf16[2,128,512]{2,1,0:T(8,128)(2,1)S(1)} %add_convert_fusion.1), channel_id=1, source_target_pairs={{2,0},{3,1},{4,2},{5,3},{6,4},{7,5},{8,6},{9,7},{10,8},{11,9},{12,... | collective-permute-start | bytes 786440 | tf_op jit(solution)/shard_map/ppermute | solution.py:50
  103.1 7.6 %collective-permute-start.30 = (bf16[256,128]{1,0:T(8,128)(2,1)S(1)}, bf16[256,128]{1,0:T(8,128)(2,1)S(1)}, u32[]{:S(2)}, u32[]{:S(2)}) collective-permute-start(bf16[256,128]{1,0:T(8,128)(2,1)S(1)} %fusion.2), channel_id=1, source_target_pairs={{0,12},{1,13},{2,14},{3,15},{4,0},{5,1},{6,2},{7,3},{8,4},{9,5},{1... | collective-permute-start | bytes 196616 | tf_op jit(solution)/shard_map/ppermute | solution.py:50
  108.3 6.1 %collective-permute-start.28 = (bf16[256,128]{1,0:T(8,128)(2,1)S(1)}, bf16[256,128]{1,0:T(8,128)(2,1)S(1)}, u32[]{:S(2)}, u32[]{:S(2)}) collective-permute-start(bf16[256,128]{1,0:T(8,128)(2,1)S(1)} %fusion.2), channel_id=1, source_target_pairs={{0,4},{1,5},{2,6},{3,7},{4,8},{5,9},{6,10},{7,11},{8,12},{9,13},{1... | collective-permute-start | bytes 196616 | tf_op jit(solution)/shard_map/ppermute | solution.py:50
  114.4 7.0 %collective-permute-start.31 = (bf16[4,256,128]{2,1,0:T(8,128)(2,1)S(1)}, bf16[4,256,128]{2,1,0:T(8,128)(2,1)S(1)}, u32[]{:S(2)}, u32[]{:S(2)}) collective-permute-start(bf16[4,256,128]{2,1,0:T(8,128)(2,1)S(1)} %pad_maximum_fusion.1.rest_3_), channel_id=1, source_target_pairs={{0,2},{1,3},{2,0},{3,1},{4,6},{5,7},{6,4},{7,5},{8,10},{9,11},{10,... | collective-permute-start | bytes 786440 | tf_op jit(solution)/shard_map/ppermute | solution.py:50
  (28 other events, 276.8 us)

commit v6 on v5

--- a/solution.py
+++ b/solution.py
@@ -50,35 +50,35 @@
     return lax.ppermute(array, "ctx", pairs)
 
 
-def gather_verticals(lines, own):
-    parts = [own] + [move(own, lines.far_pairs(by)) for by in range(1, lines.far)]
-    mine = jnp.stack(parts)
+def after(array, *others):
+    return lax.optimization_barrier((array, *others))[0]
+
+
+def plane_sum(lines, mine, to_near, to_core, to_both):
+    to_near = (to_near.astype(F32) + move(to_both, lines.core_pairs()).astype(F32)).astype(BF16)
+    from_near = move(to_near, lines.near_pairs())
+    from_core = move(to_core, lines.core_pairs())
+    return mine.astype(F32) + from_core.astype(F32) + from_near.astype(F32)
+
+
+def far_sum(lines, quarter):
+    share = quarter[0]
+    for by in range(1, lines.far):
+        share = share + move(quarter[by].astype(BF16), lines.far_pairs(by)).astype(F32)
+    share = share.astype(BF16)
+    parts = [share] + [move(share, lines.far_pairs(by)) for by in range(1, lines.far)]
+    return jnp.stack(parts)
+
+
+def plane_gather(lines, mine):
     across = move(mine, lines.near_pairs())
     core_mine = move(mine, lines.core_pairs())
     core_across = move(across, lines.core_pairs())
     return mine, across, core_mine, core_across
 
 
-def after(array, *others):
-    return lax.optimization_barrier((array, *others))[0]
-
-
-def sum_verticals(lines, mine, to_core, to_near, to_both, ahead_of_far, ahead_of_share):
-    quarter = (
-        mine.astype(F32)
-        + move(to_core, lines.core_pairs()).astype(F32)
-        + move(to_near, lines.near_pairs()).astype(F32)
-        + move(to_both, lines.both_pairs()).astype(F32)
-    )
-    quarter = after(quarter, *ahead_of_far)
-    share = quarter[0]
-    for by in range(1, lines.far):
-        share = share + move(quarter[by].astype(BF16), lines.far_pairs(by)).astype(F32)
-    return after(share.astype(BF16), *ahead_of_share)
-
-
 def wraps(me, devices):
-    return [me + 2 >= devices, me + 4 >= devices, (lax.rem(me, 2) == 1) & (me + 5 >= devices)]
+    return [me + 4 >= devices, (lax.rem(me, 2) == 1) & (me + 5 >= devices)]
 
 
 def pack_kernel(slab_index, verts, keys, values, *rest, lines, heads, nv, per_device):
@@ -89,7 +89,7 @@
     far, near, core = lines.place(me)
     _, chunk, head_dim = shares[0].shape
     copies = []
-    _, wrapped4, wrapped_mixed = wraps(me, lines.devices)
+    wrapped4, wrapped_mixed = wraps(me, lines.devices)
     for n, region in enumerate(
         (slab, slab - wrapped4.astype(jnp.int32), slab - wrapped_mixed.astype(jnp.int32))
     ):
@@ -401,7 +401,7 @@
 
 
 def assemble_kernel(slab_index, verts, home, *rest, lines, heads, nv, per_device):
-    arrived, gathered = rest[:3], rest[3:7]
+    from_near, arrived, gathered = rest[0], rest[1:3], rest[3:7]
     key_out, value_out, vert, acc, sems = rest[7:]
     slab, me = slab_index[0], lax.axis_index("ctx")
     devices = lines.devices
@@ -413,6 +413,12 @@
     slab_blocks = per_device * devices
     acc[0] = home[...]
     acc[1] = jnp.zeros_like(home)
+    _, near, _ = lines.place(me)
+
+    @pl.when(near == 0)
+    def _():
+        acc[0] += from_near[...].astype(F32)
+
     for part, wrapped in zip(arrived, wraps(me, devices)):
         acc[wrapped.astype(jnp.int32)] += part[...].astype(F32)
     key_out[...] = jnp.zeros_like(key_out)
@@ -449,7 +455,7 @@
         outs[kv][slab - 1] = acc[1, kv].astype(BF16)
 
 
-def assemble(slab_index, verticals, home, arrived, gathered, regions, lines):
+def assemble(slab_index, verticals, home, from_near, arrived, gathered, regions, lines):
     _, rows, features = home.shape
     heads, nv = verticals.shape
     smem = pl.BlockSpec(memory_space=pltpu.SMEM)
@@ -468,7 +474,7 @@
             pltpu.SemaphoreType.DMA((4 * lines.far,)),
         ],
         compiler_params=pltpu.CompilerParams(vmem_limit_bytes=VMEM_LIMIT),
-    )(slab_index, verticals, home, *arrived, *gathered)
+    )(slab_index, verticals, home, from_near, *arrived, *gathered)
 
 
 def shards(
@@ -489,32 +495,31 @@
         slab_index, verticals, context_keys, context_values, lines
     )
     recv4 = move(send4, lines.shift_pairs(4))
-    recv_mixed = move(mixed, lines.mixed_pairs())
+    quarter = plane_sum(lines, mine, to_near, to_core, to_both)
     recv2 = move(jnp.where(near == 1, recv4, own), lines.near_pairs())
+    gathered = after(far_sum(lines, after(quarter, recv4)), recv2)
+    recv_mixed = move(after(mixed, gathered), lines.mixed_pairs())
+    gathered = plane_gather(lines, gathered)
     other2 = move(recv2, lines.core_pairs())
     other4 = move(recv4, lines.core_pairs())
-    share = sum_verticals(
-        lines, mine, to_core, to_near, to_both, (recv4, recv_mixed), ()
-    )
-    gathered = gather_verticals(lines, share)
 
     query_grad, home, part2, part4, mixed, give2, give4, *shares = attend(
         slab_index, verticals, offsets, queries, output_cotangent, forward_output,
         context_keys, context_values, gathered, [recv2, recv4, recv_mixed, other2, other4], lines,
     )
 
+    arrived_mixed = move(mixed, back(lines.mixed_pairs()))
     sum2 = (part2 + move(give2, lines.core_pairs()).astype(F32)).astype(BF16)
-    sum4 = (part4 + move(give4, lines.core_pairs()).astype(F32)).astype(BF16)
-    arrived2 = move(sum2, back(lines.shift_pairs(2)))
-    arrived4 = move(sum4, back(lines.shift_pairs(4)))
-    arrived_mixed = move(mixed, back(lines.mixed_pairs()))
+    sum4 = part4 + move(give4, lines.core_pairs()).astype(F32)
     mine, to_near, to_core, to_both = shares
-    share = sum_verticals(
-        lines, mine, to_core, to_near, to_both, (arrived4, arrived_mixed), (arrived2,)
-    )
-    totals = gather_verticals(lines, share)
+    quarter = plane_sum(lines, mine, to_near, to_core, to_both)
+    from_near = move(after(sum2, quarter), lines.near_pairs())
+    totals = after(far_sum(lines, after(quarter, arrived_mixed)), from_near)
+    sum4 = (sum4 + jnp.where(near == 1, from_near.astype(F32), 0.0)).astype(BF16)
+    arrived4 = move(after(sum4, totals), back(lines.shift_pairs(4)))
+    totals = plane_gather(lines, totals)
     key_gradient, value_gradient = assemble(
-        slab_index, verticals, home, (arrived2, arrived4, arrived_mixed), totals, regions, lines
+        slab_index, verticals, home, from_near, (arrived4, arrived_mixed), totals, regions, lines
     )
     return query_grad, key_gradient, value_gradient
 

time: 129 us -> 117 us (0.907)
  starting transfers between devices: 38.2 us -> 23.7 us
    ppermute x34, starting transfers between devices: 38.2 us -> 23.7 us  [move(): return lax.ppermute(array, 'ctx', pairs)]
  transfers between devices with their start and end apart: 34 -> 34, of which waited for: 19 -> 18; matrix products, arithmetic and copies ran while one was open for 3% -> 4% of each run, Pallas kernels for 0% -> 0%
where the time goes in v6:
time: 117 us
  waiting for transfers between devices  57.4 us (49%)
  Pallas kernels  26.7 us (23%)
  starting transfers between devices  23.7 us (20%)
  other arithmetic  4.76 us (4%)
  local copies, waits for them, and re-layouts  2.38 us (2%)
  between operations  1.64 us (1%)
    ppermute x34, waiting for transfers between devices, move(): return lax.ppermute(array, 'ctx', pairs)  57.4 us
    ppermute x34, starting transfers between devices, move(): return lax.ppermute(array, 'ctx', pairs)  23.7 us
    pallas_call x1, Pallas kernels, attend(): pl.pallas_call(functools.partial(attend_kernel, lines=lines, heads=heads,...  17.3 us
    pallas_call x1, Pallas kernels, assemble(): pl.pallas_call(functools.partial(assemble_kernel, lines=lines, heads=head...  5.17 us
    pallas_call x1, Pallas kernels, pack(): pl.pallas_call(functools.partial(pack_kernel, lines=lines, heads=heads, n...  4.18 us
    unnamed x40, local copies, waits for them, and re-layouts  2.35 us
  transfers between devices with their start and end apart: 34, of which 18 were waited for; matrix products, arithmetic and copies ran while one was open for 4% of the time, Pallas kernels for 0%

profile of v6, /device:TPU:0, one launch (start us, length us, event | category | flops | bytes accessed | tf_op | source)
XLA Modules:
  0.0 116.6 jit_solution(12605339710168786078)
XLA Ops:
  1.3 4.2 %shard_map.103 = (bf16[2,128,512]{2,1,0:T(8,128)(2,1)}, bf16[2,128,512]{2,1,0:T(8,128)(2,1)}, bf16[2,128,512]{2,1,0:T(8,128)(2,1)}, bf16[4,256,128]{2,1,0:T(8,12...) custom-call(s32[1]{0:T(128)S(6)} %copy.11.slab_index, ...), custom_call_target="tpu_custom_call" | custom-call | tf_op jit(solution)/shard_map/pallas_call | solution.py:158
  8.4 2.9 %collective-permute-start.2 = (bf16[4,256,128]{2,1,0:T(8,128)(2,1)S(1)}, bf16[4,256,128]{2,1,0:T(8,128)(2,1)S(1)}, u32[]{:S(2)}, u32[]{:S(2)}) collective-permute-start(bf16[4,256,128]{2,1,0:T(8,128)(2,1)S(1)} %add_convert_fusion.3), channel_id=1, source_target_pairs={{0,2},{1,3},{2,0},{3,1},{4,6},{5,7},{6,4},{7,5},{8,10},{9,11},{10,... | collective-permute-start | bytes 786440 | tf_op jit(solution)/shard_map/ppermute | solution.py:50
  11.3 1.6 %collective-permute-start.3 = (bf16[2,128,512]{2,1,0:T(8,128)(2,1)}, bf16[2,128,512]{2,1,0:T(8,128)(2,1)S(1)}, u32[]{:S(2)}, u32[]{:S(2)}) collective-permute-start(bf16[2,128,512]{2,1,0:T(8,128)(2,1)} %get-tuple-element.34), channel_id=1, source_target_pairs={{0,4},{1,5},{2,6},{3,7},{4,8},{5,9},{6,10},{7,11},{8,12},{9,13},{1... | collective-permute-start | bytes 786440 | tf_op jit(solution)/shard_map/ppermute | solution.py:50
  12.9 5.0 %collective-permute-done.2 = bf16[4,256,128]{2,1,0:T(8,128)(2,1)S(1)} collective-permute-done((bf16[4,256,128]{2,1,0:T(8,128)(2,1)S(1)}, bf16[4,256,128]{2,1,0:T(8,128)(2,1)S(1)}, u32[]{:S(2)}, u32[]{:S(2)}) %collective-permute-start.2) | collective-permute-done | bytes 262176 | tf_op jit(solution)/shard_map/ppermute | solution.py:50
  19.0 2.4 %collective-permute-done.3.rest_5_ = bf16[2,128,512]{2,1,0:T(8,128)(2,1)S(1)} collective-permute-done((bf16[2,128,512]{2,1,0:T(8,128)(2,1)}, bf16[2,128,512]{2,1,0:T(8,128)(2,1)S(1)}, u32[]{:S(2)}, u32[]{:S(2)}) %collective-permute-start.3) | collective-permute-done | bytes 262176 | tf_op jit(solution)/shard_map/ppermute | solution.py:50
  21.6 3.8 %collective-permute-start.6 = (bf16[256,128]{1,0:T(8,128)(2,1)S(1)}, bf16[256,128]{1,0:T(8,128)(2,1)S(1)}, u32[]{:S(2)}, u32[]{:S(2)}) collective-permute-start(bf16[256,128]{1,0:T(8,128)(2,1)S(1)} %get-tuple-element.61), channel_id=1, source_target_pairs={{0,12},{1,13},{2,14},{3,15},{4,0},{5,1},{6,2},{7,3},{8,4},{9,5},{1... | collective-permute-start | bytes 196616 | tf_op jit(solution)/shard_map/ppermute | solution.py:50
  26.1 1.9 %collective-permute-done.4 = bf16[256,128]{1,0:T(8,128)(2,1)S(1)} collective-permute-done((bf16[256,128]{1,0:T(8,128)(2,1)S(1)}, bf16[256,128]{1,0:T(8,128)(2,1)S(1)}, u32[]{:S(2)}, u32[]{:S(2)}) %collective-permute-start.4) | collective-permute-done | bytes 65568 | tf_op jit(solution)/shard_map/ppermute | solution.py:50
  27.9 3.3 %collective-permute-done.5 = bf16[256,128]{1,0:T(8,128)(2,1)S(1)} collective-permute-done((bf16[256,128]{1,0:T(8,128)(2,1)S(1)}, bf16[256,128]{1,0:T(8,128)(2,1)S(1)}, u32[]{:S(2)}, u32[]{:S(2)}) %collective-permute-start.5) | collective-permute-done | bytes 65568 | tf_op jit(solution)/shard_map/ppermute | solution.py:50
  31.6 1.8 %collective-permute-start.7 = (bf16[256,128]{1,0:T(8,128)(2,1)S(1)}, bf16[256,128]{1,0:T(8,128)(2,1)S(1)}, u32[]{:S(2)}, u32[]{:S(2)}) collective-permute-start(bf16[256,128]{1,0:T(8,128)(2,1)S(1)} %fusion.5), channel_id=1, source_target_pairs={{0,4},{1,5},{2,6},{3,7},{4,8},{5,9},{6,10},{7,11},{8,12},{9,13},{1... | collective-permute-start | bytes 196616 | tf_op jit(solution)/shard_map/ppermute | solution.py:50
  33.4 2.3 %collective-permute-done.9 = bf16[256,128]{1,0:T(8,128)(2,1)S(1)} collective-permute-done((bf16[256,128]{1,0:T(8,128)(2,1)S(1)}, bf16[256,128]{1,0:T(8,128)(2,1)S(1)}, u32[]{:S(2)}, u32[]{:S(2)}) %collective-permute-start.9) | collective-permute-done | bytes 65568 | tf_op jit(solution)/shard_map/ppermute | solution.py:50
  36.7 2.0 %collective-permute-done.7 = bf16[256,128]{1,0:T(8,128)(2,1)S(1)} collective-permute-done((bf16[256,128]{1,0:T(8,128)(2,1)S(1)}, bf16[256,128]{1,0:T(8,128)(2,1)S(1)}, u32[]{:S(2)}, u32[]{:S(2)}) %collective-permute-start.7) | collective-permute-done | bytes 65568 | tf_op jit(solution)/shard_map/ppermute | solution.py:50
  40.7 4.5 %collective-permute-done.11.rest_1_ = bf16[4,256,128]{2,1,0:T(8,128)(2,1)S(1)} collective-permute-done((bf16[4,256,128]{2,1,0:T(8,128)(2,1)S(1)}, bf16[4,256,128]{2,1,0:T(8,128)(2,1)S(1)}, u32[]{:S(2)}, u32[]{:S(2)}) %collective-permute-start.11) | collective-permute-done | bytes 262176 | tf_op jit(solution)/shard_map/ppermute | solution.py:50
  45.3 4.2 %collective-permute-done.14.rest_6_ = bf16[2,128,512]{2,1,0:T(8,128)(2,1)S(1)} collective-permute-done((bf16[2,128,512]{2,1,0:T(8,128)(2,1)S(1)}, bf16[2,128,512]{2,1,0:T(8,128)(2,1)S(1)}, u32[]{:S(2)}, u32[]{:S(2)}) %collective-permute-start.14) | collective-permute-done | bytes 262176 | tf_op jit(solution)/shard_map/ppermute | solution.py:50
  51.0 17.3 %shard_map.104 = (bf16[128,4096]{1,0:T(8,128)(2,1)}, f32[2,128,512]{2,1,0:T(8,128)}, f32[2,128,512]{2,1,0:T(8,128)}, f32[2,128,512]{2,1,0:T(8,128)}, bf16[2,128,...) custom-call(s32[1]{0:T(128)S(6)} %copy.11.slab_index, ...), custom_call_target="tpu_custom_call" | custom-call | tf_op jit(solution)/shard_map/pallas_call | solution.py:363
  72.7 9.7 %collective-permute-done.20 = bf16[4,256,128]{2,1,0:T(8,128)(2,1)S(1)} collective-permute-done((bf16[4,256,128]{2,1,0:T(8,128)(2,1)S(1)}, bf16[4,256,128]{2,1,0:T(8,128)(2,1)S(1)}, u32[]{:S(2)}, u32[]{:S(2)}) %collective-permute-start.20) | collective-permute-done | bytes 262176 | tf_op jit(solution)/shard_map/ppermute | solution.py:50
  83.7 3.8 %collective-permute-start.26 = (bf16[256,128]{1,0:T(8,128)(2,1)S(1)}, bf16[256,128]{1,0:T(8,128)(2,1)S(1)}, u32[]{:S(2)}, u32[]{:S(2)}) collective-permute-start(bf16[256,128]{1,0:T(8,128)(2,1)S(1)} %get-tuple-element.58), channel_id=1, source_target_pairs={{0,12},{1,13},{2,14},{3,15},{4,0},{5,1},{6,2},{7,3},{8,4},{9,5},{1... | collective-permute-start | bytes 196616 | tf_op jit(solution)/shard_map/ppermute | solution.py:50
  87.7 2.6 %collective-permute-done.24 = bf16[256,128]{1,0:T(8,128)(2,1)S(1)} collective-permute-done((bf16[256,128]{1,0:T(8,128)(2,1)S(1)}, bf16[256,128]{1,0:T(8,128)(2,1)S(1)}, u32[]{:S(2)}, u32[]{:S(2)}) %collective-permute-start.24) | collective-permute-done | bytes 65568 | tf_op jit(solution)/shard_map/ppermute | solution.py:50
  90.3 2.8 %collective-permute-done.25 = bf16[256,128]{1,0:T(8,128)(2,1)S(1)} collective-permute-done((bf16[256,128]{1,0:T(8,128)(2,1)S(1)}, bf16[256,128]{1,0:T(8,128)(2,1)S(1)}, u32[]{:S(2)}, u32[]{:S(2)}) %collective-permute-start.25) | collective-permute-done | bytes 65568 | tf_op jit(solution)/shard_map/ppermute | solution.py:50
  93.1 1.5 %collective-permute-start.29 = (bf16[256,128]{1,0:T(8,128)(2,1)S(1)}, bf16[256,128]{1,0:T(8,128)(2,1)S(1)}, u32[]{:S(2)}, u32[]{:S(2)}) collective-permute-start(bf16[256,128]{1,0:T(8,128)(2,1)S(1)} %fusion.2), channel_id=1, source_target_pairs={{0,12},{1,13},{2,14},{3,15},{4,0},{5,1},{6,2},{7,3},{8,4},{9,5},{1... | collective-permute-start | bytes 196616 | tf_op jit(solution)/shard_map/ppermute | solution.py:50
  95.6 2.2 %collective-permute-done.29 = bf16[256,128]{1,0:T(8,128)(2,1)S(1)} collective-permute-done((bf16[256,128]{1,0:T(8,128)(2,1)S(1)}, bf16[256,128]{1,0:T(8,128)(2,1)S(1)}, u32[]{:S(2)}, u32[]{:S(2)}) %collective-permute-start.29) | collective-permute-done | bytes 65568 | tf_op jit(solution)/shard_map/ppermute | solution.py:50
  97.8 3.3 %collective-permute-done.28 = bf16[256,128]{1,0:T(8,128)(2,1)S(1)} collective-permute-done((bf16[256,128]{1,0:T(8,128)(2,1)S(1)}, bf16[256,128]{1,0:T(8,128)(2,1)S(1)}, u32[]{:S(2)}, u32[]{:S(2)}) %collective-permute-start.28) | collective-permute-done | bytes 65568 | tf_op jit(solution)/shard_map/ppermute | solution.py:50
  102.9 4.7 %collective-permute-done.31.rest_4_ = bf16[4,256,128]{2,1,0:T(8,128)(2,1)S(1)} collective-permute-done((bf16[4,256,128]{2,1,0:T(8,128)(2,1)S(1)}, bf16[4,256,128]{2,1,0:T(8,128)(2,1)S(1)}, u32[]{:S(2)}, u32[]{:S(2)}) %collective-permute-start.31) | collective-permute-done | bytes 262176 | tf_op jit(solution)/shard_map/ppermute | solution.py:50
  107.7 2.8 %collective-permute-done.30.rest_1_ = bf16[2,128,512]{2,1,0:T(8,128)(2,1)S(1)} collective-permute-done((bf16[2,128,512]{2,1,0:T(8,128)(2,1)S(1)}, bf16[2,128,512]{2,1,0:T(8,128)(2,1)S(1)}, u32[]{:S(2)}, u32[]{:S(2)}) %collective-permute-start.30) | collective-permute-done | bytes 262176 | tf_op jit(solution)/shard_map/ppermute | solution.py:50
  111.4 5.2 %shard_map.105 = (bf16[16,128,512]{2,1,0:T(8,128)(2,1)}, bf16[16,128,512]{2,1,0:T(8,128)(2,1)}) custom-call(s32[1]{0:T(128)S(6)} %copy.11.slab_index, s32[4,8]{1,0:T(4,128)} %verts.5, f32[2,128,512]{2,1,0:T(8,128)} %get-tuple-element.41.home, bf16[2,128,512]{2,1,0:T(8,128)(2,1)} %copy-done, bf16[2,128,512]{2,1,0:T(8,128)(2,1)} %copy-done.16, ...), custom_call_target="tpu_custom_call" | custom-call | tf_op jit(solution)/shard_map/pallas_call | solution.py:464
  (102 shorter events, 19.0 us)
Async XLA Ops:
  6.0 6.9 %collective-permute-start = (bf16[4,256,128]{2,1,0:T(8,128)(2,1)}, bf16[4,256,128]{2,1,0:T(8,128)(2,1)S(1)}, u32[]{:S(2)}, u32[]{:S(2)}) collective-permute-start(bf16[4,256,128]{2,1,0:T(8,128)(2,1)} %get-tuple-element.31), channel_id=1, source_target_pairs={{0,1},{1,0},{2,3},{3,2},{4,5},{5,4},{6,7},{7,6},{8,9},{9,8},{10,11... | collective-permute-start | bytes 786440 | tf_op jit(solution)/shard_map/ppermute | solution.py:50
  8.4 9.5 %collective-permute-start.2 = (bf16[4,256,128]{2,1,0:T(8,128)(2,1)S(1)}, bf16[4,256,128]{2,1,0:T(8,128)(2,1)S(1)}, u32[]{:S(2)}, u32[]{:S(2)}) collective-permute-start(bf16[4,256,128]{2,1,0:T(8,128)(2,1)S(1)} %add_convert_fusion.3), channel_id=1, source_target_pairs={{0,2},{1,3},{2,0},{3,1},{4,6},{5,7},{6,4},{7,5},{8,10},{9,11},{10,... | collective-permute-start | bytes 786440 | tf_op jit(solution)/shard_map/ppermute | solution.py:50
  11.3 10.1 %collective-permute-start.3 = (bf16[2,128,512]{2,1,0:T(8,128)(2,1)}, bf16[2,128,512]{2,1,0:T(8,128)(2,1)S(1)}, u32[]{:S(2)}, u32[]{:S(2)}) collective-permute-start(bf16[2,128,512]{2,1,0:T(8,128)(2,1)} %get-tuple-element.34), channel_id=1, source_target_pairs={{0,4},{1,5},{2,6},{3,7},{4,8},{5,9},{6,10},{7,11},{8,12},{9,13},{1... | collective-permute-start | bytes 786440 | tf_op jit(solution)/shard_map/ppermute | solution.py:50
  21.5 6.4 %collective-permute-start.4 = (bf16[256,128]{1,0:T(8,128)(2,1)S(1)}, bf16[256,128]{1,0:T(8,128)(2,1)S(1)}, u32[]{:S(2)}, u32[]{:S(2)}) collective-permute-start(bf16[256,128]{1,0:T(8,128)(2,1)S(1)} %get-tuple-element.60), channel_id=1, source_target_pairs={{0,4},{1,5},{2,6},{3,7},{4,8},{5,9},{6,10},{7,11},{8,12},{9,13},{1... | collective-permute-start | bytes 196616 | tf_op jit(solution)/shard_map/ppermute | solution.py:50
  21.6 6.3 %collective-permute-start.6 = (bf16[256,128]{1,0:T(8,128)(2,1)S(1)}, bf16[256,128]{1,0:T(8,128)(2,1)S(1)}, u32[]{:S(2)}, u32[]{:S(2)}) collective-permute-start(bf16[256,128]{1,0:T(8,128)(2,1)S(1)} %get-tuple-element.61), channel_id=1, source_target_pairs={{0,12},{1,13},{2,14},{3,15},{4,0},{5,1},{6,2},{7,3},{8,4},{9,5},{1... | collective-permute-start | bytes 196616 | tf_op jit(solution)/shard_map/ppermute | solution.py:50
  25.4 5.9 %collective-permute-start.5 = (bf16[256,128]{1,0:T(8,128)(2,1)S(1)}, bf16[256,128]{1,0:T(8,128)(2,1)S(1)}, u32[]{:S(2)}, u32[]{:S(2)}) collective-permute-start(bf16[256,128]{1,0:T(8,128)(2,1)S(1)} %get-tuple-element.62), channel_id=1, source_target_pairs={{0,8},{1,9},{2,10},{3,11},{4,12},{5,13},{6,14},{7,15},{8,0},{9,1},... | collective-permute-start | bytes 196616 | tf_op jit(solution)/shard_map/ppermute | solution.py:50
  25.5 13.3 %collective-permute-start.10 = (bf16[2,128,512]{2,1,0:T(8,128)(2,1)S(1)}, bf16[2,128,512]{2,1,0:T(8,128)(2,1)S(1)}, u32[]{:S(2)}, u32[]{:S(2)}) collective-permute-start(bf16[2,128,512]{2,1,0:T(8,128)(2,1)S(1)} %broadcast_select_fusion), channel_id=1, source_target_pairs={{0,2},{1,3},{2,0},{3,1},{4,6},{5,7},{6,4},{7,5},{8,10},{9,11},{10,... | collective-permute-start | bytes 786440 | tf_op jit(solution)/shard_map/ppermute | solution.py:50
  31.6 7.1 %collective-permute-start.7 = (bf16[256,128]{1,0:T(8,128)(2,1)S(1)}, bf16[256,128]{1,0:T(8,128)(2,1)S(1)}, u32[]{:S(2)}, u32[]{:S(2)}) collective-permute-start(bf16[256,128]{1,0:T(8,128)(2,1)S(1)} %fusion.5), channel_id=1, source_target_pairs={{0,4},{1,5},{2,6},{3,7},{4,8},{5,9},{6,10},{7,11},{8,12},{9,13},{1... | collective-permute-start | bytes 196616 | tf_op jit(solution)/shard_map/ppermute | solution.py:50
  38.8 6.5 %collective-permute-start.11 = (bf16[4,256,128]{2,1,0:T(8,128)(2,1)S(1)}, bf16[4,256,128]{2,1,0:T(8,128)(2,1)S(1)}, u32[]{:S(2)}, u32[]{:S(2)}) collective-permute-start(bf16[4,256,128]{2,1,0:T(8,128)(2,1)S(1)} %pad_maximum_fusion.rest_0_), channel_id=1, source_target_pairs={{0,2},{1,3},{2,0},{3,1},{4,6},{5,7},{6,4},{7,5},{8,10},{9,11},{10,... | collective-permute-start | bytes 786440 | tf_op jit(solution)/shard_map/ppermute | solution.py:50
  39.7 5.6 %collective-permute-start.15 = (bf16[2,128,512]{2,1,0:T(8,128)(2,1)S(1)}, bf16[2,128,512]{2,1,0:T(8,128)(2,1)S(1)}, u32[]{:S(2)}, u32[]{:S(2)}) collective-permute-start(bf16[2,128,512]{2,1,0:T(8,128)(2,1)S(1)} %collective-permute-done.10.rest_4_), channel_id=1, source_target_pairs={{0,1},{1,0},{2,3},{3,2},{4,5},{5,4},{6,7},{7,6},{8,9},{9,8},{10,11... | collective-permute-start | bytes 786440 | tf_op jit(solution)/shard_map/ppermute | solution.py:50
  40.2 9.3 %collective-permute-start.12 = (bf16[4,256,128]{2,1,0:T(8,128)(2,1)S(1)}, bf16[4,256,128]{2,1,0:T(8,128)(2,1)S(1)}, u32[]{:S(2)}, u32[]{:S(2)}) collective-permute-start(bf16[4,256,128]{2,1,0:T(8,128)(2,1)S(1)} %pad_maximum_fusion.rest_0_), channel_id=1, source_target_pairs={{0,1},{1,0},{2,3},{3,2},{4,5},{5,4},{6,7},{7,6},{8,9},{9,8},{10,11... | collective-permute-start | bytes 786440 | tf_op jit(solution)/shard_map/ppermute | solution.py:50
  40.2 9.3 %collective-permute-start.14 = (bf16[2,128,512]{2,1,0:T(8,128)(2,1)S(1)}, bf16[2,128,512]{2,1,0:T(8,128)(2,1)S(1)}, u32[]{:S(2)}, u32[]{:S(2)}) collective-permute-start(bf16[2,128,512]{2,1,0:T(8,128)(2,1)S(1)} %copy-done.19), channel_id=1, source_target_pairs={{0,1},{1,6},{2,3},{3,8},{4,5},{5,10},{6,7},{7,12},{8,9},{9,14},{10... | collective-permute-start | bytes 786440 | tf_op jit(solution)/shard_map/ppermute | solution.py:50
  71.2 11.2 %collective-permute-start.20 = (bf16[4,256,128]{2,1,0:T(8,128)(2,1)S(1)}, bf16[4,256,128]{2,1,0:T(8,128)(2,1)S(1)}, u32[]{:S(2)}, u32[]{:S(2)}) collective-permute-start(bf16[4,256,128]{2,1,0:T(8,128)(2,1)S(1)} %add_convert_fusion.1), channel_id=1, source_target_pairs={{0,2},{1,3},{2,0},{3,1},{4,6},{5,7},{6,4},{7,5},{8,10},{9,11},{10,... | collective-permute-start | bytes 786440 | tf_op jit(solution)/shard_map/ppermute | solution.py:50
  71.6 15.9 %collective-permute-start.17 = (bf16[2,128,512]{2,1,0:T(8,128)(2,1)}, bf16[2,128,512]{2,1,0:T(8,128)(2,1)S(1)}, u32[]{:S(2)}, u32[]{:S(2)}) collective-permute-start(bf16[2,128,512]{2,1,0:T(8,128)(2,1)} %get-tuple-element.43), channel_id=1, source_target_pairs={{0,1},{1,0},{2,3},{3,2},{4,5},{5,4},{6,7},{7,6},{8,9},{9,8},{10,11... | collective-permute-start | bytes 786440 | tf_op jit(solution)/shard_map/ppermute | solution.py:50
  71.6 29.9 %collective-permute-start.22 = (bf16[2,128,512]{2,1,0:T(8,128)(2,1)}, bf16[2,128,512]{2,1,0:T(8,128)(2,1)S(1)}, u32[]{:S(2)}, u32[]{:S(2)}) collective-permute-start(bf16[2,128,512]{2,1,0:T(8,128)(2,1)} %get-tuple-element.50), channel_id=1, source_target_pairs={{0,1},{1,0},{2,3},{3,2},{4,5},{5,4},{6,7},{7,6},{8,9},{9,8},{10,11... | collective-permute-start | bytes 786440 | tf_op jit(solution)/shard_map/ppermute | solution.py:50
  72.1 11.4 %collective-permute-start.23 = (bf16[2,128,512]{2,1,0:T(8,128)(2,1)}, bf16[2,128,512]{2,1,0:T(8,128)(2,1)S(1)}, u32[]{:S(2)}, u32[]{:S(2)}) collective-permute-start(bf16[2,128,512]{2,1,0:T(8,128)(2,1)} %get-tuple-element.51), channel_id=1, source_target_pairs={{1,0},{6,1},{3,2},{8,3},{5,4},{10,5},{7,6},{12,7},{9,8},{14,9},{11... | collective-permute-start | bytes 786440 | tf_op jit(solution)/shard_map/ppermute | solution.py:50
  83.7 6.6 %collective-permute-start.24 = (bf16[256,128]{1,0:T(8,128)(2,1)S(1)}, bf16[256,128]{1,0:T(8,128)(2,1)S(1)}, u32[]{:S(2)}, u32[]{:S(2)}) collective-permute-start(bf16[256,128]{1,0:T(8,128)(2,1)S(1)} %get-tuple-element.57), channel_id=1, source_target_pairs={{0,4},{1,5},{2,6},{3,7},{4,8},{5,9},{6,10},{7,11},{8,12},{9,13},{1... | collective-permute-start | bytes 196616 | tf_op jit(solution)/shard_map/ppermute | solution.py:50
  83.7 6.5 %collective-permute-start.26 = (bf16[256,128]{1,0:T(8,128)(2,1)S(1)}, bf16[256,128]{1,0:T(8,128)(2,1)S(1)}, u32[]{:S(2)}, u32[]{:S(2)}) collective-permute-start(bf16[256,128]{1,0:T(8,128)(2,1)S(1)} %get-tuple-element.58), channel_id=1, source_target_pairs={{0,12},{1,13},{2,14},{3,15},{4,0},{5,1},{6,2},{7,3},{8,4},{9,5},{1... | collective-permute-start | bytes 196616 | tf_op jit(solution)/shard_map/ppermute | solution.py:50
  87.6 13.6 %collective-permute-start.21 = (bf16[2,128,512]{2,1,0:T(8,128)(2,1)S(1)}, bf16[2,128,512]{2,1,0:T(8,128)(2,1)S(1)}, u32[]{:S(2)}, u32[]{:S(2)}) collective-permute-start(bf16[2,128,512]{2,1,0:T(8,128)(2,1)S(1)} %add_convert_fusion.2), channel_id=1, source_target_pairs={{0,2},{1,3},{2,0},{3,1},{4,6},{5,7},{6,4},{7,5},{8,10},{9,11},{10,... | collective-permute-start | bytes 786440 | tf_op jit(solution)/shard_map/ppermute | solution.py:50
  94.6 6.6 %collective-permute-start.28 = (bf16[256,128]{1,0:T(8,128)(2,1)S(1)}, bf16[256,128]{1,0:T(8,128)(2,1)S(1)}, u32[]{:S(2)}, u32[]{:S(2)}) collective-permute-start(bf16[256,128]{1,0:T(8,128)(2,1)S(1)} %fusion.2), channel_id=1, source_target_pairs={{0,8},{1,9},{2,10},{3,11},{4,12},{5,13},{6,14},{7,15},{8,0},{9,1},... | collective-permute-start | bytes 196616 | tf_op jit(solution)/shard_map/ppermute | solution.py:50
  94.6 6.6 %collective-permute-start.27 = (bf16[256,128]{1,0:T(8,128)(2,1)S(1)}, bf16[256,128]{1,0:T(8,128)(2,1)S(1)}, u32[]{:S(2)}, u32[]{:S(2)}) collective-permute-start(bf16[256,128]{1,0:T(8,128)(2,1)S(1)} %fusion.2), channel_id=1, source_target_pairs={{0,4},{1,5},{2,6},{3,7},{4,8},{5,9},{6,10},{7,11},{8,12},{9,13},{1... | collective-permute-start | bytes 196616 | tf_op jit(solution)/shard_map/ppermute | solution.py:50
  101.2 6.4 %collective-permute-start.31 = (bf16[4,256,128]{2,1,0:T(8,128)(2,1)S(1)}, bf16[4,256,128]{2,1,0:T(8,128)(2,1)S(1)}, u32[]{:S(2)}, u32[]{:S(2)}) collective-permute-start(bf16[4,256,128]{2,1,0:T(8,128)(2,1)S(1)} %pad_maximum_fusion.1.rest_3_), channel_id=1, source_target_pairs={{0,2},{1,3},{2,0},{3,1},{4,6},{5,7},{6,4},{7,5},{8,10},{9,11},{10,... | collective-permute-start | bytes 786440 | tf_op jit(solution)/shard_map/ppermute | solution.py:50
  101.6 8.9 %collective-permute-start.32 = (bf16[4,256,128]{2,1,0:T(8,128)(2,1)S(1)}, bf16[4,256,128]{2,1,0:T(8,128)(2,1)S(1)}, u32[]{:S(2)}, u32[]{:S(2)}) collective-permute-start(bf16[4,256,128]{2,1,0:T(8,128)(2,1)S(1)} %pad_maximum_fusion.1.rest_3_), channel_id=1, source_target_pairs={{0,1},{1,0},{2,3},{3,2},{4,5},{5,4},{6,7},{7,6},{8,9},{9,8},{10,11... | collective-permute-start | bytes 786440 | tf_op jit(solution)/shard_map/ppermute | solution.py:50
  101.7 8.8 %collective-permute-start.30 = (bf16[2,128,512]{2,1,0:T(8,128)(2,1)S(1)}, bf16[2,128,512]{2,1,0:T(8,128)(2,1)S(1)}, u32[]{:S(2)}, u32[]{:S(2)}) collective-permute-start(bf16[2,128,512]{2,1,0:T(8,128)(2,1)S(1)} %add_convert_fusion), channel_id=1, source_target_pairs={{4,0},{5,1},{6,2},{7,3},{8,4},{9,5},{10,6},{11,7},{12,8},{13,9},{1... | collective-permute-start | bytes 786440 | tf_op jit(solution)/shard_map/ppermute | solution.py:50
  (30 other events, 227.6 us)

commit v7 on v6

--- a/solution.py
+++ b/solution.py
@@ -10,7 +10,9 @@
 
 BLOCK = 64
 WDEV = 5
-VMEM_LIMIT = 60 * 1024 * 1024
+JOIN = 4
+FULL_VMEM = 60 * 1024 * 1024
+PART_VMEM = 32 * 1024 * 1024
 BF16 = jnp.bfloat16
 F32 = jnp.float32
 
@@ -81,23 +83,46 @@
     return [me + 4 >= devices, (lax.rem(me, 2) == 1) & (me + 5 >= devices)]
 
 
-def pack_kernel(slab_index, verts, keys, values, *rest, lines, heads, nv, per_device):
-    sends = rest[:3]
-    shares = rest[3:7]
-    picked, sems, pick_sems = rest[7:]
+def pack_window_kernel(slab_index, keys, values, *rest, lines):
+    key4, value4, mixed, own, sems = rest
     slab, me = slab_index[0], lax.axis_index("ctx")
+    copies = []
+    wrapped4, wrapped_mixed = wraps(me, lines.devices)
+    for n, (region, to) in enumerate(
+        (
+            (slab - wrapped4.astype(jnp.int32), (key4, value4)),
+            (slab - wrapped_mixed.astype(jnp.int32), (mixed.at[0], mixed.at[1])),
+            (slab, (own.at[0], own.at[1])),
+        )
+    ):
+        for kv, source in enumerate((keys, values)):
+            copy = pltpu.make_async_copy(source.at[region], to[kv], sems.at[n, kv])
+            copy.start()
+            copies.append(copy)
+    for copy in copies:
+        copy.wait()
+
+
+def pack_window(slab_index, keys, values, lines):
+    _, rows, features = keys.shape
+    hbm = pl.BlockSpec(memory_space=pl.ANY)
+    return pl.pallas_call(
+        functools.partial(pack_window_kernel, lines=lines),
+        in_specs=[pl.BlockSpec(memory_space=pltpu.SMEM), hbm, hbm],
+        out_specs=[pl.BlockSpec(memory_space=pltpu.VMEM)] * 4,
+        out_shape=[jax.ShapeDtypeStruct((rows, features), BF16)] * 2
+        + [jax.ShapeDtypeStruct((2, rows, features), BF16)] * 2,
+        scratch_shapes=[pltpu.SemaphoreType.DMA((3, 2))],
+        compiler_params=pltpu.CompilerParams(vmem_limit_bytes=FULL_VMEM),
+    )(slab_index, keys, values)
+
+
+def pack_verticals_kernel(verts, keys, values, _, *rest, lines, heads, nv, per_device):
+    shares = rest[:4]
+    picked, pick_sems = rest[4:]
+    me = lax.axis_index("ctx")
     far, near, core = lines.place(me)
     _, chunk, head_dim = shares[0].shape
-    copies = []
-    wrapped4, wrapped_mixed = wraps(me, lines.devices)
-    for n, region in enumerate(
-        (slab, slab - wrapped4.astype(jnp.int32), slab - wrapped_mixed.astype(jnp.int32))
-    ):
-        for kv, source in enumerate((keys, values)):
-            copy = pltpu.make_async_copy(source.at[region], sends[n].at[kv], sems.at[n, kv])
-            copy.start()
-            copies.append(copy)
-    picked[...] = jnp.zeros_like(picked)
     slab_blocks = per_device * lines.devices
     piece = min(BLOCK, chunk)
 
@@ -125,6 +150,7 @@
     def owned(h, m):
         return lax.div(lax.rem(verts[h, m], slab_blocks), per_device) == me
 
+    picked[...] = jnp.zeros_like(picked)
     for h in range(heads):
         for m in range(nv):
 
@@ -143,31 +169,28 @@
 
     for n, share in enumerate(shares):
         share[...] = picked[n // 2, n % 2]
-    for copy in copies:
-        copy.wait()
-
-
-def pack(slab_index, verticals, keys, values, lines):
-    regions, rows, features = keys.shape
+
+
+def pack_verticals(verticals, keys, values, ahead, lines):
     heads, nv = verticals.shape
+    rows, features = keys.shape[1:]
     head_dim = features // heads
     chunk = heads * nv * BLOCK // (2 * lines.far)
-    smem = pl.BlockSpec(memory_space=pltpu.SMEM)
     hbm = pl.BlockSpec(memory_space=pl.ANY)
     share = (lines.far, chunk, head_dim)
     return pl.pallas_call(
-        functools.partial(pack_kernel, lines=lines, heads=heads, nv=nv, per_device=rows // BLOCK),
-        in_specs=[smem, smem, hbm, hbm],
-        out_specs=[pl.BlockSpec(memory_space=pltpu.VMEM)] * 7,
-        out_shape=[jax.ShapeDtypeStruct((2, rows, features), BF16)] * 3
-        + [jax.ShapeDtypeStruct(share, BF16)] * 4,
+        functools.partial(
+            pack_verticals_kernel, lines=lines, heads=heads, nv=nv, per_device=rows // BLOCK
+        ),
+        in_specs=[pl.BlockSpec(memory_space=pltpu.SMEM), hbm, hbm, hbm],
+        out_specs=[pl.BlockSpec(memory_space=pltpu.VMEM)] * 4,
+        out_shape=[jax.ShapeDtypeStruct(share, BF16)] * 4,
         scratch_shapes=[
             pltpu.VMEM((2, 2) + share, BF16),
-            pltpu.SemaphoreType.DMA((3, 2)),
             pltpu.SemaphoreType.DMA((2, heads * nv * max(1, BLOCK // chunk))),
         ],
-        compiler_params=pltpu.CompilerParams(vmem_limit_bytes=VMEM_LIMIT),
-    )(slab_index, verticals, keys, values)
+        compiler_params=pltpu.CompilerParams(vmem_limit_bytes=FULL_VMEM),
+    )(verticals, keys, values, ahead)
 
 
 def distances(core):
@@ -196,7 +219,7 @@
 ):
     gathered, recv, rest = rest[:4], rest[4 : 4 + WDEV], rest[4 + WDEV :]
     dq, home, near_parts, shares = rest[0], rest[1], rest[2 : 2 + WDEV], rest[7:11]
-    (win, vkv, kc, vc, qs, gs, s_ref, dp_ref, w_ref, ds_ref, nacc, sems) = rest[11:]
+    (win, vkv, kc, vc, qs, gs, split, s_ref, w_ref, ds_ref, nacc, sems) = rest[11:]
     h = pl.program_id(0)
     slab, me = slab_index[0], lax.axis_index("ctx")
     far, near, core = lines.place(me)
@@ -267,24 +290,34 @@
                 to[j, (1 + nv + s) * BLOCK : (2 + nv + s) * BLOCK, :] = win[
                     kv, pl.ds(slash_at[s], BLOCK), lanes
                 ]
-        products = []
         block_rows = slice(j * BLOCK, (j + 1) * BLOCK)
         for g in range(group):
             cols = slice(g * head_dim, (g + 1) * head_dim)
-            qs[j, g * BLOCK : (g + 1) * BLOCK, :] = q[block_rows, cols]
-            gs[j, g * BLOCK : (g + 1) * BLOCK, :] = grad[block_rows, cols]
-            products.append(grad[block_rows, cols].astype(F32) * out[block_rows, cols].astype(F32))
-        delta = jnp.sum(jnp.transpose(jnp.concatenate(products, axis=0)), axis=0, keepdims=True)
-
-        s_ref[j] = lax.dot_general(kc[j], qs[j], nt, preferred_element_type=F32)
-        dp_ref[j] = lax.dot_general(vc[j], gs[j], nt, preferred_element_type=F32)
-
-        own = jnp.where(key_at <= row_at, s_ref[j, 0:BLOCK, :], neg)
-        s_ref[j, 0:BLOCK, :] = own
-        top = fold(own, jnp.maximum)
-        for c in range(1, cand):
-            best = fold(s_ref[j, c * BLOCK : (c + 1) * BLOCK, :], jnp.maximum)
-            top = jnp.maximum(top, best + jnp.where(valid[c], jnp.float32(0), neg))
+            here = slice(g * BLOCK, (g + 1) * BLOCK)
+            qs[j, here, :] = q[block_rows, cols]
+            gs[j, here, :] = grad[block_rows, cols]
+            product = grad[block_rows, cols].astype(F32) * out[block_rows, cols].astype(F32)
+            upper = product.astype(BF16)
+            split[j, here, 0:head_dim] = upper
+            split[j, here, head_dim:] = (product - upper.astype(F32)).astype(BF16)
+        ones = jnp.ones((8, 2 * head_dim), BF16)
+        delta = lax.dot_general(ones, split[j], nt, preferred_element_type=F32)[0:1, :]
+
+        top = None
+        for n in range(cand // JOIN):
+            rows_n = slice(n * JOIN * BLOCK, (n + 1) * JOIN * BLOCK)
+            s = lax.dot_general(kc[j, rows_n, :], qs[j], nt, preferred_element_type=F32)
+            for i in range(JOIN):
+                c = n * JOIN + i
+                part = s[i * BLOCK : (i + 1) * BLOCK, :]
+                if c == 0:
+                    part = jnp.where(key_at <= row_at, part, neg)
+                s_ref[j, c * BLOCK : (c + 1) * BLOCK, :] = part
+                best = fold(part, jnp.maximum)
+                if c == 0:
+                    top = best
+                else:
+                    top = jnp.maximum(top, best + jnp.where(valid[c], jnp.float32(0), neg))
         top = jnp.max(top, axis=0, keepdims=True) * log2_scale
         total = jnp.zeros((8, width), F32)
         for c in range(cand):
@@ -294,11 +327,12 @@
             s_ref[j, span, :] = p
             total = total + fold(p, jnp.add)
         inverse = 1.0 / jnp.sum(total, axis=0, keepdims=True)
-        for c in range(cand):
-            span = slice(c * BLOCK, (c + 1) * BLOCK)
+        for n in range(cand // JOIN):
+            span = slice(n * JOIN * BLOCK, (n + 1) * JOIN * BLOCK)
+            dp = lax.dot_general(vc[j, span, :], gs[j], nt, preferred_element_type=F32)
             w = s_ref[j, span, :] * inverse
             w_ref[j, span, :] = w.astype(BF16)
-            ds_ref[j, span, :] = (w * (dp_ref[j, span, :] - delta)).astype(BF16)
+            ds_ref[j, span, :] = (w * (dp - delta)).astype(BF16)
 
         dv = jnp.dot(w_ref[j], gs[j], preferred_element_type=F32)
         dk = jnp.dot(ds_ref[j], qs[j], preferred_element_type=F32) * scaling
@@ -387,14 +421,14 @@
             pltpu.VMEM((per_device, cand * BLOCK, head_dim), BF16),
             pltpu.VMEM((per_device, group * BLOCK, head_dim), BF16),
             pltpu.VMEM((per_device, group * BLOCK, head_dim), BF16),
-            pltpu.VMEM((per_device, cand * BLOCK, group * BLOCK), F32),
+            pltpu.VMEM((per_device, group * BLOCK, 2 * head_dim), BF16),
             pltpu.VMEM((per_device, cand * BLOCK, group * BLOCK), F32),
             pltpu.VMEM((per_device, cand * BLOCK, group * BLOCK), BF16),
             pltpu.VMEM((per_device, cand * BLOCK, group * BLOCK), BF16),
             pltpu.VMEM((2, (WDEV + 1) * rows, features), F32),
             pltpu.SemaphoreType.DMA((WDEV + 2 + 4 * lines.far,)),
         ],
-        compiler_params=pltpu.CompilerParams(vmem_limit_bytes=VMEM_LIMIT),
+        compiler_params=pltpu.CompilerParams(vmem_limit_bytes=PART_VMEM),
     )(
         slab_index, verticals, offsets, queries, cotangent, output, keys, values, *gathered, *recv,
     )
@@ -473,7 +507,7 @@
             pltpu.VMEM((2, 2, rows, features), F32),
             pltpu.SemaphoreType.DMA((4 * lines.far,)),
         ],
-        compiler_params=pltpu.CompilerParams(vmem_limit_bytes=VMEM_LIMIT),
+        compiler_params=pltpu.CompilerParams(vmem_limit_bytes=PART_VMEM),
     )(slab_index, verticals, home, from_near, *arrived, *gathered)
 
 
@@ -491,14 +525,18 @@
     regions = context_keys.shape[0]
     _, near, _ = lines.place(lax.axis_index("ctx"))
 
-    own, send4, mixed, mine, to_near, to_core, to_both = pack(
-        slab_index, verticals, context_keys, context_values, lines
+    key4, value4, mixed, own = pack_window(slab_index, context_keys, context_values, lines)
+    key4 = move(key4, lines.shift_pairs(4))
+    value4 = move(value4, lines.shift_pairs(4))
+    recv4 = jnp.stack([key4, value4])
+    recv_mixed = move(mixed, lines.mixed_pairs())
+    mine, to_near, to_core, to_both = pack_verticals(
+        verticals, context_keys, context_values, own, lines
     )
-    recv4 = move(send4, lines.shift_pairs(4))
+    to_both, to_core = after(to_both, key4), after(to_core, key4)
     quarter = plane_sum(lines, mine, to_near, to_core, to_both)
     recv2 = move(jnp.where(near == 1, recv4, own), lines.near_pairs())
-    gathered = after(far_sum(lines, after(quarter, recv4)), recv2)
-    recv_mixed = move(after(mixed, gathered), lines.mixed_pairs())
+    gathered = after(far_sum(lines, after(quarter, recv4, recv_mixed)), recv2)
     gathered = plane_gather(lines, gathered)
     other2 = move(recv2, lines.core_pairs())
     other4 = move(recv4, lines.core_pairs())

time: 117 us -> 118 us (level)
  starting transfers between devices: 23.7 us -> 33.2 us
  waiting for transfers between devices: 57.4 us -> 50.4 us
  local copies, waits for them, and re-layouts: 2.38 us -> 0.06 us
  Pallas kernels: 26.7 us -> 28 us
    ppermute x34 -> x35, starting transfers between devices: 23.7 us -> 33.2 us  [move(): return lax.ppermute(array, 'ctx', pairs)]
    ppermute x34 -> x35, waiting for transfers between devices: 57.4 us -> 50.4 us  [move(): return lax.ppermute(array, 'ctx', pairs)]
    unnamed x40 -> x14, local copies, waits for them, and re-layouts: 2.35 us -> 0.03 us
    pallas_call x1 -> x2, Pallas kernels: 4.18 us -> 5.68 us  [the longest x1 3.54 us: pack_verticals(): pl.pallas_call(functools.partial(pack_verticals_kernel, lines=lines, head...]
  transfers between devices with their start and end apart: 34 -> 35, of which waited for: 18 -> 19; matrix products, arithmetic and copies ran while one was open for 4% -> 4% of each run, Pallas kernels for 0% -> 3%
where the time goes in v7:
time: 118 us
  waiting for transfers between devices  50.4 us (43%)
  starting transfers between devices  33.2 us (28%)
  Pallas kernels  28 us (24%)
  other arithmetic  4.77 us (4%)
  between operations  1.5 us (1%)
    ppermute x35, waiting for transfers between devices, move(): return lax.ppermute(array, 'ctx', pairs)  50.4 us
    ppermute x35, starting transfers between devices, move(): return lax.ppermute(array, 'ctx', pairs)  33.2 us
    pallas_call x1, Pallas kernels, attend(): pl.pallas_call(functools.partial(attend_kernel, lines=lines, heads=heads,...  17.2 us
    pallas_call x1, Pallas kernels, assemble(): pl.pallas_call(functools.partial(assemble_kernel, lines=lines, heads=head...  5.17 us
    pallas_call x1, Pallas kernels, pack_verticals(): pl.pallas_call(functools.partial(pack_verticals_kernel, lines=lines, head...  3.54 us
  transfers between devices with their start and end apart: 35, of which 19 were waited for; matrix products, arithmetic and copies ran while one was open for 4% of the time, Pallas kernels for 3%

profile of v7, /device:TPU:0, one launch (start us, length us, event | category | flops | bytes accessed | tf_op | source)
XLA Modules:
  0.0 117.9 jit_solution(1262875685290856096)
XLA Ops:
  1.3 2.1 %shard_map.103 = (bf16[128,512]{1,0:T(8,128)(2,1)}, bf16[128,512]{1,0:T(8,128)(2,1)}, bf16[2,128,512]{2,1,0:T(8,128)(2,1)}, bf16[2,128,512]{2,1,0:T(8,128)(2,1)}) custom-call(s32[1]{0:T(128)S(6)} %copy.11.slab_index, bf16[16,128,512]{2,1,0:T(8,128)(2,1)} %keys.5, bf16[16,128,512]{2,1,0:T(8,128)(2,1)} %values.5), custom_call_target="tpu_custom_call" | custom-call | tf_op jit(solution)/shard_map/pallas_call | solution.py:109
  3.4 3.1 %collective-permute-start = (bf16[128,512]{1,0:T(8,128)(2,1)}, bf16[128,512]{1,0:T(8,128)(2,1)S(1)}, u32[]{:S(2)}, u32[]{:S(2)}) collective-permute-start(bf16[128,512]{1,0:T(8,128)(2,1)} %get-tuple-element.35), channel_id=1, source_target_pairs={{0,4},{1,5},{2,6},{3,7},{4,8},{5,9},{6,10},{7,11},{8,12},{9,13},{1... | collective-permute-start | bytes 393224 | tf_op jit(solution)/shard_map/ppermute | solution.py:52
  6.5 3.5 %shard_map.104 = (bf16[4,256,128]{2,1,0:T(8,128)(2,1)}, bf16[4,256,128]{2,1,0:T(8,128)(2,1)}, bf16[4,256,128]{2,1,0:T(8,128)(2,1)}, bf16[4,256,128]{2,1,0:T(8,128)(2,1)}) custom-call(s32[4,8]{1,0:T(4,128)} %verts.5, bf16[16,128,512]{2,1,0:T(8,128)(2,1)} %keys.5, bf16[16,128,512]{2,1,0:T(8,128)(2,1)} %values.5, bf16[2,128,512]{2,1,0:T(8,128)(2,1)} %get-tuple-element.32._), custom_call_target="tpu_custom_call" | custom-call | tf_op jit(solution)/shard_map/pallas_call | solution.py:181
  10.1 2.2 %collective-permute-done = bf16[128,512]{1,0:T(8,128)(2,1)S(1)} collective-permute-done((bf16[128,512]{1,0:T(8,128)(2,1)}, bf16[128,512]{1,0:T(8,128)(2,1)S(1)}, u32[]{:S(2)}, u32[]{:S(2)}) %collective-permute-start) | collective-permute-done | bytes 131104 | tf_op jit(solution)/shard_map/ppermute | solution.py:52
  17.3 3.0 %collective-permute-done.4 = bf16[128,512]{1,0:T(8,128)(2,1)} collective-permute-done((bf16[128,512]{1,0:T(8,128)(2,1)}, bf16[128,512]{1,0:T(8,128)(2,1)}, u32[]{:S(2)}, u32[]{:S(2)}) %collective-permute-start.4) | collective-permute-done | bytes 131104 | tf_op jit(solution)/shard_map/ppermute | solution.py:52
  21.5 4.8 %collective-permute-done.3 = bf16[4,256,128]{2,1,0:T(8,128)(2,1)} collective-permute-done((bf16[4,256,128]{2,1,0:T(8,128)(2,1)}, bf16[4,256,128]{2,1,0:T(8,128)(2,1)}, u32[]{:S(2)}, u32[]{:S(2)}) %collective-permute-start.3) | collective-permute-done | bytes 262176 | tf_op jit(solution)/shard_map/ppermute | solution.py:52
  28.5 2.9 %collective-permute-start.8 = (bf16[256,128]{1,0:T(8,128)(2,1)S(1)}, bf16[256,128]{1,0:T(8,128)(2,1)S(1)}, u32[]{:S(2)}, u32[]{:S(2)}) collective-permute-start(bf16[256,128]{1,0:T(8,128)(2,1)S(1)} %get-tuple-element.67), channel_id=1, source_target_pairs={{0,12},{1,13},{2,14},{3,15},{4,0},{5,1},{6,2},{7,3},{8,4},{9,5},{1... | collective-permute-start | bytes 196616 | tf_op jit(solution)/shard_map/ppermute | solution.py:52
  31.6 2.4 %collective-permute-start.12 = (bf16[2,128,512]{2,1,0:T(8,128)(2,1)S(1)}, bf16[2,128,512]{2,1,0:T(8,128)(2,1)S(1)}, u32[]{:S(2)}, u32[]{:S(2)}) collective-permute-start(bf16[2,128,512]{2,1,0:T(8,128)(2,1)S(1)} %get-tuple-element.64), channel_id=1, source_target_pairs={{0,2},{1,3},{2,0},{3,1},{4,6},{5,7},{6,4},{7,5},{8,10},{9,11},{10,... | collective-permute-start | bytes 786440 | tf_op jit(solution)/shard_map/ppermute | solution.py:52
  34.2 2.7 %collective-permute-done.7 = bf16[256,128]{1,0:T(8,128)(2,1)S(1)} collective-permute-done((bf16[256,128]{1,0:T(8,128)(2,1)S(1)}, bf16[256,128]{1,0:T(8,128)(2,1)S(1)}, u32[]{:S(2)}, u32[]{:S(2)}) %collective-permute-start.7) | collective-permute-done | bytes 65568 | tf_op jit(solution)/shard_map/ppermute | solution.py:52
  37.0 2.0 %collective-permute-start.11 = (bf16[256,128]{1,0:T(8,128)(2,1)S(1)}, bf16[256,128]{1,0:T(8,128)(2,1)S(1)}, u32[]{:S(2)}, u32[]{:S(2)}) collective-permute-start(bf16[256,128]{1,0:T(8,128)(2,1)S(1)} %fusion.5), channel_id=1, source_target_pairs={{0,12},{1,13},{2,14},{3,15},{4,0},{5,1},{6,2},{7,3},{8,4},{9,5},{1... | collective-permute-start | bytes 196616 | tf_op jit(solution)/shard_map/ppermute | solution.py:52
  41.5 4.0 %collective-permute-done.10 = bf16[256,128]{1,0:T(8,128)(2,1)S(1)} collective-permute-done((bf16[256,128]{1,0:T(8,128)(2,1)S(1)}, bf16[256,128]{1,0:T(8,128)(2,1)S(1)}, u32[]{:S(2)}, u32[]{:S(2)}) %collective-permute-start.10) | collective-permute-done | bytes 65568 | tf_op jit(solution)/shard_map/ppermute | solution.py:52
  45.6 2.0 %collective-permute-start.13 = (bf16[4,256,128]{2,1,0:T(8,128)(2,1)S(1)}, bf16[4,256,128]{2,1,0:T(8,128)(2,1)S(1)}, u32[]{:S(2)}, u32[]{:S(2)}) collective-permute-start(bf16[4,256,128]{2,1,0:T(8,128)(2,1)S(1)} %pad_maximum_fusion.1.rest_0_), channel_id=1, source_target_pairs={{0,2},{1,3},{2,0},{3,1},{4,6},{5,7},{6,4},{7,5},{8,10},{9,11},{10,... | collective-permute-start | bytes 786440 | tf_op jit(solution)/shard_map/ppermute | solution.py:52
  48.1 4.0 %collective-permute-done.13.rest_1_ = bf16[4,256,128]{2,1,0:T(8,128)(2,1)S(1)} collective-permute-done((bf16[4,256,128]{2,1,0:T(8,128)(2,1)S(1)}, bf16[4,256,128]{2,1,0:T(8,128)(2,1)S(1)}, u32[]{:S(2)}, u32[]{:S(2)}) %collective-permute-start.13) | collective-permute-done | bytes 262176 | tf_op jit(solution)/shard_map/ppermute | solution.py:52
  53.7 17.2 %shard_map.105 = (bf16[128,4096]{1,0:T(8,128)(2,1)}, f32[2,128,512]{2,1,0:T(8,128)S(1)}, f32[2,128,512]{2,1,0:T(8,128)S(1)}, f32[2,128,512]{2,1,0:T(8,128)S(1)},...) custom-call(s32[1]{0:T(128)S(6)} %copy.11.slab_index, ...), custom_call_target="tpu_custom_call" | custom-call | tf_op jit(solution)/shard_map/pallas_call | solution.py:397
  72.6 1.9 %collective-permute-start.21 = (bf16[4,256,128]{2,1,0:T(8,128)(2,1)S(1)}, bf16[4,256,128]{2,1,0:T(8,128)(2,1)S(1)}, u32[]{:S(2)}, u32[]{:S(2)}) collective-permute-start(bf16[4,256,128]{2,1,0:T(8,128)(2,1)S(1)} %add_convert_fusion.1), channel_id=1, source_target_pairs={{0,2},{1,3},{2,0},{3,1},{4,6},{5,7},{6,4},{7,5},{8,10},{9,11},{10,... | collective-permute-start | bytes 786440 | tf_op jit(solution)/shard_map/ppermute | solution.py:52
  75.0 1.9 %collective-permute-start.24 = (bf16[2,128,512]{2,1,0:T(8,128)(2,1)S(1)}, bf16[2,128,512]{2,1,0:T(8,128)(2,1)S(1)}, u32[]{:S(2)}, u32[]{:S(2)}) collective-permute-start(bf16[2,128,512]{2,1,0:T(8,128)(2,1)S(1)} %get-tuple-element.55), channel_id=1, source_target_pairs={{1,0},{6,1},{3,2},{8,3},{5,4},{10,5},{7,6},{12,7},{9,8},{14,9},{11... | collective-permute-start | bytes 786440 | tf_op jit(solution)/shard_map/ppermute | solution.py:52
  77.0 7.0 %collective-permute-done.21 = bf16[4,256,128]{2,1,0:T(8,128)(2,1)S(1)} collective-permute-done((bf16[4,256,128]{2,1,0:T(8,128)(2,1)S(1)}, bf16[4,256,128]{2,1,0:T(8,128)(2,1)S(1)}, u32[]{:S(2)}, u32[]{:S(2)}) %collective-permute-start.21) | collective-permute-done | bytes 262176 | tf_op jit(solution)/shard_map/ppermute | solution.py:52
  84.9 3.1 %collective-permute-start.27 = (bf16[256,128]{1,0:T(8,128)(2,1)S(1)}, bf16[256,128]{1,0:T(8,128)(2,1)S(1)}, u32[]{:S(2)}, u32[]{:S(2)}) collective-permute-start(bf16[256,128]{1,0:T(8,128)(2,1)S(1)} %get-tuple-element.62), channel_id=1, source_target_pairs={{0,12},{1,13},{2,14},{3,15},{4,0},{5,1},{6,2},{7,3},{8,4},{9,5},{1... | collective-permute-start | bytes 196616 | tf_op jit(solution)/shard_map/ppermute | solution.py:52
  90.8 2.8 %collective-permute-done.26 = bf16[256,128]{1,0:T(8,128)(2,1)S(1)} collective-permute-done((bf16[256,128]{1,0:T(8,128)(2,1)S(1)}, bf16[256,128]{1,0:T(8,128)(2,1)S(1)}, u32[]{:S(2)}, u32[]{:S(2)}) %collective-permute-start.26) | collective-permute-done | bytes 65568 | tf_op jit(solution)/shard_map/ppermute | solution.py:52
  93.7 2.1 %collective-permute-start.30 = (bf16[256,128]{1,0:T(8,128)(2,1)S(1)}, bf16[256,128]{1,0:T(8,128)(2,1)S(1)}, u32[]{:S(2)}, u32[]{:S(2)}) collective-permute-start(bf16[256,128]{1,0:T(8,128)(2,1)S(1)} %fusion.2), channel_id=1, source_target_pairs={{0,12},{1,13},{2,14},{3,15},{4,0},{5,1},{6,2},{7,3},{8,4},{9,5},{1... | collective-permute-start | bytes 196616 | tf_op jit(solution)/shard_map/ppermute | solution.py:52
  98.2 2.9 %collective-permute-done.29 = bf16[256,128]{1,0:T(8,128)(2,1)S(1)} collective-permute-done((bf16[256,128]{1,0:T(8,128)(2,1)S(1)}, bf16[256,128]{1,0:T(8,128)(2,1)S(1)}, u32[]{:S(2)}, u32[]{:S(2)}) %collective-permute-start.29) | collective-permute-done | bytes 65568 | tf_op jit(solution)/shard_map/ppermute | solution.py:52
  105.8 4.4 %collective-permute-done.32.rest_4_ = bf16[4,256,128]{2,1,0:T(8,128)(2,1)S(1)} collective-permute-done((bf16[4,256,128]{2,1,0:T(8,128)(2,1)S(1)}, bf16[4,256,128]{2,1,0:T(8,128)(2,1)S(1)}, u32[]{:S(2)}, u32[]{:S(2)}) %collective-permute-start.32) | collective-permute-done | bytes 262176 | tf_op jit(solution)/shard_map/ppermute | solution.py:52
  110.2 2.5 %collective-permute-done.31.rest_1_ = bf16[2,128,512]{2,1,0:T(8,128)(2,1)S(1)} collective-permute-done((bf16[2,128,512]{2,1,0:T(8,128)(2,1)S(1)}, bf16[2,128,512]{2,1,0:T(8,128)(2,1)S(1)}, u32[]{:S(2)}, u32[]{:S(2)}) %collective-permute-start.31) | collective-permute-done | bytes 262176 | tf_op jit(solution)/shard_map/ppermute | solution.py:52
  112.8 5.2 %shard_map.106 = (bf16[16,128,512]{2,1,0:T(8,128)(2,1)}, bf16[16,128,512]{2,1,0:T(8,128)(2,1)}) custom-call(s32[1]{0:T(128)S(6)} %copy.11.slab_index, s32[4,8]{1,0:T(4,128)S(1)} %copy-done.5, f32[2,128,512]{2,1,0:T(8,128)S(1)} %get-tuple-element.45.home, bf16[2,128,512]{2,1,0:T(8,128)(2,1)S(1)} %collective-permute-done.22.rest_0_, ...), custom_call_target="tpu_custom_call" | custom-call | tf_op jit(solution)/shard_map/pallas_call | solution.py:498
  (79 shorter events, 26.7 us)
Async XLA Ops:
  3.4 8.8 %collective-permute-start = (bf16[128,512]{1,0:T(8,128)(2,1)}, bf16[128,512]{1,0:T(8,128)(2,1)S(1)}, u32[]{:S(2)}, u32[]{:S(2)}) collective-permute-start(bf16[128,512]{1,0:T(8,128)(2,1)} %get-tuple-element.35), channel_id=1, source_target_pairs={{0,4},{1,5},{2,6},{3,7},{4,8},{5,9},{6,10},{7,11},{8,12},{9,13},{1... | collective-permute-start | bytes 393224 | tf_op jit(solution)/shard_map/ppermute | solution.py:52
  12.2 8.0 %collective-permute-start.4 = (bf16[128,512]{1,0:T(8,128)(2,1)}, bf16[128,512]{1,0:T(8,128)(2,1)}, u32[]{:S(2)}, u32[]{:S(2)}) collective-permute-start(bf16[128,512]{1,0:T(8,128)(2,1)} %get-tuple-element.40), channel_id=1, source_target_pairs={{0,4},{1,5},{2,6},{3,7},{4,8},{5,9},{6,10},{7,11},{8,12},{9,13},{1... | collective-permute-start | bytes 393224 | tf_op jit(solution)/shard_map/ppermute | solution.py:52
  12.2 9.2 %collective-permute-start.1 = (bf16[4,256,128]{2,1,0:T(8,128)(2,1)}, bf16[4,256,128]{2,1,0:T(8,128)(2,1)}, u32[]{:S(2)}, u32[]{:S(2)}) collective-permute-start(bf16[4,256,128]{2,1,0:T(8,128)(2,1)} %get-tuple-element.36), channel_id=1, source_target_pairs={{0,1},{1,0},{2,3},{3,2},{4,5},{5,4},{6,7},{7,6},{8,9},{9,8},{10,11... | collective-permute-start | bytes 786440 | tf_op jit(solution)/shard_map/ppermute | solution.py:52
  15.8 10.5 %collective-permute-start.3 = (bf16[4,256,128]{2,1,0:T(8,128)(2,1)}, bf16[4,256,128]{2,1,0:T(8,128)(2,1)}, u32[]{:S(2)}, u32[]{:S(2)}) collective-permute-start(bf16[4,256,128]{2,1,0:T(8,128)(2,1)} %add_convert_fusion.3), channel_id=1, source_target_pairs={{0,2},{1,3},{2,0},{3,1},{4,6},{5,7},{6,4},{7,5},{8,10},{9,11},{10,... | collective-permute-start | bytes 786440 | tf_op jit(solution)/shard_map/ppermute | solution.py:52
  17.3 10.2 %collective-permute-start.5 = (bf16[2,128,512]{2,1,0:T(8,128)(2,1)}, bf16[2,128,512]{2,1,0:T(8,128)(2,1)S(1)}, u32[]{:S(2)}, u32[]{:S(2)}) collective-permute-start(bf16[2,128,512]{2,1,0:T(8,128)(2,1)} %get-tuple-element.41), channel_id=1, source_target_pairs={{0,1},{1,6},{2,3},{3,8},{4,5},{5,10},{6,7},{7,12},{8,9},{9,14},{10... | collective-permute-start | bytes 786440 | tf_op jit(solution)/shard_map/ppermute | solution.py:52
  27.6 6.7 %collective-permute-start.6 = (bf16[256,128]{1,0:T(8,128)(2,1)S(1)}, bf16[256,128]{1,0:T(8,128)(2,1)S(1)}, u32[]{:S(2)}, u32[]{:S(2)}) collective-permute-start(bf16[256,128]{1,0:T(8,128)(2,1)S(1)} %get-tuple-element.66), channel_id=1, source_target_pairs={{0,4},{1,5},{2,6},{3,7},{4,8},{5,9},{6,10},{7,11},{8,12},{9,13},{1... | collective-permute-start | bytes 196616 | tf_op jit(solution)/shard_map/ppermute | solution.py:52
  28.5 5.7 %collective-permute-start.8 = (bf16[256,128]{1,0:T(8,128)(2,1)S(1)}, bf16[256,128]{1,0:T(8,128)(2,1)S(1)}, u32[]{:S(2)}, u32[]{:S(2)}) collective-permute-start(bf16[256,128]{1,0:T(8,128)(2,1)S(1)} %get-tuple-element.67), channel_id=1, source_target_pairs={{0,12},{1,13},{2,14},{3,15},{4,0},{5,1},{6,2},{7,3},{8,4},{9,5},{1... | collective-permute-start | bytes 196616 | tf_op jit(solution)/shard_map/ppermute | solution.py:52
  31.6 14.0 %collective-permute-start.12 = (bf16[2,128,512]{2,1,0:T(8,128)(2,1)S(1)}, bf16[2,128,512]{2,1,0:T(8,128)(2,1)S(1)}, u32[]{:S(2)}, u32[]{:S(2)}) collective-permute-start(bf16[2,128,512]{2,1,0:T(8,128)(2,1)S(1)} %get-tuple-element.64), channel_id=1, source_target_pairs={{0,2},{1,3},{2,0},{3,1},{4,6},{5,7},{6,4},{7,5},{8,10},{9,11},{10,... | collective-permute-start | bytes 786440 | tf_op jit(solution)/shard_map/ppermute | solution.py:52
  39.0 6.5 %collective-permute-start.10 = (bf16[256,128]{1,0:T(8,128)(2,1)S(1)}, bf16[256,128]{1,0:T(8,128)(2,1)S(1)}, u32[]{:S(2)}, u32[]{:S(2)}) collective-permute-start(bf16[256,128]{1,0:T(8,128)(2,1)S(1)} %fusion.5), channel_id=1, source_target_pairs={{0,8},{1,9},{2,10},{3,11},{4,12},{5,13},{6,14},{7,15},{8,0},{9,1},... | collective-permute-start | bytes 196616 | tf_op jit(solution)/shard_map/ppermute | solution.py:52
  39.0 6.5 %collective-permute-start.9 = (bf16[256,128]{1,0:T(8,128)(2,1)S(1)}, bf16[256,128]{1,0:T(8,128)(2,1)S(1)}, u32[]{:S(2)}, u32[]{:S(2)}) collective-permute-start(bf16[256,128]{1,0:T(8,128)(2,1)S(1)} %fusion.5), channel_id=1, source_target_pairs={{0,4},{1,5},{2,6},{3,7},{4,8},{5,9},{6,10},{7,11},{8,12},{9,13},{1... | collective-permute-start | bytes 196616 | tf_op jit(solution)/shard_map/ppermute | solution.py:52
  45.6 6.5 %collective-permute-start.13 = (bf16[4,256,128]{2,1,0:T(8,128)(2,1)S(1)}, bf16[4,256,128]{2,1,0:T(8,128)(2,1)S(1)}, u32[]{:S(2)}, u32[]{:S(2)}) collective-permute-start(bf16[4,256,128]{2,1,0:T(8,128)(2,1)S(1)} %pad_maximum_fusion.1.rest_0_), channel_id=1, source_target_pairs={{0,2},{1,3},{2,0},{3,1},{4,6},{5,7},{6,4},{7,5},{8,10},{9,11},{10,... | collective-permute-start | bytes 786440 | tf_op jit(solution)/shard_map/ppermute | solution.py:52
  71.1 5.9 %collective-permute-start.19 = (bf16[4,256,128]{2,1,0:T(8,128)(2,1)S(1)}, bf16[4,256,128]{2,1,0:T(8,128)(2,1)S(1)}, u32[]{:S(2)}, u32[]{:S(2)}) collective-permute-start(bf16[4,256,128]{2,1,0:T(8,128)(2,1)S(1)} %get-tuple-element.49), channel_id=1, source_target_pairs={{0,1},{1,0},{2,3},{3,2},{4,5},{5,4},{6,7},{7,6},{8,9},{9,8},{10,11... | collective-permute-start | bytes 786440 | tf_op jit(solution)/shard_map/ppermute | solution.py:52
  72.6 11.4 %collective-permute-start.21 = (bf16[4,256,128]{2,1,0:T(8,128)(2,1)S(1)}, bf16[4,256,128]{2,1,0:T(8,128)(2,1)S(1)}, u32[]{:S(2)}, u32[]{:S(2)}) collective-permute-start(bf16[4,256,128]{2,1,0:T(8,128)(2,1)S(1)} %add_convert_fusion.1), channel_id=1, source_target_pairs={{0,2},{1,3},{2,0},{3,1},{4,6},{5,7},{6,4},{7,5},{8,10},{9,11},{10,... | collective-permute-start | bytes 786440 | tf_op jit(solution)/shard_map/ppermute | solution.py:52
  74.5 14.3 %collective-permute-start.18 = (bf16[2,128,512]{2,1,0:T(8,128)(2,1)S(1)}, bf16[2,128,512]{2,1,0:T(8,128)(2,1)S(1)}, u32[]{:S(2)}, u32[]{:S(2)}) collective-permute-start(bf16[2,128,512]{2,1,0:T(8,128)(2,1)S(1)} %get-tuple-element.47), channel_id=1, source_target_pairs={{0,1},{1,0},{2,3},{3,2},{4,5},{5,4},{6,7},{7,6},{8,9},{9,8},{10,11... | collective-permute-start | bytes 786440 | tf_op jit(solution)/shard_map/ppermute | solution.py:52
  74.5 29.4 %collective-permute-start.23 = (bf16[2,128,512]{2,1,0:T(8,128)(2,1)S(1)}, bf16[2,128,512]{2,1,0:T(8,128)(2,1)S(1)}, u32[]{:S(2)}, u32[]{:S(2)}) collective-permute-start(bf16[2,128,512]{2,1,0:T(8,128)(2,1)S(1)} %get-tuple-element.54), channel_id=1, source_target_pairs={{0,1},{1,0},{2,3},{3,2},{4,5},{5,4},{6,7},{7,6},{8,9},{9,8},{10,11... | collective-permute-start | bytes 786440 | tf_op jit(solution)/shard_map/ppermute | solution.py:52
  75.0 9.0 %collective-permute-start.24 = (bf16[2,128,512]{2,1,0:T(8,128)(2,1)S(1)}, bf16[2,128,512]{2,1,0:T(8,128)(2,1)S(1)}, u32[]{:S(2)}, u32[]{:S(2)}) collective-permute-start(bf16[2,128,512]{2,1,0:T(8,128)(2,1)S(1)} %get-tuple-element.55), channel_id=1, source_target_pairs={{1,0},{6,1},{3,2},{8,3},{5,4},{10,5},{7,6},{12,7},{9,8},{14,9},{11... | collective-permute-start | bytes 786440 | tf_op jit(solution)/shard_map/ppermute | solution.py:52
  84.1 6.8 %collective-permute-start.25 = (bf16[256,128]{1,0:T(8,128)(2,1)S(1)}, bf16[256,128]{1,0:T(8,128)(2,1)S(1)}, u32[]{:S(2)}, u32[]{:S(2)}) collective-permute-start(bf16[256,128]{1,0:T(8,128)(2,1)S(1)} %get-tuple-element.61), channel_id=1, source_target_pairs={{0,4},{1,5},{2,6},{3,7},{4,8},{5,9},{6,10},{7,11},{8,12},{9,13},{1... | collective-permute-start | bytes 196616 | tf_op jit(solution)/shard_map/ppermute | solution.py:52
  84.9 6.0 %collective-permute-start.27 = (bf16[256,128]{1,0:T(8,128)(2,1)S(1)}, bf16[256,128]{1,0:T(8,128)(2,1)S(1)}, u32[]{:S(2)}, u32[]{:S(2)}) collective-permute-start(bf16[256,128]{1,0:T(8,128)(2,1)S(1)} %get-tuple-element.62), channel_id=1, source_target_pairs={{0,12},{1,13},{2,14},{3,15},{4,0},{5,1},{6,2},{7,3},{8,4},{9,5},{1... | collective-permute-start | bytes 196616 | tf_op jit(solution)/shard_map/ppermute | solution.py:52
  88.0 5.7 %collective-permute-start.26 = (bf16[256,128]{1,0:T(8,128)(2,1)S(1)}, bf16[256,128]{1,0:T(8,128)(2,1)S(1)}, u32[]{:S(2)}, u32[]{:S(2)}) collective-permute-start(bf16[256,128]{1,0:T(8,128)(2,1)S(1)} %get-tuple-element.63), channel_id=1, source_target_pairs={{0,8},{1,9},{2,10},{3,11},{4,12},{5,13},{6,14},{7,15},{8,0},{9,1},... | collective-permute-start | bytes 196616 | tf_op jit(solution)/shard_map/ppermute | solution.py:52
  88.9 13.1 %collective-permute-start.22 = (bf16[2,128,512]{2,1,0:T(8,128)(2,1)S(1)}, bf16[2,128,512]{2,1,0:T(8,128)(2,1)S(1)}, u32[]{:S(2)}, u32[]{:S(2)}) collective-permute-start(bf16[2,128,512]{2,1,0:T(8,128)(2,1)S(1)} %add_convert_fusion.2), channel_id=1, source_target_pairs={{0,2},{1,3},{2,0},{3,1},{4,6},{5,7},{6,4},{7,5},{8,10},{9,11},{10,... | collective-permute-start | bytes 786440 | tf_op jit(solution)/shard_map/ppermute | solution.py:52
  95.8 6.1 %collective-permute-start.28 = (bf16[256,128]{1,0:T(8,128)(2,1)S(1)}, bf16[256,128]{1,0:T(8,128)(2,1)S(1)}, u32[]{:S(2)}, u32[]{:S(2)}) collective-permute-start(bf16[256,128]{1,0:T(8,128)(2,1)S(1)} %fusion.2), channel_id=1, source_target_pairs={{0,4},{1,5},{2,6},{3,7},{4,8},{5,9},{6,10},{7,11},{8,12},{9,13},{1... | collective-permute-start | bytes 196616 | tf_op jit(solution)/shard_map/ppermute | solution.py:52
  101.9 8.3 %collective-permute-start.32 = (bf16[4,256,128]{2,1,0:T(8,128)(2,1)S(1)}, bf16[4,256,128]{2,1,0:T(8,128)(2,1)S(1)}, u32[]{:S(2)}, u32[]{:S(2)}) collective-permute-start(bf16[4,256,128]{2,1,0:T(8,128)(2,1)S(1)} %pad_maximum_fusion.2.rest_3_), channel_id=1, source_target_pairs={{0,2},{1,3},{2,0},{3,1},{4,6},{5,7},{6,4},{7,5},{8,10},{9,11},{10,... | collective-permute-start | bytes 786440 | tf_op jit(solution)/shard_map/ppermute | solution.py:52
  103.9 8.9 %collective-permute-start.33 = (bf16[4,256,128]{2,1,0:T(8,128)(2,1)S(1)}, bf16[4,256,128]{2,1,0:T(8,128)(2,1)S(1)}, u32[]{:S(2)}, u32[]{:S(2)}) collective-permute-start(bf16[4,256,128]{2,1,0:T(8,128)(2,1)S(1)} %pad_maximum_fusion.2.rest_3_), channel_id=1, source_target_pairs={{0,1},{1,0},{2,3},{3,2},{4,5},{5,4},{6,7},{7,6},{8,9},{9,8},{10,11... | collective-permute-start | bytes 786440 | tf_op jit(solution)/shard_map/ppermute | solution.py:52
  104.0 8.8 %collective-permute-start.31 = (bf16[2,128,512]{2,1,0:T(8,128)(2,1)S(1)}, bf16[2,128,512]{2,1,0:T(8,128)(2,1)S(1)}, u32[]{:S(2)}, u32[]{:S(2)}) collective-permute-start(bf16[2,128,512]{2,1,0:T(8,128)(2,1)S(1)} %add_convert_fusion), channel_id=1, source_target_pairs={{4,0},{5,1},{6,2},{7,3},{8,4},{9,5},{10,6},{11,7},{12,8},{13,9},{1... | collective-permute-start | bytes 786440 | tf_op jit(solution)/shard_map/ppermute | solution.py:52
  (18 other events, 307.7 us)

commit v8 on v6

v8 whole, which is shorter than its diff:
```python
import functools
import math

import jax
import jax.numpy as jnp
from jax import lax
from jax.experimental import pallas as pl
from jax.experimental.pallas import tpu as pltpu
from jax.sharding import PartitionSpec as P

BLOCK = 64
WDEV = 5
VMEM_LIMIT = 32 * 1024 * 1024
MOST_VMEM = 60 * 1024 * 1024
JOIN = 4
BF16 = jnp.bfloat16
F32 = jnp.float32


class Lines:
    def __init__(self, devices):
        self.devices = devices
        self.far = devices // 4

    def place(self, me):
        return lax.div(me, 4), lax.rem(lax.div(me, 2), 2), lax.rem(me, 2)

    def core_pairs(self):
        return [(i, i ^ 1) for i in range(self.devices)]

    def near_pairs(self):
        return [(i, i ^ 2) for i in range(self.devices)]

    def both_pairs(self):
        return [(i, i ^ 3) for i in range(self.devices)]

    def far_pairs(self, by):
        return [(i, (i + 4 * by) % self.devices) for i in range(self.devices)]

    def shift_pairs(self, by):
        return [(i, (i + by) % self.devices) for i in range(self.devices)]

    def mixed_pairs(self):
        return [(i, (i + (5 if i % 2 else 1)) % self.devices) for i in range(self.devices)]


def back(pairs):
    return [(b, a) for a, b in pairs]


def move(array, pairs):
    return lax.ppermute(array, "ctx", pairs)


def after(array, *others):
    return lax.optimization_barrier((array, *others))[0]


def core_sum(lines, to_near, to_both):
    return (to_near.astype(F32) + move(to_both, lines.core_pairs()).astype(F32)).astype(BF16)


def near_sum(lines, mine, to_near, to_core):
    from_near = move(to_near, lines.near_pairs())
    from_core = move(to_core, lines.core_pairs())
    return mine.astype(F32) + from_core.astype(F32) + from_near.astype(F32)


def far_sum(lines, quarter):
    share = quarter[0]
    for by in range(1, lines.far):
        share = share + move(quarter[by].astype(BF16), lines.far_pairs(by)).astype(F32)
    return share.astype(BF16)


def far_gather(lines, share):
    parts = [share] + [move(share, lines.far_pairs(by)) for by in range(1, lines.far)]
    return jnp.stack(parts)


def plane_gather(lines, mine):
    across = move(mine, lines.near_pairs())
    core_mine = move(mine, lines.core_pairs())
    core_across = move(across, lines.core_pairs())
    return mine, across, core_mine, core_across


def wraps(me, devices):
    return [me + 4 >= devices, (lax.rem(me, 2) == 1) & (me + 5 >= devices)]


def pack_kernel(slab_index, verts, keys, values, *rest, lines, heads, nv, per_device):
    sends = rest[:3]
    shares = rest[3:7]
    picked, sems, pick_sems = rest[7:]
    slab, me = slab_index[0], lax.axis_index("ctx")
    far, near, core = lines.place(me)
    _, chunk, head_dim = shares[0].shape
    copies = []
    wrapped4, wrapped_mixed = wraps(me, lines.devices)
    for n, region in enumerate(
        (slab, slab - wrapped4.astype(jnp.int32), slab - wrapped_mixed.astype(jnp.int32))
    ):
        for kv, source in enumerate((keys, values)):
            copy = pltpu.make_async_copy(source.at[region], sends[n].at[kv], sems.at[n, kv])
            copy.start()
            copies.append(copy)
    picked[...] = jnp.zeros_like(picked)
    slab_blocks = per_device * lines.devices
    piece = min(BLOCK, chunk)

    def unit_copies(h, m):
        inner = lax.rem(verts[h, m], slab_blocks)
        region = lax.div(verts[h, m], slab_blocks)
        row = lax.rem(inner, per_device) * BLOCK
        for p in range(BLOCK // piece):
            at = (h * nv + m) * BLOCK + p * piece
            line, at = at // (lines.far * chunk), at % (lines.far * chunk)
            slot, at = at // chunk, at % chunk
            line = lax.rem(line + near, 2)
            slot = lax.rem(slot - far + lines.far, lines.far)
            for kv, source in enumerate((keys, values)):
                yield pltpu.make_async_copy(
                    source.at[
                        region,
                        pl.ds(pl.multiple_of(row + p * piece, piece), piece),
                        pl.ds(h * head_dim, head_dim),
                    ],
                    picked.at[lax.rem(kv + core, 2), line, slot, pl.ds(at, piece), :],
                    pick_sems.at[kv, (h * nv + m) * (BLOCK // piece) + p],
                )

    def owned(h, m):
        return lax.div(lax.rem(verts[h, m], slab_blocks), per_device) == me

    for h in range(heads):
        for m in range(nv):

            @pl.when(owned(h, m))
            def _():
                for copy in unit_copies(h, m):
                    copy.start()

    for h in range(heads):
        for m in range(nv):

            @pl.when(owned(h, m))
            def _():
                for copy in unit_copies(h, m):
                    copy.wait()

    for n, share in enumerate(shares):
        share[...] = picked[n // 2, n % 2]
    for copy in copies:
        copy.wait()


def pack(slab_index, verticals, keys, values, lines):
    regions, rows, features = keys.shape
    heads, nv = verticals.shape
    head_dim = features // heads
    chunk = heads * nv * BLOCK // (2 * lines.far)
    smem = pl.BlockSpec(memory_space=pltpu.SMEM)
    hbm = pl.BlockSpec(memory_space=pltpu.HBM)
    share = (lines.far, chunk, head_dim)
    return pl.pallas_call(
        functools.partial(pack_kernel, lines=lines, heads=heads, nv=nv, per_device=rows // BLOCK),
        in_specs=[smem, smem, hbm, hbm],
        out_specs=[pl.BlockSpec(memory_space=pltpu.VMEM)] * 7,
        out_shape=[jax.ShapeDtypeStruct((2, rows, features), BF16)] * 3
        + [jax.ShapeDtypeStruct(share, BF16)] * 4,
        scratch_shapes=[
            pltpu.VMEM((2, 2) + share, BF16),
            pltpu.SemaphoreType.DMA((3, 2)),
            pltpu.SemaphoreType.DMA((2, heads * nv * max(1, BLOCK // chunk))),
        ],
        compiler_params=pltpu.CompilerParams(vmem_limit_bytes=MOST_VMEM),
    )(slab_index, verticals, keys, values)


def distances(core):
    return [2, 4, 5 - 4 * core, 1 + 2 * core, 3 + 2 * core]


def vertical_copies(lines, me, chunk, gathered, to, sems, first):
    far, near, core = lines.place(me)
    copies = []
    for n, source in enumerate(gathered):
        kv = core if n < 2 else 1 - core
        line = near if n % 2 == 0 else 1 - near
        for s in range(lines.far):
            slot = lax.rem(far - s + lines.far, lines.far)
            row = pl.multiple_of((line * lines.far + slot) * chunk, chunk)
            copies.append(
                pltpu.make_async_copy(
                    source.at[s], to.at[kv, pl.ds(row, chunk), :], sems.at[first + len(copies)]
                )
            )
    return copies


NT = (((1,), (1,)), ((), ()))


def prepare_kernel(q, grad, out, qs, gs, qt, gt, delta, *, head_dim):
    per_device = qs.shape[1]
    group = q.shape[1] // head_dim
    ones = jnp.ones((8, 2 * head_dim), BF16)
    for j in range(per_device):
        rows = slice(j * BLOCK, (j + 1) * BLOCK)
        split = []
        for g in range(group):
            cols = slice(g * head_dim, (g + 1) * head_dim)
            here = slice(g * BLOCK, (g + 1) * BLOCK)
            qs[0, j, here, :] = q[rows, cols]
            gs[0, j, here, :] = grad[rows, cols]
            product = grad[rows, cols].astype(F32) * out[rows, cols].astype(F32)
            upper = product.astype(BF16)
            lower = (product - upper.astype(F32)).astype(BF16)
            split.append(jnp.concatenate([upper, lower], axis=1))
        qt[0, j] = jnp.transpose(qs[0, j])
        gt[0, j] = jnp.transpose(gs[0, j])
        delta[0, j] = lax.dot_general(
            ones, jnp.concatenate(split, axis=0), NT, preferred_element_type=F32
        )


def prepare(queries, cotangent, output, heads, head_dim):
    rows, width = queries.shape
    per_device = rows // BLOCK
    deep = width // heads // head_dim * BLOCK
    tile = pl.BlockSpec((rows, width // heads), lambda h: (0, h))

    def by_head(*shape):
        return pl.BlockSpec((1,) + shape, lambda h: (h,) + (0,) * len(shape))

    stacked = (per_device, deep, head_dim)
    turned = (per_device, head_dim, deep)
    sums = (per_device, 8, deep)
    return pl.pallas_call(
        functools.partial(prepare_kernel, head_dim=head_dim),
        grid=(heads,),
        in_specs=[tile] * 3,
        out_specs=[by_head(*stacked)] * 2 + [by_head(*turned)] * 2 + [by_head(*sums)],
        out_shape=[jax.ShapeDtypeStruct((heads,) + stacked, BF16)] * 2
        + [jax.ShapeDtypeStruct((heads,) + turned, BF16)] * 2
        + [jax.ShapeDtypeStruct((heads,) + sums, F32)],
        compiler_params=pltpu.CompilerParams(vmem_limit_bytes=VMEM_LIMIT),
        cost_estimate=pl.CostEstimate(flops=0, bytes_accessed=7 << 20, transcendentals=0),
    )(queries, cotangent, output)


def slash_rows(offs, h, j, s, per_device):
    return pl.multiple_of((WDEV * per_device + j - offs[h, s]) * BLOCK, BLOCK)


def attend_kernel(
    slab_index, verts, offs, qs, gs, qt, gt, delta, keys, values, *rest,
    lines, heads, nv, ns, per_device,
):
    gathered, recv, rest = rest[:4], rest[4 : 4 + WDEV], rest[4 + WDEV :]
    shares, low_w, low_ds, cand_keys = rest[:4], rest[4], rest[5], rest[6]
    win, vkv, vc, s_ref, vert_w, sems = rest[7:]
    h = pl.program_id(0)
    slab, me = slab_index[0], lax.axis_index("ctx")
    far, near, core = lines.place(me)
    _, chunk, head_dim = shares[0].shape
    cand = nv + 1 + ns
    scaling = 1.0 / math.sqrt(head_dim)
    rows = per_device * BLOCK
    width = qs.shape[2]
    first_block = slab * (per_device * lines.devices) + me * per_device
    lanes = pl.ds(pl.multiple_of(h * head_dim, head_dim), head_dim)

    def window_row(d):
        return pl.multiple_of((WDEV - d) * rows, rows)

    @pl.when(h == 0)
    def _():
        own_rows = pl.ds(WDEV * rows, rows)
        copies = [
            pltpu.make_async_copy(
                recv[n], win.at[:, pl.ds(window_row(d), rows), :], sems.at[n]
            )
            for n, d in enumerate(distances(core))
        ]
        copies.append(pltpu.make_async_copy(keys.at[slab], win.at[0, own_rows, :], sems.at[WDEV]))
        copies.append(
            pltpu.make_async_copy(values.at[slab], win.at[1, own_rows, :], sems.at[WDEV + 1])
        )
        copies += vertical_copies(lines, me, chunk, gathered, vkv, sems, WDEV + 2)
        for copy in copies:
            copy.start()
        for copy in copies:
            copy.wait()

    vert_rows = pl.ds(pl.multiple_of(h * (nv * BLOCK), nv * BLOCK), nv * BLOCK)
    neg, posinf = jnp.float32(-jnp.inf), jnp.float32(jnp.inf)
    log2_scale = scaling * math.log2(math.e)
    key_at = lax.broadcasted_iota(jnp.int32, (BLOCK, width), 0)
    row_at = lax.broadcasted_iota(jnp.int32, (BLOCK, width), 1) % BLOCK

    def fold(x, op):
        y = x[0:8, :]
        for r in range(1, BLOCK // 8):
            y = op(y, x[r * 8 : (r + 1) * 8, :])
        return y

    vertical_sum = [None, None]
    for j in range(per_device):
        block = first_block + j
        own_at = (WDEV * per_device + j) * BLOCK
        valid = [verts[h, m] < block for m in range(nv)] + [None]
        for s in range(ns):
            collide = verts[h, 0] == block - offs[h, s]
            for m in range(1, nv):
                collide = collide | (verts[h, m] == block - offs[h, s])
            valid.append((offs[h, s] > 0) & jnp.logical_not(collide))
        for kv, to in enumerate((cand_keys.at[0], vc)):
            to[j, 0 : nv * BLOCK, :] = vkv[kv, vert_rows, :]
            to[j, nv * BLOCK : (nv + 1) * BLOCK, :] = win[kv, own_at : own_at + BLOCK, lanes]
            for s in range(ns):
                to[j, (nv + 1 + s) * BLOCK : (nv + 2 + s) * BLOCK, :] = win[
                    kv, pl.ds(slash_rows(offs, h, j, s, per_device), BLOCK), lanes
                ]

        top = None
        for n in range(cand // JOIN):
            span = slice(n * JOIN * BLOCK, (n + 1) * JOIN * BLOCK)
            scores = jnp.dot(cand_keys[0, j, span, :], qt[0, j], preferred_element_type=F32)
            for i in range(JOIN):
                c = n * JOIN + i
                part = scores[i * BLOCK : (i + 1) * BLOCK, :]
                if c == nv:
                    part = jnp.where(key_at <= row_at, part, neg)
                s_ref[j, c * BLOCK : (c + 1) * BLOCK, :] = part
                best = fold(part, jnp.maximum)
                if c != nv:
                    best = best + jnp.where(valid[c], jnp.float32(0), neg)
                top = best if top is None else jnp.maximum(top, best)
        top = jnp.max(top, axis=0, keepdims=True) * log2_scale
        total = jnp.zeros((8, width), F32)
        for c in range(cand):
            span = slice(c * BLOCK, (c + 1) * BLOCK)
            less = top if c == nv else top + jnp.where(valid[c], jnp.float32(0), posinf)
            p = jnp.exp2(s_ref[j, span, :] * log2_scale - less)
            s_ref[j, span, :] = p
            total = total + fold(p, jnp.add)
        inverse = 1.0 / jnp.sum(total, axis=0, keepdims=True)
        row_delta = delta[0, j, 0:1, :]
        for n in range(cand // JOIN):
            span = slice(n * JOIN * BLOCK, (n + 1) * JOIN * BLOCK)
            weight_grad = jnp.dot(vc[j, span, :], gt[0, j], preferred_element_type=F32)
            w = s_ref[j, span, :] * inverse
            if n * JOIN < nv:
                vert_w[j, span, :] = w.astype(BF16)
            else:
                low_w[0, j] = w.astype(BF16)
            low_ds[0, j, span, :] = (w * (weight_grad - row_delta)).astype(BF16)

        here = slice(0, nv * BLOCK)
        dv = jnp.dot(vert_w[j], gs[0, j], preferred_element_type=F32)
        dk = jnp.dot(low_ds[0, j, here, :], qs[0, j], preferred_element_type=F32) * scaling
        for kv, part in enumerate((dk, dv)):
            vertical_sum[kv] = part if j == 0 else vertical_sum[kv] + part

    first = core == 0
    keep = jnp.where(first, vertical_sum[0], vertical_sum[1])
    give = jnp.where(first, vertical_sum[1], vertical_sum[0])
    per_line = heads // 2
    for line in range(2):

        @pl.when(lax.rem(lax.div(h, per_line) + near, 2) == line)
        def _():
            for c in range(nv * BLOCK // chunk):
                slot = lax.rem(h, per_line) * (nv * BLOCK // chunk) + c
                slot = lax.rem(slot - far + lines.far, lines.far)
                span = slice(c * chunk, (c + 1) * chunk)
                shares[line][slot] = keep[span, :].astype(shares[line].dtype)
                shares[2 + line][slot] = give[span, :].astype(BF16)


def attend(slab_index, verticals, offsets, prepared, keys, values, gathered, recv, lines):
    heads, per_device, deep, head_dim = prepared[0].shape
    _, rows, features = keys.shape
    nv, ns = verticals.shape[1], offsets.shape[1]
    cand = nv + 1 + ns
    smem = pl.BlockSpec(memory_space=pltpu.SMEM)
    hbm = pl.BlockSpec(memory_space=pltpu.HBM)
    anywhere = pl.BlockSpec(memory_space=pl.ANY)

    def by_head(shape):
        return pl.BlockSpec((1,) + shape[1:], lambda h: (h,) + (0,) * (len(shape) - 1))

    def whole(shape):
        return pl.BlockSpec(shape, lambda h: (0,) * len(shape))

    share = (lines.far, heads * nv * BLOCK // (2 * lines.far), head_dim)
    low = (heads, per_device, cand * BLOCK, deep)
    low_tail = (heads, per_device, (1 + ns) * BLOCK, deep)
    cand_keys = (heads, per_device, cand * BLOCK, head_dim)
    return pl.pallas_call(
        functools.partial(
            attend_kernel, lines=lines, heads=heads, nv=nv, ns=ns, per_device=per_device
        ),
        grid=(heads,),
        in_specs=[smem] * 3
        + [by_head(array.shape) for array in prepared]
        + [hbm] * 2
        + [anywhere] * (4 + WDEV),
        out_specs=[whole(share)] * 4 + [by_head(low_tail), by_head(low), by_head(cand_keys)],
        out_shape=[
            jax.ShapeDtypeStruct(share, F32),
            jax.ShapeDtypeStruct(share, BF16),
            jax.ShapeDtypeStruct(share, BF16),
            jax.ShapeDtypeStruct(share, BF16),
            jax.ShapeDtypeStruct(low_tail, BF16),
            jax.ShapeDtypeStruct(low, BF16),
            jax.ShapeDtypeStruct(cand_keys, BF16),
        ],
        scratch_shapes=[
            pltpu.VMEM((2, (WDEV + 1) * rows, features), BF16),
            pltpu.VMEM((2, heads * nv * BLOCK, head_dim), BF16),
            pltpu.VMEM((per_device, cand * BLOCK, head_dim), BF16),
            pltpu.VMEM((per_device, cand * BLOCK, deep), F32),
            pltpu.VMEM((per_device, nv * BLOCK, deep), BF16),
            pltpu.SemaphoreType.DMA((WDEV + 2 + 4 * lines.far,)),
        ],
        compiler_params=pltpu.CompilerParams(vmem_limit_bytes=VMEM_LIMIT),
    )(slab_index, verticals, offsets, *prepared, keys, values, *gathered, *recv)


def window_kernel(offs, qs, gs, low_w, low_ds, home, *rest, lines, ns, per_device):
    parts, total = rest[:WDEV], rest[WDEV]
    h = pl.program_id(0)
    _, _, core = lines.place(lax.axis_index("ctx"))
    head_dim = qs.shape[3]
    rows = per_device * BLOCK
    scaling = 1.0 / math.sqrt(head_dim)
    lanes = pl.ds(pl.multiple_of(h * head_dim, head_dim), head_dim)
    total[...] = jnp.zeros_like(total)
    for j in range(per_device):
        dv = jnp.dot(low_w[0, j], gs[0, j], preferred_element_type=F32)
        dk = jnp.dot(low_ds[0, j], qs[0, j], preferred_element_type=F32) * scaling
        own_at = (WDEV * per_device + j) * BLOCK
        for kv, part in enumerate((dk, dv)):
            total[kv, own_at : own_at + BLOCK, :] += part[0:BLOCK]
            for s in range(ns):
                total[kv, pl.ds(slash_rows(offs, h, j, s, per_device), BLOCK), :] += part[
                    (1 + s) * BLOCK : (2 + s) * BLOCK
                ]
    for kv in range(2):
        home[kv, :, lanes] = total[kv, WDEV * rows :, :]
        for part, d in zip(parts, distances(core)):
            at = pl.multiple_of((WDEV - d) * rows, rows)
            part[kv, :, lanes] = total[kv, pl.ds(at, rows), :].astype(part.dtype)


def window_gradients(offsets, qs, gs, low_w, low_ds, lines, nv):
    heads, per_device, deep, head_dim = qs.shape
    ns = offsets.shape[1]
    rows, features = per_device * BLOCK, heads * head_dim
    shard = (2, rows, features)
    whole = pl.BlockSpec(shard, lambda h: (0, 0, 0))
    stacked = pl.BlockSpec((1,) + qs.shape[1:], lambda h: (h, 0, 0, 0))
    tail = (1 + ns) * BLOCK
    low_tail = pl.BlockSpec((1, per_device, tail, deep), lambda h: (h, 0, 0, 0))
    low = pl.BlockSpec(
        (1, per_device, tail, deep), lambda h: (h, 0, nv * BLOCK // tail, 0)
    )
    return pl.pallas_call(
        functools.partial(window_kernel, lines=lines, ns=ns, per_device=per_device),
        grid=(heads,),
        in_specs=[pl.BlockSpec(memory_space=pltpu.SMEM), stacked, stacked, low_tail, low],
        out_specs=[whole] * (1 + WDEV),
        out_shape=[jax.ShapeDtypeStruct(shard, F32)] * 3 + [jax.ShapeDtypeStruct(shard, BF16)] * 3,
        scratch_shapes=[pltpu.VMEM((2, (WDEV + 1) * rows, head_dim), F32)],
        compiler_params=pltpu.CompilerParams(vmem_limit_bytes=VMEM_LIMIT),
        cost_estimate=pl.CostEstimate(flops=0, bytes_accessed=9 << 20, transcendentals=0),
    )(offsets, qs, gs, low_w, low_ds)


def query_kernel(cand_keys, low_ds, dq):
    per_device, _, head_dim = cand_keys.shape[1:]
    scaling = 1.0 / math.sqrt(head_dim)
    for j in range(per_device):
        turned = lax.dot_general(
            cand_keys[0, j], low_ds[0, j], (((0,), (0,)), ((), ())), preferred_element_type=F32
        )
        stacked = (jnp.transpose(turned) * scaling).astype(BF16)
        for g in range(dq.shape[1] // head_dim):
            dq[j * BLOCK : (j + 1) * BLOCK, g * head_dim : (g + 1) * head_dim] = stacked[
                g * BLOCK : (g + 1) * BLOCK, :
            ]


def query_gradients(cand_keys, low_ds):
    heads, per_device, keys, head_dim = cand_keys.shape
    deep = low_ds.shape[3]
    rows, width = per_device * BLOCK, deep // BLOCK * head_dim

    def by_head(shape):
        return pl.BlockSpec((1,) + shape[1:], lambda h: (h, 0, 0, 0))

    return pl.pallas_call(
        query_kernel,
        grid=(heads,),
        in_specs=[by_head(cand_keys.shape), by_head(low_ds.shape)],
        out_specs=pl.BlockSpec((rows, width), lambda h: (0, h)),
        out_shape=jax.ShapeDtypeStruct((rows, heads * width), BF16),
        compiler_params=pltpu.CompilerParams(vmem_limit_bytes=VMEM_LIMIT),
        cost_estimate=pl.CostEstimate(flops=0, bytes_accessed=10 << 20, transcendentals=0),
    )(cand_keys, low_ds)


def zeros_kernel(_, key_out, value_out, blank, sems):
    blank[...] = jnp.zeros_like(blank)
    copies = [
        pltpu.make_async_copy(blank, out.at[r], sems.at[n, r])
        for n, out in enumerate((key_out, value_out))
        for r in range(out.shape[0])
    ]
    for copy in copies:
        copy.start()
    for copy in copies:
        copy.wait()


def zeros(ahead, shape):
    hbm = pl.BlockSpec(memory_space=pltpu.HBM)
    return pl.pallas_call(
        zeros_kernel,
        in_specs=[pl.BlockSpec(memory_space=pl.ANY)],
        out_specs=[hbm] * 2,
        out_shape=[jax.ShapeDtypeStruct(shape, BF16)] * 2,
        scratch_shapes=[pltpu.VMEM(shape[1:], BF16), pltpu.SemaphoreType.DMA((2, shape[0]))],
        compiler_params=pltpu.CompilerParams(vmem_limit_bytes=VMEM_LIMIT),
        cost_estimate=pl.CostEstimate(flops=0, bytes_accessed=5 << 20, transcendentals=0),
    )(ahead)


def assemble_kernel(slab_index, verts, home, *rest, lines, heads, nv, per_device):
    from_near, arrived, gathered = rest[0], rest[1:3], rest[3:7]
    outs, vert, acc, low, sems, out_sems, unit_sems = rest[9:11], *rest[11:]
    slab, me = slab_index[0], lax.axis_index("ctx")
    _, near, _ = lines.place(me)
    devices = lines.devices
    chunk, head_dim = gathered[0].shape[1:]
    slab_blocks = per_device * devices
    copies = vertical_copies(lines, me, chunk, gathered, vert, sems, 0)
    for copy in copies:
        copy.start()
    acc[0] = home[...]
    acc[1] = jnp.zeros_like(home)

    @pl.when(near == 0)
    def _():
        acc[0] += from_near[...].astype(F32)

    for part, wrapped in zip(arrived, wraps(me, devices)):
        acc[wrapped.astype(jnp.int32)] += part[...].astype(F32)
    for copy in copies:
        copy.wait()

    def unit(h, m):
        inner = lax.rem(verts[h, m], slab_blocks)
        region = lax.div(verts[h, m], slab_blocks)
        row = pl.multiple_of(lax.rem(inner, per_device) * BLOCK, BLOCK)
        close = (region == slab) | (region == slab - 1)
        return lax.div(inner, per_device) == me, close, region, row

    def unit_copies(h, m, region, row):
        at = (h * nv + m) * BLOCK
        for kv in range(2):
            yield pltpu.make_async_copy(
                vert.at[kv, pl.ds(at, BLOCK), :],
                outs[kv].at[region, pl.ds(row, BLOCK), pl.ds(h * head_dim, head_dim)],
                unit_sems.at[kv, h * nv + m],
            )

    for h in range(heads):
        lanes = slice(h * head_dim, (h + 1) * head_dim)
        for m in range(nv):
            mine, close, region, row = unit(h, m)
            at = (h * nv + m) * BLOCK

            @pl.when(mine & close)
            def _():
                for kv in range(2):
                    acc[slab - region, kv, pl.ds(row, BLOCK), lanes] += vert[
                        kv, at : at + BLOCK, :
                    ].astype(F32)

            @pl.when(mine & jnp.logical_not(close))
            def _():
                for copy in unit_copies(h, m, region, row):
                    copy.start()

    low[...] = acc[...].astype(BF16)
    copies = [
        pltpu.make_async_copy(low.at[n, kv], outs[kv].at[slab - n], out_sems.at[n, kv])
        for n in range(2)
        for kv in range(2)
    ]
    for copy in copies:
        copy.start()
    for h in range(heads):
        for m in range(nv):
            mine, close, region, row = unit(h, m)

            @pl.when(mine & jnp.logical_not(close))
            def _():
                for copy in unit_copies(h, m, region, row):
                    copy.wait()

    for copy in copies:
        copy.wait()


def assemble(slab_index, verticals, home, from_near, arrived, gathered, blank, lines):
    _, rows, features = home.shape
    heads, nv = verticals.shape
    smem = pl.BlockSpec(memory_space=pltpu.SMEM)
    vmem = pl.BlockSpec(memory_space=pltpu.VMEM)
    anywhere = pl.BlockSpec(memory_space=pl.ANY)
    hbm = pl.BlockSpec(memory_space=pltpu.HBM)
    return pl.pallas_call(
        functools.partial(
            assemble_kernel, lines=lines, heads=heads, nv=nv, per_device=rows // BLOCK
        ),
        in_specs=[smem] * 2 + [vmem] * 4 + [anywhere] * 4 + [hbm] * 2,
        out_specs=[hbm] * 2,
        out_shape=[jax.ShapeDtypeStruct(blank[0].shape, BF16)] * 2,
        input_output_aliases={10: 0, 11: 1},
        scratch_shapes=[
            pltpu.VMEM((2, heads * nv * BLOCK, features // heads), BF16),
            pltpu.VMEM((2, 2, rows, features), F32),
            pltpu.VMEM((2, 2, rows, features), BF16),
            pltpu.SemaphoreType.DMA((4 * lines.far,)),
            pltpu.SemaphoreType.DMA((2, 2)),
            pltpu.SemaphoreType.DMA((2, heads * nv)),
        ],
        compiler_params=pltpu.CompilerParams(vmem_limit_bytes=VMEM_LIMIT),
    )(slab_index, verticals, home, from_near, *arrived, *gathered, *blank)


def shards(
    queries,
    context_keys,
    context_values,
    forward_output,
    output_cotangent,
    verticals,
    offsets,
    slab_index,
):
    lines = Lines(lax.axis_size("ctx"))
    heads, nv = verticals.shape
    head_dim = context_keys.shape[2] // heads
    _, near, _ = lines.place(lax.axis_index("ctx"))

    own, send4, mixed, mine, to_near, to_core, to_both = pack(
        slab_index, verticals, context_keys, context_values, lines
    )
    recv4 = move(send4, lines.shift_pairs(4))
    to_near = core_sum(lines, to_near, to_both)
    quarter = near_sum(lines, mine, to_near, to_core)
    prepared = prepare(after(queries, to_near), output_cotangent, forward_output, heads, head_dim)
    quarter = after(quarter, recv4, *prepared)
    share = far_sum(lines, quarter)
    recv2 = move(jnp.where(near == 1, recv4, own), lines.near_pairs())
    other4 = move(recv4, lines.core_pairs())
    blank = zeros(share, context_keys.shape)
    gathered = far_gather(lines, after(share, other4))
    other2 = move(recv2, lines.core_pairs())
    gathered = after(gathered, other2, *blank)
    recv_mixed = move(after(mixed, gathered), lines.mixed_pairs())
    gathered = plane_gather(lines, gathered)

    *shares, low_w, low_ds, cand_keys = attend(
        slab_index, verticals, offsets, prepared, context_keys, context_values, gathered,
        [recv2, recv4, recv_mixed, other2, other4], lines,
    )

    mine, to_near, to_core, to_both = shares
    to_near = core_sum(lines, to_near, to_both)
    home, part2, part4, mixed, give2, give4 = window_gradients(
        after(offsets, to_near), prepared[0], prepared[1], low_w, low_ds, lines, nv
    )
    arrived_mixed = move(mixed, back(lines.mixed_pairs()))
    quarter = near_sum(lines, mine, to_near, to_core)
    quarter = after(quarter, home)
    sum2 = (part2 + move(give2, lines.core_pairs()).astype(F32)).astype(BF16)
    sum4 = part4 + move(give4, lines.core_pairs()).astype(F32)
    from_near = move(after(sum2, quarter), lines.near_pairs())
    share = far_sum(lines, quarter)
    totals = after(far_gather(lines, share), from_near, arrived_mixed)
    sum4 = (sum4 + jnp.where(near == 1, from_near.astype(F32), 0.0)).astype(BF16)
    arrived4 = move(after(sum4, totals), back(lines.shift_pairs(4)))
    query_grad = query_gradients(after(cand_keys, totals), low_ds)
    totals = plane_gather(lines, totals)
    key_gradient, value_gradient = assemble(
        slab_index, verticals, after(home, query_grad), from_near, (arrived4, arrived_mixed),
        totals, blank, lines,
    )
    return query_grad, key_gradient, value_gradient


def solution(mesh):
    in_specs = (
        P(("groups", "ctx"), None),
        P("groups", "ctx", None),
        P("groups", "ctx", None),
        P(("groups", "ctx"), None),
        P(("groups", "ctx"), None),
        P("groups", None),
        P("groups", None),
        P("groups"),
    )
    out_specs = (P(("groups", "ctx"), None), P("groups", "ctx", None), P("groups", "ctx", None))
    return jax.shard_map(shards, mesh=mesh, in_specs=in_specs, out_specs=out_specs, check_vma=False)
```

time: 117 us -> 111 us (0.949)
  waiting for transfers between devices: 57.4 us -> 44.2 us
  starting transfers between devices: 23.7 us -> 28.6 us
  Pallas kernels: 26.7 us -> 31.3 us
  local copies, waits for them, and re-layouts: 2.38 us -> 0.07 us
    ppermute x34, waiting for transfers between devices: 57.4 us -> 44.2 us  [move(): return lax.ppermute(array, 'ctx', pairs)]
    pallas_call x0 -> x4, Pallas kernels: none -> 9.54 us  [the longest x1 2.93 us: query_gradients(): pl.pallas_call(query_kernel, grid=(heads,), in_specs=[by_head(cand_keys.s...]
    ppermute x34, starting transfers between devices: 23.7 us -> 28.6 us  [move(): return lax.ppermute(array, 'ctx', pairs)]
    pallas_call x1, Pallas kernels: 17.3 us -> 13 us  [attend(): pl.pallas_call(functools.partial(attend_kernel, lines=lines, heads=heads,...]
    unnamed x40 -> x18, local copies, waits for them, and re-layouts: 2.35 us -> 0.04 us
  transfers between devices with their start and end apart: 34 -> 34, of which waited for: 18 -> 16; matrix products, arithmetic and copies ran while one was open for 4% -> 4% of each run, Pallas kernels for 0% -> 9%
where the time goes in v8:
time: 111 us; the launch traced here: 110 us
  waiting for transfers between devices  44.2 us (40%)
  Pallas kernels  31.3 us (28%)
  starting transfers between devices  28.6 us (26%)
  other arithmetic  4.55 us (4%)
  between operations  1.58 us (1%)
    ppermute x34, waiting for transfers between devices, move(): return lax.ppermute(array, 'ctx', pairs)  44.2 us
    ppermute x34, starting transfers between devices, move(): return lax.ppermute(array, 'ctx', pairs)  28.6 us
    pallas_call x1, Pallas kernels, attend(): pl.pallas_call(functools.partial(attend_kernel, lines=lines, heads=heads,...  13 us
    pallas_call x1, Pallas kernels, assemble(): pl.pallas_call(functools.partial(assemble_kernel, lines=lines, heads=head...  4.42 us
    pallas_call x1, Pallas kernels, pack(): pl.pallas_call(functools.partial(pack_kernel, lines=lines, heads=heads, n...  4.3 us
    pallas_call x1, Pallas kernels, query_gradients(): pl.pallas_call(query_kernel, grid=(heads,), in_specs=[by_head(cand_keys.s...  2.93 us
    pallas_call x1, Pallas kernels, window_gradients(): pl.pallas_call(functools.partial(window_kernel, lines=lines, ns=ns, per_d...  2.89 us
    pallas_call x1, Pallas kernels, zeros(): pl.pallas_call(zeros_kernel, in_specs=[pl.BlockSpec(memory_space=pl.ANY)]...  2.27 us
  transfers between devices with their start and end apart: 34, of which 16 were waited for; matrix products, arithmetic and copies ran while one was open for 4% of the time, Pallas kernels for 9%

profile of v8, /device:TPU:0, one launch (start us, length us, event | category | flops | bytes accessed | tf_op | source)
XLA Modules:
  0.0 110.4 jit_solution(3394841791518302543)
XLA Ops:
  1.3 4.3 %shard_map.103 = (bf16[2,128,512]{2,1,0:T(8,128)(2,1)}, bf16[2,128,512]{2,1,0:T(8,128)(2,1)}, bf16[2,128,512]{2,1,0:T(8,128)(2,1)}, bf16[4,256,128]{2,1,0:T(8,12...) custom-call(s32[1]{0:T(128)S(6)} %copy.15.slab_index, ...), custom_call_target="tpu_custom_call" | custom-call | tf_op jit(solution)/shard_map/pallas_call | solution.py:166
  6.2 2.6 %collective-permute-start.3 = (bf16[2,128,512]{2,1,0:T(8,128)(2,1)}, bf16[2,128,512]{2,1,0:T(8,128)(2,1)S(1)}, u32[]{:S(2)}, u32[]{:S(2)}) collective-permute-start(bf16[2,128,512]{2,1,0:T(8,128)(2,1)} %get-tuple-element.54), channel_id=1, source_target_pairs={{0,4},{1,5},{2,6},{3,7},{4,8},{5,9},{6,10},{7,11},{8,12},{9,13},{1... | collective-permute-start | bytes 786440 | tf_op jit(solution)/shard_map/ppermute | solution.py:52
  12.2 5.8 %collective-permute-done.3.rest_5_ = bf16[2,128,512]{2,1,0:T(8,128)(2,1)S(1)} collective-permute-done((bf16[2,128,512]{2,1,0:T(8,128)(2,1)}, bf16[2,128,512]{2,1,0:T(8,128)(2,1)S(1)}, u32[]{:S(2)}, u32[]{:S(2)}) %collective-permute-start.3) | collective-permute-done | bytes 262176 | tf_op jit(solution)/shard_map/ppermute | solution.py:52
  22.6 3.7 %collective-permute-start.6 = (bf16[256,128]{1,0:T(8,128)(2,1)S(1)}, bf16[256,128]{1,0:T(8,128)(2,1)S(1)}, u32[]{:S(2)}, u32[]{:S(2)}) collective-permute-start(bf16[256,128]{1,0:T(8,128)(2,1)S(1)} %get-tuple-element.89), channel_id=1, source_target_pairs={{0,12},{1,13},{2,14},{3,15},{4,0},{5,1},{6,2},{7,3},{8,4},{9,5},{1... | collective-permute-start | bytes 196616 | tf_op jit(solution)/shard_map/ppermute | solution.py:52
  27.1 2.1 %collective-permute-done.4 = bf16[256,128]{1,0:T(8,128)(2,1)S(1)} collective-permute-done((bf16[256,128]{1,0:T(8,128)(2,1)S(1)}, bf16[256,128]{1,0:T(8,128)(2,1)S(1)}, u32[]{:S(2)}, u32[]{:S(2)}) %collective-permute-start.4) | collective-permute-done | bytes 65568 | tf_op jit(solution)/shard_map/ppermute | solution.py:52
  29.2 2.2 %collective-permute-done.5 = bf16[256,128]{1,0:T(8,128)(2,1)S(1)} collective-permute-done((bf16[256,128]{1,0:T(8,128)(2,1)S(1)}, bf16[256,128]{1,0:T(8,128)(2,1)S(1)}, u32[]{:S(2)}, u32[]{:S(2)}) %collective-permute-start.5) | collective-permute-done | bytes 65568 | tf_op jit(solution)/shard_map/ppermute | solution.py:52
  31.5 2.0 %collective-permute-start.10 = (bf16[256,128]{1,0:T(8,128)(2,1)S(1)}, bf16[256,128]{1,0:T(8,128)(2,1)S(1)}, u32[]{:S(2)}, u32[]{:S(2)}) collective-permute-start(bf16[256,128]{1,0:T(8,128)(2,1)S(1)} %fusion.5._), channel_id=1, source_target_pairs={{0,12},{1,13},{2,14},{3,15},{4,0},{5,1},{6,2},{7,3},{8,4},{9,5},{1... | collective-permute-start | bytes 196616 | tf_op jit(solution)/shard_map/ppermute | solution.py:52
  34.3 2.3 %shard_map.105 = (bf16[16,128,512]{2,1,0:T(8,128)(2,1)}, bf16[16,128,512]{2,1,0:T(8,128)(2,1)}) custom-call(bf16[256,128]{1,0:T(8,128)(2,1)S(1)} %fusion.5._), custom_call_target="tpu_custom_call" | custom-call | bytes 5242880 | tf_op jit(solution)/shard_map/pallas_call | solution.py:531
  36.6 2.3 %collective-permute-done.9 = bf16[256,128]{1,0:T(8,128)(2,1)S(1)} collective-permute-done((bf16[256,128]{1,0:T(8,128)(2,1)S(1)}, bf16[256,128]{1,0:T(8,128)(2,1)S(1)}, u32[]{:S(2)}, u32[]{:S(2)}) %collective-permute-start.9) | collective-permute-done | bytes 65568 | tf_op jit(solution)/shard_map/ppermute | solution.py:52
  42.0 6.2 %collective-permute-done.13.rest_1_ = bf16[4,256,128]{2,1,0:T(8,128)(2,1)S(1)} collective-permute-done((bf16[4,256,128]{2,1,0:T(8,128)(2,1)S(1)}, bf16[4,256,128]{2,1,0:T(8,128)(2,1)S(1)}, u32[]{:S(2)}, u32[]{:S(2)}) %collective-permute-start.13) | collective-permute-done | bytes 262176 | tf_op jit(solution)/shard_map/ppermute | solution.py:52
  48.2 2.7 %collective-permute-done.16.rest_6_ = bf16[2,128,512]{2,1,0:T(8,128)(2,1)S(1)} collective-permute-done((bf16[2,128,512]{2,1,0:T(8,128)(2,1)S(1)}, bf16[2,128,512]{2,1,0:T(8,128)(2,1)S(1)}, u32[]{:S(2)}, u32[]{:S(2)}) %collective-permute-start.16) | collective-permute-done | bytes 262176 | tf_op jit(solution)/shard_map/ppermute | solution.py:52
  51.0 13.0 %shard_map.106 = (f32[4,256,128]{2,1,0:T(8,128)S(1)}, bf16[4,256,128]{2,1,0:T(8,128)(2,1)S(1)}, bf16[4,256,128]{2,1,0:T(8,128)(2,1)S(1)}, bf16[4,256,128]{2,1,0:...) custom-call(s32[1]{0:T(128)S(6)} %copy.15.slab_index, ...), custom_call_target="tpu_custom_call" | custom-call | tf_op jit(solution)/shard_map/pallas_call | solution.py:402
  67.0 2.9 %shard_map.107 = (f32[2,128,512]{2,1,0:T(8,128)S(1)}, f32[2,128,512]{2,1,0:T(8,128)S(1)}, f32[2,128,512]{2,1,0:T(8,128)S(1)}, bf16[2,128,512]{2,1,0:T(8,128)(2,1...) custom-call(s32[4,3]{1,0:T(4,128)S(1)} %copy-done.6, ...), custom_call_target="tpu_custom_call" | custom-call | bytes 9437184 | tf_op jit(solution)/shard_map/pallas_call | solution.py:471
  71.5 2.6 %collective-permute-done.19 = bf16[4,256,128]{2,1,0:T(8,128)(2,1)S(1)} collective-permute-done((bf16[4,256,128]{2,1,0:T(8,128)(2,1)S(1)}, bf16[4,256,128]{2,1,0:T(8,128)(2,1)S(1)}, u32[]{:S(2)}, u32[]{:S(2)}) %collective-permute-start.19) | collective-permute-done | bytes 262176 | tf_op jit(solution)/shard_map/ppermute | solution.py:52
  74.3 3.8 %collective-permute-start.22 = (bf16[256,128]{1,0:T(8,128)(2,1)S(1)}, bf16[256,128]{1,0:T(8,128)(2,1)S(1)}, u32[]{:S(2)}, u32[]{:S(2)}) collective-permute-start(bf16[256,128]{1,0:T(8,128)(2,1)S(1)} %get-tuple-element.86), channel_id=1, source_target_pairs={{0,12},{1,13},{2,14},{3,15},{4,0},{5,1},{6,2},{7,3},{8,4},{9,5},{1... | collective-permute-start | bytes 196616 | tf_op jit(solution)/shard_map/ppermute | solution.py:52
  78.2 2.7 %collective-permute-done.20 = bf16[256,128]{1,0:T(8,128)(2,1)S(1)} collective-permute-done((bf16[256,128]{1,0:T(8,128)(2,1)S(1)}, bf16[256,128]{1,0:T(8,128)(2,1)S(1)}, u32[]{:S(2)}, u32[]{:S(2)}) %collective-permute-start.20) | collective-permute-done | bytes 65568 | tf_op jit(solution)/shard_map/ppermute | solution.py:52
  82.2 2.8 %collective-permute-done.21 = bf16[256,128]{1,0:T(8,128)(2,1)S(1)} collective-permute-done((bf16[256,128]{1,0:T(8,128)(2,1)S(1)}, bf16[256,128]{1,0:T(8,128)(2,1)S(1)}, u32[]{:S(2)}, u32[]{:S(2)}) %collective-permute-start.21) | collective-permute-done | bytes 65568 | tf_op jit(solution)/shard_map/ppermute | solution.py:52
  85.0 3.1 %collective-permute-start.25 = (bf16[256,128]{1,0:T(8,128)(2,1)S(1)}, bf16[256,128]{1,0:T(8,128)(2,1)S(1)}, u32[]{:S(2)}, u32[]{:S(2)}) collective-permute-start(bf16[256,128]{1,0:T(8,128)(2,1)S(1)} %fusion.2), channel_id=1, source_target_pairs={{0,12},{1,13},{2,14},{3,15},{4,0},{5,1},{6,2},{7,3},{8,4},{9,5},{1... | collective-permute-start | bytes 196616 | tf_op jit(solution)/shard_map/ppermute | solution.py:52
  90.2 3.1 %collective-permute-done.24 = bf16[256,128]{1,0:T(8,128)(2,1)S(1)} collective-permute-done((bf16[256,128]{1,0:T(8,128)(2,1)S(1)}, bf16[256,128]{1,0:T(8,128)(2,1)S(1)}, u32[]{:S(2)}, u32[]{:S(2)}) %collective-permute-start.24) | collective-permute-done | bytes 65568 | tf_op jit(solution)/shard_map/ppermute | solution.py:52
  93.3 3.2 %collective-permute-done.23 = bf16[256,128]{1,0:T(8,128)(2,1)S(1)} collective-permute-done((bf16[256,128]{1,0:T(8,128)(2,1)S(1)}, bf16[256,128]{1,0:T(8,128)(2,1)S(1)}, u32[]{:S(2)}, u32[]{:S(2)}) %collective-permute-start.23) | collective-permute-done | bytes 65568 | tf_op jit(solution)/shard_map/ppermute | solution.py:52
  97.0 2.1 %collective-permute-start.30 = (bf16[2,128,512]{2,1,0:T(8,128)(2,1)S(1)}, bf16[2,128,512]{2,1,0:T(8,128)(2,1)S(1)}, u32[]{:S(2)}, u32[]{:S(2)}) collective-permute-start(bf16[2,128,512]{2,1,0:T(8,128)(2,1)S(1)} %add_convert_fusion), channel_id=1, source_target_pairs={{4,0},{5,1},{6,2},{7,3},{8,4},{9,5},{10,6},{11,7},{12,8},{13,9},{1... | collective-permute-start | bytes 786440 | tf_op jit(solution)/shard_map/ppermute | solution.py:52
  99.1 3.9 %collective-permute-done.31.rest_4_ = bf16[4,256,128]{2,1,0:T(8,128)(2,1)S(1)} collective-permute-done((bf16[4,256,128]{2,1,0:T(8,128)(2,1)S(1)}, bf16[4,256,128]{2,1,0:T(8,128)(2,1)S(1)}, u32[]{:S(2)}, u32[]{:S(2)}) %collective-permute-start.31) | collective-permute-done | bytes 262176 | tf_op jit(solution)/shard_map/ppermute | solution.py:52
  103.0 2.9 %shard_map.108 = bf16[128,4096]{1,0:T(8,128)(2,1)} custom-call(bf16[4,2,768,128]{3,2,1,0:T(8,128)(2,1)S(1)} %get-tuple-element.78.cand_keys, bf16[4,2,768,512]{3,2,1,0:T(8,128)(2,1)S(1)} %get-tuple-element.70.low_ds), custom_call_target="tpu_custom_call" | custom-call | bytes 10485760 | tf_op jit(solution)/shard_map/pallas_call | solution.py:505
  105.9 4.4 %shard_map.109 = (bf16[16,128,512]{2,1,0:T(8,128)(2,1)}, bf16[16,128,512]{2,1,0:T(8,128)(2,1)}) custom-call(s32[1]{0:T(128)S(6)} %copy.15.slab_index, s32[4,8]{1,0:T(4,128)S(1)} %copy-done.5, f32[2,128,512]{2,1,0:T(8,128)S(1)} %get-tuple-element.79.home, ...), custom_call_target="tpu_custom_call", output_to_operand_aliasing={{0}: (10, {}), {1}: (11, {})} | custom-call | tf_op jit(solution)/shard_map/pallas_call | solution.py:627
  (84 shorter events, 22.0 us)
Async XLA Ops:
  6.2 11.8 %collective-permute-start.3 = (bf16[2,128,512]{2,1,0:T(8,128)(2,1)}, bf16[2,128,512]{2,1,0:T(8,128)(2,1)S(1)}, u32[]{:S(2)}, u32[]{:S(2)}) collective-permute-start(bf16[2,128,512]{2,1,0:T(8,128)(2,1)} %get-tuple-element.54), channel_id=1, source_target_pairs={{0,4},{1,5},{2,6},{3,7},{4,8},{5,9},{6,10},{7,11},{8,12},{9,13},{1... | collective-permute-start | bytes 786440 | tf_op jit(solution)/shard_map/ppermute | solution.py:52
  8.8 12.2 %collective-permute-start.1 = (bf16[4,256,128]{2,1,0:T(8,128)(2,1)}, bf16[4,256,128]{2,1,0:T(8,128)(2,1)}, u32[]{:S(2)}, u32[]{:S(2)}) collective-permute-start(bf16[4,256,128]{2,1,0:T(8,128)(2,1)} %get-tuple-element.53), channel_id=1, source_target_pairs={{0,1},{1,0},{2,3},{3,2},{4,5},{5,4},{6,7},{7,6},{8,9},{9,8},{10,11... | collective-permute-start | bytes 786440 | tf_op jit(solution)/shard_map/ppermute | solution.py:52
  10.7 10.4 %collective-permute-start.2 = (bf16[4,256,128]{2,1,0:T(8,128)(2,1)}, bf16[4,256,128]{2,1,0:T(8,128)(2,1)}, u32[]{:S(2)}, u32[]{:S(2)}) collective-permute-start(bf16[4,256,128]{2,1,0:T(8,128)(2,1)} %add_convert_fusion.3), channel_id=1, source_target_pairs={{0,2},{1,3},{2,0},{3,1},{4,6},{5,7},{6,4},{7,5},{8,10},{9,11},{10,... | collective-permute-start | bytes 786440 | tf_op jit(solution)/shard_map/ppermute | solution.py:52
  19.0 8.1 %collective-permute-start.11 = (bf16[2,128,512]{2,1,0:T(8,128)(2,1)S(1)}, bf16[2,128,512]{2,1,0:T(8,128)(2,1)S(1)}, u32[]{:S(2)}, u32[]{:S(2)}) collective-permute-start(bf16[2,128,512]{2,1,0:T(8,128)(2,1)S(1)} %broadcast_select_fusion), channel_id=1, source_target_pairs={{0,2},{1,3},{2,0},{3,1},{4,6},{5,7},{6,4},{7,5},{8,10},{9,11},{10,... | collective-permute-start | bytes 786440 | tf_op jit(solution)/shard_map/ppermute | solution.py:52
  22.4 6.8 %collective-permute-start.4 = (bf16[256,128]{1,0:T(8,128)(2,1)S(1)}, bf16[256,128]{1,0:T(8,128)(2,1)S(1)}, u32[]{:S(2)}, u32[]{:S(2)}) collective-permute-start(bf16[256,128]{1,0:T(8,128)(2,1)S(1)} %get-tuple-element.88), channel_id=1, source_target_pairs={{0,4},{1,5},{2,6},{3,7},{4,8},{5,9},{6,10},{7,11},{8,12},{9,13},{1... | collective-permute-start | bytes 196616 | tf_op jit(solution)/shard_map/ppermute | solution.py:52
  22.6 6.6 %collective-permute-start.6 = (bf16[256,128]{1,0:T(8,128)(2,1)S(1)}, bf16[256,128]{1,0:T(8,128)(2,1)S(1)}, u32[]{:S(2)}, u32[]{:S(2)}) collective-permute-start(bf16[256,128]{1,0:T(8,128)(2,1)S(1)} %get-tuple-element.89), channel_id=1, source_target_pairs={{0,12},{1,13},{2,14},{3,15},{4,0},{5,1},{6,2},{7,3},{8,4},{9,5},{1... | collective-permute-start | bytes 196616 | tf_op jit(solution)/shard_map/ppermute | solution.py:52
  27.1 12.5 %collective-permute-start.12 = (bf16[2,128,512]{2,1,0:T(8,128)(2,1)S(1)}, bf16[2,128,512]{2,1,0:T(8,128)(2,1)S(1)}, u32[]{:S(2)}, u32[]{:S(2)}) collective-permute-start(bf16[2,128,512]{2,1,0:T(8,128)(2,1)S(1)} %collective-permute-done.11.rest_4_), channel_id=1, source_target_pairs={{0,1},{1,0},{2,3},{3,2},{4,5},{5,4},{6,7},{7,6},{8,9},{9,8},{10,11... | collective-permute-start | bytes 786440 | tf_op jit(solution)/shard_map/ppermute | solution.py:52
  33.5 6.1 %collective-permute-start.8 = (bf16[256,128]{1,0:T(8,128)(2,1)S(1)}, bf16[256,128]{1,0:T(8,128)(2,1)S(1)}, u32[]{:S(2)}, u32[]{:S(2)}) collective-permute-start(bf16[256,128]{1,0:T(8,128)(2,1)S(1)} %fusion.5._), channel_id=1, source_target_pairs={{0,4},{1,5},{2,6},{3,7},{4,8},{5,9},{6,10},{7,11},{8,12},{9,13},{1... | collective-permute-start | bytes 196616 | tf_op jit(solution)/shard_map/ppermute | solution.py:52
  39.6 8.6 %collective-permute-start.13 = (bf16[4,256,128]{2,1,0:T(8,128)(2,1)S(1)}, bf16[4,256,128]{2,1,0:T(8,128)(2,1)S(1)}, u32[]{:S(2)}, u32[]{:S(2)}) collective-permute-start(bf16[4,256,128]{2,1,0:T(8,128)(2,1)S(1)} %pad_maximum_fusion.rest_0_), channel_id=1, source_target_pairs={{0,2},{1,3},{2,0},{3,1},{4,6},{5,7},{6,4},{7,5},{8,10},{9,11},{10,... | collective-permute-start | bytes 786440 | tf_op jit(solution)/shard_map/ppermute | solution.py:52
  41.5 9.4 %collective-permute-start.14 = (bf16[4,256,128]{2,1,0:T(8,128)(2,1)S(1)}, bf16[4,256,128]{2,1,0:T(8,128)(2,1)S(1)}, u32[]{:S(2)}, u32[]{:S(2)}) collective-permute-start(bf16[4,256,128]{2,1,0:T(8,128)(2,1)S(1)} %pad_maximum_fusion.rest_0_), channel_id=1, source_target_pairs={{0,1},{1,0},{2,3},{3,2},{4,5},{5,4},{6,7},{7,6},{8,9},{9,8},{10,11... | collective-permute-start | bytes 786440 | tf_op jit(solution)/shard_map/ppermute | solution.py:52
  41.5 9.4 %collective-permute-start.16 = (bf16[2,128,512]{2,1,0:T(8,128)(2,1)S(1)}, bf16[2,128,512]{2,1,0:T(8,128)(2,1)S(1)}, u32[]{:S(2)}, u32[]{:S(2)}) collective-permute-start(bf16[2,128,512]{2,1,0:T(8,128)(2,1)S(1)} %copy-done.8), channel_id=1, source_target_pairs={{0,1},{1,6},{2,3},{3,8},{4,5},{5,10},{6,7},{7,12},{8,9},{9,14},{10... | collective-permute-start | bytes 786440 | tf_op jit(solution)/shard_map/ppermute | solution.py:52
  64.1 7.4 %collective-permute-start.17 = (bf16[4,256,128]{2,1,0:T(8,128)(2,1)S(1)}, bf16[4,256,128]{2,1,0:T(8,128)(2,1)S(1)}, u32[]{:S(2)}, u32[]{:S(2)}) collective-permute-start(bf16[4,256,128]{2,1,0:T(8,128)(2,1)S(1)} %get-tuple-element.65), channel_id=1, source_target_pairs={{0,1},{1,0},{2,3},{3,2},{4,5},{5,4},{6,7},{7,6},{8,9},{9,8},{10,11... | collective-permute-start | bytes 786440 | tf_op jit(solution)/shard_map/ppermute | solution.py:52
  65.7 8.4 %collective-permute-start.19 = (bf16[4,256,128]{2,1,0:T(8,128)(2,1)S(1)}, bf16[4,256,128]{2,1,0:T(8,128)(2,1)S(1)}, u32[]{:S(2)}, u32[]{:S(2)}) collective-permute-start(bf16[4,256,128]{2,1,0:T(8,128)(2,1)S(1)} %add_convert_fusion.2), channel_id=1, source_target_pairs={{0,2},{1,3},{2,0},{3,1},{4,6},{5,7},{6,4},{7,5},{8,10},{9,11},{10,... | collective-permute-start | bytes 786440 | tf_op jit(solution)/shard_map/ppermute | solution.py:52
  69.9 8.2 %collective-permute-start.26 = (bf16[2,128,512]{2,1,0:T(8,128)(2,1)S(1)}, bf16[2,128,512]{2,1,0:T(8,128)(2,1)S(1)}, u32[]{:S(2)}, u32[]{:S(2)}) collective-permute-start(bf16[2,128,512]{2,1,0:T(8,128)(2,1)S(1)} %get-tuple-element.74), channel_id=1, source_target_pairs={{0,1},{1,0},{2,3},{3,2},{4,5},{5,4},{6,7},{7,6},{8,9},{9,8},{10,11... | collective-permute-start | bytes 786440 | tf_op jit(solution)/shard_map/ppermute | solution.py:52
  70.0 26.6 %collective-permute-start.28 = (bf16[2,128,512]{2,1,0:T(8,128)(2,1)S(1)}, bf16[2,128,512]{2,1,0:T(8,128)(2,1)S(1)}, u32[]{:S(2)}, u32[]{:S(2)}) collective-permute-start(bf16[2,128,512]{2,1,0:T(8,128)(2,1)S(1)} %get-tuple-element.76), channel_id=1, source_target_pairs={{1,0},{6,1},{3,2},{8,3},{5,4},{10,5},{7,6},{12,7},{9,8},{14,9},{11... | collective-permute-start | bytes 786440 | tf_op jit(solution)/shard_map/ppermute | solution.py:52
  71.5 25.4 %collective-permute-start.29 = (bf16[2,128,512]{2,1,0:T(8,128)(2,1)S(1)}, bf16[2,128,512]{2,1,0:T(8,128)(2,1)S(1)}, u32[]{:S(2)}, u32[]{:S(2)}) collective-permute-start(bf16[2,128,512]{2,1,0:T(8,128)(2,1)S(1)} %get-tuple-element.81), channel_id=1, source_target_pairs={{0,1},{1,0},{2,3},{3,2},{4,5},{5,4},{6,7},{7,6},{8,9},{9,8},{10,11... | collective-permute-start | bytes 786440 | tf_op jit(solution)/shard_map/ppermute | solution.py:52
  74.2 6.7 %collective-permute-start.20 = (bf16[256,128]{1,0:T(8,128)(2,1)S(1)}, bf16[256,128]{1,0:T(8,128)(2,1)S(1)}, u32[]{:S(2)}, u32[]{:S(2)}) collective-permute-start(bf16[256,128]{1,0:T(8,128)(2,1)S(1)} %get-tuple-element.85), channel_id=1, source_target_pairs={{0,4},{1,5},{2,6},{3,7},{4,8},{5,9},{6,10},{7,11},{8,12},{9,13},{1... | collective-permute-start | bytes 196616 | tf_op jit(solution)/shard_map/ppermute | solution.py:52
  74.3 7.9 %collective-permute-start.22 = (bf16[256,128]{1,0:T(8,128)(2,1)S(1)}, bf16[256,128]{1,0:T(8,128)(2,1)S(1)}, u32[]{:S(2)}, u32[]{:S(2)}) collective-permute-start(bf16[256,128]{1,0:T(8,128)(2,1)S(1)} %get-tuple-element.86), channel_id=1, source_target_pairs={{0,12},{1,13},{2,14},{3,15},{4,0},{5,1},{6,2},{7,3},{8,4},{9,5},{1... | collective-permute-start | bytes 196616 | tf_op jit(solution)/shard_map/ppermute | solution.py:52
  78.1 6.9 %collective-permute-start.21 = (bf16[256,128]{1,0:T(8,128)(2,1)S(1)}, bf16[256,128]{1,0:T(8,128)(2,1)S(1)}, u32[]{:S(2)}, u32[]{:S(2)}) collective-permute-start(bf16[256,128]{1,0:T(8,128)(2,1)S(1)} %get-tuple-element.87), channel_id=1, source_target_pairs={{0,8},{1,9},{2,10},{3,11},{4,12},{5,13},{6,14},{7,15},{8,0},{9,1},... | collective-permute-start | bytes 196616 | tf_op jit(solution)/shard_map/ppermute | solution.py:52
  80.9 15.7 %collective-permute-start.27 = (bf16[2,128,512]{2,1,0:T(8,128)(2,1)S(1)}, bf16[2,128,512]{2,1,0:T(8,128)(2,1)S(1)}, u32[]{:S(2)}, u32[]{:S(2)}) collective-permute-start(bf16[2,128,512]{2,1,0:T(8,128)(2,1)S(1)} %add_convert_fusion.1), channel_id=1, source_target_pairs={{0,2},{1,3},{2,0},{3,1},{4,6},{5,7},{6,4},{7,5},{8,10},{9,11},{10,... | collective-permute-start | bytes 786440 | tf_op jit(solution)/shard_map/ppermute | solution.py:52
  90.0 6.5 %collective-permute-start.23 = (bf16[256,128]{1,0:T(8,128)(2,1)S(1)}, bf16[256,128]{1,0:T(8,128)(2,1)S(1)}, u32[]{:S(2)}, u32[]{:S(2)}) collective-permute-start(bf16[256,128]{1,0:T(8,128)(2,1)S(1)} %fusion.2), channel_id=1, source_target_pairs={{0,4},{1,5},{2,6},{3,7},{4,8},{5,9},{6,10},{7,11},{8,12},{9,13},{1... | collective-permute-start | bytes 196616 | tf_op jit(solution)/shard_map/ppermute | solution.py:52
  96.6 6.4 %collective-permute-start.31 = (bf16[4,256,128]{2,1,0:T(8,128)(2,1)S(1)}, bf16[4,256,128]{2,1,0:T(8,128)(2,1)S(1)}, u32[]{:S(2)}, u32[]{:S(2)}) collective-permute-start(bf16[4,256,128]{2,1,0:T(8,128)(2,1)S(1)} %pad_maximum_fusion.1.rest_3_), channel_id=1, source_target_pairs={{0,2},{1,3},{2,0},{3,1},{4,6},{5,7},{6,4},{7,5},{8,10},{9,11},{10,... | collective-permute-start | bytes 786440 | tf_op jit(solution)/shard_map/ppermute | solution.py:52
  96.9 9.1 %collective-permute-start.32 = (bf16[4,256,128]{2,1,0:T(8,128)(2,1)S(1)}, bf16[4,256,128]{2,1,0:T(8,128)(2,1)S(1)}, u32[]{:S(2)}, u32[]{:S(2)}) collective-permute-start(bf16[4,256,128]{2,1,0:T(8,128)(2,1)S(1)} %pad_maximum_fusion.1.rest_3_), channel_id=1, source_target_pairs={{0,1},{1,0},{2,3},{3,2},{4,5},{5,4},{6,7},{7,6},{8,9},{9,8},{10,11... | collective-permute-start | bytes 786440 | tf_op jit(solution)/shard_map/ppermute | solution.py:52
  97.0 8.9 %collective-permute-start.30 = (bf16[2,128,512]{2,1,0:T(8,128)(2,1)S(1)}, bf16[2,128,512]{2,1,0:T(8,128)(2,1)S(1)}, u32[]{:S(2)}, u32[]{:S(2)}) collective-permute-start(bf16[2,128,512]{2,1,0:T(8,128)(2,1)S(1)} %add_convert_fusion), channel_id=1, source_target_pairs={{4,0},{5,1},{6,2},{7,3},{8,4},{9,5},{10,6},{11,7},{12,8},{13,9},{1... | collective-permute-start | bytes 786440 | tf_op jit(solution)/shard_map/ppermute | solution.py:52
  (19 other events, 246.9 us)

commit v9 on v8

--- a/solution.py
+++ b/solution.py
@@ -11,7 +11,7 @@
 BLOCK = 64
 WDEV = 5
 VMEM_LIMIT = 32 * 1024 * 1024
-MOST_VMEM = 60 * 1024 * 1024
+PACK_VMEM = 52 * 1024 * 1024
 JOIN = 4
 BF16 = jnp.bfloat16
 F32 = jnp.float32
@@ -60,16 +60,18 @@
     return (to_near.astype(F32) + move(to_both, lines.core_pairs()).astype(F32)).astype(BF16)
 
 
-def near_sum(lines, mine, to_near, to_core):
-    from_near = move(to_near, lines.near_pairs())
+def near_sum(lines, mine, from_near, to_core):
     from_core = move(to_core, lines.core_pairs())
     return mine.astype(F32) + from_core.astype(F32) + from_near.astype(F32)
 
 
 def far_sum(lines, quarter):
+    parts = [
+        move(quarter[by].astype(BF16), lines.far_pairs(by)) for by in range(1, lines.far)
+    ]
     share = quarter[0]
-    for by in range(1, lines.far):
-        share = share + move(quarter[by].astype(BF16), lines.far_pairs(by)).astype(F32)
+    for part in parts:
+        share = share + part.astype(F32)
     return share.astype(BF16)
 
 
@@ -174,7 +176,7 @@
             pltpu.SemaphoreType.DMA((3, 2)),
             pltpu.SemaphoreType.DMA((2, heads * nv * max(1, BLOCK // chunk))),
         ],
-        compiler_params=pltpu.CompilerParams(vmem_limit_bytes=MOST_VMEM),
+        compiler_params=pltpu.CompilerParams(vmem_limit_bytes=PACK_VMEM),
     )(slab_index, verticals, keys, values)
 
 
@@ -182,12 +184,10 @@
     return [2, 4, 5 - 4 * core, 1 + 2 * core, 3 + 2 * core]
 
 
-def vertical_copies(lines, me, chunk, gathered, to, sems, first):
-    far, near, core = lines.place(me)
+def vertical_copies(lines, me, line, chunk, gathered, to, sems, first):
+    far, _, core = lines.place(me)
     copies = []
-    for n, source in enumerate(gathered):
-        kv = core if n < 2 else 1 - core
-        line = near if n % 2 == 0 else 1 - near
+    for kv, source in zip((core, 1 - core), gathered):
         for s in range(lines.far):
             slot = lax.rem(far - s + lines.far, lines.far)
             row = pl.multiple_of((line * lines.far + slot) * chunk, chunk)
@@ -255,46 +255,52 @@
 
 
 def attend_kernel(
-    slab_index, verts, offs, qs, gs, qt, gt, delta, keys, values, *rest,
-    lines, heads, nv, ns, per_device,
+    base, slab_index, verts, offs, qs, gs, qt, gt, delta, keys, values, *rest,
+    lines, nv, ns, per_device, continued,
 ):
-    gathered, recv, rest = rest[:4], rest[4 : 4 + WDEV], rest[4 + WDEV :]
-    shares, low_w, low_ds, cand_keys = rest[:4], rest[4], rest[5], rest[6]
-    win, vkv, vc, s_ref, vert_w, sems = rest[7:]
-    h = pl.program_id(0)
+    gathered, recv, rest = rest[:2], rest[2 : 2 + WDEV], rest[2 + WDEV :]
+    rest = rest[3:] if continued else rest
+    (share, give, low_w, low_ds, cand_keys), scratch = rest[:5], rest[5:]
+    win, vkv, vc, s_ref, vert_w, hold, sems = scratch
+    i = pl.program_id(0)
+    h = base[0] + i
     slab, me = slab_index[0], lax.axis_index("ctx")
     far, near, core = lines.place(me)
-    _, chunk, head_dim = shares[0].shape
+    _, chunk, head_dim = share.shape
     cand = nv + 1 + ns
     scaling = 1.0 / math.sqrt(head_dim)
     rows = per_device * BLOCK
     width = qs.shape[2]
     first_block = slab * (per_device * lines.devices) + me * per_device
-    lanes = pl.ds(pl.multiple_of(h * head_dim, head_dim), head_dim)
+    lanes = pl.ds(pl.multiple_of(i * head_dim, head_dim), head_dim)
 
     def window_row(d):
         return pl.multiple_of((WDEV - d) * rows, rows)
 
-    @pl.when(h == 0)
+    @pl.when(i == 0)
     def _():
+        half = win.shape[2]
         own_rows = pl.ds(WDEV * rows, rows)
+        side = pl.ds(pl.multiple_of(base[0] * head_dim, half), half)
         copies = [
             pltpu.make_async_copy(
-                recv[n], win.at[:, pl.ds(window_row(d), rows), :], sems.at[n]
+                recv[n].at[:, :, side], win.at[:, pl.ds(window_row(d), rows), :], sems.at[n]
             )
             for n, d in enumerate(distances(core))
         ]
-        copies.append(pltpu.make_async_copy(keys.at[slab], win.at[0, own_rows, :], sems.at[WDEV]))
-        copies.append(
-            pltpu.make_async_copy(values.at[slab], win.at[1, own_rows, :], sems.at[WDEV + 1])
-        )
-        copies += vertical_copies(lines, me, chunk, gathered, vkv, sems, WDEV + 2)
+        for kv, source in enumerate((keys, values)):
+            copies.append(
+                pltpu.make_async_copy(
+                    source.at[slab, :, side], win.at[kv, own_rows, :], sems.at[WDEV + kv]
+                )
+            )
+        copies += vertical_copies(lines, me, 0, chunk, gathered, vkv, sems, WDEV + 2)
         for copy in copies:
             copy.start()
         for copy in copies:
             copy.wait()
 
-    vert_rows = pl.ds(pl.multiple_of(h * (nv * BLOCK), nv * BLOCK), nv * BLOCK)
+    vert_rows = pl.ds(pl.multiple_of(i * (nv * BLOCK), nv * BLOCK), nv * BLOCK)
     neg, posinf = jnp.float32(-jnp.inf), jnp.float32(jnp.inf)
     log2_scale = scaling * math.log2(math.e)
     key_at = lax.broadcasted_iota(jnp.int32, (BLOCK, width), 0)
@@ -328,9 +334,9 @@
         for n in range(cand // JOIN):
             span = slice(n * JOIN * BLOCK, (n + 1) * JOIN * BLOCK)
             scores = jnp.dot(cand_keys[0, j, span, :], qt[0, j], preferred_element_type=F32)
-            for i in range(JOIN):
-                c = n * JOIN + i
-                part = scores[i * BLOCK : (i + 1) * BLOCK, :]
+            for k in range(JOIN):
+                c = n * JOIN + k
+                part = scores[k * BLOCK : (k + 1) * BLOCK, :]
                 if c == nv:
                     part = jnp.where(key_at <= row_at, part, neg)
                 s_ref[j, c * BLOCK : (c + 1) * BLOCK, :] = part
@@ -365,69 +371,77 @@
             vertical_sum[kv] = part if j == 0 else vertical_sum[kv] + part
 
     first = core == 0
-    keep = jnp.where(first, vertical_sum[0], vertical_sum[1])
-    give = jnp.where(first, vertical_sum[1], vertical_sum[0])
-    per_line = heads // 2
-    for line in range(2):
-
-        @pl.when(lax.rem(lax.div(h, per_line) + near, 2) == line)
-        def _():
-            for c in range(nv * BLOCK // chunk):
-                slot = lax.rem(h, per_line) * (nv * BLOCK // chunk) + c
-                slot = lax.rem(slot - far + lines.far, lines.far)
-                span = slice(c * chunk, (c + 1) * chunk)
-                shares[line][slot] = keep[span, :].astype(shares[line].dtype)
-                shares[2 + line][slot] = give[span, :].astype(BF16)
-
-
-def attend(slab_index, verticals, offsets, prepared, keys, values, gathered, recv, lines):
+    parts = (
+        jnp.where(first, vertical_sum[0], vertical_sum[1]),
+        jnp.where(first, vertical_sum[1], vertical_sum[0]),
+    )
+    for c in range(nv * BLOCK // chunk):
+        slot = lax.rem(i * (nv * BLOCK // chunk) + c - far + lines.far, lines.far)
+        for n, part in enumerate(parts):
+            hold[n, slot] = part[c * chunk : (c + 1) * chunk, :]
+
+    @pl.when(i == pl.num_programs(0) - 1)
+    def _():
+        share[...] = hold[0].astype(share.dtype)
+        give[...] = hold[1].astype(give.dtype)
+
+
+def attend(base, slab_index, verticals, offsets, prepared, keys, values, gathered, recv, lines, lows):
     heads, per_device, deep, head_dim = prepared[0].shape
     _, rows, features = keys.shape
     nv, ns = verticals.shape[1], offsets.shape[1]
     cand = nv + 1 + ns
-    smem = pl.BlockSpec(memory_space=pltpu.SMEM)
+    half = heads // 2
     hbm = pl.BlockSpec(memory_space=pltpu.HBM)
     anywhere = pl.BlockSpec(memory_space=pl.ANY)
 
     def by_head(shape):
-        return pl.BlockSpec((1,) + shape[1:], lambda h: (h,) + (0,) * (len(shape) - 1))
-
-    def whole(shape):
-        return pl.BlockSpec(shape, lambda h: (0,) * len(shape))
-
-    share = (lines.far, heads * nv * BLOCK // (2 * lines.far), head_dim)
-    low = (heads, per_device, cand * BLOCK, deep)
-    low_tail = (heads, per_device, (1 + ns) * BLOCK, deep)
-    cand_keys = (heads, per_device, cand * BLOCK, head_dim)
+        return pl.BlockSpec(
+            (1,) + shape[1:], lambda i, base, *_: (base[0] + i,) + (0,) * (len(shape) - 1)
+        )
+
+    share = (lines.far, half * nv * BLOCK // lines.far, head_dim)
+    shares = pl.BlockSpec(share, lambda i, *_: (0, 0, 0))
+    low_shapes = [
+        (heads, per_device, (1 + ns) * BLOCK, deep),
+        (heads, per_device, cand * BLOCK, deep),
+        (heads, per_device, cand * BLOCK, head_dim),
+    ]
+    before = 4 + len(prepared) + 2 + 2 + WDEV
     return pl.pallas_call(
         functools.partial(
-            attend_kernel, lines=lines, heads=heads, nv=nv, ns=ns, per_device=per_device
+            attend_kernel, lines=lines, nv=nv, ns=ns, per_device=per_device, continued=bool(lows)
         ),
-        grid=(heads,),
-        in_specs=[smem] * 3
-        + [by_head(array.shape) for array in prepared]
-        + [hbm] * 2
-        + [anywhere] * (4 + WDEV),
-        out_specs=[whole(share)] * 4 + [by_head(low_tail), by_head(low), by_head(cand_keys)],
+        grid_spec=pltpu.PrefetchScalarGridSpec(
+            num_scalar_prefetch=4,
+            grid=(half,),
+            in_specs=[by_head(array.shape) for array in prepared]
+            + [hbm] * 2
+            + [anywhere] * (2 + WDEV + len(lows)),
+            out_specs=[shares] * 2 + [by_head(shape) for shape in low_shapes],
+            scratch_shapes=[
+                pltpu.VMEM((2, (WDEV + 1) * rows, features // 2), BF16),
+                pltpu.VMEM((2, half * nv * BLOCK, head_dim), BF16),
+                pltpu.VMEM((per_device, cand * BLOCK, head_dim), BF16),
+                pltpu.VMEM((per_device, cand * BLOCK, deep), F32),
+                pltpu.VMEM((per_device, nv * BLOCK, deep), BF16),
+                pltpu.VMEM((2,) + share, F32),
+                pltpu.SemaphoreType.DMA((WDEV + 2 + 2 * lines.far,)),
+            ],
+        ),
         out_shape=[
-            jax.ShapeDtypeStruct(share, F32),
+            jax.ShapeDtypeStruct(share, F32 if lows else BF16),
             jax.ShapeDtypeStruct(share, BF16),
-            jax.ShapeDtypeStruct(share, BF16),
-            jax.ShapeDtypeStruct(share, BF16),
-            jax.ShapeDtypeStruct(low_tail, BF16),
-            jax.ShapeDtypeStruct(low, BF16),
-            jax.ShapeDtypeStruct(cand_keys, BF16),
-        ],
-        scratch_shapes=[
-            pltpu.VMEM((2, (WDEV + 1) * rows, features), BF16),
-            pltpu.VMEM((2, heads * nv * BLOCK, head_dim), BF16),
-            pltpu.VMEM((per_device, cand * BLOCK, head_dim), BF16),
-            pltpu.VMEM((per_device, cand * BLOCK, deep), F32),
-            pltpu.VMEM((per_device, nv * BLOCK, deep), BF16),
-            pltpu.SemaphoreType.DMA((WDEV + 2 + 4 * lines.far,)),
-        ],
+        ]
+        + [jax.ShapeDtypeStruct(shape, BF16) for shape in low_shapes],
+        input_output_aliases={before + n: 2 + n for n in range(len(lows))},
         compiler_params=pltpu.CompilerParams(vmem_limit_bytes=VMEM_LIMIT),
-    )(slab_index, verticals, offsets, *prepared, keys, values, *gathered, *recv)
+        cost_estimate=pl.CostEstimate(
+            flops=2 * 5 * half * per_device * cand * BLOCK * deep * head_dim,
+            bytes_accessed=12 << 20,
+            transcendentals=half * per_device * cand * BLOCK * deep,
+        ),
+    )(base, slab_index, verticals, offsets, *prepared, keys, values, *gathered, *recv, *lows)
 
 
 def window_kernel(offs, qs, gs, low_w, low_ds, home, *rest, lines, ns, per_device):
@@ -547,7 +561,8 @@
     devices = lines.devices
     chunk, head_dim = gathered[0].shape[1:]
     slab_blocks = per_device * devices
-    copies = vertical_copies(lines, me, chunk, gathered, vert, sems, 0)
+    copies = vertical_copies(lines, me, 1 - near, chunk, gathered[0::2], vert, sems, 0)
+    copies += vertical_copies(lines, me, near, chunk, gathered[1::2], vert, sems, 2 * lines.far)
     for copy in copies:
         copy.start()
     acc[0] = home[...]
@@ -664,36 +679,41 @@
     )
     recv4 = move(send4, lines.shift_pairs(4))
     to_near = core_sum(lines, to_near, to_both)
-    quarter = near_sum(lines, mine, to_near, to_core)
+    quarter = near_sum(lines, mine, move(to_near, lines.near_pairs()), to_core)
     prepared = prepare(after(queries, to_near), output_cotangent, forward_output, heads, head_dim)
     quarter = after(quarter, recv4, *prepared)
     share = far_sum(lines, quarter)
+    recv_mixed = move(after(mixed, quarter), lines.mixed_pairs())
     recv2 = move(jnp.where(near == 1, recv4, own), lines.near_pairs())
     other4 = move(recv4, lines.core_pairs())
     blank = zeros(share, context_keys.shape)
     gathered = far_gather(lines, after(share, other4))
     other2 = move(recv2, lines.core_pairs())
-    gathered = after(gathered, other2, *blank)
-    recv_mixed = move(after(mixed, gathered), lines.mixed_pairs())
+    gathered = after(gathered, other2, recv_mixed, *blank)
     gathered = plane_gather(lines, gathered)
-
-    *shares, low_w, low_ds, cand_keys = attend(
-        slab_index, verticals, offsets, prepared, context_keys, context_values, gathered,
-        [recv2, recv4, recv_mixed, other2, other4], lines,
+    recv = [recv2, recv4, recv_mixed, other2, other4]
+
+    def attend_line(line, gathered, lows):
+        base = (line * (heads // 2)).astype(jnp.int32).reshape(1)
+        return attend(
+            base, slab_index, verticals, offsets, prepared, context_keys, context_values,
+            gathered, recv, lines, lows,
+        )
+
+    to_near, to_both, *lows = attend_line(near, gathered[0::2], ())
+    to_near = core_sum(lines, to_near, to_both)
+    from_near = move(to_near, lines.near_pairs())
+    mine, to_core, low_w, low_ds, cand_keys = attend_line(1 - near, gathered[1::2], lows)
+
+    home, part2, part4, mixed, give2, give4 = window_gradients(
+        after(offsets, from_near), prepared[0], prepared[1], low_w, low_ds, lines, nv
     )
-
-    mine, to_near, to_core, to_both = shares
-    to_near = core_sum(lines, to_near, to_both)
-    home, part2, part4, mixed, give2, give4 = window_gradients(
-        after(offsets, to_near), prepared[0], prepared[1], low_w, low_ds, lines, nv
-    )
+    quarter = after(near_sum(lines, mine, from_near, to_core), home)
+    share = far_sum(lines, quarter)
     arrived_mixed = move(mixed, back(lines.mixed_pairs()))
-    quarter = near_sum(lines, mine, to_near, to_core)
-    quarter = after(quarter, home)
     sum2 = (part2 + move(give2, lines.core_pairs()).astype(F32)).astype(BF16)
     sum4 = part4 + move(give4, lines.core_pairs()).astype(F32)
-    from_near = move(after(sum2, quarter), lines.near_pairs())
-    share = far_sum(lines, quarter)
+    from_near = move(sum2, lines.near_pairs())
     totals = after(far_gather(lines, share), from_near, arrived_mixed)
     sum4 = (sum4 + jnp.where(near == 1, from_near.astype(F32), 0.0)).astype(BF16)
     arrived4 = move(after(sum4, totals), back(lines.shift_pairs(4)))

time: 111 us -> 149 us (1.34)
  local copies, waits for them, and re-layouts: 0.07 us -> 46.4 us
  waiting for transfers between devices: 44.2 us -> 23.5 us
  starting transfers between devices: 28.6 us -> 40.2 us
    unnamed x18 -> x94, local copies, waits for them, and re-layouts: 0.04 us -> 46.3 us
    ppermute x34, waiting for transfers between devices: 44.2 us -> 23.5 us  [move(): return lax.ppermute(array, 'ctx', pairs)]
    ppermute x34, starting transfers between devices: 28.6 us -> 40.2 us  [move(): return lax.ppermute(array, 'ctx', pairs)]
    pallas_call x1 -> x2, Pallas kernels: 13 us -> 14.1 us  [attend(): pl.pallas_call(functools.partial(attend_kernel, lines=lines, nv=nv, ns=ns...]
  transfers between devices with their start and end apart: 34 -> 34, of which waited for: 16 -> 12; matrix products, arithmetic and copies ran while one was open for 4% -> 3% of each run, Pallas kernels for 9% -> 16%
where the time goes in v9:
time: 149 us; the launch traced here: 148 us
  local copies, waits for them, and re-layouts  46.4 us (31%)
  starting transfers between devices  40.2 us (27%)
  Pallas kernels  31.5 us (21%)
  waiting for transfers between devices  23.5 us (16%)
  other arithmetic  4.43 us (3%)
  between operations  1.6 us (1%)
    unnamed x94, local copies, waits for them, and re-layouts  46.3 us
    ppermute x34, starting transfers between devices, move(): return lax.ppermute(array, 'ctx', pairs)  40.2 us
    ppermute x34, waiting for transfers between devices, move(): return lax.ppermute(array, 'ctx', pairs)  23.5 us
    pallas_call x2, Pallas kernels, attend(): pl.pallas_call(functools.partial(attend_kernel, lines=lines, nv=nv, ns=ns...  14.1 us
    pallas_call x1, Pallas kernels, assemble(): pl.pallas_call(functools.partial(assemble_kernel, lines=lines, heads=head...  4.4 us
    pallas_call x1, Pallas kernels, pack(): pl.pallas_call(functools.partial(pack_kernel, lines=lines, heads=heads, n...  3.56 us
  transfers between devices with their start and end apart: 34, of which 12 were waited for; matrix products, arithmetic and copies ran while one was open for 3% of the time, Pallas kernels for 16%

profile of v9, /device:TPU:0, one launch (start us, length us, event | category | flops | bytes accessed | tf_op | source)
XLA Modules:
  0.0 147.6 jit_solution(12373713327390761125)
XLA Ops:
  2.0 3.6 %shard_map.103 = (bf16[2,128,512]{2,1,0:T(8,128)(2,1)S(1)}, bf16[2,128,512]{2,1,0:T(8,128)(2,1)S(1)}, bf16[2,128,512]{2,1,0:T(8,128)(2,1)S(1)}, bf16[4,256,128]{...) custom-call(s32[1]{0:T(128)S(6)} %copy.21.slab_index, ...), custom_call_target="tpu_custom_call" | custom-call | tf_op jit(solution)/shard_map/pallas_call | solution.py:168
  6.7 2.6 %collective-permute-start.3 = (bf16[2,128,512]{2,1,0:T(8,128)(2,1)S(1)}, bf16[2,128,512]{2,1,0:T(8,128)(2,1)S(1)}, u32[]{:S(2)}, u32[]{:S(2)}) collective-permute-start(bf16[2,128,512]{2,1,0:T(8,128)(2,1)S(1)} %get-tuple-element.56), channel_id=1, source_target_pairs={{0,4},{1,5},{2,6},{3,7},{4,8},{5,9},{6,10},{7,11},{8,12},{9,13},{1... | collective-permute-start | bytes 786440 | tf_op jit(solution)/shard_map/ppermute | solution.py:52
  11.8 6.5 %collective-permute-done.3.rest_3_ = bf16[2,128,512]{2,1,0:T(8,128)(2,1)S(1)} collective-permute-done((bf16[2,128,512]{2,1,0:T(8,128)(2,1)S(1)}, bf16[2,128,512]{2,1,0:T(8,128)(2,1)S(1)}, u32[]{:S(2)}, u32[]{:S(2)}) %collective-permute-start.3) | collective-permute-done | bytes 262176 | tf_op jit(solution)/shard_map/ppermute | solution.py:52
  26.9 2.3 %collective-permute-start.5 = (bf16[256,128]{1,0:T(8,128)(2,1)S(1)}, bf16[256,128]{1,0:T(8,128)(2,1)S(1)}, u32[]{:S(2)}, u32[]{:S(2)}) collective-permute-start(bf16[256,128]{1,0:T(8,128)(2,1)S(1)} %get-tuple-element.94), channel_id=1, source_target_pairs={{0,8},{1,9},{2,10},{3,11},{4,12},{5,13},{6,14},{7,15},{8,0},{9,1},... | collective-permute-start | bytes 196616 | tf_op jit(solution)/shard_map/ppermute | solution.py:52
  31.3 2.3 %collective-permute-done.4 = bf16[256,128]{1,0:T(8,128)(2,1)S(1)} collective-permute-done((bf16[256,128]{1,0:T(8,128)(2,1)S(1)}, bf16[256,128]{1,0:T(8,128)(2,1)S(1)}, u32[]{:S(2)}, u32[]{:S(2)}) %collective-permute-start.4) | collective-permute-done | bytes 65568 | tf_op jit(solution)/shard_map/ppermute | solution.py:52
  35.0 4.2 %collective-permute-start.8 = (bf16[256,128]{1,0:T(8,128)(2,1)S(1)}, bf16[256,128]{1,0:T(8,128)(2,1)S(1)}, u32[]{:S(2)}, u32[]{:S(2)}) collective-permute-start(bf16[256,128]{1,0:T(8,128)(2,1)S(1)} %fusion.5._), channel_id=1, source_target_pairs={{0,4},{1,5},{2,6},{3,7},{4,8},{5,9},{6,10},{7,11},{8,12},{9,13},{1... | collective-permute-start | bytes 196616 | tf_op jit(solution)/shard_map/ppermute | solution.py:52
  39.2 2.4 %collective-permute-start.10 = (bf16[256,128]{1,0:T(8,128)(2,1)S(1)}, bf16[256,128]{1,0:T(8,128)(2,1)S(1)}, u32[]{:S(2)}, u32[]{:S(2)}) collective-permute-start(bf16[256,128]{1,0:T(8,128)(2,1)S(1)} %fusion.5._), channel_id=1, source_target_pairs={{0,12},{1,13},{2,14},{3,15},{4,0},{5,1},{6,2},{7,3},{8,4},{9,5},{1... | collective-permute-start | bytes 196616 | tf_op jit(solution)/shard_map/ppermute | solution.py:52
  41.7 2.3 %shard_map.105 = (bf16[16,128,512]{2,1,0:T(8,128)(2,1)}, bf16[16,128,512]{2,1,0:T(8,128)(2,1)}) custom-call(bf16[256,128]{1,0:T(8,128)(2,1)S(1)} %fusion.5._), custom_call_target="tpu_custom_call" | custom-call | bytes 5242880 | tf_op jit(solution)/shard_map/pallas_call | solution.py:545
  46.8 2.3 %collective-permute-start.14 = (bf16[4,256,128]{2,1,0:T(8,128)(2,1)}, bf16[4,256,128]{2,1,0:T(8,128)(2,1)}, u32[]{:S(2)}, u32[]{:S(2)}) collective-permute-start(bf16[4,256,128]{2,1,0:T(8,128)(2,1)} %pad_maximum_fusion.rest_0_), channel_id=1, source_target_pairs={{0,2},{1,3},{2,0},{3,1},{4,6},{5,7},{6,4},{7,5},{8,10},{9,11},{10,... | collective-permute-start | bytes 786440 | tf_op jit(solution)/shard_map/ppermute | solution.py:52
  58.2 7.4 %shard_map.106 = (bf16[4,256,128]{2,1,0:T(8,128)(2,1)S(1)}, bf16[4,256,128]{2,1,0:T(8,128)(2,1)}, bf16[4,2,256,512]{3,2,1,0:T(8,128)(2,1)S(1)}, bf16[4,2,768,512...) custom-call(s32[1]{0:T(128)} %bitcast.9.base, s32[1]{0:T(128)S(6)} %copy.21.slab_index, s32[4,8]{1,0:T(4,128)S(1)} %copy-done.43, ...), custom_call_target="tpu_custom_call" | custom-call | flops 2013265920 | bytes 12582912 | tf_op jit(solution)/shard_map/pallas_call | solution.py:411
  65.6 2.6 %copy-done = bf16[4,2,768,512]{3,2,1,0:T(8,128)(2,1)} copy-done((bf16[4,2,768,512]{3,2,1,0:T(8,128)(2,1)}, bf16[4,2,768,512]{3,2,1,0:T(8,128)(2,1)S(1)}, u32[]{:S(2)}) %copy-start) | copy-done | bytes 6291480
  76.4 2.8 %copy-done.1 = bf16[4,2,768,512]{3,2,1,0:T(8,128)(2,1)S(1)} copy-done((bf16[4,2,768,512]{3,2,1,0:T(8,128)(2,1)S(1)}, bf16[4,2,768,512]{3,2,1,0:T(8,128)(2,1)}, u32[]{:S(2)}) %copy-start.1) | copy-done | bytes 6291480
  91.2 6.7 %shard_map.107 = (f32[4,256,128]{2,1,0:T(8,128)S(1)}, bf16[4,256,128]{2,1,0:T(8,128)(2,1)S(1)}, bf16[4,2,256,512]{3,2,1,0:T(8,128)(2,1)S(1)}, bf16[4,2,768,512]{...) custom-call(s32[1]{0:T(128)} %bitcast.base, ...), custom_call_target="tpu_custom_call", output_to_operand_aliasing={{2}: (18, {}), {3}: (19, {}), {4}: (20, {})} | custom-call | flops 2013265920 | bytes 12582912 | tf_op jit(solution)/shard_map/pallas_call | solution.py:411
  98.0 2.6 %copy-done.2 = bf16[4,2,768,512]{3,2,1,0:T(8,128)(2,1)} copy-done((bf16[4,2,768,512]{3,2,1,0:T(8,128)(2,1)}, bf16[4,2,768,512]{3,2,1,0:T(8,128)(2,1)S(1)}, u32[]{:S(2)}) %copy-start.2) | copy-done | bytes 6291480
  103.1 2.8 %copy-done.3 = bf16[4,2,768,512]{3,2,1,0:T(8,128)(2,1)S(1)} copy-done((bf16[4,2,768,512]{3,2,1,0:T(8,128)(2,1)S(1)}, bf16[4,2,768,512]{3,2,1,0:T(8,128)(2,1)}, u32[]{:S(2)}) %copy-start.3) | copy-done | bytes 6291480
  107.5 2.9 %shard_map.108 = (f32[2,128,512]{2,1,0:T(8,128)S(1)}, f32[2,128,512]{2,1,0:T(8,128)S(1)}, f32[2,128,512]{2,1,0:T(8,128)S(1)}, bf16[2,128,512]{2,1,0:T(8,128)(2,1...) custom-call(s32[4,3]{1,0:T(4,128)S(1)} %copy-done.44, ...), custom_call_target="tpu_custom_call" | custom-call | bytes 9437184 | tf_op jit(solution)/shard_map/pallas_call | solution.py:485
  112.5 2.3 %collective-permute-start.21 = (bf16[256,128]{1,0:T(8,128)(2,1)S(1)}, bf16[256,128]{1,0:T(8,128)(2,1)S(1)}, u32[]{:S(2)}, u32[]{:S(2)}) collective-permute-start(bf16[256,128]{1,0:T(8,128)(2,1)S(1)} %get-tuple-element.91), channel_id=1, source_target_pairs={{0,8},{1,9},{2,10},{3,11},{4,12},{5,13},{6,14},{7,15},{8,0},{9,1},... | collective-permute-start | bytes 196616 | tf_op jit(solution)/shard_map/ppermute | solution.py:52
  118.2 2.2 %collective-permute-done.21 = bf16[256,128]{1,0:T(8,128)(2,1)S(1)} collective-permute-done((bf16[256,128]{1,0:T(8,128)(2,1)S(1)}, bf16[256,128]{1,0:T(8,128)(2,1)S(1)}, u32[]{:S(2)}, u32[]{:S(2)}) %collective-permute-start.21) | collective-permute-done | bytes 65568 | tf_op jit(solution)/shard_map/ppermute | solution.py:52
  120.5 4.7 %collective-permute-start.23 = (bf16[256,128]{1,0:T(8,128)(2,1)S(1)}, bf16[256,128]{1,0:T(8,128)(2,1)S(1)}, u32[]{:S(2)}, u32[]{:S(2)}) collective-permute-start(bf16[256,128]{1,0:T(8,128)(2,1)S(1)} %fusion.2), channel_id=1, source_target_pairs={{0,4},{1,5},{2,6},{3,7},{4,8},{5,9},{6,10},{7,11},{8,12},{9,13},{1... | collective-permute-start | bytes 196616 | tf_op jit(solution)/shard_map/ppermute | solution.py:52
  128.2 2.3 %collective-permute-start.25 = (bf16[256,128]{1,0:T(8,128)(2,1)S(1)}, bf16[256,128]{1,0:T(8,128)(2,1)S(1)}, u32[]{:S(2)}, u32[]{:S(2)}) collective-permute-start(bf16[256,128]{1,0:T(8,128)(2,1)S(1)} %fusion.2), channel_id=1, source_target_pairs={{0,12},{1,13},{2,14},{3,15},{4,0},{5,1},{6,2},{7,3},{8,4},{9,5},{1... | collective-permute-start | bytes 196616 | tf_op jit(solution)/shard_map/ppermute | solution.py:52
  133.2 3.8 %collective-permute-start.30 = (bf16[2,128,512]{2,1,0:T(8,128)(2,1)S(1)}, bf16[2,128,512]{2,1,0:T(8,128)(2,1)S(1)}, u32[]{:S(2)}, u32[]{:S(2)}) collective-permute-start(bf16[2,128,512]{2,1,0:T(8,128)(2,1)S(1)} %add_convert_fusion), channel_id=1, source_target_pairs={{4,0},{5,1},{6,2},{7,3},{8,4},{9,5},{10,6},{11,7},{12,8},{13,9},{1... | collective-permute-start | bytes 786440 | tf_op jit(solution)/shard_map/ppermute | solution.py:52
  137.0 3.1 %collective-permute-done.31.rest_4_ = bf16[4,256,128]{2,1,0:T(8,128)(2,1)S(1)} collective-permute-done((bf16[4,256,128]{2,1,0:T(8,128)(2,1)S(1)}, bf16[4,256,128]{2,1,0:T(8,128)(2,1)S(1)}, u32[]{:S(2)}, u32[]{:S(2)}) %collective-permute-start.31) | collective-permute-done | bytes 262176 | tf_op jit(solution)/shard_map/ppermute | solution.py:52
  140.1 3.0 %shard_map.109 = bf16[128,4096]{1,0:T(8,128)(2,1)} custom-call(bf16[4,2,768,128]{3,2,1,0:T(8,128)(2,1)S(1)} %copy-done.18, bf16[4,2,768,512]{3,2,1,0:T(8,128)(2,1)S(1)} %copy-done.4), custom_call_target="tpu_custom_call" | custom-call | bytes 10485760 | tf_op jit(solution)/shard_map/pallas_call | solution.py:519
  143.2 4.4 %shard_map.110 = (bf16[16,128,512]{2,1,0:T(8,128)(2,1)}, bf16[16,128,512]{2,1,0:T(8,128)(2,1)}) custom-call(s32[1]{0:T(128)S(6)} %copy.21.slab_index, s32[4,8]{1,0:T(4,128)S(1)} %copy-done.43, f32[2,128,512]{2,1,0:T(8,128)S(1)} %get-tuple-element.83.home, ...), custom_call_target="tpu_custom_call", output_to_operand_aliasing={{0}: (10, {}), {1}: (11, {})} | custom-call | tf_op jit(solution)/shard_map/pallas_call | solution.py:642
  (161 shorter events, 64.0 us)
Async XLA Ops:
  6.7 11.5 %collective-permute-start.3 = (bf16[2,128,512]{2,1,0:T(8,128)(2,1)S(1)}, bf16[2,128,512]{2,1,0:T(8,128)(2,1)S(1)}, u32[]{:S(2)}, u32[]{:S(2)}) collective-permute-start(bf16[2,128,512]{2,1,0:T(8,128)(2,1)S(1)} %get-tuple-element.56), channel_id=1, source_target_pairs={{0,4},{1,5},{2,6},{3,7},{4,8},{5,9},{6,10},{7,11},{8,12},{9,13},{1... | collective-permute-start | bytes 786440 | tf_op jit(solution)/shard_map/ppermute | solution.py:52
  9.3 16.2 %collective-permute-start.1 = (bf16[4,256,128]{2,1,0:T(8,128)(2,1)}, bf16[4,256,128]{2,1,0:T(8,128)(2,1)}, u32[]{:S(2)}, u32[]{:S(2)}) collective-permute-start(bf16[4,256,128]{2,1,0:T(8,128)(2,1)} %get-tuple-element.55), channel_id=1, source_target_pairs={{0,1},{1,0},{2,3},{3,2},{4,5},{5,4},{6,7},{7,6},{8,9},{9,8},{10,11... | collective-permute-start | bytes 786440 | tf_op jit(solution)/shard_map/ppermute | solution.py:52
  10.3 15.2 %collective-permute-start.2 = (bf16[4,256,128]{2,1,0:T(8,128)(2,1)}, bf16[4,256,128]{2,1,0:T(8,128)(2,1)}, u32[]{:S(2)}, u32[]{:S(2)}) collective-permute-start(bf16[4,256,128]{2,1,0:T(8,128)(2,1)} %add_convert_fusion.3), channel_id=1, source_target_pairs={{0,2},{1,3},{2,0},{3,1},{4,6},{5,7},{6,4},{7,5},{8,10},{9,11},{10,... | collective-permute-start | bytes 786440 | tf_op jit(solution)/shard_map/ppermute | solution.py:52
  18.3 12.5 %collective-permute-start.11 = (bf16[2,128,512]{2,1,0:T(8,128)(2,1)S(1)}, bf16[2,128,512]{2,1,0:T(8,128)(2,1)S(1)}, u32[]{:S(2)}, u32[]{:S(2)}) collective-permute-start(bf16[2,128,512]{2,1,0:T(8,128)(2,1)S(1)} %broadcast_select_fusion), channel_id=1, source_target_pairs={{0,2},{1,3},{2,0},{3,1},{4,6},{5,7},{6,4},{7,5},{8,10},{9,11},{10,... | collective-permute-start | bytes 786440 | tf_op jit(solution)/shard_map/ppermute | solution.py:52
  26.9 6.8 %collective-permute-start.4 = (bf16[256,128]{1,0:T(8,128)(2,1)S(1)}, bf16[256,128]{1,0:T(8,128)(2,1)S(1)}, u32[]{:S(2)}, u32[]{:S(2)}) collective-permute-start(bf16[256,128]{1,0:T(8,128)(2,1)S(1)} %get-tuple-element.92), channel_id=1, source_target_pairs={{0,4},{1,5},{2,6},{3,7},{4,8},{5,9},{6,10},{7,11},{8,12},{9,13},{1... | collective-permute-start | bytes 196616 | tf_op jit(solution)/shard_map/ppermute | solution.py:52
  26.9 8.0 %collective-permute-start.5 = (bf16[256,128]{1,0:T(8,128)(2,1)S(1)}, bf16[256,128]{1,0:T(8,128)(2,1)S(1)}, u32[]{:S(2)}, u32[]{:S(2)}) collective-permute-start(bf16[256,128]{1,0:T(8,128)(2,1)S(1)} %get-tuple-element.94), channel_id=1, source_target_pairs={{0,8},{1,9},{2,10},{3,11},{4,12},{5,13},{6,14},{7,15},{8,0},{9,1},... | collective-permute-start | bytes 196616 | tf_op jit(solution)/shard_map/ppermute | solution.py:52
  29.2 5.7 %collective-permute-start.6 = (bf16[256,128]{1,0:T(8,128)(2,1)S(1)}, bf16[256,128]{1,0:T(8,128)(2,1)S(1)}, u32[]{:S(2)}, u32[]{:S(2)}) collective-permute-start(bf16[256,128]{1,0:T(8,128)(2,1)S(1)} %get-tuple-element.93), channel_id=1, source_target_pairs={{0,12},{1,13},{2,14},{3,15},{4,0},{5,1},{6,2},{7,3},{8,4},{9,5},{1... | collective-permute-start | bytes 196616 | tf_op jit(solution)/shard_map/ppermute | solution.py:52
  30.8 14.6 %collective-permute-start.13 = (bf16[2,128,512]{2,1,0:T(8,128)(2,1)S(1)}, bf16[2,128,512]{2,1,0:T(8,128)(2,1)S(1)}, u32[]{:S(2)}, u32[]{:S(2)}) collective-permute-start(bf16[2,128,512]{2,1,0:T(8,128)(2,1)S(1)} %copy-done.46), channel_id=1, source_target_pairs={{0,1},{1,6},{2,3},{3,8},{4,5},{5,10},{6,7},{7,12},{8,9},{9,14},{10... | collective-permute-start | bytes 786440 | tf_op jit(solution)/shard_map/ppermute | solution.py:52
  33.6 12.4 %collective-permute-start.12 = (bf16[2,128,512]{2,1,0:T(8,128)(2,1)S(1)}, bf16[2,128,512]{2,1,0:T(8,128)(2,1)S(1)}, u32[]{:S(2)}, u32[]{:S(2)}) collective-permute-start(bf16[2,128,512]{2,1,0:T(8,128)(2,1)S(1)} %collective-permute-done.11.rest_2_), channel_id=1, source_target_pairs={{0,1},{1,0},{2,3},{3,2},{4,5},{5,4},{6,7},{7,6},{8,9},{9,8},{10,11... | collective-permute-start | bytes 786440 | tf_op jit(solution)/shard_map/ppermute | solution.py:52
  35.0 8.9 %collective-permute-start.8 = (bf16[256,128]{1,0:T(8,128)(2,1)S(1)}, bf16[256,128]{1,0:T(8,128)(2,1)S(1)}, u32[]{:S(2)}, u32[]{:S(2)}) collective-permute-start(bf16[256,128]{1,0:T(8,128)(2,1)S(1)} %fusion.5._), channel_id=1, source_target_pairs={{0,4},{1,5},{2,6},{3,7},{4,8},{5,9},{6,10},{7,11},{8,12},{9,13},{1... | collective-permute-start | bytes 196616 | tf_op jit(solution)/shard_map/ppermute | solution.py:52
  46.8 24.9 %collective-permute-start.14 = (bf16[4,256,128]{2,1,0:T(8,128)(2,1)}, bf16[4,256,128]{2,1,0:T(8,128)(2,1)}, u32[]{:S(2)}, u32[]{:S(2)}) collective-permute-start(bf16[4,256,128]{2,1,0:T(8,128)(2,1)} %pad_maximum_fusion.rest_0_), channel_id=1, source_target_pairs={{0,2},{1,3},{2,0},{3,1},{4,6},{5,7},{6,4},{7,5},{8,10},{9,11},{10,... | collective-permute-start | bytes 786440 | tf_op jit(solution)/shard_map/ppermute | solution.py:52
  74.5 28.7 %collective-permute-start.19 = (bf16[4,256,128]{2,1,0:T(8,128)(2,1)S(1)}, bf16[4,256,128]{2,1,0:T(8,128)(2,1)S(1)}, u32[]{:S(2)}, u32[]{:S(2)}) collective-permute-start(bf16[4,256,128]{2,1,0:T(8,128)(2,1)S(1)} %add_convert_fusion.2), channel_id=1, source_target_pairs={{0,2},{1,3},{2,0},{3,1},{4,6},{5,7},{6,4},{7,5},{8,10},{9,11},{10,... | collective-permute-start | bytes 786440 | tf_op jit(solution)/shard_map/ppermute | solution.py:52
  103.1 7.9 %collective-permute-start.17 = (bf16[4,256,128]{2,1,0:T(8,128)(2,1)S(1)}, bf16[4,256,128]{2,1,0:T(8,128)(2,1)S(1)}, u32[]{:S(2)}, u32[]{:S(2)}) collective-permute-start(bf16[4,256,128]{2,1,0:T(8,128)(2,1)S(1)} %get-tuple-element.70), channel_id=1, source_target_pairs={{0,1},{1,0},{2,3},{3,2},{4,5},{5,4},{6,7},{7,6},{8,9},{9,8},{10,11... | collective-permute-start | bytes 786440 | tf_op jit(solution)/shard_map/ppermute | solution.py:52
  111.0 22.1 %collective-permute-start.29 = (bf16[2,128,512]{2,1,0:T(8,128)(2,1)S(1)}, bf16[2,128,512]{2,1,0:T(8,128)(2,1)S(1)}, u32[]{:S(2)}, u32[]{:S(2)}) collective-permute-start(bf16[2,128,512]{2,1,0:T(8,128)(2,1)S(1)} %get-tuple-element.85), channel_id=1, source_target_pairs={{0,1},{1,0},{2,3},{3,2},{4,5},{5,4},{6,7},{7,6},{8,9},{9,8},{10,11... | collective-permute-start | bytes 786440 | tf_op jit(solution)/shard_map/ppermute | solution.py:52
  111.2 6.8 %collective-permute-start.20 = (bf16[256,128]{1,0:T(8,128)(2,1)S(1)}, bf16[256,128]{1,0:T(8,128)(2,1)S(1)}, u32[]{:S(2)}, u32[]{:S(2)}) collective-permute-start(bf16[256,128]{1,0:T(8,128)(2,1)S(1)} %get-tuple-element.89), channel_id=1, source_target_pairs={{0,4},{1,5},{2,6},{3,7},{4,8},{5,9},{6,10},{7,11},{8,12},{9,13},{1... | collective-permute-start | bytes 196616 | tf_op jit(solution)/shard_map/ppermute | solution.py:52
  112.5 7.9 %collective-permute-start.21 = (bf16[256,128]{1,0:T(8,128)(2,1)S(1)}, bf16[256,128]{1,0:T(8,128)(2,1)S(1)}, u32[]{:S(2)}, u32[]{:S(2)}) collective-permute-start(bf16[256,128]{1,0:T(8,128)(2,1)S(1)} %get-tuple-element.91), channel_id=1, source_target_pairs={{0,8},{1,9},{2,10},{3,11},{4,12},{5,13},{6,14},{7,15},{8,0},{9,1},... | collective-permute-start | bytes 196616 | tf_op jit(solution)/shard_map/ppermute | solution.py:52
  114.9 5.6 %collective-permute-start.22 = (bf16[256,128]{1,0:T(8,128)(2,1)S(1)}, bf16[256,128]{1,0:T(8,128)(2,1)S(1)}, u32[]{:S(2)}, u32[]{:S(2)}) collective-permute-start(bf16[256,128]{1,0:T(8,128)(2,1)S(1)} %get-tuple-element.90), channel_id=1, source_target_pairs={{0,12},{1,13},{2,14},{3,15},{4,0},{5,1},{6,2},{7,3},{8,4},{9,5},{1... | collective-permute-start | bytes 196616 | tf_op jit(solution)/shard_map/ppermute | solution.py:52
  115.9 16.7 %collective-permute-start.28 = (bf16[2,128,512]{2,1,0:T(8,128)(2,1)S(1)}, bf16[2,128,512]{2,1,0:T(8,128)(2,1)S(1)}, u32[]{:S(2)}, u32[]{:S(2)}) collective-permute-start(bf16[2,128,512]{2,1,0:T(8,128)(2,1)S(1)} %get-tuple-element.80), channel_id=1, source_target_pairs={{1,0},{6,1},{3,2},{8,3},{5,4},{10,5},{7,6},{12,7},{9,8},{14,9},{11... | collective-permute-start | bytes 786440 | tf_op jit(solution)/shard_map/ppermute | solution.py:52
  118.0 14.6 %collective-permute-start.27 = (bf16[2,128,512]{2,1,0:T(8,128)(2,1)S(1)}, bf16[2,128,512]{2,1,0:T(8,128)(2,1)S(1)}, u32[]{:S(2)}, u32[]{:S(2)}) collective-permute-start(bf16[2,128,512]{2,1,0:T(8,128)(2,1)S(1)} %add_convert_fusion.1), channel_id=1, source_target_pairs={{0,2},{1,3},{2,0},{3,1},{4,6},{5,7},{6,4},{7,5},{8,10},{9,11},{10,... | collective-permute-start | bytes 786440 | tf_op jit(solution)/shard_map/ppermute | solution.py:52
  120.5 7.7 %collective-permute-start.23 = (bf16[256,128]{1,0:T(8,128)(2,1)S(1)}, bf16[256,128]{1,0:T(8,128)(2,1)S(1)}, u32[]{:S(2)}, u32[]{:S(2)}) collective-permute-start(bf16[256,128]{1,0:T(8,128)(2,1)S(1)} %fusion.2), channel_id=1, source_target_pairs={{0,4},{1,5},{2,6},{3,7},{4,8},{5,9},{6,10},{7,11},{8,12},{9,13},{1... | collective-permute-start | bytes 196616 | tf_op jit(solution)/shard_map/ppermute | solution.py:52
  125.2 6.9 %collective-permute-start.24 = (bf16[256,128]{1,0:T(8,128)(2,1)S(1)}, bf16[256,128]{1,0:T(8,128)(2,1)S(1)}, u32[]{:S(2)}, u32[]{:S(2)}) collective-permute-start(bf16[256,128]{1,0:T(8,128)(2,1)S(1)} %fusion.2), channel_id=1, source_target_pairs={{0,8},{1,9},{2,10},{3,11},{4,12},{5,13},{6,14},{7,15},{8,0},{9,1},... | collective-permute-start | bytes 196616 | tf_op jit(solution)/shard_map/ppermute | solution.py:52
  132.7 7.5 %collective-permute-start.31 = (bf16[4,256,128]{2,1,0:T(8,128)(2,1)S(1)}, bf16[4,256,128]{2,1,0:T(8,128)(2,1)S(1)}, u32[]{:S(2)}, u32[]{:S(2)}) collective-permute-start(bf16[4,256,128]{2,1,0:T(8,128)(2,1)S(1)} %pad_maximum_fusion.1.rest_3_), channel_id=1, source_target_pairs={{0,2},{1,3},{2,0},{3,1},{4,6},{5,7},{6,4},{7,5},{8,10},{9,11},{10,... | collective-permute-start | bytes 786440 | tf_op jit(solution)/shard_map/ppermute | solution.py:52
  133.1 10.2 %collective-permute-start.32 = (bf16[4,256,128]{2,1,0:T(8,128)(2,1)S(1)}, bf16[4,256,128]{2,1,0:T(8,128)(2,1)S(1)}, u32[]{:S(2)}, u32[]{:S(2)}) collective-permute-start(bf16[4,256,128]{2,1,0:T(8,128)(2,1)S(1)} %pad_maximum_fusion.1.rest_3_), channel_id=1, source_target_pairs={{0,1},{1,0},{2,3},{3,2},{4,5},{5,4},{6,7},{7,6},{8,9},{9,8},{10,11... | collective-permute-start | bytes 786440 | tf_op jit(solution)/shard_map/ppermute | solution.py:52
  133.2 10.0 %collective-permute-start.30 = (bf16[2,128,512]{2,1,0:T(8,128)(2,1)S(1)}, bf16[2,128,512]{2,1,0:T(8,128)(2,1)S(1)}, u32[]{:S(2)}, u32[]{:S(2)}) collective-permute-start(bf16[2,128,512]{2,1,0:T(8,128)(2,1)S(1)} %add_convert_fusion), channel_id=1, source_target_pairs={{4,0},{5,1},{6,2},{7,3},{8,4},{9,5},{10,6},{11,7},{12,8},{13,9},{1... | collective-permute-start | bytes 786440 | tf_op jit(solution)/shard_map/ppermute | solution.py:52
  (57 other events, 284.0 us)

commit v10 on v9

--- a/solution.py
+++ b/solution.py
@@ -10,8 +10,8 @@
 
 BLOCK = 64
 WDEV = 5
-VMEM_LIMIT = 32 * 1024 * 1024
-PACK_VMEM = 52 * 1024 * 1024
+VMEM_LIMIT = 20 * 1024 * 1024
+PACK_VMEM = 60 * 1024 * 1024
 JOIN = 4
 BF16 = jnp.bfloat16
 F32 = jnp.float32
@@ -255,7 +255,7 @@
 
 
 def attend_kernel(
-    base, slab_index, verts, offs, qs, gs, qt, gt, delta, keys, values, *rest,
+    base, slab_index, verts, offs, qs, gs, qt, gt, delta, own, *rest,
     lines, nv, ns, per_device, continued,
 ):
     gathered, recv, rest = rest[:2], rest[2 : 2 + WDEV], rest[2 + WDEV :]
@@ -288,13 +288,10 @@
             )
             for n, d in enumerate(distances(core))
         ]
-        for kv, source in enumerate((keys, values)):
-            copies.append(
-                pltpu.make_async_copy(
-                    source.at[slab, :, side], win.at[kv, own_rows, :], sems.at[WDEV + kv]
-                )
-            )
-        copies += vertical_copies(lines, me, 0, chunk, gathered, vkv, sems, WDEV + 2)
+        copies.append(
+            pltpu.make_async_copy(own.at[:, :, side], win.at[:, own_rows, :], sems.at[WDEV])
+        )
+        copies += vertical_copies(lines, me, 0, chunk, gathered, vkv, sems, WDEV + 1)
         for copy in copies:
             copy.start()
         for copy in copies:
@@ -386,13 +383,12 @@
         give[...] = hold[1].astype(give.dtype)
 
 
-def attend(base, slab_index, verticals, offsets, prepared, keys, values, gathered, recv, lines, lows):
+def attend(base, slab_index, verticals, offsets, prepared, own, gathered, recv, lines, lows):
     heads, per_device, deep, head_dim = prepared[0].shape
-    _, rows, features = keys.shape
+    _, rows, features = own.shape
     nv, ns = verticals.shape[1], offsets.shape[1]
     cand = nv + 1 + ns
     half = heads // 2
-    hbm = pl.BlockSpec(memory_space=pltpu.HBM)
     anywhere = pl.BlockSpec(memory_space=pl.ANY)
 
     def by_head(shape):
@@ -407,7 +403,7 @@
         (heads, per_device, cand * BLOCK, deep),
         (heads, per_device, cand * BLOCK, head_dim),
     ]
-    before = 4 + len(prepared) + 2 + 2 + WDEV
+    before = 4 + len(prepared) + 1 + 2 + WDEV
     return pl.pallas_call(
         functools.partial(
             attend_kernel, lines=lines, nv=nv, ns=ns, per_device=per_device, continued=bool(lows)
@@ -416,8 +412,7 @@
             num_scalar_prefetch=4,
             grid=(half,),
             in_specs=[by_head(array.shape) for array in prepared]
-            + [hbm] * 2
-            + [anywhere] * (2 + WDEV + len(lows)),
+            + [anywhere] * (3 + WDEV + len(lows)),
             out_specs=[shares] * 2 + [by_head(shape) for shape in low_shapes],
             scratch_shapes=[
                 pltpu.VMEM((2, (WDEV + 1) * rows, features // 2), BF16),
@@ -426,7 +421,7 @@
                 pltpu.VMEM((per_device, cand * BLOCK, deep), F32),
                 pltpu.VMEM((per_device, nv * BLOCK, deep), BF16),
                 pltpu.VMEM((2,) + share, F32),
-                pltpu.SemaphoreType.DMA((WDEV + 2 + 2 * lines.far,)),
+                pltpu.SemaphoreType.DMA((WDEV + 1 + 2 * lines.far,)),
             ],
         ),
         out_shape=[
@@ -441,7 +436,7 @@
             bytes_accessed=12 << 20,
             transcendentals=half * per_device * cand * BLOCK * deep,
         ),
-    )(base, slab_index, verticals, offsets, *prepared, keys, values, *gathered, *recv, *lows)
+    )(base, slab_index, verticals, offsets, *prepared, own, *gathered, *recv, *lows)
 
 
 def window_kernel(offs, qs, gs, low_w, low_ds, home, *rest, lines, ns, per_device):
@@ -696,8 +691,7 @@
     def attend_line(line, gathered, lows):
         base = (line * (heads // 2)).astype(jnp.int32).reshape(1)
         return attend(
-            base, slab_index, verticals, offsets, prepared, context_keys, context_values,
-            gathered, recv, lines, lows,
+            base, slab_index, verticals, offsets, prepared, own, gathered, recv, lines, lows
         )
 
     to_near, to_both, *lows = attend_line(near, gathered[0::2], ())

time: 149 us -> 143 us (0.960)
  local copies, waits for them, and re-layouts: 46.4 us -> 38.8 us
  other arithmetic: 4.43 us -> 6.52 us
  starting transfers between devices: 40.2 us -> 38.5 us
    unnamed x94 -> x88, local copies, waits for them, and re-layouts: 46.3 us -> 38.7 us
    ppermute x34, starting transfers between devices: 40.2 us -> 38.5 us  [move(): return lax.ppermute(array, 'ctx', pairs)]
  transfers between devices with their start and end apart: 34 -> 34, of which waited for: 12 -> 12; matrix products, arithmetic and copies ran while one was open for 3% -> 5% of each run, Pallas kernels for 16% -> 16%
where the time goes in v10:
time: 143 us; the launch traced here: 142 us
  local copies, waits for them, and re-layouts  38.8 us (27%)
  starting transfers between devices  38.5 us (27%)
  Pallas kernels  32.2 us (23%)
  waiting for transfers between devices  24.7 us (17%)
  other arithmetic  6.52 us (5%)
  between operations  1.61 us (1%)
    unnamed x88, local copies, waits for them, and re-layouts  38.7 us
    ppermute x34, starting transfers between devices, move(): return lax.ppermute(array, 'ctx', pairs)  38.5 us
    ppermute x34, waiting for transfers between devices, move(): return lax.ppermute(array, 'ctx', pairs)  24.7 us
    pallas_call x2, Pallas kernels, attend(): pl.pallas_call(functools.partial(attend_kernel, lines=lines, nv=nv, ns=ns...  14 us
    pallas_call x1, Pallas kernels, assemble(): pl.pallas_call(functools.partial(assemble_kernel, lines=lines, heads=head...  4.4 us
    pallas_call x1, Pallas kernels, pack(): pl.pallas_call(functools.partial(pack_kernel, lines=lines, heads=heads, n...  4.33 us
    pallas_call x1, Pallas kernels, query_gradients(): pl.pallas_call(query_kernel, grid=(heads,), in_specs=[by_head(cand_keys.s...  2.97 us
    pallas_call x1, Pallas kernels, window_gradients(): pl.pallas_call(functools.partial(window_kernel, lines=lines, ns=ns, per_d...  2.86 us
  transfers between devices with their start and end apart: 34, of which 12 were waited for; matrix products, arithmetic and copies ran while one was open for 5% of the time, Pallas kernels for 16%

profile of v10, /device:TPU:0, one launch (start us, length us, event | category | flops | bytes accessed | tf_op | source)
XLA Modules:
  0.0 142.3 jit_solution(11389925433807847483)
XLA Ops:
  1.3 4.3 %shard_map.103 = (bf16[2,128,512]{2,1,0:T(8,128)(2,1)}, bf16[2,128,512]{2,1,0:T(8,128)(2,1)}, bf16[2,128,512]{2,1,0:T(8,128)(2,1)}, bf16[4,256,128]{2,1,0:T(8,12...) custom-call(s32[1]{0:T(128)S(6)} %copy.21.slab_index, ...), custom_call_target="tpu_custom_call" | custom-call | tf_op jit(solution)/shard_map/pallas_call | solution.py:168
  6.1 2.6 %collective-permute-start.3 = (bf16[2,128,512]{2,1,0:T(8,128)(2,1)}, bf16[2,128,512]{2,1,0:T(8,128)(2,1)S(1)}, u32[]{:S(2)}, u32[]{:S(2)}) collective-permute-start(bf16[2,128,512]{2,1,0:T(8,128)(2,1)} %get-tuple-element.57), channel_id=1, source_target_pairs={{0,4},{1,5},{2,6},{3,7},{4,8},{5,9},{6,10},{7,11},{8,12},{9,13},{1... | collective-permute-start | bytes 786440 | tf_op jit(solution)/shard_map/ppermute | solution.py:52
  12.2 5.8 %collective-permute-done.3.rest_3_ = bf16[2,128,512]{2,1,0:T(8,128)(2,1)S(1)} collective-permute-done((bf16[2,128,512]{2,1,0:T(8,128)(2,1)}, bf16[2,128,512]{2,1,0:T(8,128)(2,1)S(1)}, u32[]{:S(2)}, u32[]{:S(2)}) %collective-permute-start.3) | collective-permute-done | bytes 262176 | tf_op jit(solution)/shard_map/ppermute | solution.py:52
  25.9 2.3 %collective-permute-start.5 = (bf16[256,128]{1,0:T(8,128)(2,1)S(1)}, bf16[256,128]{1,0:T(8,128)(2,1)S(1)}, u32[]{:S(2)}, u32[]{:S(2)}) collective-permute-start(bf16[256,128]{1,0:T(8,128)(2,1)S(1)} %get-tuple-element.94), channel_id=1, source_target_pairs={{0,8},{1,9},{2,10},{3,11},{4,12},{5,13},{6,14},{7,15},{8,0},{9,1},... | collective-permute-start | bytes 196616 | tf_op jit(solution)/shard_map/ppermute | solution.py:52
  30.3 2.3 %collective-permute-done.4 = bf16[256,128]{1,0:T(8,128)(2,1)S(1)} collective-permute-done((bf16[256,128]{1,0:T(8,128)(2,1)S(1)}, bf16[256,128]{1,0:T(8,128)(2,1)S(1)}, u32[]{:S(2)}, u32[]{:S(2)}) %collective-permute-start.4) | collective-permute-done | bytes 65568 | tf_op jit(solution)/shard_map/ppermute | solution.py:52
  37.9 2.3 %shard_map.105 = (bf16[16,128,512]{2,1,0:T(8,128)(2,1)}, bf16[16,128,512]{2,1,0:T(8,128)(2,1)}) custom-call(bf16[256,128]{1,0:T(8,128)(2,1)S(1)} %fusion.5._), custom_call_target="tpu_custom_call" | custom-call | bytes 5242880 | tf_op jit(solution)/shard_map/pallas_call | solution.py:540
  40.9 1.8 %collective-permute-done.9 = bf16[256,128]{1,0:T(8,128)(2,1)S(1)} collective-permute-done((bf16[256,128]{1,0:T(8,128)(2,1)S(1)}, bf16[256,128]{1,0:T(8,128)(2,1)S(1)}, u32[]{:S(2)}, u32[]{:S(2)}) %collective-permute-start.9) | collective-permute-done | bytes 65568 | tf_op jit(solution)/shard_map/ppermute | solution.py:52
  45.0 4.2 %collective-permute-start.14 = (bf16[4,256,128]{2,1,0:T(8,128)(2,1)}, bf16[4,256,128]{2,1,0:T(8,128)(2,1)}, u32[]{:S(2)}, u32[]{:S(2)}) collective-permute-start(bf16[4,256,128]{2,1,0:T(8,128)(2,1)} %pad_maximum_fusion.rest_0_), channel_id=1, source_target_pairs={{0,2},{1,3},{2,0},{3,1},{4,6},{5,7},{6,4},{7,5},{8,10},{9,11},{10,... | collective-permute-start | bytes 786440 | tf_op jit(solution)/shard_map/ppermute | solution.py:52
  59.3 7.3 %shard_map.106 = (bf16[4,256,128]{2,1,0:T(8,128)(2,1)S(1)}, bf16[4,256,128]{2,1,0:T(8,128)(2,1)}, bf16[4,2,256,512]{3,2,1,0:T(8,128)(2,1)S(1)}, bf16[4,2,768,512...) custom-call(s32[1]{0:T(128)} %bitcast.9.base, s32[1]{0:T(128)S(6)} %copy.21.slab_index, s32[4,8]{1,0:T(4,128)S(1)} %copy-done.38, ...), custom_call_target="tpu_custom_call" | custom-call | flops 2013265920 | bytes 12582912 | tf_op jit(solution)/shard_map/pallas_call | solution.py:407
  66.6 2.6 %copy-done = bf16[4,2,768,512]{3,2,1,0:T(8,128)(2,1)} copy-done((bf16[4,2,768,512]{3,2,1,0:T(8,128)(2,1)}, bf16[4,2,768,512]{3,2,1,0:T(8,128)(2,1)S(1)}, u32[]{:S(2)}) %copy-start) | copy-done | bytes 6291480
  75.9 2.8 %copy-done.1 = bf16[4,2,768,512]{3,2,1,0:T(8,128)(2,1)S(1)} copy-done((bf16[4,2,768,512]{3,2,1,0:T(8,128)(2,1)S(1)}, bf16[4,2,768,512]{3,2,1,0:T(8,128)(2,1)}, u32[]{:S(2)}) %copy-start.1) | copy-done | bytes 6291480
  88.5 6.7 %shard_map.107 = (f32[4,256,128]{2,1,0:T(8,128)S(1)}, bf16[4,256,128]{2,1,0:T(8,128)(2,1)S(1)}, bf16[4,2,256,512]{3,2,1,0:T(8,128)(2,1)S(1)}, bf16[4,2,768,512]{...) custom-call(s32[1]{0:T(128)} %bitcast.base, ...), custom_call_target="tpu_custom_call", output_to_operand_aliasing={{2}: (17, {}), {3}: (18, {}), {4}: (19, {})} | custom-call | flops 2013265920 | bytes 12582912 | tf_op jit(solution)/shard_map/pallas_call | solution.py:407
  95.2 2.6 %copy-done.2 = bf16[4,2,768,512]{3,2,1,0:T(8,128)(2,1)} copy-done((bf16[4,2,768,512]{3,2,1,0:T(8,128)(2,1)}, bf16[4,2,768,512]{3,2,1,0:T(8,128)(2,1)S(1)}, u32[]{:S(2)}) %copy-start.2) | copy-done | bytes 6291480
  99.1 2.8 %copy-done.3 = bf16[4,2,768,512]{3,2,1,0:T(8,128)(2,1)S(1)} copy-done((bf16[4,2,768,512]{3,2,1,0:T(8,128)(2,1)S(1)}, bf16[4,2,768,512]{3,2,1,0:T(8,128)(2,1)}, u32[]{:S(2)}) %copy-start.3) | copy-done | bytes 6291480
  101.9 2.9 %shard_map.108 = (f32[2,128,512]{2,1,0:T(8,128)S(1)}, f32[2,128,512]{2,1,0:T(8,128)S(1)}, f32[2,128,512]{2,1,0:T(8,128)S(1)}, bf16[2,128,512]{2,1,0:T(8,128)(2,1...) custom-call(s32[4,3]{1,0:T(4,128)S(1)} %copy-done.39, ...), custom_call_target="tpu_custom_call" | custom-call | bytes 9437184 | tf_op jit(solution)/shard_map/pallas_call | solution.py:480
  106.8 2.1 %collective-permute-start.21 = (bf16[256,128]{1,0:T(8,128)(2,1)S(1)}, bf16[256,128]{1,0:T(8,128)(2,1)S(1)}, u32[]{:S(2)}, u32[]{:S(2)}) collective-permute-start(bf16[256,128]{1,0:T(8,128)(2,1)S(1)} %get-tuple-element.91), channel_id=1, source_target_pairs={{0,8},{1,9},{2,10},{3,11},{4,12},{5,13},{6,14},{7,15},{8,0},{9,1},... | collective-permute-start | bytes 196616 | tf_op jit(solution)/shard_map/ppermute | solution.py:52
  110.5 1.9 %collective-permute-done.20 = bf16[256,128]{1,0:T(8,128)(2,1)S(1)} collective-permute-done((bf16[256,128]{1,0:T(8,128)(2,1)S(1)}, bf16[256,128]{1,0:T(8,128)(2,1)S(1)}, u32[]{:S(2)}, u32[]{:S(2)}) %collective-permute-start.20) | collective-permute-done | bytes 65568 | tf_op jit(solution)/shard_map/ppermute | solution.py:52
  112.7 2.1 %collective-permute-done.21 = bf16[256,128]{1,0:T(8,128)(2,1)S(1)} collective-permute-done((bf16[256,128]{1,0:T(8,128)(2,1)S(1)}, bf16[256,128]{1,0:T(8,128)(2,1)S(1)}, u32[]{:S(2)}, u32[]{:S(2)}) %collective-permute-start.21) | collective-permute-done | bytes 65568 | tf_op jit(solution)/shard_map/ppermute | solution.py:52
  114.8 4.7 %collective-permute-start.23 = (bf16[256,128]{1,0:T(8,128)(2,1)S(1)}, bf16[256,128]{1,0:T(8,128)(2,1)S(1)}, u32[]{:S(2)}, u32[]{:S(2)}) collective-permute-start(bf16[256,128]{1,0:T(8,128)(2,1)S(1)} %fusion.2), channel_id=1, source_target_pairs={{0,4},{1,5},{2,6},{3,7},{4,8},{5,9},{6,10},{7,11},{8,12},{9,13},{1... | collective-permute-start | bytes 196616 | tf_op jit(solution)/shard_map/ppermute | solution.py:52
  122.5 2.5 %collective-permute-start.25 = (bf16[256,128]{1,0:T(8,128)(2,1)S(1)}, bf16[256,128]{1,0:T(8,128)(2,1)S(1)}, u32[]{:S(2)}, u32[]{:S(2)}) collective-permute-start(bf16[256,128]{1,0:T(8,128)(2,1)S(1)} %fusion.2), channel_id=1, source_target_pairs={{0,12},{1,13},{2,14},{3,15},{4,0},{5,1},{6,2},{7,3},{8,4},{9,5},{1... | collective-permute-start | bytes 196616 | tf_op jit(solution)/shard_map/ppermute | solution.py:52
  127.8 3.6 %collective-permute-start.30 = (bf16[2,128,512]{2,1,0:T(8,128)(2,1)S(1)}, bf16[2,128,512]{2,1,0:T(8,128)(2,1)S(1)}, u32[]{:S(2)}, u32[]{:S(2)}) collective-permute-start(bf16[2,128,512]{2,1,0:T(8,128)(2,1)S(1)} %add_convert_fusion), channel_id=1, source_target_pairs={{4,0},{5,1},{6,2},{7,3},{8,4},{9,5},{10,6},{11,7},{12,8},{13,9},{1... | collective-permute-start | bytes 786440 | tf_op jit(solution)/shard_map/ppermute | solution.py:52
  131.4 3.5 %collective-permute-done.31.rest_4_ = bf16[4,256,128]{2,1,0:T(8,128)(2,1)S(1)} collective-permute-done((bf16[4,256,128]{2,1,0:T(8,128)(2,1)S(1)}, bf16[4,256,128]{2,1,0:T(8,128)(2,1)S(1)}, u32[]{:S(2)}, u32[]{:S(2)}) %collective-permute-start.31) | collective-permute-done | bytes 262176 | tf_op jit(solution)/shard_map/ppermute | solution.py:52
  134.9 3.0 %shard_map.109 = bf16[128,4096]{1,0:T(8,128)(2,1)} custom-call(bf16[4,2,768,128]{3,2,1,0:T(8,128)(2,1)S(1)} %copy-done.8, bf16[4,2,768,512]{3,2,1,0:T(8,128)(2,1)S(1)} %copy-done.4), custom_call_target="tpu_custom_call" | custom-call | bytes 10485760 | tf_op jit(solution)/shard_map/pallas_call | solution.py:514
  137.9 4.4 %shard_map.110 = (bf16[16,128,512]{2,1,0:T(8,128)(2,1)}, bf16[16,128,512]{2,1,0:T(8,128)(2,1)}) custom-call(s32[1]{0:T(128)S(6)} %copy.21.slab_index, s32[4,8]{1,0:T(4,128)S(1)} %copy-done.38, f32[2,128,512]{2,1,0:T(8,128)S(1)} %get-tuple-element.83.home, ...), custom_call_target="tpu_custom_call", output_to_operand_aliasing={{0}: (10, {}), {1}: (11, {})} | custom-call | tf_op jit(solution)/shard_map/pallas_call | solution.py:637
  (155 shorter events, 59.8 us)
Async XLA Ops:
  6.1 11.8 %collective-permute-start.3 = (bf16[2,128,512]{2,1,0:T(8,128)(2,1)}, bf16[2,128,512]{2,1,0:T(8,128)(2,1)S(1)}, u32[]{:S(2)}, u32[]{:S(2)}) collective-permute-start(bf16[2,128,512]{2,1,0:T(8,128)(2,1)} %get-tuple-element.57), channel_id=1, source_target_pairs={{0,4},{1,5},{2,6},{3,7},{4,8},{5,9},{6,10},{7,11},{8,12},{9,13},{1... | collective-permute-start | bytes 786440 | tf_op jit(solution)/shard_map/ppermute | solution.py:52
  8.8 15.6 %collective-permute-start.1 = (bf16[4,256,128]{2,1,0:T(8,128)(2,1)}, bf16[4,256,128]{2,1,0:T(8,128)(2,1)S(1)}, u32[]{:S(2)}, u32[]{:S(2)}) collective-permute-start(bf16[4,256,128]{2,1,0:T(8,128)(2,1)} %get-tuple-element.56), channel_id=1, source_target_pairs={{0,1},{1,0},{2,3},{3,2},{4,5},{5,4},{6,7},{7,6},{8,9},{9,8},{10,11... | collective-permute-start | bytes 786440 | tf_op jit(solution)/shard_map/ppermute | solution.py:52
  10.7 13.7 %collective-permute-start.2 = (bf16[4,256,128]{2,1,0:T(8,128)(2,1)}, bf16[4,256,128]{2,1,0:T(8,128)(2,1)}, u32[]{:S(2)}, u32[]{:S(2)}) collective-permute-start(bf16[4,256,128]{2,1,0:T(8,128)(2,1)} %add_convert_fusion.3), channel_id=1, source_target_pairs={{0,2},{1,3},{2,0},{3,1},{4,6},{5,7},{6,4},{7,5},{8,10},{9,11},{10,... | collective-permute-start | bytes 786440 | tf_op jit(solution)/shard_map/ppermute | solution.py:52
  19.0 10.8 %collective-permute-start.11 = (bf16[2,128,512]{2,1,0:T(8,128)(2,1)S(1)}, bf16[2,128,512]{2,1,0:T(8,128)(2,1)S(1)}, u32[]{:S(2)}, u32[]{:S(2)}) collective-permute-start(bf16[2,128,512]{2,1,0:T(8,128)(2,1)S(1)} %broadcast_select_fusion), channel_id=1, source_target_pairs={{0,2},{1,3},{2,0},{3,1},{4,6},{5,7},{6,4},{7,5},{8,10},{9,11},{10,... | collective-permute-start | bytes 786440 | tf_op jit(solution)/shard_map/ppermute | solution.py:52
  25.9 6.7 %collective-permute-start.4 = (bf16[256,128]{1,0:T(8,128)(2,1)S(1)}, bf16[256,128]{1,0:T(8,128)(2,1)S(1)}, u32[]{:S(2)}, u32[]{:S(2)}) collective-permute-start(bf16[256,128]{1,0:T(8,128)(2,1)S(1)} %get-tuple-element.92), channel_id=1, source_target_pairs={{0,4},{1,5},{2,6},{3,7},{4,8},{5,9},{6,10},{7,11},{8,12},{9,13},{1... | collective-permute-start | bytes 196616 | tf_op jit(solution)/shard_map/ppermute | solution.py:52
  25.9 8.0 %collective-permute-start.5 = (bf16[256,128]{1,0:T(8,128)(2,1)S(1)}, bf16[256,128]{1,0:T(8,128)(2,1)S(1)}, u32[]{:S(2)}, u32[]{:S(2)}) collective-permute-start(bf16[256,128]{1,0:T(8,128)(2,1)S(1)} %get-tuple-element.94), channel_id=1, source_target_pairs={{0,8},{1,9},{2,10},{3,11},{4,12},{5,13},{6,14},{7,15},{8,0},{9,1},... | collective-permute-start | bytes 196616 | tf_op jit(solution)/shard_map/ppermute | solution.py:52
  29.8 13.8 %collective-permute-start.13 = (bf16[2,128,512]{2,1,0:T(8,128)(2,1)S(1)}, bf16[2,128,512]{2,1,0:T(8,128)(2,1)S(1)}, u32[]{:S(2)}, u32[]{:S(2)}) collective-permute-start(bf16[2,128,512]{2,1,0:T(8,128)(2,1)S(1)} %copy-done.43), channel_id=1, source_target_pairs={{0,1},{1,6},{2,3},{3,8},{4,5},{5,10},{6,7},{7,12},{8,9},{9,14},{10... | collective-permute-start | bytes 786440 | tf_op jit(solution)/shard_map/ppermute | solution.py:52
  32.6 11.7 %collective-permute-start.12 = (bf16[2,128,512]{2,1,0:T(8,128)(2,1)S(1)}, bf16[2,128,512]{2,1,0:T(8,128)(2,1)S(1)}, u32[]{:S(2)}, u32[]{:S(2)}) collective-permute-start(bf16[2,128,512]{2,1,0:T(8,128)(2,1)S(1)} %collective-permute-done.11.rest_2_), channel_id=1, source_target_pairs={{0,1},{1,0},{2,3},{3,2},{4,5},{5,4},{6,7},{7,6},{8,9},{9,8},{10,11... | collective-permute-start | bytes 786440 | tf_op jit(solution)/shard_map/ppermute | solution.py:52
  34.0 7.0 %collective-permute-start.8 = (bf16[256,128]{1,0:T(8,128)(2,1)S(1)}, bf16[256,128]{1,0:T(8,128)(2,1)S(1)}, u32[]{:S(2)}, u32[]{:S(2)}) collective-permute-start(bf16[256,128]{1,0:T(8,128)(2,1)S(1)} %fusion.5._), channel_id=1, source_target_pairs={{0,4},{1,5},{2,6},{3,7},{4,8},{5,9},{6,10},{7,11},{8,12},{9,13},{1... | collective-permute-start | bytes 196616 | tf_op jit(solution)/shard_map/ppermute | solution.py:52
  35.4 7.4 %collective-permute-start.9 = (bf16[256,128]{1,0:T(8,128)(2,1)S(1)}, bf16[256,128]{1,0:T(8,128)(2,1)S(1)}, u32[]{:S(2)}, u32[]{:S(2)}) collective-permute-start(bf16[256,128]{1,0:T(8,128)(2,1)S(1)} %fusion.5._), channel_id=1, source_target_pairs={{0,8},{1,9},{2,10},{3,11},{4,12},{5,13},{6,14},{7,15},{8,0},{9,1},... | collective-permute-start | bytes 196616 | tf_op jit(solution)/shard_map/ppermute | solution.py:52
  45.0 26.4 %collective-permute-start.14 = (bf16[4,256,128]{2,1,0:T(8,128)(2,1)}, bf16[4,256,128]{2,1,0:T(8,128)(2,1)}, u32[]{:S(2)}, u32[]{:S(2)}) collective-permute-start(bf16[4,256,128]{2,1,0:T(8,128)(2,1)} %pad_maximum_fusion.rest_0_), channel_id=1, source_target_pairs={{0,2},{1,3},{2,0},{3,1},{4,6},{5,7},{6,4},{7,5},{8,10},{9,11},{10,... | collective-permute-start | bytes 786440 | tf_op jit(solution)/shard_map/ppermute | solution.py:52
  74.1 25.0 %collective-permute-start.19 = (bf16[4,256,128]{2,1,0:T(8,128)(2,1)S(1)}, bf16[4,256,128]{2,1,0:T(8,128)(2,1)S(1)}, u32[]{:S(2)}, u32[]{:S(2)}) collective-permute-start(bf16[4,256,128]{2,1,0:T(8,128)(2,1)S(1)} %add_convert_fusion.2), channel_id=1, source_target_pairs={{0,2},{1,3},{2,0},{3,1},{4,6},{5,7},{6,4},{7,5},{8,10},{9,11},{10,... | collective-permute-start | bytes 786440 | tf_op jit(solution)/shard_map/ppermute | solution.py:52
  99.1 6.3 %collective-permute-start.17 = (bf16[4,256,128]{2,1,0:T(8,128)(2,1)S(1)}, bf16[4,256,128]{2,1,0:T(8,128)(2,1)S(1)}, u32[]{:S(2)}, u32[]{:S(2)}) collective-permute-start(bf16[4,256,128]{2,1,0:T(8,128)(2,1)S(1)} %get-tuple-element.70), channel_id=1, source_target_pairs={{0,1},{1,0},{2,3},{3,2},{4,5},{5,4},{6,7},{7,6},{8,9},{9,8},{10,11... | collective-permute-start | bytes 786440 | tf_op jit(solution)/shard_map/ppermute | solution.py:52
  105.3 22.4 %collective-permute-start.29 = (bf16[2,128,512]{2,1,0:T(8,128)(2,1)S(1)}, bf16[2,128,512]{2,1,0:T(8,128)(2,1)S(1)}, u32[]{:S(2)}, u32[]{:S(2)}) collective-permute-start(bf16[2,128,512]{2,1,0:T(8,128)(2,1)S(1)} %get-tuple-element.85), channel_id=1, source_target_pairs={{0,1},{1,0},{2,3},{3,2},{4,5},{5,4},{6,7},{7,6},{8,9},{9,8},{10,11... | collective-permute-start | bytes 786440 | tf_op jit(solution)/shard_map/ppermute | solution.py:52
  105.6 6.8 %collective-permute-start.20 = (bf16[256,128]{1,0:T(8,128)(2,1)S(1)}, bf16[256,128]{1,0:T(8,128)(2,1)S(1)}, u32[]{:S(2)}, u32[]{:S(2)}) collective-permute-start(bf16[256,128]{1,0:T(8,128)(2,1)S(1)} %get-tuple-element.89), channel_id=1, source_target_pairs={{0,4},{1,5},{2,6},{3,7},{4,8},{5,9},{6,10},{7,11},{8,12},{9,13},{1... | collective-permute-start | bytes 196616 | tf_op jit(solution)/shard_map/ppermute | solution.py:52
  106.8 7.9 %collective-permute-start.21 = (bf16[256,128]{1,0:T(8,128)(2,1)S(1)}, bf16[256,128]{1,0:T(8,128)(2,1)S(1)}, u32[]{:S(2)}, u32[]{:S(2)}) collective-permute-start(bf16[256,128]{1,0:T(8,128)(2,1)S(1)} %get-tuple-element.91), channel_id=1, source_target_pairs={{0,8},{1,9},{2,10},{3,11},{4,12},{5,13},{6,14},{7,15},{8,0},{9,1},... | collective-permute-start | bytes 196616 | tf_op jit(solution)/shard_map/ppermute | solution.py:52
  108.9 5.9 %collective-permute-start.22 = (bf16[256,128]{1,0:T(8,128)(2,1)S(1)}, bf16[256,128]{1,0:T(8,128)(2,1)S(1)}, u32[]{:S(2)}, u32[]{:S(2)}) collective-permute-start(bf16[256,128]{1,0:T(8,128)(2,1)S(1)} %get-tuple-element.90), channel_id=1, source_target_pairs={{0,12},{1,13},{2,14},{3,15},{4,0},{5,1},{6,2},{7,3},{8,4},{9,5},{1... | collective-permute-start | bytes 196616 | tf_op jit(solution)/shard_map/ppermute | solution.py:52
  109.9 17.2 %collective-permute-start.28 = (bf16[2,128,512]{2,1,0:T(8,128)(2,1)S(1)}, bf16[2,128,512]{2,1,0:T(8,128)(2,1)S(1)}, u32[]{:S(2)}, u32[]{:S(2)}) collective-permute-start(bf16[2,128,512]{2,1,0:T(8,128)(2,1)S(1)} %get-tuple-element.80), channel_id=1, source_target_pairs={{1,0},{6,1},{3,2},{8,3},{5,4},{10,5},{7,6},{12,7},{9,8},{14,9},{11... | collective-permute-start | bytes 786440 | tf_op jit(solution)/shard_map/ppermute | solution.py:52
  112.4 14.7 %collective-permute-start.27 = (bf16[2,128,512]{2,1,0:T(8,128)(2,1)S(1)}, bf16[2,128,512]{2,1,0:T(8,128)(2,1)S(1)}, u32[]{:S(2)}, u32[]{:S(2)}) collective-permute-start(bf16[2,128,512]{2,1,0:T(8,128)(2,1)S(1)} %add_convert_fusion.1), channel_id=1, source_target_pairs={{0,2},{1,3},{2,0},{3,1},{4,6},{5,7},{6,4},{7,5},{8,10},{9,11},{10,... | collective-permute-start | bytes 786440 | tf_op jit(solution)/shard_map/ppermute | solution.py:52
  114.8 7.7 %collective-permute-start.23 = (bf16[256,128]{1,0:T(8,128)(2,1)S(1)}, bf16[256,128]{1,0:T(8,128)(2,1)S(1)}, u32[]{:S(2)}, u32[]{:S(2)}) collective-permute-start(bf16[256,128]{1,0:T(8,128)(2,1)S(1)} %fusion.2), channel_id=1, source_target_pairs={{0,4},{1,5},{2,6},{3,7},{4,8},{5,9},{6,10},{7,11},{8,12},{9,13},{1... | collective-permute-start | bytes 196616 | tf_op jit(solution)/shard_map/ppermute | solution.py:52
  119.5 6.9 %collective-permute-start.24 = (bf16[256,128]{1,0:T(8,128)(2,1)S(1)}, bf16[256,128]{1,0:T(8,128)(2,1)S(1)}, u32[]{:S(2)}, u32[]{:S(2)}) collective-permute-start(bf16[256,128]{1,0:T(8,128)(2,1)S(1)} %fusion.2), channel_id=1, source_target_pairs={{0,8},{1,9},{2,10},{3,11},{4,12},{5,13},{6,14},{7,15},{8,0},{9,1},... | collective-permute-start | bytes 196616 | tf_op jit(solution)/shard_map/ppermute | solution.py:52
  127.1 7.8 %collective-permute-start.31 = (bf16[4,256,128]{2,1,0:T(8,128)(2,1)S(1)}, bf16[4,256,128]{2,1,0:T(8,128)(2,1)S(1)}, u32[]{:S(2)}, u32[]{:S(2)}) collective-permute-start(bf16[4,256,128]{2,1,0:T(8,128)(2,1)S(1)} %pad_maximum_fusion.1.rest_3_), channel_id=1, source_target_pairs={{0,2},{1,3},{2,0},{3,1},{4,6},{5,7},{6,4},{7,5},{8,10},{9,11},{10,... | collective-permute-start | bytes 786440 | tf_op jit(solution)/shard_map/ppermute | solution.py:52
  127.7 10.2 %collective-permute-start.32 = (bf16[4,256,128]{2,1,0:T(8,128)(2,1)S(1)}, bf16[4,256,128]{2,1,0:T(8,128)(2,1)S(1)}, u32[]{:S(2)}, u32[]{:S(2)}) collective-permute-start(bf16[4,256,128]{2,1,0:T(8,128)(2,1)S(1)} %pad_maximum_fusion.1.rest_3_), channel_id=1, source_target_pairs={{0,1},{1,0},{2,3},{3,2},{4,5},{5,4},{6,7},{7,6},{8,9},{9,8},{10,11... | collective-permute-start | bytes 786440 | tf_op jit(solution)/shard_map/ppermute | solution.py:52
  127.8 10.1 %collective-permute-start.30 = (bf16[2,128,512]{2,1,0:T(8,128)(2,1)S(1)}, bf16[2,128,512]{2,1,0:T(8,128)(2,1)S(1)}, u32[]{:S(2)}, u32[]{:S(2)}) collective-permute-start(bf16[2,128,512]{2,1,0:T(8,128)(2,1)S(1)} %add_convert_fusion), channel_id=1, source_target_pairs={{4,0},{5,1},{6,2},{7,3},{8,4},{9,5},{10,6},{11,7},{12,8},{13,9},{1... | collective-permute-start | bytes 786440 | tf_op jit(solution)/shard_map/ppermute | solution.py:52
  (54 other events, 327.1 us)

commit v11 on v10

--- a/solution.py
+++ b/solution.py
@@ -10,7 +10,7 @@
 
 BLOCK = 64
 WDEV = 5
-VMEM_LIMIT = 20 * 1024 * 1024
+VMEM_LIMIT = 60 * 1024 * 1024
 PACK_VMEM = 60 * 1024 * 1024
 JOIN = 4
 BF16 = jnp.bfloat16

time: 143 us -> 121 us (0.85)
  local copies, waits for them, and re-layouts: 38.8 us -> 2.93 us
  Pallas kernels: 32.2 us -> 47.2 us
  other arithmetic: 6.52 us -> 4.55 us
    unnamed x88 -> x46, local copies, waits for them, and re-layouts: 38.7 us -> 2.9 us
    pallas_call x2, Pallas kernels: 14 us -> 19.8 us  [attend(): pl.pallas_call(functools.partial(attend_kernel, lines=lines, nv=nv, ns=ns...]
    pallas_call x1, Pallas kernels: 1.37 us -> 4.58 us  [prepare(): pl.pallas_call(functools.partial(prepare_kernel, head_dim=head_dim), grid...]
    pallas_call x1, Pallas kernels: 2.86 us -> 5.98 us  [window_gradients(): pl.pallas_call(functools.partial(window_kernel, lines=lines, ns=ns, per_d...]
    pallas_call x1, Pallas kernels: 2.97 us -> 5.77 us  [query_gradients(): pl.pallas_call(query_kernel, grid=(heads,), in_specs=[by_head(cand_keys.s...]
  transfers between devices with their start and end apart: 34 -> 34, of which waited for: 12 -> 12; matrix products, arithmetic and copies ran while one was open for 5% -> 4% of each run, Pallas kernels for 16% -> 32%
where the time goes in v11:
time: 121 us; the launch traced here: 120 us
  Pallas kernels  47.2 us (39%)
  starting transfers between devices  38.9 us (32%)
  waiting for transfers between devices  24.9 us (21%)
  other arithmetic  4.55 us (4%)
  local copies, waits for them, and re-layouts  2.93 us (2%)
  between operations  1.71 us (1%)
    ppermute x34, starting transfers between devices, move(): return lax.ppermute(array, 'ctx', pairs)  38.9 us
    ppermute x34, waiting for transfers between devices, move(): return lax.ppermute(array, 'ctx', pairs)  24.9 us
    pallas_call x2, Pallas kernels, attend(): pl.pallas_call(functools.partial(attend_kernel, lines=lines, nv=nv, ns=ns...  19.8 us
    pallas_call x1, Pallas kernels, window_gradients(): pl.pallas_call(functools.partial(window_kernel, lines=lines, ns=ns, per_d...  5.98 us
    pallas_call x1, Pallas kernels, query_gradients(): pl.pallas_call(query_kernel, grid=(heads,), in_specs=[by_head(cand_keys.s...  5.77 us
    pallas_call x1, Pallas kernels, prepare(): pl.pallas_call(functools.partial(prepare_kernel, head_dim=head_dim), grid...  4.58 us
    pallas_call x1, Pallas kernels, assemble(): pl.pallas_call(functools.partial(assemble_kernel, lines=lines, heads=head...  4.56 us
    pallas_call x1, Pallas kernels, pack(): pl.pallas_call(functools.partial(pack_kernel, lines=lines, heads=heads, n...  4.19 us
  transfers between devices with their start and end apart: 34, of which 12 were waited for; matrix products, arithmetic and copies ran while one was open for 4% of the time, Pallas kernels for 32%

profile of v11, /device:TPU:0, one launch (start us, length us, event | category | flops | bytes accessed | tf_op | source)
XLA Modules:
  0.0 120.2 jit_solution(9893561002532964907)
XLA Ops:
  1.3 4.2 %shard_map.103 = (bf16[2,128,512]{2,1,0:T(8,128)(2,1)}, bf16[2,128,512]{2,1,0:T(8,128)(2,1)}, bf16[2,128,512]{2,1,0:T(8,128)(2,1)}, bf16[4,256,128]{2,1,0:T(8,12...) custom-call(s32[1]{0:T(128)S(6)} %copy.21.slab_index, ...), custom_call_target="tpu_custom_call" | custom-call | tf_op jit(solution)/shard_map/pallas_call | solution.py:168
  6.0 2.6 %collective-permute-start.3 = (bf16[2,128,512]{2,1,0:T(8,128)(2,1)}, bf16[2,128,512]{2,1,0:T(8,128)(2,1)S(1)}, u32[]{:S(2)}, u32[]{:S(2)}) collective-permute-start(bf16[2,128,512]{2,1,0:T(8,128)(2,1)} %get-tuple-element.57), channel_id=1, source_target_pairs={{0,4},{1,5},{2,6},{3,7},{4,8},{5,9},{6,10},{7,11},{8,12},{9,13},{1... | collective-permute-start | bytes 786440 | tf_op jit(solution)/shard_map/ppermute | solution.py:52
  11.4 6.4 %collective-permute-done.3.rest_3_ = bf16[2,128,512]{2,1,0:T(8,128)(2,1)S(1)} collective-permute-done((bf16[2,128,512]{2,1,0:T(8,128)(2,1)}, bf16[2,128,512]{2,1,0:T(8,128)(2,1)S(1)}, u32[]{:S(2)}, u32[]{:S(2)}) %collective-permute-start.3) | collective-permute-done | bytes 262176 | tf_op jit(solution)/shard_map/ppermute | solution.py:52
  19.4 4.6 %shard_map.104 = (bf16[4,2,512,128]{3,2,1,0:T(8,128)(2,1)}, bf16[4,2,512,128]{3,2,1,0:T(8,128)(2,1)}, bf16[4,2,128,512]{3,2,1,0:T(8,128)(2,1)}, bf16[4,2,128,512]{3,2,1,0:T(8,128)(2,1)}, f32[4,2,8,512]{3,2,1,0:T(8,128)}) custom-call(bf16[128,4096]{1,0:T(8,128)(2,1)} %q, bf16[128,4096]{1,0:T(8,128)(2,1)} %grad.1, bf16[128,4096]{1,0:T(8,128)(2,1)} %out.1), custom_call_target="tpu_custom_call" | custom-call | bytes 7340032 | tf_op jit(solution)/shard_map/pallas_call | solution.py:240
  24.2 2.3 %collective-permute-start.5 = (bf16[256,128]{1,0:T(8,128)(2,1)S(1)}, bf16[256,128]{1,0:T(8,128)(2,1)S(1)}, u32[]{:S(2)}, u32[]{:S(2)}) collective-permute-start(bf16[256,128]{1,0:T(8,128)(2,1)S(1)} %get-tuple-element.94), channel_id=1, source_target_pairs={{0,8},{1,9},{2,10},{3,11},{4,12},{5,13},{6,14},{7,15},{8,0},{9,1},... | collective-permute-start | bytes 196616 | tf_op jit(solution)/shard_map/ppermute | solution.py:52
  28.6 2.3 %collective-permute-done.4 = bf16[256,128]{1,0:T(8,128)(2,1)S(1)} collective-permute-done((bf16[256,128]{1,0:T(8,128)(2,1)S(1)}, bf16[256,128]{1,0:T(8,128)(2,1)S(1)}, u32[]{:S(2)}, u32[]{:S(2)}) %collective-permute-start.4) | collective-permute-done | bytes 65568 | tf_op jit(solution)/shard_map/ppermute | solution.py:52
  33.7 1.6 %collective-permute-start.9 = (bf16[256,128]{1,0:T(8,128)(2,1)S(1)}, bf16[256,128]{1,0:T(8,128)(2,1)S(1)}, u32[]{:S(2)}, u32[]{:S(2)}) collective-permute-start(bf16[256,128]{1,0:T(8,128)(2,1)S(1)} %fusion.5._), channel_id=1, source_target_pairs={{0,8},{1,9},{2,10},{3,11},{4,12},{5,13},{6,14},{7,15},{8,0},{9,1},... | collective-permute-start | bytes 196616 | tf_op jit(solution)/shard_map/ppermute | solution.py:52
  36.2 2.3 %shard_map.105 = (bf16[16,128,512]{2,1,0:T(8,128)(2,1)}, bf16[16,128,512]{2,1,0:T(8,128)(2,1)}) custom-call(bf16[256,128]{1,0:T(8,128)(2,1)} %copy-done.3), custom_call_target="tpu_custom_call" | custom-call | bytes 5242880 | tf_op jit(solution)/shard_map/pallas_call | solution.py:540
  39.3 1.8 %collective-permute-done.9 = bf16[256,128]{1,0:T(8,128)(2,1)S(1)} collective-permute-done((bf16[256,128]{1,0:T(8,128)(2,1)S(1)}, bf16[256,128]{1,0:T(8,128)(2,1)S(1)}, u32[]{:S(2)}, u32[]{:S(2)}) %collective-permute-start.9) | collective-permute-done | bytes 65568 | tf_op jit(solution)/shard_map/ppermute | solution.py:52
  42.1 4.3 %collective-permute-start.14 = (bf16[4,256,128]{2,1,0:T(8,128)(2,1)S(1)}, bf16[4,256,128]{2,1,0:T(8,128)(2,1)S(1)}, u32[]{:S(2)}, u32[]{:S(2)}) collective-permute-start(bf16[4,256,128]{2,1,0:T(8,128)(2,1)S(1)} %pad_maximum_fusion.rest_0_), channel_id=1, source_target_pairs={{0,2},{1,3},{2,0},{3,1},{4,6},{5,7},{6,4},{7,5},{8,10},{9,11},{10,... | collective-permute-start | bytes 786440 | tf_op jit(solution)/shard_map/ppermute | solution.py:52
  47.1 9.8 %shard_map.106 = (bf16[4,256,128]{2,1,0:T(8,128)(2,1)}, bf16[4,256,128]{2,1,0:T(8,128)(2,1)}, bf16[4,2,256,512]{3,2,1,0:T(8,128)(2,1)}, bf16[4,2,768,512]{3,2,1,0:T(8,128)(2,1)}, bf16[4,2,768,128]{3,2,1,0:T(8,128)(2,1)}) custom-call(s32[1]{0:T(128)} %bitcast.9.base, s32[1]{0:T(128)S(6)} %copy.21.slab_index, s32[4,8]{1,0:T(4,128)} %verts.7, s32[4,3]{1,0:T(4,128)} %offs.4, ...), custom_call_target="tpu_custom_call" | custom-call | flops 2013265920 | bytes 12582912 | tf_op jit(solution)/shard_map/pallas_call | solution.py:407
  59.8 1.6 %collective-permute-start.19 = (bf16[4,256,128]{2,1,0:T(8,128)(2,1)S(1)}, bf16[4,256,128]{2,1,0:T(8,128)(2,1)S(1)}, u32[]{:S(2)}, u32[]{:S(2)}) collective-permute-start(bf16[4,256,128]{2,1,0:T(8,128)(2,1)S(1)} %add_convert_fusion.2), channel_id=1, source_target_pairs={{0,2},{1,3},{2,0},{3,1},{4,6},{5,7},{6,4},{7,5},{8,10},{9,11},{10,... | collective-permute-start | bytes 786440 | tf_op jit(solution)/shard_map/ppermute | solution.py:52
  62.1 10.0 %shard_map.107 = (f32[4,256,128]{2,1,0:T(8,128)}, bf16[4,256,128]{2,1,0:T(8,128)(2,1)}, bf16[4,2,256,512]{3,2,1,0:T(8,128)(2,1)}, bf16[4,2,768,512]{3,2,1,0:T(8,128)(2,1)}, bf16[4,2,768,128]{3,2,1,0:T(8,128)(2,1)}) custom-call(s32[1]{0:T(128)} %bitcast.base, s32[1]{0:T(128)S(6)} %copy.21.slab_index, ...), custom_call_target="tpu_custom_call", output_to_operand_aliasing={{2}: (17, {}), {3}: (18, {}), {4}: (19, {})} | custom-call | flops 2013265920 | bytes 12582912 | tf_op jit(solution)/shard_map/pallas_call | solution.py:407
  72.2 6.0 %shard_map.108 = (f32[2,128,512]{2,1,0:T(8,128)}, f32[2,128,512]{2,1,0:T(8,128)}, f32[2,128,512]{2,1,0:T(8,128)}, bf16[2,128,512]{2,1,0:T(8,128)(2,1)}, bf16[2,1...) custom-call(s32[4,3]{1,0:T(4,128)} %offs.4, bf16[4,2,512,128]{3,2,1,0:T(8,128)(2,1)} %get-tuple-element.49.qs, ...), custom_call_target="tpu_custom_call" | custom-call | bytes 9437184 | tf_op jit(solution)/shard_map/pallas_call | solution.py:480
  80.2 2.1 %collective-permute-start.21 = (bf16[256,128]{1,0:T(8,128)(2,1)S(1)}, bf16[256,128]{1,0:T(8,128)(2,1)S(1)}, u32[]{:S(2)}, u32[]{:S(2)}) collective-permute-start(bf16[256,128]{1,0:T(8,128)(2,1)S(1)} %get-tuple-element.91), channel_id=1, source_target_pairs={{0,8},{1,9},{2,10},{3,11},{4,12},{5,13},{6,14},{7,15},{8,0},{9,1},... | collective-permute-start | bytes 196616 | tf_op jit(solution)/shard_map/ppermute | solution.py:52
  84.1 1.8 %collective-permute-done.20 = bf16[256,128]{1,0:T(8,128)(2,1)S(1)} collective-permute-done((bf16[256,128]{1,0:T(8,128)(2,1)S(1)}, bf16[256,128]{1,0:T(8,128)(2,1)S(1)}, u32[]{:S(2)}, u32[]{:S(2)}) %collective-permute-start.20) | collective-permute-done | bytes 65568 | tf_op jit(solution)/shard_map/ppermute | solution.py:52
  86.3 1.9 %collective-permute-done.21 = bf16[256,128]{1,0:T(8,128)(2,1)S(1)} collective-permute-done((bf16[256,128]{1,0:T(8,128)(2,1)S(1)}, bf16[256,128]{1,0:T(8,128)(2,1)S(1)}, u32[]{:S(2)}, u32[]{:S(2)}) %collective-permute-start.21) | collective-permute-done | bytes 65568 | tf_op jit(solution)/shard_map/ppermute | solution.py:52
  88.2 4.7 %collective-permute-start.23 = (bf16[256,128]{1,0:T(8,128)(2,1)S(1)}, bf16[256,128]{1,0:T(8,128)(2,1)S(1)}, u32[]{:S(2)}, u32[]{:S(2)}) collective-permute-start(bf16[256,128]{1,0:T(8,128)(2,1)S(1)} %fusion.2), channel_id=1, source_target_pairs={{0,4},{1,5},{2,6},{3,7},{4,8},{5,9},{6,10},{7,11},{8,12},{9,13},{1... | collective-permute-start | bytes 196616 | tf_op jit(solution)/shard_map/ppermute | solution.py:52
  94.2 1.7 %collective-permute-done.23 = bf16[256,128]{1,0:T(8,128)(2,1)S(1)} collective-permute-done((bf16[256,128]{1,0:T(8,128)(2,1)S(1)}, bf16[256,128]{1,0:T(8,128)(2,1)S(1)}, u32[]{:S(2)}, u32[]{:S(2)}) %collective-permute-start.23) | collective-permute-done | bytes 65568 | tf_op jit(solution)/shard_map/ppermute | solution.py:52
  95.9 2.5 %collective-permute-start.25 = (bf16[256,128]{1,0:T(8,128)(2,1)S(1)}, bf16[256,128]{1,0:T(8,128)(2,1)S(1)}, u32[]{:S(2)}, u32[]{:S(2)}) collective-permute-start(bf16[256,128]{1,0:T(8,128)(2,1)S(1)} %fusion.2), channel_id=1, source_target_pairs={{0,12},{1,13},{2,14},{3,15},{4,0},{5,1},{6,2},{7,3},{8,4},{9,5},{1... | collective-permute-start | bytes 196616 | tf_op jit(solution)/shard_map/ppermute | solution.py:52
  101.4 3.5 %collective-permute-start.30 = (bf16[2,128,512]{2,1,0:T(8,128)(2,1)S(1)}, bf16[2,128,512]{2,1,0:T(8,128)(2,1)S(1)}, u32[]{:S(2)}, u32[]{:S(2)}) collective-permute-start(bf16[2,128,512]{2,1,0:T(8,128)(2,1)S(1)} %add_convert_fusion), channel_id=1, source_target_pairs={{4,0},{5,1},{6,2},{7,3},{8,4},{9,5},{10,6},{11,7},{12,8},{13,9},{1... | collective-permute-start | bytes 786440 | tf_op jit(solution)/shard_map/ppermute | solution.py:52
  104.9 3.5 %collective-permute-done.31.rest_4_ = bf16[4,256,128]{2,1,0:T(8,128)(2,1)S(1)} collective-permute-done((bf16[4,256,128]{2,1,0:T(8,128)(2,1)S(1)}, bf16[4,256,128]{2,1,0:T(8,128)(2,1)S(1)}, u32[]{:S(2)}, u32[]{:S(2)}) %collective-permute-start.31) | collective-permute-done | bytes 262176 | tf_op jit(solution)/shard_map/ppermute | solution.py:52
  108.4 5.8 %shard_map.109 = bf16[128,4096]{1,0:T(8,128)(2,1)} custom-call(bf16[4,2,768,128]{3,2,1,0:T(8,128)(2,1)} %get-tuple-element.82.cand_keys, bf16[4,2,768,512]{3,2,1,0:T(8,128)(2,1)} %get-tuple-element.75.low_ds), custom_call_target="tpu_custom_call" | custom-call | bytes 10485760 | tf_op jit(solution)/shard_map/pallas_call | solution.py:514
  115.7 4.6 %shard_map.110 = (bf16[16,128,512]{2,1,0:T(8,128)(2,1)}, bf16[16,128,512]{2,1,0:T(8,128)(2,1)}) custom-call(s32[1]{0:T(128)S(6)} %copy.21.slab_index, s32[4,8]{1,0:T(4,128)} %verts.7, f32[2,128,512]{2,1,0:T(8,128)} %get-tuple-element.83.home, bf16[2,128,512]{2,1,0:T(8,128)(2,1)} %copy-done.1, ...), custom_call_target="tpu_custom_call", output_to_operand_aliasing={{0}: (10, {}), {1}: (11, {})} | custom-call | tf_op jit(solution)/shard_map/pallas_call | solution.py:637
  (113 shorter events, 26.7 us)
Async XLA Ops:
  6.0 11.8 %collective-permute-start.3 = (bf16[2,128,512]{2,1,0:T(8,128)(2,1)}, bf16[2,128,512]{2,1,0:T(8,128)(2,1)S(1)}, u32[]{:S(2)}, u32[]{:S(2)}) collective-permute-start(bf16[2,128,512]{2,1,0:T(8,128)(2,1)} %get-tuple-element.57), channel_id=1, source_target_pairs={{0,4},{1,5},{2,6},{3,7},{4,8},{5,9},{6,10},{7,11},{8,12},{9,13},{1... | collective-permute-start | bytes 786440 | tf_op jit(solution)/shard_map/ppermute | solution.py:52
  8.7 15.3 %collective-permute-start.1 = (bf16[4,256,128]{2,1,0:T(8,128)(2,1)}, bf16[4,256,128]{2,1,0:T(8,128)(2,1)S(1)}, u32[]{:S(2)}, u32[]{:S(2)}) collective-permute-start(bf16[4,256,128]{2,1,0:T(8,128)(2,1)} %get-tuple-element.56), channel_id=1, source_target_pairs={{0,1},{1,0},{2,3},{3,2},{4,5},{5,4},{6,7},{7,6},{8,9},{9,8},{10,11... | collective-permute-start | bytes 786440 | tf_op jit(solution)/shard_map/ppermute | solution.py:52
  9.9 14.1 %collective-permute-start.2 = (bf16[4,256,128]{2,1,0:T(8,128)(2,1)S(1)}, bf16[4,256,128]{2,1,0:T(8,128)(2,1)S(1)}, u32[]{:S(2)}, u32[]{:S(2)}) collective-permute-start(bf16[4,256,128]{2,1,0:T(8,128)(2,1)S(1)} %add_convert_fusion.3), channel_id=1, source_target_pairs={{0,2},{1,3},{2,0},{3,1},{4,6},{5,7},{6,4},{7,5},{8,10},{9,11},{10,... | collective-permute-start | bytes 786440 | tf_op jit(solution)/shard_map/ppermute | solution.py:52
  18.9 9.1 %collective-permute-start.11 = (bf16[2,128,512]{2,1,0:T(8,128)(2,1)S(1)}, bf16[2,128,512]{2,1,0:T(8,128)(2,1)S(1)}, u32[]{:S(2)}, u32[]{:S(2)}) collective-permute-start(bf16[2,128,512]{2,1,0:T(8,128)(2,1)S(1)} %broadcast_select_fusion), channel_id=1, source_target_pairs={{0,2},{1,3},{2,0},{3,1},{4,6},{5,7},{6,4},{7,5},{8,10},{9,11},{10,... | collective-permute-start | bytes 786440 | tf_op jit(solution)/shard_map/ppermute | solution.py:52
  24.2 6.7 %collective-permute-start.4 = (bf16[256,128]{1,0:T(8,128)(2,1)S(1)}, bf16[256,128]{1,0:T(8,128)(2,1)S(1)}, u32[]{:S(2)}, u32[]{:S(2)}) collective-permute-start(bf16[256,128]{1,0:T(8,128)(2,1)S(1)} %get-tuple-element.92), channel_id=1, source_target_pairs={{0,4},{1,5},{2,6},{3,7},{4,8},{5,9},{6,10},{7,11},{8,12},{9,13},{1... | collective-permute-start | bytes 196616 | tf_op jit(solution)/shard_map/ppermute | solution.py:52
  24.2 8.0 %collective-permute-start.5 = (bf16[256,128]{1,0:T(8,128)(2,1)S(1)}, bf16[256,128]{1,0:T(8,128)(2,1)S(1)}, u32[]{:S(2)}, u32[]{:S(2)}) collective-permute-start(bf16[256,128]{1,0:T(8,128)(2,1)S(1)} %get-tuple-element.94), channel_id=1, source_target_pairs={{0,8},{1,9},{2,10},{3,11},{4,12},{5,13},{6,14},{7,15},{8,0},{9,1},... | collective-permute-start | bytes 196616 | tf_op jit(solution)/shard_map/ppermute | solution.py:52
  28.1 13.9 %collective-permute-start.13 = (bf16[2,128,512]{2,1,0:T(8,128)(2,1)S(1)}, bf16[2,128,512]{2,1,0:T(8,128)(2,1)S(1)}, u32[]{:S(2)}, u32[]{:S(2)}) collective-permute-start(bf16[2,128,512]{2,1,0:T(8,128)(2,1)S(1)} %copy-done.20), channel_id=1, source_target_pairs={{0,1},{1,6},{2,3},{3,8},{4,5},{5,10},{6,7},{7,12},{8,9},{9,14},{10... | collective-permute-start | bytes 786440 | tf_op jit(solution)/shard_map/ppermute | solution.py:52
  30.9 11.1 %collective-permute-start.12 = (bf16[2,128,512]{2,1,0:T(8,128)(2,1)S(1)}, bf16[2,128,512]{2,1,0:T(8,128)(2,1)S(1)}, u32[]{:S(2)}, u32[]{:S(2)}) collective-permute-start(bf16[2,128,512]{2,1,0:T(8,128)(2,1)S(1)} %collective-permute-done.11.rest_2_), channel_id=1, source_target_pairs={{0,1},{1,0},{2,3},{3,2},{4,5},{5,4},{6,7},{7,6},{8,9},{9,8},{10,11... | collective-permute-start | bytes 786440 | tf_op jit(solution)/shard_map/ppermute | solution.py:52
  32.3 7.0 %collective-permute-start.8 = (bf16[256,128]{1,0:T(8,128)(2,1)S(1)}, bf16[256,128]{1,0:T(8,128)(2,1)S(1)}, u32[]{:S(2)}, u32[]{:S(2)}) collective-permute-start(bf16[256,128]{1,0:T(8,128)(2,1)S(1)} %fusion.5._), channel_id=1, source_target_pairs={{0,4},{1,5},{2,6},{3,7},{4,8},{5,9},{6,10},{7,11},{8,12},{9,13},{1... | collective-permute-start | bytes 196616 | tf_op jit(solution)/shard_map/ppermute | solution.py:52
  33.7 7.4 %collective-permute-start.9 = (bf16[256,128]{1,0:T(8,128)(2,1)S(1)}, bf16[256,128]{1,0:T(8,128)(2,1)S(1)}, u32[]{:S(2)}, u32[]{:S(2)}) collective-permute-start(bf16[256,128]{1,0:T(8,128)(2,1)S(1)} %fusion.5._), channel_id=1, source_target_pairs={{0,8},{1,9},{2,10},{3,11},{4,12},{5,13},{6,14},{7,15},{8,0},{9,1},... | collective-permute-start | bytes 196616 | tf_op jit(solution)/shard_map/ppermute | solution.py:52
  42.1 15.1 %collective-permute-start.14 = (bf16[4,256,128]{2,1,0:T(8,128)(2,1)S(1)}, bf16[4,256,128]{2,1,0:T(8,128)(2,1)S(1)}, u32[]{:S(2)}, u32[]{:S(2)}) collective-permute-start(bf16[4,256,128]{2,1,0:T(8,128)(2,1)S(1)} %pad_maximum_fusion.rest_0_), channel_id=1, source_target_pairs={{0,2},{1,3},{2,0},{3,1},{4,6},{5,7},{6,4},{7,5},{8,10},{9,11},{10,... | collective-permute-start | bytes 786440 | tf_op jit(solution)/shard_map/ppermute | solution.py:52
  59.8 12.4 %collective-permute-start.19 = (bf16[4,256,128]{2,1,0:T(8,128)(2,1)S(1)}, bf16[4,256,128]{2,1,0:T(8,128)(2,1)S(1)}, u32[]{:S(2)}, u32[]{:S(2)}) collective-permute-start(bf16[4,256,128]{2,1,0:T(8,128)(2,1)S(1)} %add_convert_fusion.2), channel_id=1, source_target_pairs={{0,2},{1,3},{2,0},{3,1},{4,6},{5,7},{6,4},{7,5},{8,10},{9,11},{10,... | collective-permute-start | bytes 786440 | tf_op jit(solution)/shard_map/ppermute | solution.py:52
  72.1 6.7 %collective-permute-start.17 = (bf16[4,256,128]{2,1,0:T(8,128)(2,1)}, bf16[4,256,128]{2,1,0:T(8,128)(2,1)S(1)}, u32[]{:S(2)}, u32[]{:S(2)}) collective-permute-start(bf16[4,256,128]{2,1,0:T(8,128)(2,1)} %get-tuple-element.70), channel_id=1, source_target_pairs={{0,1},{1,0},{2,3},{3,2},{4,5},{5,4},{6,7},{7,6},{8,9},{9,8},{10,11... | collective-permute-start | bytes 786440 | tf_op jit(solution)/shard_map/ppermute | solution.py:52
  78.8 22.5 %collective-permute-start.29 = (bf16[2,128,512]{2,1,0:T(8,128)(2,1)}, bf16[2,128,512]{2,1,0:T(8,128)(2,1)S(1)}, u32[]{:S(2)}, u32[]{:S(2)}) collective-permute-start(bf16[2,128,512]{2,1,0:T(8,128)(2,1)} %get-tuple-element.85), channel_id=1, source_target_pairs={{0,1},{1,0},{2,3},{3,2},{4,5},{5,4},{6,7},{7,6},{8,9},{9,8},{10,11... | collective-permute-start | bytes 786440 | tf_op jit(solution)/shard_map/ppermute | solution.py:52
  79.0 6.8 %collective-permute-start.20 = (bf16[256,128]{1,0:T(8,128)(2,1)S(1)}, bf16[256,128]{1,0:T(8,128)(2,1)S(1)}, u32[]{:S(2)}, u32[]{:S(2)}) collective-permute-start(bf16[256,128]{1,0:T(8,128)(2,1)S(1)} %get-tuple-element.89), channel_id=1, source_target_pairs={{0,4},{1,5},{2,6},{3,7},{4,8},{5,9},{6,10},{7,11},{8,12},{9,13},{1... | collective-permute-start | bytes 196616 | tf_op jit(solution)/shard_map/ppermute | solution.py:52
  80.2 7.9 %collective-permute-start.21 = (bf16[256,128]{1,0:T(8,128)(2,1)S(1)}, bf16[256,128]{1,0:T(8,128)(2,1)S(1)}, u32[]{:S(2)}, u32[]{:S(2)}) collective-permute-start(bf16[256,128]{1,0:T(8,128)(2,1)S(1)} %get-tuple-element.91), channel_id=1, source_target_pairs={{0,8},{1,9},{2,10},{3,11},{4,12},{5,13},{6,14},{7,15},{8,0},{9,1},... | collective-permute-start | bytes 196616 | tf_op jit(solution)/shard_map/ppermute | solution.py:52
  82.3 5.9 %collective-permute-start.22 = (bf16[256,128]{1,0:T(8,128)(2,1)S(1)}, bf16[256,128]{1,0:T(8,128)(2,1)S(1)}, u32[]{:S(2)}, u32[]{:S(2)}) collective-permute-start(bf16[256,128]{1,0:T(8,128)(2,1)S(1)} %get-tuple-element.90), channel_id=1, source_target_pairs={{0,12},{1,13},{2,14},{3,15},{4,0},{5,1},{6,2},{7,3},{8,4},{9,5},{1... | collective-permute-start | bytes 196616 | tf_op jit(solution)/shard_map/ppermute | solution.py:52
  83.4 17.2 %collective-permute-start.28 = (bf16[2,128,512]{2,1,0:T(8,128)(2,1)S(1)}, bf16[2,128,512]{2,1,0:T(8,128)(2,1)S(1)}, u32[]{:S(2)}, u32[]{:S(2)}) collective-permute-start(bf16[2,128,512]{2,1,0:T(8,128)(2,1)S(1)} %copy-done.21), channel_id=1, source_target_pairs={{1,0},{6,1},{3,2},{8,3},{5,4},{10,5},{7,6},{12,7},{9,8},{14,9},{11... | collective-permute-start | bytes 786440 | tf_op jit(solution)/shard_map/ppermute | solution.py:52
  85.8 14.7 %collective-permute-start.27 = (bf16[2,128,512]{2,1,0:T(8,128)(2,1)S(1)}, bf16[2,128,512]{2,1,0:T(8,128)(2,1)S(1)}, u32[]{:S(2)}, u32[]{:S(2)}) collective-permute-start(bf16[2,128,512]{2,1,0:T(8,128)(2,1)S(1)} %add_convert_fusion.1), channel_id=1, source_target_pairs={{0,2},{1,3},{2,0},{3,1},{4,6},{5,7},{6,4},{7,5},{8,10},{9,11},{10,... | collective-permute-start | bytes 786440 | tf_op jit(solution)/shard_map/ppermute | solution.py:52
  88.2 7.7 %collective-permute-start.23 = (bf16[256,128]{1,0:T(8,128)(2,1)S(1)}, bf16[256,128]{1,0:T(8,128)(2,1)S(1)}, u32[]{:S(2)}, u32[]{:S(2)}) collective-permute-start(bf16[256,128]{1,0:T(8,128)(2,1)S(1)} %fusion.2), channel_id=1, source_target_pairs={{0,4},{1,5},{2,6},{3,7},{4,8},{5,9},{6,10},{7,11},{8,12},{9,13},{1... | collective-permute-start | bytes 196616 | tf_op jit(solution)/shard_map/ppermute | solution.py:52
  93.0 6.8 %collective-permute-start.24 = (bf16[256,128]{1,0:T(8,128)(2,1)S(1)}, bf16[256,128]{1,0:T(8,128)(2,1)S(1)}, u32[]{:S(2)}, u32[]{:S(2)}) collective-permute-start(bf16[256,128]{1,0:T(8,128)(2,1)S(1)} %fusion.2), channel_id=1, source_target_pairs={{0,8},{1,9},{2,10},{3,11},{4,12},{5,13},{6,14},{7,15},{8,0},{9,1},... | collective-permute-start | bytes 196616 | tf_op jit(solution)/shard_map/ppermute | solution.py:52
  100.6 7.8 %collective-permute-start.31 = (bf16[4,256,128]{2,1,0:T(8,128)(2,1)S(1)}, bf16[4,256,128]{2,1,0:T(8,128)(2,1)S(1)}, u32[]{:S(2)}, u32[]{:S(2)}) collective-permute-start(bf16[4,256,128]{2,1,0:T(8,128)(2,1)S(1)} %pad_maximum_fusion.1.rest_3_), channel_id=1, source_target_pairs={{0,2},{1,3},{2,0},{3,1},{4,6},{5,7},{6,4},{7,5},{8,10},{9,11},{10,... | collective-permute-start | bytes 786440 | tf_op jit(solution)/shard_map/ppermute | solution.py:52
  101.3 12.9 %collective-permute-start.32 = (bf16[4,256,128]{2,1,0:T(8,128)(2,1)S(1)}, bf16[4,256,128]{2,1,0:T(8,128)(2,1)S(1)}, u32[]{:S(2)}, u32[]{:S(2)}) collective-permute-start(bf16[4,256,128]{2,1,0:T(8,128)(2,1)S(1)} %pad_maximum_fusion.1.rest_3_), channel_id=1, source_target_pairs={{0,1},{1,0},{2,3},{3,2},{4,5},{5,4},{6,7},{7,6},{8,9},{9,8},{10,11... | collective-permute-start | bytes 786440 | tf_op jit(solution)/shard_map/ppermute | solution.py:52
  101.4 12.8 %collective-permute-start.30 = (bf16[2,128,512]{2,1,0:T(8,128)(2,1)S(1)}, bf16[2,128,512]{2,1,0:T(8,128)(2,1)S(1)}, u32[]{:S(2)}, u32[]{:S(2)}) collective-permute-start(bf16[2,128,512]{2,1,0:T(8,128)(2,1)S(1)} %add_convert_fusion), channel_id=1, source_target_pairs={{4,0},{5,1},{6,2},{7,3},{8,4},{9,5},{10,6},{11,7},{12,8},{13,9},{1... | collective-permute-start | bytes 786440 | tf_op jit(solution)/shard_map/ppermute | solution.py:52
  (33 other events, 222.7 us)

commit v12 on v11

--- a/solution.py
+++ b/solution.py
@@ -10,7 +10,7 @@
 
 BLOCK = 64
 WDEV = 5
-VMEM_LIMIT = 60 * 1024 * 1024
+VMEM_LIMIT = 24 * 1024 * 1024
 PACK_VMEM = 60 * 1024 * 1024
 JOIN = 4
 BF16 = jnp.bfloat16
@@ -256,10 +256,9 @@
 
 def attend_kernel(
     base, slab_index, verts, offs, qs, gs, qt, gt, delta, own, *rest,
-    lines, nv, ns, per_device, continued,
+    lines, nv, ns, per_device,
 ):
     gathered, recv, rest = rest[:2], rest[2 : 2 + WDEV], rest[2 + WDEV :]
-    rest = rest[3:] if continued else rest
     (share, give, low_w, low_ds, cand_keys), scratch = rest[:5], rest[5:]
     win, vkv, vc, s_ref, vert_w, hold, sems = scratch
     i = pl.program_id(0)
@@ -383,7 +382,7 @@
         give[...] = hold[1].astype(give.dtype)
 
 
-def attend(base, slab_index, verticals, offsets, prepared, own, gathered, recv, lines, lows):
+def attend(base, slab_index, verticals, offsets, prepared, own, gathered, recv, lines, kept_as):
     heads, per_device, deep, head_dim = prepared[0].shape
     _, rows, features = own.shape
     nv, ns = verticals.shape[1], offsets.shape[1]
@@ -396,24 +395,26 @@
             (1,) + shape[1:], lambda i, base, *_: (base[0] + i,) + (0,) * (len(shape) - 1)
         )
 
+    def by_turn(shape):
+        return pl.BlockSpec((1,) + shape[1:], lambda i, *_: (i,) + (0,) * (len(shape) - 1))
+
     share = (lines.far, half * nv * BLOCK // lines.far, head_dim)
     shares = pl.BlockSpec(share, lambda i, *_: (0, 0, 0))
     low_shapes = [
-        (heads, per_device, (1 + ns) * BLOCK, deep),
-        (heads, per_device, cand * BLOCK, deep),
-        (heads, per_device, cand * BLOCK, head_dim),
+        (half, per_device, (1 + ns) * BLOCK, deep),
+        (half, per_device, cand * BLOCK, deep),
+        (half, per_device, cand * BLOCK, head_dim),
     ]
-    before = 4 + len(prepared) + 1 + 2 + WDEV
     return pl.pallas_call(
         functools.partial(
-            attend_kernel, lines=lines, nv=nv, ns=ns, per_device=per_device, continued=bool(lows)
+            attend_kernel, lines=lines, nv=nv, ns=ns, per_device=per_device
         ),
         grid_spec=pltpu.PrefetchScalarGridSpec(
             num_scalar_prefetch=4,
             grid=(half,),
             in_specs=[by_head(array.shape) for array in prepared]
-            + [anywhere] * (3 + WDEV + len(lows)),
-            out_specs=[shares] * 2 + [by_head(shape) for shape in low_shapes],
+            + [anywhere] * (3 + WDEV),
+            out_specs=[shares] * 2 + [by_turn(shape) for shape in low_shapes],
             scratch_shapes=[
                 pltpu.VMEM((2, (WDEV + 1) * rows, features // 2), BF16),
                 pltpu.VMEM((2, half * nv * BLOCK, head_dim), BF16),
@@ -425,39 +426,55 @@
             ],
         ),
         out_shape=[
-            jax.ShapeDtypeStruct(share, F32 if lows else BF16),
+            jax.ShapeDtypeStruct(share, kept_as),
             jax.ShapeDtypeStruct(share, BF16),
         ]
         + [jax.ShapeDtypeStruct(shape, BF16) for shape in low_shapes],
-        input_output_aliases={before + n: 2 + n for n in range(len(lows))},
         compiler_params=pltpu.CompilerParams(vmem_limit_bytes=VMEM_LIMIT),
         cost_estimate=pl.CostEstimate(
             flops=2 * 5 * half * per_device * cand * BLOCK * deep * head_dim,
             bytes_accessed=12 << 20,
             transcendentals=half * per_device * cand * BLOCK * deep,
         ),
-    )(base, slab_index, verticals, offsets, *prepared, own, *gathered, *recv, *lows)
-
-
-def window_kernel(offs, qs, gs, low_w, low_ds, home, *rest, lines, ns, per_device):
-    parts, total = rest[:WDEV], rest[WDEV]
-    h = pl.program_id(0)
+    )(base, slab_index, verticals, offsets, *prepared, own, *gathered, *recv)
+
+
+def turn_to_head(t, bases, half):
+    return bases[lax.div(t, half)] + lax.rem(t, half)
+
+
+def of_call(call, half, shape, block=0):
+    def index(t, *_):
+        turn = jnp.minimum(t, half - 1) if call == 0 else jnp.maximum(t - half, 0)
+        return (turn, 0, block, 0)
+
+    return pl.BlockSpec((1,) + tuple(shape), index)
+
+
+def window_kernel(bases, offs, qs, gs, *rest, lines, half, ns, per_device):
+    lows, home, parts, total = (rest[0:2], rest[2:4]), rest[4], rest[5 : 5 + WDEV], rest[5 + WDEV]
+    t = pl.program_id(0)
+    h = turn_to_head(t, bases, half)
     _, _, core = lines.place(lax.axis_index("ctx"))
     head_dim = qs.shape[3]
     rows = per_device * BLOCK
     scaling = 1.0 / math.sqrt(head_dim)
     lanes = pl.ds(pl.multiple_of(h * head_dim, head_dim), head_dim)
     total[...] = jnp.zeros_like(total)
-    for j in range(per_device):
-        dv = jnp.dot(low_w[0, j], gs[0, j], preferred_element_type=F32)
-        dk = jnp.dot(low_ds[0, j], qs[0, j], preferred_element_type=F32) * scaling
-        own_at = (WDEV * per_device + j) * BLOCK
-        for kv, part in enumerate((dk, dv)):
-            total[kv, own_at : own_at + BLOCK, :] += part[0:BLOCK]
-            for s in range(ns):
-                total[kv, pl.ds(slash_rows(offs, h, j, s, per_device), BLOCK), :] += part[
-                    (1 + s) * BLOCK : (2 + s) * BLOCK
-                ]
+    for call, (low_w, low_ds) in enumerate(lows):
+
+        @pl.when(lax.div(t, half) == call)
+        def _():
+            for j in range(per_device):
+                dv = jnp.dot(low_w[0, j], gs[0, j], preferred_element_type=F32)
+                dk = jnp.dot(low_ds[0, j], qs[0, j], preferred_element_type=F32) * scaling
+                own_at = (WDEV * per_device + j) * BLOCK
+                for kv, part in enumerate((dk, dv)):
+                    total[kv, own_at : own_at + BLOCK, :] += part[0:BLOCK]
+                    for s in range(ns):
+                        at = slash_rows(offs, h, j, s, per_device)
+                        total[kv, pl.ds(at, BLOCK), :] += part[(1 + s) * BLOCK : (2 + s) * BLOCK]
+
     for kv in range(2):
         home[kv, :, lanes] = total[kv, WDEV * rows :, :]
         for part, d in zip(parts, distances(core)):
@@ -465,61 +482,81 @@
             part[kv, :, lanes] = total[kv, pl.ds(at, rows), :].astype(part.dtype)
 
 
-def window_gradients(offsets, qs, gs, low_w, low_ds, lines, nv):
+def window_gradients(bases, offsets, qs, gs, lows, lines, nv):
     heads, per_device, deep, head_dim = qs.shape
     ns = offsets.shape[1]
+    half = heads // 2
     rows, features = per_device * BLOCK, heads * head_dim
     shard = (2, rows, features)
-    whole = pl.BlockSpec(shard, lambda h: (0, 0, 0))
-    stacked = pl.BlockSpec((1,) + qs.shape[1:], lambda h: (h, 0, 0, 0))
+    whole = pl.BlockSpec(shard, lambda t, *_: (0, 0, 0))
+    stacked = pl.BlockSpec(
+        (1,) + qs.shape[1:], lambda t, bases, _: (turn_to_head(t, bases, half), 0, 0, 0)
+    )
     tail = (1 + ns) * BLOCK
-    low_tail = pl.BlockSpec((1, per_device, tail, deep), lambda h: (h, 0, 0, 0))
-    low = pl.BlockSpec(
-        (1, per_device, tail, deep), lambda h: (h, 0, nv * BLOCK // tail, 0)
-    )
+    block = (per_device, tail, deep)
+    specs = []
+    for call in range(2):
+        specs += [of_call(call, half, block), of_call(call, half, block, nv * BLOCK // tail)]
     return pl.pallas_call(
-        functools.partial(window_kernel, lines=lines, ns=ns, per_device=per_device),
-        grid=(heads,),
-        in_specs=[pl.BlockSpec(memory_space=pltpu.SMEM), stacked, stacked, low_tail, low],
-        out_specs=[whole] * (1 + WDEV),
+        functools.partial(window_kernel, lines=lines, half=half, ns=ns, per_device=per_device),
+        grid_spec=pltpu.PrefetchScalarGridSpec(
+            num_scalar_prefetch=2,
+            grid=(heads,),
+            in_specs=[stacked] * 2 + specs,
+            out_specs=[whole] * (1 + WDEV),
+            scratch_shapes=[pltpu.VMEM((2, (WDEV + 1) * rows, head_dim), F32)],
+        ),
         out_shape=[jax.ShapeDtypeStruct(shard, F32)] * 3 + [jax.ShapeDtypeStruct(shard, BF16)] * 3,
-        scratch_shapes=[pltpu.VMEM((2, (WDEV + 1) * rows, head_dim), F32)],
         compiler_params=pltpu.CompilerParams(vmem_limit_bytes=VMEM_LIMIT),
         cost_estimate=pl.CostEstimate(flops=0, bytes_accessed=9 << 20, transcendentals=0),
-    )(offsets, qs, gs, low_w, low_ds)
-
-
-def query_kernel(cand_keys, low_ds, dq):
-    per_device, _, head_dim = cand_keys.shape[1:]
+    )(bases, offsets, qs, gs, *lows[0][:2], *lows[1][:2])
+
+
+def query_kernel(bases, *rest):
+    calls, dq = (rest[0:2], rest[2:4]), rest[4]
+    t = pl.program_id(0)
+    per_device, _, head_dim = rest[0].shape[1:]
     scaling = 1.0 / math.sqrt(head_dim)
-    for j in range(per_device):
-        turned = lax.dot_general(
-            cand_keys[0, j], low_ds[0, j], (((0,), (0,)), ((), ())), preferred_element_type=F32
-        )
-        stacked = (jnp.transpose(turned) * scaling).astype(BF16)
-        for g in range(dq.shape[1] // head_dim):
-            dq[j * BLOCK : (j + 1) * BLOCK, g * head_dim : (g + 1) * head_dim] = stacked[
-                g * BLOCK : (g + 1) * BLOCK, :
-            ]
-
-
-def query_gradients(cand_keys, low_ds):
-    heads, per_device, keys, head_dim = cand_keys.shape
-    deep = low_ds.shape[3]
+    half = pl.num_programs(0) // 2
+    for call, (cand_keys, low_ds) in enumerate(calls):
+
+        @pl.when(lax.div(t, half) == call)
+        def _():
+            for j in range(per_device):
+                turned = lax.dot_general(
+                    cand_keys[0, j],
+                    low_ds[0, j],
+                    (((0,), (0,)), ((), ())),
+                    preferred_element_type=F32,
+                )
+                stacked = (jnp.transpose(turned) * scaling).astype(BF16)
+                for g in range(dq.shape[1] // head_dim):
+                    dq[j * BLOCK : (j + 1) * BLOCK, g * head_dim : (g + 1) * head_dim] = stacked[
+                        g * BLOCK : (g + 1) * BLOCK, :
+                    ]
+
+
+def query_gradients(bases, lows):
+    half, per_device, _, head_dim = lows[0][2].shape
+    deep = lows[0][1].shape[3]
     rows, width = per_device * BLOCK, deep // BLOCK * head_dim
-
-    def by_head(shape):
-        return pl.BlockSpec((1,) + shape[1:], lambda h: (h, 0, 0, 0))
-
+    specs = []
+    for call in range(2):
+        specs += [of_call(call, half, lows[0][n].shape[1:]) for n in (2, 1)]
     return pl.pallas_call(
         query_kernel,
-        grid=(heads,),
-        in_specs=[by_head(cand_keys.shape), by_head(low_ds.shape)],
-        out_specs=pl.BlockSpec((rows, width), lambda h: (0, h)),
-        out_shape=jax.ShapeDtypeStruct((rows, heads * width), BF16),
+        grid_spec=pltpu.PrefetchScalarGridSpec(
+            num_scalar_prefetch=1,
+            grid=(2 * half,),
+            in_specs=specs,
+            out_specs=pl.BlockSpec(
+                (rows, width), lambda t, bases: (0, turn_to_head(t, bases, half))
+            ),
+        ),
+        out_shape=jax.ShapeDtypeStruct((rows, 2 * half * width), BF16),
         compiler_params=pltpu.CompilerParams(vmem_limit_bytes=VMEM_LIMIT),
         cost_estimate=pl.CostEstimate(flops=0, bytes_accessed=10 << 20, transcendentals=0),
-    )(cand_keys, low_ds)
+    )(bases, lows[0][2], lows[0][1], lows[1][2], lows[1][1])
 
 
 def zeros_kernel(_, key_out, value_out, blank, sems):
@@ -688,19 +725,22 @@
     gathered = plane_gather(lines, gathered)
     recv = [recv2, recv4, recv_mixed, other2, other4]
 
-    def attend_line(line, gathered, lows):
-        base = (line * (heads // 2)).astype(jnp.int32).reshape(1)
+    bases = (jnp.stack([near, 1 - near]) * (heads // 2)).astype(jnp.int32)
+
+    def attend_line(call, gathered, kept_as):
         return attend(
-            base, slab_index, verticals, offsets, prepared, own, gathered, recv, lines, lows
+            bases[call : call + 1], slab_index, verticals, offsets, prepared, own, gathered, recv,
+            lines, kept_as,
         )
 
-    to_near, to_both, *lows = attend_line(near, gathered[0::2], ())
+    to_near, to_both, *first_lows = attend_line(0, gathered[0::2], BF16)
     to_near = core_sum(lines, to_near, to_both)
     from_near = move(to_near, lines.near_pairs())
-    mine, to_core, low_w, low_ds, cand_keys = attend_line(1 - near, gathered[1::2], lows)
+    mine, to_core, *second_lows = attend_line(1, gathered[1::2], F32)
+    lows = (first_lows, second_lows)
 
     home, part2, part4, mixed, give2, give4 = window_gradients(
-        after(offsets, from_near), prepared[0], prepared[1], low_w, low_ds, lines, nv
+        bases, after(offsets, from_near), prepared[0], prepared[1], lows, lines, nv
     )
     quarter = after(near_sum(lines, mine, from_near, to_core), home)
     share = far_sum(lines, quarter)
@@ -711,7 +751,7 @@
     totals = after(far_gather(lines, share), from_near, arrived_mixed)
     sum4 = (sum4 + jnp.where(near == 1, from_near.astype(F32), 0.0)).astype(BF16)
     arrived4 = move(after(sum4, totals), back(lines.shift_pairs(4)))
-    query_grad = query_gradients(after(cand_keys, totals), low_ds)
+    query_grad = query_gradients(after(bases, totals), lows)
     totals = plane_gather(lines, totals)
     key_gradient, value_gradient = assemble(
         slab_index, verticals, after(home, query_grad), from_near, (arrived4, arrived_mixed),

time: 121 us -> 114 us (0.942)
  Pallas kernels: 47.2 us -> 33.9 us
  starting transfers between devices: 38.9 us -> 30.7 us
  waiting for transfers between devices: 24.9 us -> 31.9 us
  local copies, waits for them, and re-layouts: 2.93 us -> 9.43 us
    ppermute x34, starting transfers between devices: 38.9 us -> 30.7 us  [move(): return lax.ppermute(array, 'ctx', pairs)]
    ppermute x34, waiting for transfers between devices: 24.9 us -> 31.9 us  [move(): return lax.ppermute(array, 'ctx', pairs)]
    unnamed x46 -> x48, local copies, waits for them, and re-layouts: 2.9 us -> 8.74 us
    pallas_call x2, Pallas kernels: 11.7 us -> 6.65 us  [the longest x1 3.57 us: query_gradients(): pl.pallas_call(query_kernel, grid_spec=pltpu.PrefetchScalarGridSpec(num_s...]
    pallas_call x2, Pallas kernels: 19.8 us -> 14.8 us  [attend(): pl.pallas_call(functools.partial(attend_kernel, lines=lines, nv=nv, ns=ns...]
    pallas_call x1, Pallas kernels: 4.58 us -> 1.38 us  [prepare(): pl.pallas_call(functools.partial(prepare_kernel, head_dim=head_dim), grid...]
    add x2, other arithmetic: 0.16 us -> 1.98 us  [near_sum(): return mine.astype(F32) + from_core.astype(F32) + from_near.astype(F32)]
  transfers between devices with their start and end apart: 34 -> 34, of which waited for: 12 -> 12; matrix products, arithmetic and copies ran while one was open for 4% -> 5% of each run, Pallas kernels for 32% -> 22%
where the time goes in v12:
time: 114 us; the launch traced here: 113 us
  Pallas kernels  33.9 us (30%)
  waiting for transfers between devices  31.9 us (28%)
  starting transfers between devices  30.7 us (27%)
  local copies, waits for them, and re-layouts  9.43 us (8%)
  other arithmetic  5.28 us (5%)
  between operations  1.83 us (2%)
    ppermute x34, waiting for transfers between devices, move(): return lax.ppermute(array, 'ctx', pairs)  31.9 us
    ppermute x34, starting transfers between devices, move(): return lax.ppermute(array, 'ctx', pairs)  30.7 us
    pallas_call x2, Pallas kernels, attend(): pl.pallas_call(functools.partial(attend_kernel, lines=lines, nv=nv, ns=ns...  14.8 us
    unnamed x48, local copies, waits for them, and re-layouts  8.74 us
    pallas_call x1, Pallas kernels, assemble(): pl.pallas_call(functools.partial(assemble_kernel, lines=lines, heads=head...  4.41 us
    pallas_call x1, Pallas kernels, pack(): pl.pallas_call(functools.partial(pack_kernel, lines=lines, heads=heads, n...  4.34 us
    pallas_call x1, Pallas kernels, query_gradients(): pl.pallas_call(query_kernel, grid_spec=pltpu.PrefetchScalarGridSpec(num_s...  3.57 us
    pallas_call x1, Pallas kernels, window_gradients(): pl.pallas_call(functools.partial(window_kernel, lines=lines, half=half, n...  3.08 us
  transfers between devices with their start and end apart: 34, of which 12 were waited for; matrix products, arithmetic and copies ran while one was open for 5% of the time, Pallas kernels for 22%

profile of v12, /device:TPU:0, one launch (start us, length us, event | category | flops | bytes accessed | tf_op | source)
XLA Modules:
  0.0 113.0 jit_solution(5933015867815616439)
XLA Ops:
  1.3 4.3 %shard_map.103 = (bf16[2,128,512]{2,1,0:T(8,128)(2,1)}, bf16[2,128,512]{2,1,0:T(8,128)(2,1)}, bf16[2,128,512]{2,1,0:T(8,128)(2,1)}, bf16[4,256,128]{2,1,0:T(8,12...) custom-call(s32[1]{0:T(128)S(6)} %copy.15.slab_index, ...), custom_call_target="tpu_custom_call" | custom-call | tf_op jit(solution)/shard_map/pallas_call | solution.py:168
  6.2 2.6 %collective-permute-start.3 = (bf16[2,128,512]{2,1,0:T(8,128)(2,1)}, bf16[2,128,512]{2,1,0:T(8,128)(2,1)S(1)}, u32[]{:S(2)}, u32[]{:S(2)}) collective-permute-start(bf16[2,128,512]{2,1,0:T(8,128)(2,1)} %get-tuple-element.57), channel_id=1, source_target_pairs={{0,4},{1,5},{2,6},{3,7},{4,8},{5,9},{6,10},{7,11},{8,12},{9,13},{1... | collective-permute-start | bytes 786440 | tf_op jit(solution)/shard_map/ppermute | solution.py:52
  9.0 1.7 %add_convert_fusion.3 = bf16[4,256,128]{2,1,0:T(8,128)(2,1)} fusion(bf16[4,256,128]{2,1,0:T(8,128)(2,1)S(1)} %collective-permute-done, bf16[4,256,128]{2,1,0:T(8,128)(2,1)} %get-tuple-element.46), kind=kLoop, calls=%fused_computation.5 | loop fusion | flops 524288 | bytes 786432 | tf_op jit(solution)/shard_map/convert_element_type | solution.py:60
  12.2 5.8 %collective-permute-done.3.rest_3_ = bf16[2,128,512]{2,1,0:T(8,128)(2,1)S(1)} collective-permute-done((bf16[2,128,512]{2,1,0:T(8,128)(2,1)}, bf16[2,128,512]{2,1,0:T(8,128)(2,1)S(1)}, u32[]{:S(2)}, u32[]{:S(2)}) %collective-permute-start.3) | collective-permute-done | bytes 262176 | tf_op jit(solution)/shard_map/ppermute | solution.py:52
  23.0 1.9 %convert_add_fusion.1 = f32[4,256,128]{2,1,0:T(8,128)S(1)} fusion(bf16[4,256,128]{2,1,0:T(8,128)(2,1)} %collective-permute-done.2, bf16[4,256,128]{2,1,0:T(8,128)(2,1)} %collective-permute-done.1, bf16[4,256,128]{2,1,0:T(8,128)(2,1)S(1)} %copy-done.22), kind=kLoop, calls=%fused_computation.4 | loop fusion | flops 655360 | bytes 1310720 | tf_op jit(solution)/shard_map/add | solution.py:65
  25.0 1.8 %collective-permute-start.6 = (bf16[256,128]{1,0:T(8,128)(2,1)S(1)}, bf16[256,128]{1,0:T(8,128)(2,1)S(1)}, u32[]{:S(2)}, u32[]{:S(2)}) collective-permute-start(bf16[256,128]{1,0:T(8,128)(2,1)S(1)} %get-tuple-element.93), channel_id=1, source_target_pairs={{0,12},{1,13},{2,14},{3,15},{4,0},{5,1},{6,2},{7,3},{8,4},{9,5},{1... | collective-permute-start | bytes 196616 | tf_op jit(solution)/shard_map/ppermute | solution.py:52
  29.3 2.1 %collective-permute-start.12 = (bf16[2,128,512]{2,1,0:T(8,128)(2,1)S(1)}, bf16[2,128,512]{2,1,0:T(8,128)(2,1)S(1)}, u32[]{:S(2)}, u32[]{:S(2)}) collective-permute-start(bf16[2,128,512]{2,1,0:T(8,128)(2,1)S(1)} %collective-permute-done.11.rest_2_), channel_id=1, source_target_pairs={{0,1},{1,0},{2,3},{3,2},{4,5},{5,4},{6,7},{7,6},{8,9},{9,8},{10,11... | collective-permute-start | bytes 786440 | tf_op jit(solution)/shard_map/ppermute | solution.py:52
  31.4 2.1 %collective-permute-done.5 = bf16[256,128]{1,0:T(8,128)(2,1)S(1)} collective-permute-done((bf16[256,128]{1,0:T(8,128)(2,1)S(1)}, bf16[256,128]{1,0:T(8,128)(2,1)S(1)}, u32[]{:S(2)}, u32[]{:S(2)}) %collective-permute-start.5) | collective-permute-done | bytes 65568 | tf_op jit(solution)/shard_map/ppermute | solution.py:52
  35.5 1.9 %collective-permute-start.8 = (bf16[256,128]{1,0:T(8,128)(2,1)S(1)}, bf16[256,128]{1,0:T(8,128)(2,1)S(1)}, u32[]{:S(2)}, u32[]{:S(2)}) collective-permute-start(bf16[256,128]{1,0:T(8,128)(2,1)S(1)} %fusion.5._), channel_id=1, source_target_pairs={{0,4},{1,5},{2,6},{3,7},{4,8},{5,9},{6,10},{7,11},{8,12},{9,13},{1... | collective-permute-start | bytes 196616 | tf_op jit(solution)/shard_map/ppermute | solution.py:52
  37.4 2.3 %shard_map.105 = (bf16[16,128,512]{2,1,0:T(8,128)(2,1)}, bf16[16,128,512]{2,1,0:T(8,128)(2,1)}) custom-call(bf16[256,128]{1,0:T(8,128)(2,1)S(1)} %fusion.5._), custom_call_target="tpu_custom_call" | custom-call | bytes 5242880 | tf_op jit(solution)/shard_map/pallas_call | solution.py:577
  39.7 2.3 %collective-permute-done.9 = bf16[256,128]{1,0:T(8,128)(2,1)S(1)} collective-permute-done((bf16[256,128]{1,0:T(8,128)(2,1)S(1)}, bf16[256,128]{1,0:T(8,128)(2,1)S(1)}, u32[]{:S(2)}, u32[]{:S(2)}) %collective-permute-start.9) | collective-permute-done | bytes 65568 | tf_op jit(solution)/shard_map/ppermute | solution.py:52
  44.3 5.3 %collective-permute-start.14 = (bf16[4,256,128]{2,1,0:T(8,128)(2,1)S(1)}, bf16[4,256,128]{2,1,0:T(8,128)(2,1)S(1)}, u32[]{:S(2)}, u32[]{:S(2)}) collective-permute-start(bf16[4,256,128]{2,1,0:T(8,128)(2,1)S(1)} %pad_maximum_fusion.rest_0_), channel_id=1, source_target_pairs={{0,2},{1,3},{2,0},{3,1},{4,6},{5,7},{6,4},{7,5},{8,10},{9,11},{10,... | collective-permute-start | bytes 786440 | tf_op jit(solution)/shard_map/ppermute | solution.py:52
  54.9 7.7 %shard_map.107 = (bf16[4,256,128]{2,1,0:T(8,128)(2,1)S(1)}, bf16[4,256,128]{2,1,0:T(8,128)(2,1)S(1)}, bf16[2,2,256,512]{3,2,1,0:T(8,128)(2,1)S(1)}, bf16[2,2,768...) custom-call(s32[1]{0:T(128)} %get-tuple-element.96.base, s32[1]{0:T(128)S(6)} %copy.15.slab_index, ...), custom_call_target="tpu_custom_call" | custom-call | flops 2013265920 | bytes 12582912 | tf_op jit(solution)/shard_map/pallas_call | solution.py:408
  65.2 7.2 %shard_map.106 = (f32[4,256,128]{2,1,0:T(8,128)S(1)}, bf16[4,256,128]{2,1,0:T(8,128)(2,1)S(1)}, bf16[2,2,256,512]{3,2,1,0:T(8,128)(2,1)S(1)}, bf16[2,2,768,512]{...) custom-call(s32[1]{0:T(128)} %get-tuple-element.95.base, s32[1]{0:T(128)S(6)} %copy.15.slab_index, s32[4,8]{1,0:T(4,128)S(1)} %copy-done.8, ...), custom_call_target="tpu_custom_call" | custom-call | flops 2013265920 | bytes 12582912 | tf_op jit(solution)/shard_map/pallas_call | solution.py:408
  72.8 3.1 %shard_map.108 = (f32[2,128,512]{2,1,0:T(8,128)S(1)}, f32[2,128,512]{2,1,0:T(8,128)S(1)}, f32[2,128,512]{2,1,0:T(8,128)S(1)}, bf16[2,128,512]{2,1,0:T(8,128)(2,1...) custom-call(s32[2]{0:T(128)S(1)} %add_multiply_fusion.bases, s32[4,3]{1,0:T(4,128)S(1)} %copy-done.9, ...), custom_call_target="tpu_custom_call" | custom-call | bytes 9437184 | tf_op jit(solution)/shard_map/pallas_call | solution.py:500
  78.9 1.8 %collective-permute-start.28 = (bf16[2,128,512]{2,1,0:T(8,128)(2,1)S(1)}, bf16[2,128,512]{2,1,0:T(8,128)(2,1)S(1)}, u32[]{:S(2)}, u32[]{:S(2)}) collective-permute-start(bf16[2,128,512]{2,1,0:T(8,128)(2,1)S(1)} %get-tuple-element.78), channel_id=1, source_target_pairs={{1,0},{6,1},{3,2},{8,3},{5,4},{10,5},{7,6},{12,7},{9,8},{14,9},{11... | collective-permute-start | bytes 786440 | tf_op jit(solution)/shard_map/ppermute | solution.py:52
  82.5 5.1 %collective-permute-done.21 = bf16[256,128]{1,0:T(8,128)(2,1)S(1)} collective-permute-done((bf16[256,128]{1,0:T(8,128)(2,1)S(1)}, bf16[256,128]{1,0:T(8,128)(2,1)S(1)}, u32[]{:S(2)}, u32[]{:S(2)}) %collective-permute-start.21) | collective-permute-done | bytes 65568 | tf_op jit(solution)/shard_map/ppermute | solution.py:52
  87.7 1.7 %collective-permute-start.24 = (bf16[256,128]{1,0:T(8,128)(2,1)S(1)}, bf16[256,128]{1,0:T(8,128)(2,1)S(1)}, u32[]{:S(2)}, u32[]{:S(2)}) collective-permute-start(bf16[256,128]{1,0:T(8,128)(2,1)S(1)} %fusion.2), channel_id=1, source_target_pairs={{0,8},{1,9},{2,10},{3,11},{4,12},{5,13},{6,14},{7,15},{8,0},{9,1},... | collective-permute-start | bytes 196616 | tf_op jit(solution)/shard_map/ppermute | solution.py:52
  89.4 2.9 %collective-permute-done.25 = bf16[256,128]{1,0:T(8,128)(2,1)S(1)} collective-permute-done((bf16[256,128]{1,0:T(8,128)(2,1)S(1)}, bf16[256,128]{1,0:T(8,128)(2,1)S(1)}, u32[]{:S(2)}, u32[]{:S(2)}) %collective-permute-start.25) | collective-permute-done | bytes 65568 | tf_op jit(solution)/shard_map/ppermute | solution.py:52
  93.2 1.5 %collective-permute-done.24 = bf16[256,128]{1,0:T(8,128)(2,1)S(1)} collective-permute-done((bf16[256,128]{1,0:T(8,128)(2,1)S(1)}, bf16[256,128]{1,0:T(8,128)(2,1)S(1)}, u32[]{:S(2)}, u32[]{:S(2)}) %collective-permute-start.24) | collective-permute-done | bytes 65568 | tf_op jit(solution)/shard_map/ppermute | solution.py:52
  94.7 3.7 %collective-permute-done.23 = bf16[256,128]{1,0:T(8,128)(2,1)S(1)} collective-permute-done((bf16[256,128]{1,0:T(8,128)(2,1)S(1)}, bf16[256,128]{1,0:T(8,128)(2,1)S(1)}, u32[]{:S(2)}, u32[]{:S(2)}) %collective-permute-start.23) | collective-permute-done | bytes 65568 | tf_op jit(solution)/shard_map/ppermute | solution.py:52
  99.2 5.7 %collective-permute-done.31.rest_4_ = bf16[4,256,128]{2,1,0:T(8,128)(2,1)S(1)} collective-permute-done((bf16[4,256,128]{2,1,0:T(8,128)(2,1)S(1)}, bf16[4,256,128]{2,1,0:T(8,128)(2,1)S(1)}, u32[]{:S(2)}, u32[]{:S(2)}) %collective-permute-start.31) | collective-permute-done | bytes 262176 | tf_op jit(solution)/shard_map/ppermute | solution.py:52
  104.9 3.6 %shard_map.109 = bf16[128,4096]{1,0:T(8,128)(2,1)} custom-call(s32[2]{0:T(128)S(1)} %add_multiply_fusion.bases, bf16[2,2,768,128]{3,2,1,0:T(8,128)(2,1)S(1)} %get-tuple-element.81.rest_0_, bf16[2,2,768,512]{3,2,1,0:T(8,128)(2,1)S(1)} %get-tuple-element.71.rest_1_, bf16[2,2,768,128]{3,2,1,0:T(8,128)(2,1)S(1)} %get-tuple-element.82.rest_2_, ...), custom_call_target="tpu_custom_call" | custom-call | bytes 10485760 | tf_op jit(solution)/shard_map/pallas_call | solution.py:546
  108.5 4.4 %shard_map.110 = (bf16[16,128,512]{2,1,0:T(8,128)(2,1)}, bf16[16,128,512]{2,1,0:T(8,128)(2,1)}) custom-call(s32[1]{0:T(128)S(6)} %copy.15.slab_index, s32[4,8]{1,0:T(4,128)S(1)} %copy-done.8, f32[2,128,512]{2,1,0:T(8,128)S(1)} %get-tuple-element.83.home, ...), custom_call_target="tpu_custom_call", output_to_operand_aliasing={{0}: (10, {}), {1}: (11, {})} | custom-call | tf_op jit(solution)/shard_map/pallas_call | solution.py:674
  (117 shorter events, 28.8 us)
Async XLA Ops:
  6.2 11.8 %collective-permute-start.3 = (bf16[2,128,512]{2,1,0:T(8,128)(2,1)}, bf16[2,128,512]{2,1,0:T(8,128)(2,1)S(1)}, u32[]{:S(2)}, u32[]{:S(2)}) collective-permute-start(bf16[2,128,512]{2,1,0:T(8,128)(2,1)} %get-tuple-element.57), channel_id=1, source_target_pairs={{0,4},{1,5},{2,6},{3,7},{4,8},{5,9},{6,10},{7,11},{8,12},{9,13},{1... | collective-permute-start | bytes 786440 | tf_op jit(solution)/shard_map/ppermute | solution.py:52
  8.8 14.1 %collective-permute-start.1 = (bf16[4,256,128]{2,1,0:T(8,128)(2,1)}, bf16[4,256,128]{2,1,0:T(8,128)(2,1)}, u32[]{:S(2)}, u32[]{:S(2)}) collective-permute-start(bf16[4,256,128]{2,1,0:T(8,128)(2,1)} %get-tuple-element.56), channel_id=1, source_target_pairs={{0,1},{1,0},{2,3},{3,2},{4,5},{5,4},{6,7},{7,6},{8,9},{9,8},{10,11... | collective-permute-start | bytes 786440 | tf_op jit(solution)/shard_map/ppermute | solution.py:52
  10.7 12.3 %collective-permute-start.2 = (bf16[4,256,128]{2,1,0:T(8,128)(2,1)}, bf16[4,256,128]{2,1,0:T(8,128)(2,1)}, u32[]{:S(2)}, u32[]{:S(2)}) collective-permute-start(bf16[4,256,128]{2,1,0:T(8,128)(2,1)} %add_convert_fusion.3), channel_id=1, source_target_pairs={{0,2},{1,3},{2,0},{3,1},{4,6},{5,7},{6,4},{7,5},{8,10},{9,11},{10,... | collective-permute-start | bytes 786440 | tf_op jit(solution)/shard_map/ppermute | solution.py:52
  19.0 8.8 %collective-permute-start.11 = (bf16[2,128,512]{2,1,0:T(8,128)(2,1)S(1)}, bf16[2,128,512]{2,1,0:T(8,128)(2,1)S(1)}, u32[]{:S(2)}, u32[]{:S(2)}) collective-permute-start(bf16[2,128,512]{2,1,0:T(8,128)(2,1)S(1)} %broadcast_select_fusion), channel_id=1, source_target_pairs={{0,2},{1,3},{2,0},{3,1},{4,6},{5,7},{6,4},{7,5},{8,10},{9,11},{10,... | collective-permute-start | bytes 786440 | tf_op jit(solution)/shard_map/ppermute | solution.py:52
  26.8 6.7 %collective-permute-start.5 = (bf16[256,128]{1,0:T(8,128)(2,1)S(1)}, bf16[256,128]{1,0:T(8,128)(2,1)S(1)}, u32[]{:S(2)}, u32[]{:S(2)}) collective-permute-start(bf16[256,128]{1,0:T(8,128)(2,1)S(1)} %get-tuple-element.94), channel_id=1, source_target_pairs={{0,8},{1,9},{2,10},{3,11},{4,12},{5,13},{6,14},{7,15},{8,0},{9,1},... | collective-permute-start | bytes 196616 | tf_op jit(solution)/shard_map/ppermute | solution.py:52
  26.8 6.7 %collective-permute-start.4 = (bf16[256,128]{1,0:T(8,128)(2,1)S(1)}, bf16[256,128]{1,0:T(8,128)(2,1)S(1)}, u32[]{:S(2)}, u32[]{:S(2)}) collective-permute-start(bf16[256,128]{1,0:T(8,128)(2,1)S(1)} %get-tuple-element.92), channel_id=1, source_target_pairs={{0,4},{1,5},{2,6},{3,7},{4,8},{5,9},{6,10},{7,11},{8,12},{9,13},{1... | collective-permute-start | bytes 196616 | tf_op jit(solution)/shard_map/ppermute | solution.py:52
  27.8 15.0 %collective-permute-start.13 = (bf16[2,128,512]{2,1,0:T(8,128)(2,1)S(1)}, bf16[2,128,512]{2,1,0:T(8,128)(2,1)S(1)}, u32[]{:S(2)}, u32[]{:S(2)}) collective-permute-start(bf16[2,128,512]{2,1,0:T(8,128)(2,1)S(1)} %copy-done.23), channel_id=1, source_target_pairs={{0,1},{1,6},{2,3},{3,8},{4,5},{5,10},{6,7},{7,12},{8,9},{9,14},{10... | collective-permute-start | bytes 786440 | tf_op jit(solution)/shard_map/ppermute | solution.py:52
  29.3 12.7 %collective-permute-start.12 = (bf16[2,128,512]{2,1,0:T(8,128)(2,1)S(1)}, bf16[2,128,512]{2,1,0:T(8,128)(2,1)S(1)}, u32[]{:S(2)}, u32[]{:S(2)}) collective-permute-start(bf16[2,128,512]{2,1,0:T(8,128)(2,1)S(1)} %collective-permute-done.11.rest_2_), channel_id=1, source_target_pairs={{0,1},{1,0},{2,3},{3,2},{4,5},{5,4},{6,7},{7,6},{8,9},{9,8},{10,11... | collective-permute-start | bytes 786440 | tf_op jit(solution)/shard_map/ppermute | solution.py:52
  33.5 6.2 %collective-permute-start.10 = (bf16[256,128]{1,0:T(8,128)(2,1)S(1)}, bf16[256,128]{1,0:T(8,128)(2,1)S(1)}, u32[]{:S(2)}, u32[]{:S(2)}) collective-permute-start(bf16[256,128]{1,0:T(8,128)(2,1)S(1)} %fusion.5._), channel_id=1, source_target_pairs={{0,12},{1,13},{2,14},{3,15},{4,0},{5,1},{6,2},{7,3},{8,4},{9,5},{1... | collective-permute-start | bytes 196616 | tf_op jit(solution)/shard_map/ppermute | solution.py:52
  34.9 7.1 %collective-permute-start.9 = (bf16[256,128]{1,0:T(8,128)(2,1)S(1)}, bf16[256,128]{1,0:T(8,128)(2,1)S(1)}, u32[]{:S(2)}, u32[]{:S(2)}) collective-permute-start(bf16[256,128]{1,0:T(8,128)(2,1)S(1)} %fusion.5._), channel_id=1, source_target_pairs={{0,8},{1,9},{2,10},{3,11},{4,12},{5,13},{6,14},{7,15},{8,0},{9,1},... | collective-permute-start | bytes 196616 | tf_op jit(solution)/shard_map/ppermute | solution.py:52
  35.5 6.5 %collective-permute-start.8 = (bf16[256,128]{1,0:T(8,128)(2,1)S(1)}, bf16[256,128]{1,0:T(8,128)(2,1)S(1)}, u32[]{:S(2)}, u32[]{:S(2)}) collective-permute-start(bf16[256,128]{1,0:T(8,128)(2,1)S(1)} %fusion.5._), channel_id=1, source_target_pairs={{0,4},{1,5},{2,6},{3,7},{4,8},{5,9},{6,10},{7,11},{8,12},{9,13},{1... | collective-permute-start | bytes 196616 | tf_op jit(solution)/shard_map/ppermute | solution.py:52
  43.5 6.1 %collective-permute-start.17 = (bf16[4,256,128]{2,1,0:T(8,128)(2,1)S(1)}, bf16[4,256,128]{2,1,0:T(8,128)(2,1)}, u32[]{:S(2)}, u32[]{:S(2)}) collective-permute-start(bf16[4,256,128]{2,1,0:T(8,128)(2,1)S(1)} %pad_maximum_fusion.rest_0_), channel_id=1, source_target_pairs={{0,1},{1,0},{2,3},{3,2},{4,5},{5,4},{6,7},{7,6},{8,9},{9,8},{10,11... | collective-permute-start | bytes 786440 | tf_op jit(solution)/shard_map/ppermute | solution.py:52
  44.3 18.6 %collective-permute-start.14 = (bf16[4,256,128]{2,1,0:T(8,128)(2,1)S(1)}, bf16[4,256,128]{2,1,0:T(8,128)(2,1)S(1)}, u32[]{:S(2)}, u32[]{:S(2)}) collective-permute-start(bf16[4,256,128]{2,1,0:T(8,128)(2,1)S(1)} %pad_maximum_fusion.rest_0_), channel_id=1, source_target_pairs={{0,2},{1,3},{2,0},{3,1},{4,6},{5,7},{6,4},{7,5},{8,10},{9,11},{10,... | collective-permute-start | bytes 786440 | tf_op jit(solution)/shard_map/ppermute | solution.py:52
  64.3 8.5 %collective-permute-start.19 = (bf16[4,256,128]{2,1,0:T(8,128)(2,1)S(1)}, bf16[4,256,128]{2,1,0:T(8,128)(2,1)S(1)}, u32[]{:S(2)}, u32[]{:S(2)}) collective-permute-start(bf16[4,256,128]{2,1,0:T(8,128)(2,1)S(1)} %add_convert_fusion.2), channel_id=1, source_target_pairs={{0,2},{1,3},{2,0},{3,1},{4,6},{5,7},{6,4},{7,5},{8,10},{9,11},{10,... | collective-permute-start | bytes 786440 | tf_op jit(solution)/shard_map/ppermute | solution.py:52
  77.1 10.5 %collective-permute-start.21 = (bf16[256,128]{1,0:T(8,128)(2,1)S(1)}, bf16[256,128]{1,0:T(8,128)(2,1)S(1)}, u32[]{:S(2)}, u32[]{:S(2)}) collective-permute-start(bf16[256,128]{1,0:T(8,128)(2,1)S(1)} %get-tuple-element.91), channel_id=1, source_target_pairs={{0,8},{1,9},{2,10},{3,11},{4,12},{5,13},{6,14},{7,15},{8,0},{9,1},... | collective-permute-start | bytes 196616 | tf_op jit(solution)/shard_map/ppermute | solution.py:52
  78.0 9.6 %collective-permute-start.20 = (bf16[256,128]{1,0:T(8,128)(2,1)S(1)}, bf16[256,128]{1,0:T(8,128)(2,1)S(1)}, u32[]{:S(2)}, u32[]{:S(2)}) collective-permute-start(bf16[256,128]{1,0:T(8,128)(2,1)S(1)} %get-tuple-element.89), channel_id=1, source_target_pairs={{0,4},{1,5},{2,6},{3,7},{4,8},{5,9},{6,10},{7,11},{8,12},{9,13},{1... | collective-permute-start | bytes 196616 | tf_op jit(solution)/shard_map/ppermute | solution.py:52
  78.9 19.5 %collective-permute-start.28 = (bf16[2,128,512]{2,1,0:T(8,128)(2,1)S(1)}, bf16[2,128,512]{2,1,0:T(8,128)(2,1)S(1)}, u32[]{:S(2)}, u32[]{:S(2)}) collective-permute-start(bf16[2,128,512]{2,1,0:T(8,128)(2,1)S(1)} %get-tuple-element.78), channel_id=1, source_target_pairs={{1,0},{6,1},{3,2},{8,3},{5,4},{10,5},{7,6},{12,7},{9,8},{14,9},{11... | collective-permute-start | bytes 786440 | tf_op jit(solution)/shard_map/ppermute | solution.py:52
  80.7 17.9 %collective-permute-start.29 = (bf16[2,128,512]{2,1,0:T(8,128)(2,1)S(1)}, bf16[2,128,512]{2,1,0:T(8,128)(2,1)S(1)}, u32[]{:S(2)}, u32[]{:S(2)}) collective-permute-start(bf16[2,128,512]{2,1,0:T(8,128)(2,1)S(1)} %get-tuple-element.85), channel_id=1, source_target_pairs={{0,1},{1,0},{2,3},{3,2},{4,5},{5,4},{6,7},{7,6},{8,9},{9,8},{10,11... | collective-permute-start | bytes 786440 | tf_op jit(solution)/shard_map/ppermute | solution.py:52
  81.4 17.1 %collective-permute-start.27 = (bf16[2,128,512]{2,1,0:T(8,128)(2,1)S(1)}, bf16[2,128,512]{2,1,0:T(8,128)(2,1)S(1)}, u32[]{:S(2)}, u32[]{:S(2)}) collective-permute-start(bf16[2,128,512]{2,1,0:T(8,128)(2,1)S(1)} %add_convert_fusion.1), channel_id=1, source_target_pairs={{0,2},{1,3},{2,0},{3,1},{4,6},{5,7},{6,4},{7,5},{8,10},{9,11},{10,... | collective-permute-start | bytes 786440 | tf_op jit(solution)/shard_map/ppermute | solution.py:52
  87.7 7.0 %collective-permute-start.24 = (bf16[256,128]{1,0:T(8,128)(2,1)S(1)}, bf16[256,128]{1,0:T(8,128)(2,1)S(1)}, u32[]{:S(2)}, u32[]{:S(2)}) collective-permute-start(bf16[256,128]{1,0:T(8,128)(2,1)S(1)} %fusion.2), channel_id=1, source_target_pairs={{0,8},{1,9},{2,10},{3,11},{4,12},{5,13},{6,14},{7,15},{8,0},{9,1},... | collective-permute-start | bytes 196616 | tf_op jit(solution)/shard_map/ppermute | solution.py:52
  92.3 6.1 %collective-permute-start.23 = (bf16[256,128]{1,0:T(8,128)(2,1)S(1)}, bf16[256,128]{1,0:T(8,128)(2,1)S(1)}, u32[]{:S(2)}, u32[]{:S(2)}) collective-permute-start(bf16[256,128]{1,0:T(8,128)(2,1)S(1)} %fusion.2), channel_id=1, source_target_pairs={{0,4},{1,5},{2,6},{3,7},{4,8},{5,9},{6,10},{7,11},{8,12},{9,13},{1... | collective-permute-start | bytes 196616 | tf_op jit(solution)/shard_map/ppermute | solution.py:52
  98.5 6.4 %collective-permute-start.31 = (bf16[4,256,128]{2,1,0:T(8,128)(2,1)S(1)}, bf16[4,256,128]{2,1,0:T(8,128)(2,1)S(1)}, u32[]{:S(2)}, u32[]{:S(2)}) collective-permute-start(bf16[4,256,128]{2,1,0:T(8,128)(2,1)S(1)} %pad_maximum_fusion.1.rest_3_), channel_id=1, source_target_pairs={{0,2},{1,3},{2,0},{3,1},{4,6},{5,7},{6,4},{7,5},{8,10},{9,11},{10,... | collective-permute-start | bytes 786440 | tf_op jit(solution)/shard_map/ppermute | solution.py:52
  98.5 9.9 %collective-permute-start.32 = (bf16[4,256,128]{2,1,0:T(8,128)(2,1)S(1)}, bf16[4,256,128]{2,1,0:T(8,128)(2,1)S(1)}, u32[]{:S(2)}, u32[]{:S(2)}) collective-permute-start(bf16[4,256,128]{2,1,0:T(8,128)(2,1)S(1)} %pad_maximum_fusion.1.rest_3_), channel_id=1, source_target_pairs={{0,1},{1,0},{2,3},{3,2},{4,5},{5,4},{6,7},{7,6},{8,9},{9,8},{10,11... | collective-permute-start | bytes 786440 | tf_op jit(solution)/shard_map/ppermute | solution.py:52
  98.8 9.7 %collective-permute-start.30 = (bf16[2,128,512]{2,1,0:T(8,128)(2,1)S(1)}, bf16[2,128,512]{2,1,0:T(8,128)(2,1)S(1)}, u32[]{:S(2)}, u32[]{:S(2)}) collective-permute-start(bf16[2,128,512]{2,1,0:T(8,128)(2,1)S(1)} %add_convert_fusion), channel_id=1, source_target_pairs={{4,0},{5,1},{6,2},{7,3},{8,4},{9,5},{10,6},{11,7},{12,8},{13,9},{1... | collective-permute-start | bytes 786440 | tf_op jit(solution)/shard_map/ppermute | solution.py:52
  (34 other events, 333.0 us)

commit v13 on v12

--- a/solution.py
+++ b/solution.py
@@ -10,8 +10,8 @@
 
 BLOCK = 64
 WDEV = 5
-VMEM_LIMIT = 24 * 1024 * 1024
-PACK_VMEM = 60 * 1024 * 1024
+MIB = 1024 * 1024
+PACK_VMEM = 60 * MIB
 JOIN = 4
 BF16 = jnp.bfloat16
 F32 = jnp.float32
@@ -245,7 +245,7 @@
         out_shape=[jax.ShapeDtypeStruct((heads,) + stacked, BF16)] * 2
         + [jax.ShapeDtypeStruct((heads,) + turned, BF16)] * 2
         + [jax.ShapeDtypeStruct((heads,) + sums, F32)],
-        compiler_params=pltpu.CompilerParams(vmem_limit_bytes=VMEM_LIMIT),
+        compiler_params=pltpu.CompilerParams(vmem_limit_bytes=16 * MIB),
         cost_estimate=pl.CostEstimate(flops=0, bytes_accessed=7 << 20, transcendentals=0),
     )(queries, cotangent, output)
 
@@ -255,14 +255,15 @@
 
 
 def attend_kernel(
-    base, slab_index, verts, offs, qs, gs, qt, gt, delta, own, *rest,
-    lines, nv, ns, per_device,
+    bases, slab_index, verts, offs, qs, gs, qt, gt, delta, own, *rest,
+    lines, nv, ns, per_device, call,
 ):
     gathered, recv, rest = rest[:2], rest[2 : 2 + WDEV], rest[2 + WDEV :]
     (share, give, low_w, low_ds, cand_keys), scratch = rest[:5], rest[5:]
     win, vkv, vc, s_ref, vert_w, hold, sems = scratch
     i = pl.program_id(0)
-    h = base[0] + i
+    base = bases[call]
+    h = base + i
     slab, me = slab_index[0], lax.axis_index("ctx")
     far, near, core = lines.place(me)
     _, chunk, head_dim = share.shape
@@ -280,7 +281,7 @@
     def _():
         half = win.shape[2]
         own_rows = pl.ds(WDEV * rows, rows)
-        side = pl.ds(pl.multiple_of(base[0] * head_dim, half), half)
+        side = pl.ds(pl.multiple_of(base * head_dim, half), half)
         copies = [
             pltpu.make_async_copy(
                 recv[n].at[:, :, side], win.at[:, pl.ds(window_row(d), rows), :], sems.at[n]
@@ -382,7 +383,9 @@
         give[...] = hold[1].astype(give.dtype)
 
 
-def attend(base, slab_index, verticals, offsets, prepared, own, gathered, recv, lines, kept_as):
+def attend(
+    call, bases, slab_index, verticals, offsets, prepared, own, gathered, recv, lines, kept_as
+):
     heads, per_device, deep, head_dim = prepared[0].shape
     _, rows, features = own.shape
     nv, ns = verticals.shape[1], offsets.shape[1]
@@ -392,7 +395,7 @@
 
     def by_head(shape):
         return pl.BlockSpec(
-            (1,) + shape[1:], lambda i, base, *_: (base[0] + i,) + (0,) * (len(shape) - 1)
+            (1,) + shape[1:], lambda i, bases, *_: (bases[call] + i,) + (0,) * (len(shape) - 1)
         )
 
     def by_turn(shape):
@@ -407,7 +410,7 @@
     ]
     return pl.pallas_call(
         functools.partial(
-            attend_kernel, lines=lines, nv=nv, ns=ns, per_device=per_device
+            attend_kernel, lines=lines, nv=nv, ns=ns, per_device=per_device, call=call
         ),
         grid_spec=pltpu.PrefetchScalarGridSpec(
             num_scalar_prefetch=4,
@@ -430,13 +433,13 @@
             jax.ShapeDtypeStruct(share, BF16),
         ]
         + [jax.ShapeDtypeStruct(shape, BF16) for shape in low_shapes],
-        compiler_params=pltpu.CompilerParams(vmem_limit_bytes=VMEM_LIMIT),
+        compiler_params=pltpu.CompilerParams(vmem_limit_bytes=18 * MIB),
         cost_estimate=pl.CostEstimate(
             flops=2 * 5 * half * per_device * cand * BLOCK * deep * head_dim,
             bytes_accessed=12 << 20,
             transcendentals=half * per_device * cand * BLOCK * deep,
         ),
-    )(base, slab_index, verticals, offsets, *prepared, own, *gathered, *recv)
+    )(bases, slab_index, verticals, offsets, *prepared, own, *gathered, *recv)
 
 
 def turn_to_head(t, bases, half):
@@ -507,7 +510,7 @@
             scratch_shapes=[pltpu.VMEM((2, (WDEV + 1) * rows, head_dim), F32)],
         ),
         out_shape=[jax.ShapeDtypeStruct(shard, F32)] * 3 + [jax.ShapeDtypeStruct(shard, BF16)] * 3,
-        compiler_params=pltpu.CompilerParams(vmem_limit_bytes=VMEM_LIMIT),
+        compiler_params=pltpu.CompilerParams(vmem_limit_bytes=16 * MIB),
         cost_estimate=pl.CostEstimate(flops=0, bytes_accessed=9 << 20, transcendentals=0),
     )(bases, offsets, qs, gs, *lows[0][:2], *lows[1][:2])
 
@@ -554,7 +557,7 @@
             ),
         ),
         out_shape=jax.ShapeDtypeStruct((rows, 2 * half * width), BF16),
-        compiler_params=pltpu.CompilerParams(vmem_limit_bytes=VMEM_LIMIT),
+        compiler_params=pltpu.CompilerParams(vmem_limit_bytes=16 * MIB),
         cost_estimate=pl.CostEstimate(flops=0, bytes_accessed=10 << 20, transcendentals=0),
     )(bases, lows[0][2], lows[0][1], lows[1][2], lows[1][1])
 
@@ -580,7 +583,7 @@
         out_specs=[hbm] * 2,
         out_shape=[jax.ShapeDtypeStruct(shape, BF16)] * 2,
         scratch_shapes=[pltpu.VMEM(shape[1:], BF16), pltpu.SemaphoreType.DMA((2, shape[0]))],
-        compiler_params=pltpu.CompilerParams(vmem_limit_bytes=VMEM_LIMIT),
+        compiler_params=pltpu.CompilerParams(vmem_limit_bytes=2 * MIB),
         cost_estimate=pl.CostEstimate(flops=0, bytes_accessed=5 << 20, transcendentals=0),
     )(ahead)
 
@@ -687,7 +690,7 @@
             pltpu.SemaphoreType.DMA((2, 2)),
             pltpu.SemaphoreType.DMA((2, heads * nv)),
         ],
-        compiler_params=pltpu.CompilerParams(vmem_limit_bytes=VMEM_LIMIT),
+        compiler_params=pltpu.CompilerParams(vmem_limit_bytes=12 * MIB),
     )(slab_index, verticals, home, from_near, *arrived, *gathered, *blank)
 
 
@@ -729,8 +732,8 @@
 
     def attend_line(call, gathered, kept_as):
         return attend(
-            bases[call : call + 1], slab_index, verticals, offsets, prepared, own, gathered, recv,
-            lines, kept_as,
+            call, bases, slab_index, verticals, offsets, prepared, own, gathered, recv, lines,
+            kept_as,
         )
 
     to_near, to_both, *first_lows = attend_line(0, gathered[0::2], BF16)

time: 114 us -> 114 us (level)
  waiting for transfers between devices: 31.9 us -> 29.1 us
  local copies, waits for them, and re-layouts: 9.43 us -> 12.1 us
  starting transfers between devices: 30.7 us -> 33.2 us
  Pallas kernels: 33.9 us -> 32.2 us
    unnamed x48 -> x54, local copies, waits for them, and re-layouts: 8.74 us -> 12.1 us
    ppermute x34, waiting for transfers between devices: 31.9 us -> 29.1 us  [move(): return lax.ppermute(array, 'ctx', pairs)]
    ppermute x34, starting transfers between devices: 30.7 us -> 33.2 us  [move(): return lax.ppermute(array, 'ctx', pairs)]
    pallas_call x2, Pallas kernels: 14.8 us -> 13.2 us  [attend(): pl.pallas_call(functools.partial(attend_kernel, lines=lines, nv=nv, ns=ns...]
  transfers between devices with their start and end apart: 34 -> 34, of which waited for: 12 -> 11; matrix products, arithmetic and copies ran while one was open for 5% -> 5% of each run, Pallas kernels for 22% -> 21%
where the time goes in v13:
time: 114 us
  starting transfers between devices  33.2 us (29%)
  Pallas kernels  32.2 us (28%)
  waiting for transfers between devices  29.1 us (26%)
  local copies, waits for them, and re-layouts  12.1 us (11%)
  other arithmetic  5.27 us (5%)
  between operations  1.83 us (2%)
    ppermute x34, starting transfers between devices, move(): return lax.ppermute(array, 'ctx', pairs)  33.2 us
    ppermute x34, waiting for transfers between devices, move(): return lax.ppermute(array, 'ctx', pairs)  29.1 us
    pallas_call x2, Pallas kernels, attend(): pl.pallas_call(functools.partial(attend_kernel, lines=lines, nv=nv, ns=ns...  13.2 us
    unnamed x54, local copies, waits for them, and re-layouts  12.1 us
    pallas_call x1, Pallas kernels, assemble(): pl.pallas_call(functools.partial(assemble_kernel, lines=lines, heads=head...  4.42 us
    pallas_call x1, Pallas kernels, pack(): pl.pallas_call(functools.partial(pack_kernel, lines=lines, heads=heads, n...  4.34 us
    pallas_call x1, Pallas kernels, query_gradients(): pl.pallas_call(query_kernel, grid_spec=pltpu.PrefetchScalarGridSpec(num_s...  3.56 us
    pallas_call x1, Pallas kernels, window_gradients(): pl.pallas_call(functools.partial(window_kernel, lines=lines, half=half, n...  3.07 us
  transfers between devices with their start and end apart: 34, of which 11 were waited for; matrix products, arithmetic and copies ran while one was open for 5% of the time, Pallas kernels for 21%

profile of v13, /device:TPU:0, one launch (start us, length us, event | category | flops | bytes accessed | tf_op | source)
XLA Modules:
  0.0 113.7 jit_solution(325387296457184155)
XLA Ops:
  1.3 4.3 %shard_map.103 = (bf16[2,128,512]{2,1,0:T(8,128)(2,1)}, bf16[2,128,512]{2,1,0:T(8,128)(2,1)}, bf16[2,128,512]{2,1,0:T(8,128)(2,1)}, bf16[4,256,128]{2,1,0:T(8,12...) custom-call(s32[1]{0:T(128)S(6)} %copy.15.slab_index, ...), custom_call_target="tpu_custom_call" | custom-call | tf_op jit(solution)/shard_map/pallas_call | solution.py:168
  6.2 2.6 %collective-permute-start.3 = (bf16[2,128,512]{2,1,0:T(8,128)(2,1)}, bf16[2,128,512]{2,1,0:T(8,128)(2,1)S(1)}, u32[]{:S(2)}, u32[]{:S(2)}) collective-permute-start(bf16[2,128,512]{2,1,0:T(8,128)(2,1)} %get-tuple-element.57), channel_id=1, source_target_pairs={{0,4},{1,5},{2,6},{3,7},{4,8},{5,9},{6,10},{7,11},{8,12},{9,13},{1... | collective-permute-start | bytes 786440 | tf_op jit(solution)/shard_map/ppermute | solution.py:52
  9.0 1.7 %add_convert_fusion.3 = bf16[4,256,128]{2,1,0:T(8,128)(2,1)} fusion(bf16[4,256,128]{2,1,0:T(8,128)(2,1)S(1)} %collective-permute-done, bf16[4,256,128]{2,1,0:T(8,128)(2,1)} %get-tuple-element.46), kind=kLoop, calls=%fused_computation.5 | loop fusion | flops 524288 | bytes 786432 | tf_op jit(solution)/shard_map/convert_element_type | solution.py:60
  12.2 5.7 %collective-permute-done.3.rest_3_ = bf16[2,128,512]{2,1,0:T(8,128)(2,1)S(1)} collective-permute-done((bf16[2,128,512]{2,1,0:T(8,128)(2,1)}, bf16[2,128,512]{2,1,0:T(8,128)(2,1)S(1)}, u32[]{:S(2)}, u32[]{:S(2)}) %collective-permute-start.3) | collective-permute-done | bytes 262176 | tf_op jit(solution)/shard_map/ppermute | solution.py:52
  23.0 1.9 %convert_add_fusion.1 = f32[4,256,128]{2,1,0:T(8,128)S(1)} fusion(bf16[4,256,128]{2,1,0:T(8,128)(2,1)} %collective-permute-done.2, bf16[4,256,128]{2,1,0:T(8,128)(2,1)} %collective-permute-done.1, bf16[4,256,128]{2,1,0:T(8,128)(2,1)S(1)} %copy-done.25), kind=kLoop, calls=%fused_computation.4 | loop fusion | flops 655360 | bytes 1310720 | tf_op jit(solution)/shard_map/add | solution.py:65
  25.0 1.8 %collective-permute-start.6 = (bf16[256,128]{1,0:T(8,128)(2,1)S(1)}, bf16[256,128]{1,0:T(8,128)(2,1)S(1)}, u32[]{:S(2)}, u32[]{:S(2)}) collective-permute-start(bf16[256,128]{1,0:T(8,128)(2,1)S(1)} %get-tuple-element.93), channel_id=1, source_target_pairs={{0,12},{1,13},{2,14},{3,15},{4,0},{5,1},{6,2},{7,3},{8,4},{9,5},{1... | collective-permute-start | bytes 196616 | tf_op jit(solution)/shard_map/ppermute | solution.py:52
  29.3 2.1 %collective-permute-start.12 = (bf16[2,128,512]{2,1,0:T(8,128)(2,1)S(1)}, bf16[2,128,512]{2,1,0:T(8,128)(2,1)S(1)}, u32[]{:S(2)}, u32[]{:S(2)}) collective-permute-start(bf16[2,128,512]{2,1,0:T(8,128)(2,1)S(1)} %collective-permute-done.11.rest_2_), channel_id=1, source_target_pairs={{0,1},{1,0},{2,3},{3,2},{4,5},{5,4},{6,7},{7,6},{8,9},{9,8},{10,11... | collective-permute-start | bytes 786440 | tf_op jit(solution)/shard_map/ppermute | solution.py:52
  31.4 2.1 %collective-permute-done.5 = bf16[256,128]{1,0:T(8,128)(2,1)S(1)} collective-permute-done((bf16[256,128]{1,0:T(8,128)(2,1)S(1)}, bf16[256,128]{1,0:T(8,128)(2,1)S(1)}, u32[]{:S(2)}, u32[]{:S(2)}) %collective-permute-start.5) | collective-permute-done | bytes 65568 | tf_op jit(solution)/shard_map/ppermute | solution.py:52
  36.1 2.0 %collective-permute-start.8 = (bf16[256,128]{1,0:T(8,128)(2,1)S(1)}, bf16[256,128]{1,0:T(8,128)(2,1)S(1)}, u32[]{:S(2)}, u32[]{:S(2)}) collective-permute-start(bf16[256,128]{1,0:T(8,128)(2,1)S(1)} %fusion.5._), channel_id=1, source_target_pairs={{0,4},{1,5},{2,6},{3,7},{4,8},{5,9},{6,10},{7,11},{8,12},{9,13},{1... | collective-permute-start | bytes 196616 | tf_op jit(solution)/shard_map/ppermute | solution.py:52
  38.1 2.3 %shard_map.105 = (bf16[16,128,512]{2,1,0:T(8,128)(2,1)}, bf16[16,128,512]{2,1,0:T(8,128)(2,1)}) custom-call(bf16[256,128]{1,0:T(8,128)(2,1)S(1)} %fusion.5._), custom_call_target="tpu_custom_call" | custom-call | bytes 5242880 | tf_op jit(solution)/shard_map/pallas_call | solution.py:580
  40.4 2.2 %collective-permute-done.9 = bf16[256,128]{1,0:T(8,128)(2,1)S(1)} collective-permute-done((bf16[256,128]{1,0:T(8,128)(2,1)S(1)}, bf16[256,128]{1,0:T(8,128)(2,1)S(1)}, u32[]{:S(2)}, u32[]{:S(2)}) %collective-permute-start.9) | collective-permute-done | bytes 65568 | tf_op jit(solution)/shard_map/ppermute | solution.py:52
  44.2 3.9 %collective-permute-start.14 = (bf16[4,256,128]{2,1,0:T(8,128)(2,1)S(1)}, bf16[4,256,128]{2,1,0:T(8,128)(2,1)S(1)}, u32[]{:S(2)}, u32[]{:S(2)}) collective-permute-start(bf16[4,256,128]{2,1,0:T(8,128)(2,1)S(1)} %pad_maximum_fusion.rest_0_), channel_id=1, source_target_pairs={{0,2},{1,3},{2,0},{3,1},{4,6},{5,7},{6,4},{7,5},{8,10},{9,11},{10,... | collective-permute-start | bytes 786440 | tf_op jit(solution)/shard_map/ppermute | solution.py:52
  56.0 6.6 %shard_map.107 = (bf16[4,256,128]{2,1,0:T(8,128)(2,1)S(1)}, bf16[4,256,128]{2,1,0:T(8,128)(2,1)S(1)}, bf16[2,2,256,512]{3,2,1,0:T(8,128)(2,1)S(1)}, bf16[2,2,768...) custom-call(s32[2]{0:T(128)S(1)} %add_multiply_fusion.bases, s32[1]{0:T(128)S(6)} %copy.15.slab_index, ...), custom_call_target="tpu_custom_call" | custom-call | flops 2013265920 | bytes 12582912 | tf_op jit(solution)/shard_map/pallas_call | solution.py:411
  65.8 6.6 %shard_map.106 = (f32[4,256,128]{2,1,0:T(8,128)S(1)}, bf16[4,256,128]{2,1,0:T(8,128)(2,1)S(1)}, bf16[2,2,256,512]{3,2,1,0:T(8,128)(2,1)S(1)}, bf16[2,2,768,512]{...) custom-call(s32[2]{0:T(128)S(1)} %add_multiply_fusion.bases, s32[1]{0:T(128)S(6)} %copy.15.slab_index, ...), custom_call_target="tpu_custom_call" | custom-call | flops 2013265920 | bytes 12582912 | tf_op jit(solution)/shard_map/pallas_call | solution.py:411
  72.8 3.1 %shard_map.108 = (f32[2,128,512]{2,1,0:T(8,128)S(1)}, f32[2,128,512]{2,1,0:T(8,128)S(1)}, f32[2,128,512]{2,1,0:T(8,128)S(1)}, bf16[2,128,512]{2,1,0:T(8,128)(2,1...) custom-call(s32[2]{0:T(128)S(1)} %add_multiply_fusion.bases, s32[4,3]{1,0:T(4,128)S(1)} %copy-done.9, ...), custom_call_target="tpu_custom_call" | custom-call | bytes 9437184 | tf_op jit(solution)/shard_map/pallas_call | solution.py:503
  76.3 1.8 %collective-permute-start.22 = (bf16[256,128]{1,0:T(8,128)(2,1)S(1)}, bf16[256,128]{1,0:T(8,128)(2,1)S(1)}, u32[]{:S(2)}, u32[]{:S(2)}) collective-permute-start(bf16[256,128]{1,0:T(8,128)(2,1)S(1)} %get-tuple-element.90), channel_id=1, source_target_pairs={{0,12},{1,13},{2,14},{3,15},{4,0},{5,1},{6,2},{7,3},{8,4},{9,5},{1... | collective-permute-start | bytes 196616 | tf_op jit(solution)/shard_map/ppermute | solution.py:52
  79.3 1.8 %collective-permute-start.28 = (bf16[2,128,512]{2,1,0:T(8,128)(2,1)S(1)}, bf16[2,128,512]{2,1,0:T(8,128)(2,1)S(1)}, u32[]{:S(2)}, u32[]{:S(2)}) collective-permute-start(bf16[2,128,512]{2,1,0:T(8,128)(2,1)S(1)} %get-tuple-element.78), channel_id=1, source_target_pairs={{1,0},{6,1},{3,2},{8,3},{5,4},{10,5},{7,6},{12,7},{9,8},{14,9},{11... | collective-permute-start | bytes 786440 | tf_op jit(solution)/shard_map/ppermute | solution.py:52
  82.9 5.6 %collective-permute-done.21 = bf16[256,128]{1,0:T(8,128)(2,1)S(1)} collective-permute-done((bf16[256,128]{1,0:T(8,128)(2,1)S(1)}, bf16[256,128]{1,0:T(8,128)(2,1)S(1)}, u32[]{:S(2)}, u32[]{:S(2)}) %collective-permute-start.21) | collective-permute-done | bytes 65568 | tf_op jit(solution)/shard_map/ppermute | solution.py:52
  88.5 2.2 %collective-permute-start.24 = (bf16[256,128]{1,0:T(8,128)(2,1)S(1)}, bf16[256,128]{1,0:T(8,128)(2,1)S(1)}, u32[]{:S(2)}, u32[]{:S(2)}) collective-permute-start(bf16[256,128]{1,0:T(8,128)(2,1)S(1)} %fusion.2), channel_id=1, source_target_pairs={{0,8},{1,9},{2,10},{3,11},{4,12},{5,13},{6,14},{7,15},{8,0},{9,1},... | collective-permute-start | bytes 196616 | tf_op jit(solution)/shard_map/ppermute | solution.py:52
  90.7 2.3 %collective-permute-done.25 = bf16[256,128]{1,0:T(8,128)(2,1)S(1)} collective-permute-done((bf16[256,128]{1,0:T(8,128)(2,1)S(1)}, bf16[256,128]{1,0:T(8,128)(2,1)S(1)}, u32[]{:S(2)}, u32[]{:S(2)}) %collective-permute-start.25) | collective-permute-done | bytes 65568 | tf_op jit(solution)/shard_map/ppermute | solution.py:52
  95.5 3.6 %collective-permute-done.23 = bf16[256,128]{1,0:T(8,128)(2,1)S(1)} collective-permute-done((bf16[256,128]{1,0:T(8,128)(2,1)S(1)}, bf16[256,128]{1,0:T(8,128)(2,1)S(1)}, u32[]{:S(2)}, u32[]{:S(2)}) %collective-permute-start.23) | collective-permute-done | bytes 65568 | tf_op jit(solution)/shard_map/ppermute | solution.py:52
  101.1 4.5 %collective-permute-done.31.rest_4_ = bf16[4,256,128]{2,1,0:T(8,128)(2,1)S(1)} collective-permute-done((bf16[4,256,128]{2,1,0:T(8,128)(2,1)S(1)}, bf16[4,256,128]{2,1,0:T(8,128)(2,1)S(1)}, u32[]{:S(2)}, u32[]{:S(2)}) %collective-permute-start.31) | collective-permute-done | bytes 262176 | tf_op jit(solution)/shard_map/ppermute | solution.py:52
  105.6 3.6 %shard_map.109 = bf16[128,4096]{1,0:T(8,128)(2,1)} custom-call(s32[2]{0:T(128)S(1)} %add_multiply_fusion.bases, bf16[2,2,768,128]{3,2,1,0:T(8,128)(2,1)S(1)} %get-tuple-element.81.rest_0_, bf16[2,2,768,512]{3,2,1,0:T(8,128)(2,1)S(1)} %get-tuple-element.71.rest_1_, bf16[2,2,768,128]{3,2,1,0:T(8,128)(2,1)S(1)} %get-tuple-element.82.rest_2_, ...), custom_call_target="tpu_custom_call" | custom-call | bytes 10485760 | tf_op jit(solution)/shard_map/pallas_call | solution.py:549
  109.1 4.4 %shard_map.110 = (bf16[16,128,512]{2,1,0:T(8,128)(2,1)}, bf16[16,128,512]{2,1,0:T(8,128)(2,1)}) custom-call(s32[1]{0:T(128)S(6)} %copy.15.slab_index, s32[4,8]{1,0:T(4,128)S(1)} %copy-done.8, f32[2,128,512]{2,1,0:T(8,128)S(1)} %get-tuple-element.83.home, ...), custom_call_target="tpu_custom_call", output_to_operand_aliasing={{0}: (10, {}), {1}: (11, {})} | custom-call | tf_op jit(solution)/shard_map/pallas_call | solution.py:677
  (122 shorter events, 33.3 us)
Async XLA Ops:
  6.2 11.8 %collective-permute-start.3 = (bf16[2,128,512]{2,1,0:T(8,128)(2,1)}, bf16[2,128,512]{2,1,0:T(8,128)(2,1)S(1)}, u32[]{:S(2)}, u32[]{:S(2)}) collective-permute-start(bf16[2,128,512]{2,1,0:T(8,128)(2,1)} %get-tuple-element.57), channel_id=1, source_target_pairs={{0,4},{1,5},{2,6},{3,7},{4,8},{5,9},{6,10},{7,11},{8,12},{9,13},{1... | collective-permute-start | bytes 786440 | tf_op jit(solution)/shard_map/ppermute | solution.py:52
  8.8 14.2 %collective-permute-start.1 = (bf16[4,256,128]{2,1,0:T(8,128)(2,1)}, bf16[4,256,128]{2,1,0:T(8,128)(2,1)}, u32[]{:S(2)}, u32[]{:S(2)}) collective-permute-start(bf16[4,256,128]{2,1,0:T(8,128)(2,1)} %get-tuple-element.56), channel_id=1, source_target_pairs={{0,1},{1,0},{2,3},{3,2},{4,5},{5,4},{6,7},{7,6},{8,9},{9,8},{10,11... | collective-permute-start | bytes 786440 | tf_op jit(solution)/shard_map/ppermute | solution.py:52
  10.7 12.3 %collective-permute-start.2 = (bf16[4,256,128]{2,1,0:T(8,128)(2,1)}, bf16[4,256,128]{2,1,0:T(8,128)(2,1)}, u32[]{:S(2)}, u32[]{:S(2)}) collective-permute-start(bf16[4,256,128]{2,1,0:T(8,128)(2,1)} %add_convert_fusion.3), channel_id=1, source_target_pairs={{0,2},{1,3},{2,0},{3,1},{4,6},{5,7},{6,4},{7,5},{8,10},{9,11},{10,... | collective-permute-start | bytes 786440 | tf_op jit(solution)/shard_map/ppermute | solution.py:52
  19.0 8.8 %collective-permute-start.11 = (bf16[2,128,512]{2,1,0:T(8,128)(2,1)S(1)}, bf16[2,128,512]{2,1,0:T(8,128)(2,1)S(1)}, u32[]{:S(2)}, u32[]{:S(2)}) collective-permute-start(bf16[2,128,512]{2,1,0:T(8,128)(2,1)S(1)} %broadcast_select_fusion), channel_id=1, source_target_pairs={{0,2},{1,3},{2,0},{3,1},{4,6},{5,7},{6,4},{7,5},{8,10},{9,11},{10,... | collective-permute-start | bytes 786440 | tf_op jit(solution)/shard_map/ppermute | solution.py:52
  26.8 6.7 %collective-permute-start.5 = (bf16[256,128]{1,0:T(8,128)(2,1)S(1)}, bf16[256,128]{1,0:T(8,128)(2,1)S(1)}, u32[]{:S(2)}, u32[]{:S(2)}) collective-permute-start(bf16[256,128]{1,0:T(8,128)(2,1)S(1)} %get-tuple-element.94), channel_id=1, source_target_pairs={{0,8},{1,9},{2,10},{3,11},{4,12},{5,13},{6,14},{7,15},{8,0},{9,1},... | collective-permute-start | bytes 196616 | tf_op jit(solution)/shard_map/ppermute | solution.py:52
  26.8 6.7 %collective-permute-start.4 = (bf16[256,128]{1,0:T(8,128)(2,1)S(1)}, bf16[256,128]{1,0:T(8,128)(2,1)S(1)}, u32[]{:S(2)}, u32[]{:S(2)}) collective-permute-start(bf16[256,128]{1,0:T(8,128)(2,1)S(1)} %get-tuple-element.92), channel_id=1, source_target_pairs={{0,4},{1,5},{2,6},{3,7},{4,8},{5,9},{6,10},{7,11},{8,12},{9,13},{1... | collective-permute-start | bytes 196616 | tf_op jit(solution)/shard_map/ppermute | solution.py:52
  27.8 5.7 %collective-permute-start.7 = (bf16[2,128,512]{2,1,0:T(8,128)(2,1)S(1)}, bf16[2,128,512]{2,1,0:T(8,128)(2,1)S(1)}, u32[]{:S(2)}, u32[]{:S(2)}) collective-permute-start(bf16[2,128,512]{2,1,0:T(8,128)(2,1)S(1)} %collective-permute-done.3.rest_3_), channel_id=1, source_target_pairs={{0,1},{1,0},{2,3},{3,2},{4,5},{5,4},{6,7},{7,6},{8,9},{9,8},{10,11... | collective-permute-start | bytes 786440 | tf_op jit(solution)/shard_map/ppermute | solution.py:52
  27.8 15.6 %collective-permute-start.13 = (bf16[2,128,512]{2,1,0:T(8,128)(2,1)S(1)}, bf16[2,128,512]{2,1,0:T(8,128)(2,1)S(1)}, u32[]{:S(2)}, u32[]{:S(2)}) collective-permute-start(bf16[2,128,512]{2,1,0:T(8,128)(2,1)S(1)} %copy-done.26), channel_id=1, source_target_pairs={{0,1},{1,6},{2,3},{3,8},{4,5},{5,10},{6,7},{7,12},{8,9},{9,14},{10... | collective-permute-start | bytes 786440 | tf_op jit(solution)/shard_map/ppermute | solution.py:52
  29.3 13.3 %collective-permute-start.12 = (bf16[2,128,512]{2,1,0:T(8,128)(2,1)S(1)}, bf16[2,128,512]{2,1,0:T(8,128)(2,1)S(1)}, u32[]{:S(2)}, u32[]{:S(2)}) collective-permute-start(bf16[2,128,512]{2,1,0:T(8,128)(2,1)S(1)} %collective-permute-done.11.rest_2_), channel_id=1, source_target_pairs={{0,1},{1,0},{2,3},{3,2},{4,5},{5,4},{6,7},{7,6},{8,9},{9,8},{10,11... | collective-permute-start | bytes 786440 | tf_op jit(solution)/shard_map/ppermute | solution.py:52
  34.3 6.1 %collective-permute-start.10 = (bf16[256,128]{1,0:T(8,128)(2,1)S(1)}, bf16[256,128]{1,0:T(8,128)(2,1)S(1)}, u32[]{:S(2)}, u32[]{:S(2)}) collective-permute-start(bf16[256,128]{1,0:T(8,128)(2,1)S(1)} %fusion.5._), channel_id=1, source_target_pairs={{0,12},{1,13},{2,14},{3,15},{4,0},{5,1},{6,2},{7,3},{8,4},{9,5},{1... | collective-permute-start | bytes 196616 | tf_op jit(solution)/shard_map/ppermute | solution.py:52
  35.6 7.0 %collective-permute-start.9 = (bf16[256,128]{1,0:T(8,128)(2,1)S(1)}, bf16[256,128]{1,0:T(8,128)(2,1)S(1)}, u32[]{:S(2)}, u32[]{:S(2)}) collective-permute-start(bf16[256,128]{1,0:T(8,128)(2,1)S(1)} %fusion.5._), channel_id=1, source_target_pairs={{0,8},{1,9},{2,10},{3,11},{4,12},{5,13},{6,14},{7,15},{8,0},{9,1},... | collective-permute-start | bytes 196616 | tf_op jit(solution)/shard_map/ppermute | solution.py:52
  36.1 6.5 %collective-permute-start.8 = (bf16[256,128]{1,0:T(8,128)(2,1)S(1)}, bf16[256,128]{1,0:T(8,128)(2,1)S(1)}, u32[]{:S(2)}, u32[]{:S(2)}) collective-permute-start(bf16[256,128]{1,0:T(8,128)(2,1)S(1)} %fusion.5._), channel_id=1, source_target_pairs={{0,4},{1,5},{2,6},{3,7},{4,8},{5,9},{6,10},{7,11},{8,12},{9,13},{1... | collective-permute-start | bytes 196616 | tf_op jit(solution)/shard_map/ppermute | solution.py:52
  44.2 18.7 %collective-permute-start.14 = (bf16[4,256,128]{2,1,0:T(8,128)(2,1)S(1)}, bf16[4,256,128]{2,1,0:T(8,128)(2,1)S(1)}, u32[]{:S(2)}, u32[]{:S(2)}) collective-permute-start(bf16[4,256,128]{2,1,0:T(8,128)(2,1)S(1)} %pad_maximum_fusion.rest_0_), channel_id=1, source_target_pairs={{0,2},{1,3},{2,0},{3,1},{4,6},{5,7},{6,4},{7,5},{8,10},{9,11},{10,... | collective-permute-start | bytes 786440 | tf_op jit(solution)/shard_map/ppermute | solution.py:52
  64.3 8.5 %collective-permute-start.19 = (bf16[4,256,128]{2,1,0:T(8,128)(2,1)S(1)}, bf16[4,256,128]{2,1,0:T(8,128)(2,1)S(1)}, u32[]{:S(2)}, u32[]{:S(2)}) collective-permute-start(bf16[4,256,128]{2,1,0:T(8,128)(2,1)S(1)} %add_convert_fusion.2), channel_id=1, source_target_pairs={{0,2},{1,3},{2,0},{3,1},{4,6},{5,7},{6,4},{7,5},{8,10},{9,11},{10,... | collective-permute-start | bytes 786440 | tf_op jit(solution)/shard_map/ppermute | solution.py:52
  78.0 10.4 %collective-permute-start.21 = (bf16[256,128]{1,0:T(8,128)(2,1)S(1)}, bf16[256,128]{1,0:T(8,128)(2,1)S(1)}, u32[]{:S(2)}, u32[]{:S(2)}) collective-permute-start(bf16[256,128]{1,0:T(8,128)(2,1)S(1)} %get-tuple-element.91), channel_id=1, source_target_pairs={{0,8},{1,9},{2,10},{3,11},{4,12},{5,13},{6,14},{7,15},{8,0},{9,1},... | collective-permute-start | bytes 196616 | tf_op jit(solution)/shard_map/ppermute | solution.py:52
  78.1 10.4 %collective-permute-start.20 = (bf16[256,128]{1,0:T(8,128)(2,1)S(1)}, bf16[256,128]{1,0:T(8,128)(2,1)S(1)}, u32[]{:S(2)}, u32[]{:S(2)}) collective-permute-start(bf16[256,128]{1,0:T(8,128)(2,1)S(1)} %get-tuple-element.89), channel_id=1, source_target_pairs={{0,4},{1,5},{2,6},{3,7},{4,8},{5,9},{6,10},{7,11},{8,12},{9,13},{1... | collective-permute-start | bytes 196616 | tf_op jit(solution)/shard_map/ppermute | solution.py:52
  79.3 19.8 %collective-permute-start.28 = (bf16[2,128,512]{2,1,0:T(8,128)(2,1)S(1)}, bf16[2,128,512]{2,1,0:T(8,128)(2,1)S(1)}, u32[]{:S(2)}, u32[]{:S(2)}) collective-permute-start(bf16[2,128,512]{2,1,0:T(8,128)(2,1)S(1)} %get-tuple-element.78), channel_id=1, source_target_pairs={{1,0},{6,1},{3,2},{8,3},{5,4},{10,5},{7,6},{12,7},{9,8},{14,9},{11... | collective-permute-start | bytes 786440 | tf_op jit(solution)/shard_map/ppermute | solution.py:52
  81.2 18.1 %collective-permute-start.29 = (bf16[2,128,512]{2,1,0:T(8,128)(2,1)S(1)}, bf16[2,128,512]{2,1,0:T(8,128)(2,1)S(1)}, u32[]{:S(2)}, u32[]{:S(2)}) collective-permute-start(bf16[2,128,512]{2,1,0:T(8,128)(2,1)S(1)} %get-tuple-element.85), channel_id=1, source_target_pairs={{0,1},{1,0},{2,3},{3,2},{4,5},{5,4},{6,7},{7,6},{8,9},{9,8},{10,11... | collective-permute-start | bytes 786440 | tf_op jit(solution)/shard_map/ppermute | solution.py:52
  81.3 17.8 %collective-permute-start.27 = (bf16[2,128,512]{2,1,0:T(8,128)(2,1)S(1)}, bf16[2,128,512]{2,1,0:T(8,128)(2,1)S(1)}, u32[]{:S(2)}, u32[]{:S(2)}) collective-permute-start(bf16[2,128,512]{2,1,0:T(8,128)(2,1)S(1)} %add_convert_fusion.1), channel_id=1, source_target_pairs={{0,2},{1,3},{2,0},{3,1},{4,6},{5,7},{6,4},{7,5},{8,10},{9,11},{10,... | collective-permute-start | bytes 786440 | tf_op jit(solution)/shard_map/ppermute | solution.py:52
  88.5 6.9 %collective-permute-start.24 = (bf16[256,128]{1,0:T(8,128)(2,1)S(1)}, bf16[256,128]{1,0:T(8,128)(2,1)S(1)}, u32[]{:S(2)}, u32[]{:S(2)}) collective-permute-start(bf16[256,128]{1,0:T(8,128)(2,1)S(1)} %fusion.2), channel_id=1, source_target_pairs={{0,8},{1,9},{2,10},{3,11},{4,12},{5,13},{6,14},{7,15},{8,0},{9,1},... | collective-permute-start | bytes 196616 | tf_op jit(solution)/shard_map/ppermute | solution.py:52
  93.0 6.1 %collective-permute-start.23 = (bf16[256,128]{1,0:T(8,128)(2,1)S(1)}, bf16[256,128]{1,0:T(8,128)(2,1)S(1)}, u32[]{:S(2)}, u32[]{:S(2)}) collective-permute-start(bf16[256,128]{1,0:T(8,128)(2,1)S(1)} %fusion.2), channel_id=1, source_target_pairs={{0,4},{1,5},{2,6},{3,7},{4,8},{5,9},{6,10},{7,11},{8,12},{9,13},{1... | collective-permute-start | bytes 196616 | tf_op jit(solution)/shard_map/ppermute | solution.py:52
  99.1 6.4 %collective-permute-start.31 = (bf16[4,256,128]{2,1,0:T(8,128)(2,1)S(1)}, bf16[4,256,128]{2,1,0:T(8,128)(2,1)S(1)}, u32[]{:S(2)}, u32[]{:S(2)}) collective-permute-start(bf16[4,256,128]{2,1,0:T(8,128)(2,1)S(1)} %pad_maximum_fusion.1.rest_3_), channel_id=1, source_target_pairs={{0,2},{1,3},{2,0},{3,1},{4,6},{5,7},{6,4},{7,5},{8,10},{9,11},{10,... | collective-permute-start | bytes 786440 | tf_op jit(solution)/shard_map/ppermute | solution.py:52
  99.2 9.9 %collective-permute-start.32 = (bf16[4,256,128]{2,1,0:T(8,128)(2,1)S(1)}, bf16[4,256,128]{2,1,0:T(8,128)(2,1)S(1)}, u32[]{:S(2)}, u32[]{:S(2)}) collective-permute-start(bf16[4,256,128]{2,1,0:T(8,128)(2,1)S(1)} %pad_maximum_fusion.1.rest_3_), channel_id=1, source_target_pairs={{0,1},{1,0},{2,3},{3,2},{4,5},{5,4},{6,7},{7,6},{8,9},{9,8},{10,11... | collective-permute-start | bytes 786440 | tf_op jit(solution)/shard_map/ppermute | solution.py:52
  99.4 9.7 %collective-permute-start.30 = (bf16[2,128,512]{2,1,0:T(8,128)(2,1)S(1)}, bf16[2,128,512]{2,1,0:T(8,128)(2,1)S(1)}, u32[]{:S(2)}, u32[]{:S(2)}) collective-permute-start(bf16[2,128,512]{2,1,0:T(8,128)(2,1)S(1)} %add_convert_fusion), channel_id=1, source_target_pairs={{4,0},{5,1},{6,2},{7,3},{8,4},{9,5},{10,6},{11,7},{12,8},{13,9},{1... | collective-permute-start | bytes 786440 | tf_op jit(solution)/shard_map/ppermute | solution.py:52
  (37 other events, 322.2 us)

commit v14 on v13

--- a/solution.py
+++ b/solution.py
@@ -202,7 +202,29 @@
 NT = (((1,), (1,)), ((), ()))
 
 
-def prepare_kernel(q, grad, out, qs, gs, qt, gt, delta, *, head_dim):
+def turn_to_head(t, bases, half):
+    return bases[lax.div(t, half)] + lax.rem(t, half)
+
+
+def of_call(call, half, shape, block=0):
+    def index(t, *_):
+        turn = jnp.minimum(t, half - 1) if call == 0 else jnp.maximum(t - half, 0)
+        return (turn, 0, block, 0)
+
+    return pl.BlockSpec((1,) + tuple(shape), index)
+
+
+def prepare_kernel(bases, q, grad, out, *sets, head_dim):
+    t = pl.program_id(0)
+    half = pl.num_programs(0) // 2
+    for call in range(2):
+
+        @pl.when(lax.div(t, half) == call)
+        def _():
+            prepare_head(q, grad, out, *sets[5 * call : 5 * call + 5], head_dim=head_dim)
+
+
+def prepare_head(q, grad, out, qs, gs, qt, gt, delta, *, head_dim):
     per_device = qs.shape[1]
     group = q.shape[1] // head_dim
     ones = jnp.ones((8, 2 * head_dim), BF16)
@@ -225,29 +247,34 @@
         )
 
 
-def prepare(queries, cotangent, output, heads, head_dim):
+def prepare(bases, queries, cotangent, output, heads, head_dim):
     rows, width = queries.shape
     per_device = rows // BLOCK
     deep = width // heads // head_dim * BLOCK
-    tile = pl.BlockSpec((rows, width // heads), lambda h: (0, h))
-
-    def by_head(*shape):
-        return pl.BlockSpec((1,) + shape, lambda h: (h,) + (0,) * len(shape))
-
+    half = heads // 2
+    tile = pl.BlockSpec(
+        (rows, width // heads), lambda t, bases: (0, turn_to_head(t, bases, half))
+    )
     stacked = (per_device, deep, head_dim)
     turned = (per_device, head_dim, deep)
-    sums = (per_device, 8, deep)
-    return pl.pallas_call(
+    shapes = [stacked, stacked, turned, turned, (per_device, 8, deep)]
+    types = [BF16] * 4 + [F32]
+    arrays = pl.pallas_call(
         functools.partial(prepare_kernel, head_dim=head_dim),
-        grid=(heads,),
-        in_specs=[tile] * 3,
-        out_specs=[by_head(*stacked)] * 2 + [by_head(*turned)] * 2 + [by_head(*sums)],
-        out_shape=[jax.ShapeDtypeStruct((heads,) + stacked, BF16)] * 2
-        + [jax.ShapeDtypeStruct((heads,) + turned, BF16)] * 2
-        + [jax.ShapeDtypeStruct((heads,) + sums, F32)],
+        grid_spec=pltpu.PrefetchScalarGridSpec(
+            num_scalar_prefetch=1,
+            grid=(heads,),
+            in_specs=[tile] * 3,
+            out_specs=[of_call(call, half, shape) for call in range(2) for shape in shapes],
+        ),
+        out_shape=[
+            jax.ShapeDtypeStruct((half,) + shape, kind) for shape, kind in zip(shapes, types)
+        ]
+        * 2,
         compiler_params=pltpu.CompilerParams(vmem_limit_bytes=16 * MIB),
         cost_estimate=pl.CostEstimate(flops=0, bytes_accessed=7 << 20, transcendentals=0),
-    )(queries, cotangent, output)
+    )(bases, queries, cotangent, output)
+    return arrays[:5], arrays[5:]
 
 
 def slash_rows(offs, h, j, s, per_device):
@@ -255,11 +282,13 @@
 
 
 def attend_kernel(
-    bases, slab_index, verts, offs, qs, gs, qt, gt, delta, own, *rest,
+    bases, slab_index, verts, offs, qs, gs, qt, gt, delta, *rest,
     lines, nv, ns, per_device, call,
 ):
-    gathered, recv, rest = rest[:2], rest[2 : 2 + WDEV], rest[2 + WDEV :]
-    (share, give, low_w, low_ds, cand_keys), scratch = rest[:5], rest[5:]
+    sources = 1 if call else 1 + WDEV
+    gathered, recv, rest = rest[:2], rest[2 : 2 + sources], rest[2 + sources :]
+    (share, give, low_w, low_ds, cand_keys), rest = rest[:5], rest[5:]
+    scratch = rest if call else rest[1:]
     win, vkv, vc, s_ref, vert_w, hold, sems = scratch
     i = pl.program_id(0)
     base = bases[call]
@@ -280,18 +309,21 @@
     @pl.when(i == 0)
     def _():
         half = win.shape[2]
-        own_rows = pl.ds(WDEV * rows, rows)
-        side = pl.ds(pl.multiple_of(base * head_dim, half), half)
-        copies = [
-            pltpu.make_async_copy(
-                recv[n].at[:, :, side], win.at[:, pl.ds(window_row(d), rows), :], sems.at[n]
-            )
-            for n, d in enumerate(distances(core))
-        ]
-        copies.append(
-            pltpu.make_async_copy(own.at[:, :, side], win.at[:, own_rows, :], sems.at[WDEV])
-        )
-        copies += vertical_copies(lines, me, 0, chunk, gathered, vkv, sems, WDEV + 1)
+        copies = []
+        if call:
+            copies.append(pltpu.make_async_copy(recv[0], win, sems.at[0]))
+        else:
+            for m, to in enumerate((win, rest[0])):
+                side = pl.ds(pl.multiple_of(bases[m] * head_dim, half), half)
+                for n, d in enumerate([0] + distances(core)):
+                    copies.append(
+                        pltpu.make_async_copy(
+                            recv[n].at[:, :, side],
+                            to.at[:, pl.ds(window_row(d), rows), :],
+                            sems.at[m * (1 + WDEV) + n],
+                        )
+                    )
+        copies += vertical_copies(lines, me, 0, chunk, gathered, vkv, sems, 2 + 2 * WDEV)
         for copy in copies:
             copy.start()
         for copy in copies:
@@ -384,23 +416,19 @@
 
 
 def attend(
-    call, bases, slab_index, verticals, offsets, prepared, own, gathered, recv, lines, kept_as
+    call, bases, slab_index, verticals, offsets, prepared, gathered, recv, lines, kept_as
 ):
-    heads, per_device, deep, head_dim = prepared[0].shape
-    _, rows, features = own.shape
+    half, per_device, deep, head_dim = prepared[0].shape
+    heads = 2 * half
+    rows, features = per_device * BLOCK, heads * head_dim
     nv, ns = verticals.shape[1], offsets.shape[1]
     cand = nv + 1 + ns
-    half = heads // 2
     anywhere = pl.BlockSpec(memory_space=pl.ANY)
-
-    def by_head(shape):
-        return pl.BlockSpec(
-            (1,) + shape[1:], lambda i, bases, *_: (bases[call] + i,) + (0,) * (len(shape) - 1)
-        )
 
     def by_turn(shape):
         return pl.BlockSpec((1,) + shape[1:], lambda i, *_: (i,) + (0,) * (len(shape) - 1))
 
+    window = (2, (WDEV + 1) * rows, features // 2)
     share = (lines.far, half * nv * BLOCK // lines.far, head_dim)
     shares = pl.BlockSpec(share, lambda i, *_: (0, 0, 0))
     low_shapes = [
@@ -415,56 +443,47 @@
         grid_spec=pltpu.PrefetchScalarGridSpec(
             num_scalar_prefetch=4,
             grid=(half,),
-            in_specs=[by_head(array.shape) for array in prepared]
-            + [anywhere] * (3 + WDEV),
-            out_specs=[shares] * 2 + [by_turn(shape) for shape in low_shapes],
+            in_specs=[by_turn(array.shape) for array in prepared]
+            + [anywhere] * (2 + len(recv)),
+            out_specs=[shares] * 2
+            + [by_turn(shape) for shape in low_shapes]
+            + [anywhere] * (1 - call),
             scratch_shapes=[
-                pltpu.VMEM((2, (WDEV + 1) * rows, features // 2), BF16),
+                pltpu.VMEM(window, BF16),
                 pltpu.VMEM((2, half * nv * BLOCK, head_dim), BF16),
                 pltpu.VMEM((per_device, cand * BLOCK, head_dim), BF16),
                 pltpu.VMEM((per_device, cand * BLOCK, deep), F32),
                 pltpu.VMEM((per_device, nv * BLOCK, deep), BF16),
                 pltpu.VMEM((2,) + share, F32),
-                pltpu.SemaphoreType.DMA((WDEV + 1 + 2 * lines.far,)),
+                pltpu.SemaphoreType.DMA((2 + 2 * WDEV + 2 * lines.far,)),
             ],
         ),
         out_shape=[
             jax.ShapeDtypeStruct(share, kept_as),
             jax.ShapeDtypeStruct(share, BF16),
         ]
-        + [jax.ShapeDtypeStruct(shape, BF16) for shape in low_shapes],
+        + [jax.ShapeDtypeStruct(shape, BF16) for shape in low_shapes]
+        + [jax.ShapeDtypeStruct(window, BF16)] * (1 - call),
         compiler_params=pltpu.CompilerParams(vmem_limit_bytes=18 * MIB),
         cost_estimate=pl.CostEstimate(
             flops=2 * 5 * half * per_device * cand * BLOCK * deep * head_dim,
             bytes_accessed=12 << 20,
             transcendentals=half * per_device * cand * BLOCK * deep,
         ),
-    )(bases, slab_index, verticals, offsets, *prepared, own, *gathered, *recv)
-
-
-def turn_to_head(t, bases, half):
-    return bases[lax.div(t, half)] + lax.rem(t, half)
-
-
-def of_call(call, half, shape, block=0):
-    def index(t, *_):
-        turn = jnp.minimum(t, half - 1) if call == 0 else jnp.maximum(t - half, 0)
-        return (turn, 0, block, 0)
-
-    return pl.BlockSpec((1,) + tuple(shape), index)
-
-
-def window_kernel(bases, offs, qs, gs, *rest, lines, half, ns, per_device):
-    lows, home, parts, total = (rest[0:2], rest[2:4]), rest[4], rest[5 : 5 + WDEV], rest[5 + WDEV]
+    )(bases, slab_index, verticals, offsets, *prepared, *gathered, *recv)
+
+
+def window_kernel(bases, offs, *rest, lines, half, ns, per_device):
+    calls, home, parts, total = (rest[0:4], rest[4:8]), rest[8], rest[9 : 9 + WDEV], rest[9 + WDEV]
     t = pl.program_id(0)
     h = turn_to_head(t, bases, half)
     _, _, core = lines.place(lax.axis_index("ctx"))
-    head_dim = qs.shape[3]
+    head_dim = rest[0].shape[3]
     rows = per_device * BLOCK
     scaling = 1.0 / math.sqrt(head_dim)
     lanes = pl.ds(pl.multiple_of(h * head_dim, head_dim), head_dim)
     total[...] = jnp.zeros_like(total)
-    for call, (low_w, low_ds) in enumerate(lows):
+    for call, (qs, gs, low_w, low_ds) in enumerate(calls):
 
         @pl.when(lax.div(t, half) == call)
         def _():
@@ -485,34 +504,33 @@
             part[kv, :, lanes] = total[kv, pl.ds(at, rows), :].astype(part.dtype)
 
 
-def window_gradients(bases, offsets, qs, gs, lows, lines, nv):
-    heads, per_device, deep, head_dim = qs.shape
+def window_gradients(bases, offsets, prepared, lows, lines, nv):
+    half, per_device, deep, head_dim = prepared[0][0].shape
+    heads = 2 * half
     ns = offsets.shape[1]
-    half = heads // 2
     rows, features = per_device * BLOCK, heads * head_dim
     shard = (2, rows, features)
     whole = pl.BlockSpec(shard, lambda t, *_: (0, 0, 0))
-    stacked = pl.BlockSpec(
-        (1,) + qs.shape[1:], lambda t, bases, _: (turn_to_head(t, bases, half), 0, 0, 0)
-    )
+    stacked = (per_device, deep, head_dim)
     tail = (1 + ns) * BLOCK
     block = (per_device, tail, deep)
     specs = []
     for call in range(2):
+        specs += [of_call(call, half, stacked)] * 2
         specs += [of_call(call, half, block), of_call(call, half, block, nv * BLOCK // tail)]
     return pl.pallas_call(
         functools.partial(window_kernel, lines=lines, half=half, ns=ns, per_device=per_device),
         grid_spec=pltpu.PrefetchScalarGridSpec(
             num_scalar_prefetch=2,
             grid=(heads,),
-            in_specs=[stacked] * 2 + specs,
+            in_specs=specs,
             out_specs=[whole] * (1 + WDEV),
             scratch_shapes=[pltpu.VMEM((2, (WDEV + 1) * rows, head_dim), F32)],
         ),
         out_shape=[jax.ShapeDtypeStruct(shard, F32)] * 3 + [jax.ShapeDtypeStruct(shard, BF16)] * 3,
         compiler_params=pltpu.CompilerParams(vmem_limit_bytes=16 * MIB),
         cost_estimate=pl.CostEstimate(flops=0, bytes_accessed=9 << 20, transcendentals=0),
-    )(bases, offsets, qs, gs, *lows[0][:2], *lows[1][:2])
+    )(bases, offsets, *prepared[0][:2], *lows[0][:2], *prepared[1][:2], *lows[1][:2])
 
 
 def query_kernel(bases, *rest):
@@ -715,8 +733,11 @@
     recv4 = move(send4, lines.shift_pairs(4))
     to_near = core_sum(lines, to_near, to_both)
     quarter = near_sum(lines, mine, move(to_near, lines.near_pairs()), to_core)
-    prepared = prepare(after(queries, to_near), output_cotangent, forward_output, heads, head_dim)
-    quarter = after(quarter, recv4, *prepared)
+    bases = (jnp.stack([near, 1 - near]) * (heads // 2)).astype(jnp.int32)
+    prepared = prepare(
+        bases, after(queries, to_near), output_cotangent, forward_output, heads, head_dim
+    )
+    quarter = after(quarter, recv4, *prepared[0], *prepared[1])
     share = far_sum(lines, quarter)
     recv_mixed = move(after(mixed, quarter), lines.mixed_pairs())
     recv2 = move(jnp.where(near == 1, recv4, own), lines.near_pairs())
@@ -726,24 +747,22 @@
     other2 = move(recv2, lines.core_pairs())
     gathered = after(gathered, other2, recv_mixed, *blank)
     gathered = plane_gather(lines, gathered)
-    recv = [recv2, recv4, recv_mixed, other2, other4]
-
-    bases = (jnp.stack([near, 1 - near]) * (heads // 2)).astype(jnp.int32)
-
-    def attend_line(call, gathered, kept_as):
+    recv = [own, recv2, recv4, recv_mixed, other2, other4]
+
+    def attend_line(call, gathered, recv, kept_as):
         return attend(
-            call, bases, slab_index, verticals, offsets, prepared, own, gathered, recv, lines,
+            call, bases, slab_index, verticals, offsets, prepared[call], gathered, recv, lines,
             kept_as,
         )
 
-    to_near, to_both, *first_lows = attend_line(0, gathered[0::2], BF16)
+    to_near, to_both, *first_lows, window = attend_line(0, gathered[0::2], recv, BF16)
     to_near = core_sum(lines, to_near, to_both)
     from_near = move(to_near, lines.near_pairs())
-    mine, to_core, *second_lows = attend_line(1, gathered[1::2], F32)
+    mine, to_core, *second_lows = attend_line(1, gathered[1::2], [window], F32)
     lows = (first_lows, second_lows)
 
     home, part2, part4, mixed, give2, give4 = window_gradients(
-        bases, after(offsets, from_near), prepared[0], prepared[1], lows, lines, nv
+        bases, after(offsets, from_near), prepared, lows, lines, nv
     )
     quarter = after(near_sum(lines, mine, from_near, to_core), home)
     share = far_sum(lines, quarter)

time: 114 us -> 105 us (0.921)
  local copies, waits for them, and re-layouts: 12.1 us -> 0.07 us
  waiting for transfers between devices: 29.1 us -> 33.8 us
  starting transfers between devices: 33.2 us -> 31.9 us
    unnamed x54 -> x16, local copies, waits for them, and re-layouts: 12.1 us -> 0.04 us
    ppermute x34, waiting for transfers between devices: 29.1 us -> 33.8 us  [move(): return lax.ppermute(array, 'ctx', pairs)]
    ppermute x34, starting transfers between devices: 33.2 us -> 31.9 us  [move(): return lax.ppermute(array, 'ctx', pairs)]
  transfers between devices with their start and end apart: 34 -> 34, of which waited for: 11 -> 12; matrix products, arithmetic and copies ran while one was open for 5% -> 4% of each run, Pallas kernels for 21% -> 23%
where the time goes in v14:
time: 105 us
  waiting for transfers between devices  33.8 us (32%)
  Pallas kernels  33.1 us (32%)
  starting transfers between devices  31.9 us (30%)
  other arithmetic  4.57 us (4%)
  between operations  1.78 us (2%)
    ppermute x34, waiting for transfers between devices, move(): return lax.ppermute(array, 'ctx', pairs)  33.8 us
    ppermute x34, starting transfers between devices, move(): return lax.ppermute(array, 'ctx', pairs)  31.9 us
    pallas_call x2, Pallas kernels, attend(): pl.pallas_call(functools.partial(attend_kernel, lines=lines, nv=nv, ns=ns...  13.4 us
    pallas_call x1, Pallas kernels, assemble(): pl.pallas_call(functools.partial(assemble_kernel, lines=lines, heads=head...  4.4 us
    pallas_call x1, Pallas kernels, pack(): pl.pallas_call(functools.partial(pack_kernel, lines=lines, heads=heads, n...  4.3 us
    pallas_call x1, Pallas kernels, query_gradients(): pl.pallas_call(query_kernel, grid_spec=pltpu.PrefetchScalarGridSpec(num_s...  3.56 us
    pallas_call x1, Pallas kernels, window_gradients(): pl.pallas_call(functools.partial(window_kernel, lines=lines, half=half, n...  3.09 us
    pallas_call x1, Pallas kernels, zeros(): pl.pallas_call(zeros_kernel, in_specs=[pl.BlockSpec(memory_space=pl.ANY)]...  2.27 us
  transfers between devices with their start and end apart: 34, of which 12 were waited for; matrix products, arithmetic and copies ran while one was open for 4% of the time, Pallas kernels for 23%

profile of v14, /device:TPU:0, one launch (start us, length us, event | category | flops | bytes accessed | tf_op | source)
XLA Modules:
  0.0 105.2 jit_solution(1754117717070942392)
XLA Ops:
  1.3 4.3 %shard_map.103 = (bf16[2,128,512]{2,1,0:T(8,128)(2,1)}, bf16[2,128,512]{2,1,0:T(8,128)(2,1)}, bf16[2,128,512]{2,1,0:T(8,128)(2,1)}, bf16[4,256,128]{2,1,0:T(8,12...) custom-call(s32[1]{0:T(128)S(6)} %copy.15.slab_index, ...), custom_call_target="tpu_custom_call" | custom-call | tf_op jit(solution)/shard_map/pallas_call | solution.py:168
  6.3 3.0 %collective-permute-start.3 = (bf16[2,128,512]{2,1,0:T(8,128)(2,1)}, bf16[2,128,512]{2,1,0:T(8,128)(2,1)S(1)}, u32[]{:S(2)}, u32[]{:S(2)}) collective-permute-start(bf16[2,128,512]{2,1,0:T(8,128)(2,1)} %get-tuple-element.62), channel_id=1, source_target_pairs={{0,4},{1,5},{2,6},{3,7},{4,8},{5,9},{6,10},{7,11},{8,12},{9,13},{1... | collective-permute-start | bytes 786440 | tf_op jit(solution)/shard_map/ppermute | solution.py:52
  9.2 1.8 %add_convert_fusion.3 = bf16[4,256,128]{2,1,0:T(8,128)(2,1)} fusion(bf16[4,256,128]{2,1,0:T(8,128)(2,1)} %collective-permute-done, bf16[4,256,128]{2,1,0:T(8,128)(2,1)} %get-tuple-element.52), kind=kLoop, calls=%fused_computation.5 | loop fusion | flops 524288 | bytes 786432 | tf_op jit(solution)/shard_map/convert_element_type | solution.py:60
  12.6 5.4 %collective-permute-done.3.rest_4_ = bf16[2,128,512]{2,1,0:T(8,128)(2,1)S(1)} collective-permute-done((bf16[2,128,512]{2,1,0:T(8,128)(2,1)}, bf16[2,128,512]{2,1,0:T(8,128)(2,1)S(1)}, u32[]{:S(2)}, u32[]{:S(2)}) %collective-permute-start.3) | collective-permute-done | bytes 262176 | tf_op jit(solution)/shard_map/ppermute | solution.py:52
  19.6 2.1 %shard_map.104 = (bf16[2,2,512,128]{3,2,1,0:T(8,128)(2,1)S(1)}, bf16[2,2,512,128]{3,2,1,0:T(8,128)(2,1)S(1)}, bf16[2,2,128,512]{3,2,1,0:T(8,128)(2,1)S(1)}, bf16...) custom-call(s32[2]{0:T(128)S(1)} %add_multiply_fusion.bases, ...), custom_call_target="tpu_custom_call" | custom-call | bytes 7340032 | tf_op jit(solution)/shard_map/pallas_call | solution.py:262
  23.1 3.8 %collective-permute-start.6 = (bf16[256,128]{1,0:T(8,128)(2,1)S(1)}, bf16[256,128]{1,0:T(8,128)(2,1)S(1)}, u32[]{:S(2)}, u32[]{:S(2)}) collective-permute-start(bf16[256,128]{1,0:T(8,128)(2,1)S(1)} %get-tuple-element.105), channel_id=1, source_target_pairs={{0,12},{1,13},{2,14},{3,15},{4,0},{5,1},{6,2},{7,3},{8,4},{9,5},{1... | collective-permute-start | bytes 196616 | tf_op jit(solution)/shard_map/ppermute | solution.py:52
  27.4 2.0 %collective-permute-done.4 = bf16[256,128]{1,0:T(8,128)(2,1)S(1)} collective-permute-done((bf16[256,128]{1,0:T(8,128)(2,1)S(1)}, bf16[256,128]{1,0:T(8,128)(2,1)S(1)}, u32[]{:S(2)}, u32[]{:S(2)}) %collective-permute-start.4) | collective-permute-done | bytes 65568 | tf_op jit(solution)/shard_map/ppermute | solution.py:52
  29.4 2.6 %collective-permute-done.5 = bf16[256,128]{1,0:T(8,128)(2,1)S(1)} collective-permute-done((bf16[256,128]{1,0:T(8,128)(2,1)S(1)}, bf16[256,128]{1,0:T(8,128)(2,1)S(1)}, u32[]{:S(2)}, u32[]{:S(2)}) %collective-permute-start.5) | collective-permute-done | bytes 65568 | tf_op jit(solution)/shard_map/ppermute | solution.py:52
  33.1 1.9 %collective-permute-start.8 = (bf16[256,128]{1,0:T(8,128)(2,1)S(1)}, bf16[256,128]{1,0:T(8,128)(2,1)S(1)}, u32[]{:S(2)}, u32[]{:S(2)}) collective-permute-start(bf16[256,128]{1,0:T(8,128)(2,1)S(1)} %fusion.5._), channel_id=1, source_target_pairs={{0,4},{1,5},{2,6},{3,7},{4,8},{5,9},{6,10},{7,11},{8,12},{9,13},{1... | collective-permute-start | bytes 196616 | tf_op jit(solution)/shard_map/ppermute | solution.py:52
  35.0 2.3 %shard_map.105 = (bf16[16,128,512]{2,1,0:T(8,128)(2,1)}, bf16[16,128,512]{2,1,0:T(8,128)(2,1)}) custom-call(bf16[256,128]{1,0:T(8,128)(2,1)S(1)} %fusion.5._), custom_call_target="tpu_custom_call" | custom-call | bytes 5242880 | tf_op jit(solution)/shard_map/pallas_call | solution.py:598
  37.3 3.8 %collective-permute-done.9 = bf16[256,128]{1,0:T(8,128)(2,1)S(1)} collective-permute-done((bf16[256,128]{1,0:T(8,128)(2,1)S(1)}, bf16[256,128]{1,0:T(8,128)(2,1)S(1)}, u32[]{:S(2)}, u32[]{:S(2)}) %collective-permute-start.9) | collective-permute-done | bytes 65568 | tf_op jit(solution)/shard_map/ppermute | solution.py:52
  41.2 3.8 %collective-permute-start.14 = (bf16[4,256,128]{2,1,0:T(8,128)(2,1)S(1)}, bf16[4,256,128]{2,1,0:T(8,128)(2,1)S(1)}, u32[]{:S(2)}, u32[]{:S(2)}) collective-permute-start(bf16[4,256,128]{2,1,0:T(8,128)(2,1)S(1)} %pad_maximum_fusion.rest_0_), channel_id=1, source_target_pairs={{0,2},{1,3},{2,0},{3,1},{4,6},{5,7},{6,4},{7,5},{8,10},{9,11},{10,... | collective-permute-start | bytes 786440 | tf_op jit(solution)/shard_map/ppermute | solution.py:52
  45.1 6.7 %shard_map.106 = (bf16[4,256,128]{2,1,0:T(8,128)(2,1)S(1)}, bf16[4,256,128]{2,1,0:T(8,128)(2,1)S(1)}, bf16[2,2,256,512]{3,2,1,0:T(8,128)(2,1)S(1)}, bf16[2,2,768...) custom-call(s32[2]{0:T(128)S(1)} %add_multiply_fusion.bases, ...), custom_call_target="tpu_custom_call" | custom-call | flops 2013265920 | bytes 12582912 | tf_op jit(solution)/shard_map/pallas_call | solution.py:439
  55.0 6.6 %shard_map.107 = (f32[4,256,128]{2,1,0:T(8,128)S(1)}, bf16[4,256,128]{2,1,0:T(8,128)(2,1)S(1)}, bf16[2,2,256,512]{3,2,1,0:T(8,128)(2,1)S(1)}, bf16[2,2,768,512]{...) custom-call(s32[2]{0:T(128)S(1)} %add_multiply_fusion.bases, s32[1]{0:T(128)S(6)} %copy.15.slab_index, ...), custom_call_target="tpu_custom_call" | custom-call | flops 2013265920 | bytes 12582912 | tf_op jit(solution)/shard_map/pallas_call | solution.py:439
  62.0 3.1 %shard_map.108 = (f32[2,128,512]{2,1,0:T(8,128)S(1)}, f32[2,128,512]{2,1,0:T(8,128)S(1)}, f32[2,128,512]{2,1,0:T(8,128)S(1)}, bf16[2,128,512]{2,1,0:T(8,128)(2,1...) custom-call(s32[2]{0:T(128)S(1)} %add_multiply_fusion.bases, s32[4,3]{1,0:T(4,128)S(1)} %copy-done.5, ...), custom_call_target="tpu_custom_call" | custom-call | bytes 9437184 | tf_op jit(solution)/shard_map/pallas_call | solution.py:521
  65.6 3.8 %collective-permute-start.22 = (bf16[256,128]{1,0:T(8,128)(2,1)S(1)}, bf16[256,128]{1,0:T(8,128)(2,1)S(1)}, u32[]{:S(2)}, u32[]{:S(2)}) collective-permute-start(bf16[256,128]{1,0:T(8,128)(2,1)S(1)} %get-tuple-element.102), channel_id=1, source_target_pairs={{0,12},{1,13},{2,14},{3,15},{4,0},{5,1},{6,2},{7,3},{8,4},{9,5},{1... | collective-permute-start | bytes 196616 | tf_op jit(solution)/shard_map/ppermute | solution.py:52
  69.4 2.8 %collective-permute-start.28 = (bf16[2,128,512]{2,1,0:T(8,128)(2,1)S(1)}, bf16[2,128,512]{2,1,0:T(8,128)(2,1)S(1)}, u32[]{:S(2)}, u32[]{:S(2)}) collective-permute-start(bf16[2,128,512]{2,1,0:T(8,128)(2,1)S(1)} %get-tuple-element.90), channel_id=1, source_target_pairs={{1,0},{6,1},{3,2},{8,3},{5,4},{10,5},{7,6},{12,7},{9,8},{14,9},{11... | collective-permute-start | bytes 786440 | tf_op jit(solution)/shard_map/ppermute | solution.py:52
  73.5 5.2 %collective-permute-done.21 = bf16[256,128]{1,0:T(8,128)(2,1)S(1)} collective-permute-done((bf16[256,128]{1,0:T(8,128)(2,1)S(1)}, bf16[256,128]{1,0:T(8,128)(2,1)S(1)}, u32[]{:S(2)}, u32[]{:S(2)}) %collective-permute-start.21) | collective-permute-done | bytes 65568 | tf_op jit(solution)/shard_map/ppermute | solution.py:52
  78.9 4.9 %collective-permute-done.25 = bf16[256,128]{1,0:T(8,128)(2,1)S(1)} collective-permute-done((bf16[256,128]{1,0:T(8,128)(2,1)S(1)}, bf16[256,128]{1,0:T(8,128)(2,1)S(1)}, u32[]{:S(2)}, u32[]{:S(2)}) %collective-permute-start.25) | collective-permute-done | bytes 65568 | tf_op jit(solution)/shard_map/ppermute | solution.py:52
  84.5 5.3 %collective-permute-done.23 = bf16[256,128]{1,0:T(8,128)(2,1)S(1)} collective-permute-done((bf16[256,128]{1,0:T(8,128)(2,1)S(1)}, bf16[256,128]{1,0:T(8,128)(2,1)S(1)}, u32[]{:S(2)}, u32[]{:S(2)}) %collective-permute-start.23) | collective-permute-done | bytes 65568 | tf_op jit(solution)/shard_map/ppermute | solution.py:52
  91.7 2.3 %collective-permute-start.30 = (bf16[2,128,512]{2,1,0:T(8,128)(2,1)S(1)}, bf16[2,128,512]{2,1,0:T(8,128)(2,1)S(1)}, u32[]{:S(2)}, u32[]{:S(2)}) collective-permute-start(bf16[2,128,512]{2,1,0:T(8,128)(2,1)S(1)} %add_convert_fusion), channel_id=1, source_target_pairs={{4,0},{5,1},{6,2},{7,3},{8,4},{9,5},{10,6},{11,7},{12,8},{13,9},{1... | collective-permute-start | bytes 786440 | tf_op jit(solution)/shard_map/ppermute | solution.py:52
  93.9 3.0 %collective-permute-done.31.rest_4_ = bf16[4,256,128]{2,1,0:T(8,128)(2,1)S(1)} collective-permute-done((bf16[4,256,128]{2,1,0:T(8,128)(2,1)S(1)}, bf16[4,256,128]{2,1,0:T(8,128)(2,1)S(1)}, u32[]{:S(2)}, u32[]{:S(2)}) %collective-permute-start.31) | collective-permute-done | bytes 262176 | tf_op jit(solution)/shard_map/ppermute | solution.py:52
  97.0 3.6 %shard_map.109 = bf16[128,4096]{1,0:T(8,128)(2,1)} custom-call(s32[2]{0:T(128)S(1)} %add_multiply_fusion.bases, bf16[2,2,768,128]{3,2,1,0:T(8,128)(2,1)S(1)} %get-tuple-element.93.rest_0_, bf16[2,2,768,512]{3,2,1,0:T(8,128)(2,1)S(1)} %get-tuple-element.83.rest_3_.rest_1_, bf16[2,2,768,128]{3,2,1,0:T(8,128)(2,1)S(1)} %get-tuple-element.94.rest_2_, ...), custom_call_target="tpu_custom_call" | custom-call | bytes 10485760 | tf_op jit(solution)/shard_map/pallas_call | solution.py:567
  100.6 4.4 %shard_map.110 = (bf16[16,128,512]{2,1,0:T(8,128)(2,1)}, bf16[16,128,512]{2,1,0:T(8,128)(2,1)}) custom-call(s32[1]{0:T(128)S(6)} %copy.15.slab_index, s32[4,8]{1,0:T(4,128)S(1)} %copy-done.4, f32[2,128,512]{2,1,0:T(8,128)S(1)} %get-tuple-element.95.home, ...), custom_call_target="tpu_custom_call", output_to_operand_aliasing={{0}: (10, {}), {1}: (11, {})} | custom-call | tf_op jit(solution)/shard_map/pallas_call | solution.py:695
  (84 shorter events, 14.9 us)
Async XLA Ops:
  6.2 15.6 %collective-permute-start.1 = (bf16[4,256,128]{2,1,0:T(8,128)(2,1)}, bf16[4,256,128]{2,1,0:T(8,128)(2,1)}, u32[]{:S(2)}, u32[]{:S(2)}) collective-permute-start(bf16[4,256,128]{2,1,0:T(8,128)(2,1)} %get-tuple-element.61), channel_id=1, source_target_pairs={{0,1},{1,0},{2,3},{3,2},{4,5},{5,4},{6,7},{7,6},{8,9},{9,8},{10,11... | collective-permute-start | bytes 786440 | tf_op jit(solution)/shard_map/ppermute | solution.py:52
  6.3 11.7 %collective-permute-start.3 = (bf16[2,128,512]{2,1,0:T(8,128)(2,1)}, bf16[2,128,512]{2,1,0:T(8,128)(2,1)S(1)}, u32[]{:S(2)}, u32[]{:S(2)}) collective-permute-start(bf16[2,128,512]{2,1,0:T(8,128)(2,1)} %get-tuple-element.62), channel_id=1, source_target_pairs={{0,4},{1,5},{2,6},{3,7},{4,8},{5,9},{6,10},{7,11},{8,12},{9,13},{1... | collective-permute-start | bytes 786440 | tf_op jit(solution)/shard_map/ppermute | solution.py:52
  11.0 10.7 %collective-permute-start.2 = (bf16[4,256,128]{2,1,0:T(8,128)(2,1)}, bf16[4,256,128]{2,1,0:T(8,128)(2,1)}, u32[]{:S(2)}, u32[]{:S(2)}) collective-permute-start(bf16[4,256,128]{2,1,0:T(8,128)(2,1)} %add_convert_fusion.3), channel_id=1, source_target_pairs={{0,2},{1,3},{2,0},{3,1},{4,6},{5,7},{6,4},{7,5},{8,10},{9,11},{10,... | collective-permute-start | bytes 786440 | tf_op jit(solution)/shard_map/ppermute | solution.py:52
  19.0 7.9 %collective-permute-start.11 = (bf16[2,128,512]{2,1,0:T(8,128)(2,1)S(1)}, bf16[2,128,512]{2,1,0:T(8,128)(2,1)S(1)}, u32[]{:S(2)}, u32[]{:S(2)}) collective-permute-start(bf16[2,128,512]{2,1,0:T(8,128)(2,1)S(1)} %broadcast_select_fusion), channel_id=1, source_target_pairs={{0,2},{1,3},{2,0},{3,1},{4,6},{5,7},{6,4},{7,5},{8,10},{9,11},{10,... | collective-permute-start | bytes 786440 | tf_op jit(solution)/shard_map/ppermute | solution.py:52
  23.0 6.4 %collective-permute-start.4 = (bf16[256,128]{1,0:T(8,128)(2,1)S(1)}, bf16[256,128]{1,0:T(8,128)(2,1)S(1)}, u32[]{:S(2)}, u32[]{:S(2)}) collective-permute-start(bf16[256,128]{1,0:T(8,128)(2,1)S(1)} %get-tuple-element.104), channel_id=1, source_target_pairs={{0,4},{1,5},{2,6},{3,7},{4,8},{5,9},{6,10},{7,11},{8,12},{9,13},{1... | collective-permute-start | bytes 196616 | tf_op jit(solution)/shard_map/ppermute | solution.py:52
  23.1 6.3 %collective-permute-start.6 = (bf16[256,128]{1,0:T(8,128)(2,1)S(1)}, bf16[256,128]{1,0:T(8,128)(2,1)S(1)}, u32[]{:S(2)}, u32[]{:S(2)}) collective-permute-start(bf16[256,128]{1,0:T(8,128)(2,1)S(1)} %get-tuple-element.105), channel_id=1, source_target_pairs={{0,12},{1,13},{2,14},{3,15},{4,0},{5,1},{6,2},{7,3},{8,4},{9,5},{1... | collective-permute-start | bytes 196616 | tf_op jit(solution)/shard_map/ppermute | solution.py:52
  26.9 14.2 %collective-permute-start.13 = (bf16[2,128,512]{2,1,0:T(8,128)(2,1)S(1)}, bf16[2,128,512]{2,1,0:T(8,128)(2,1)S(1)}, u32[]{:S(2)}, u32[]{:S(2)}) collective-permute-start(bf16[2,128,512]{2,1,0:T(8,128)(2,1)S(1)} %copy-done.7), channel_id=1, source_target_pairs={{0,1},{1,6},{2,3},{3,8},{4,5},{5,10},{6,7},{7,12},{8,9},{9,14},{10... | collective-permute-start | bytes 786440 | tf_op jit(solution)/shard_map/ppermute | solution.py:52
  29.4 11.7 %collective-permute-start.12 = (bf16[2,128,512]{2,1,0:T(8,128)(2,1)S(1)}, bf16[2,128,512]{2,1,0:T(8,128)(2,1)S(1)}, u32[]{:S(2)}, u32[]{:S(2)}) collective-permute-start(bf16[2,128,512]{2,1,0:T(8,128)(2,1)S(1)} %collective-permute-done.11.rest_3_), channel_id=1, source_target_pairs={{0,1},{1,0},{2,3},{3,2},{4,5},{5,4},{6,7},{7,6},{8,9},{9,8},{10,11... | collective-permute-start | bytes 786440 | tf_op jit(solution)/shard_map/ppermute | solution.py:52
  33.1 8.0 %collective-permute-start.9 = (bf16[256,128]{1,0:T(8,128)(2,1)S(1)}, bf16[256,128]{1,0:T(8,128)(2,1)S(1)}, u32[]{:S(2)}, u32[]{:S(2)}) collective-permute-start(bf16[256,128]{1,0:T(8,128)(2,1)S(1)} %fusion.5._), channel_id=1, source_target_pairs={{0,8},{1,9},{2,10},{3,11},{4,12},{5,13},{6,14},{7,15},{8,0},{9,1},... | collective-permute-start | bytes 196616 | tf_op jit(solution)/shard_map/ppermute | solution.py:52
  33.1 8.0 %collective-permute-start.8 = (bf16[256,128]{1,0:T(8,128)(2,1)S(1)}, bf16[256,128]{1,0:T(8,128)(2,1)S(1)}, u32[]{:S(2)}, u32[]{:S(2)}) collective-permute-start(bf16[256,128]{1,0:T(8,128)(2,1)S(1)} %fusion.5._), channel_id=1, source_target_pairs={{0,4},{1,5},{2,6},{3,7},{4,8},{5,9},{6,10},{7,11},{8,12},{9,13},{1... | collective-permute-start | bytes 196616 | tf_op jit(solution)/shard_map/ppermute | solution.py:52
  41.2 10.8 %collective-permute-start.14 = (bf16[4,256,128]{2,1,0:T(8,128)(2,1)S(1)}, bf16[4,256,128]{2,1,0:T(8,128)(2,1)S(1)}, u32[]{:S(2)}, u32[]{:S(2)}) collective-permute-start(bf16[4,256,128]{2,1,0:T(8,128)(2,1)S(1)} %pad_maximum_fusion.rest_0_), channel_id=1, source_target_pairs={{0,2},{1,3},{2,0},{3,1},{4,6},{5,7},{6,4},{7,5},{8,10},{9,11},{10,... | collective-permute-start | bytes 786440 | tf_op jit(solution)/shard_map/ppermute | solution.py:52
  53.5 8.4 %collective-permute-start.19 = (bf16[4,256,128]{2,1,0:T(8,128)(2,1)S(1)}, bf16[4,256,128]{2,1,0:T(8,128)(2,1)S(1)}, u32[]{:S(2)}, u32[]{:S(2)}) collective-permute-start(bf16[4,256,128]{2,1,0:T(8,128)(2,1)S(1)} %add_convert_fusion.2), channel_id=1, source_target_pairs={{0,2},{1,3},{2,0},{3,1},{4,6},{5,7},{6,4},{7,5},{8,10},{9,11},{10,... | collective-permute-start | bytes 786440 | tf_op jit(solution)/shard_map/ppermute | solution.py:52
  65.1 7.2 %collective-permute-start.26 = (bf16[2,128,512]{2,1,0:T(8,128)(2,1)S(1)}, bf16[2,128,512]{2,1,0:T(8,128)(2,1)S(1)}, u32[]{:S(2)}, u32[]{:S(2)}) collective-permute-start(bf16[2,128,512]{2,1,0:T(8,128)(2,1)S(1)} %get-tuple-element.89), channel_id=1, source_target_pairs={{0,1},{1,0},{2,3},{3,2},{4,5},{5,4},{6,7},{7,6},{8,9},{9,8},{10,11... | collective-permute-start | bytes 786440 | tf_op jit(solution)/shard_map/ppermute | solution.py:52
  65.5 6.8 %collective-permute-start.20 = (bf16[256,128]{1,0:T(8,128)(2,1)S(1)}, bf16[256,128]{1,0:T(8,128)(2,1)S(1)}, u32[]{:S(2)}, u32[]{:S(2)}) collective-permute-start(bf16[256,128]{1,0:T(8,128)(2,1)S(1)} %get-tuple-element.101), channel_id=1, source_target_pairs={{0,4},{1,5},{2,6},{3,7},{4,8},{5,9},{6,10},{7,11},{8,12},{9,13},{1... | collective-permute-start | bytes 196616 | tf_op jit(solution)/shard_map/ppermute | solution.py:52
  65.6 7.9 %collective-permute-start.22 = (bf16[256,128]{1,0:T(8,128)(2,1)S(1)}, bf16[256,128]{1,0:T(8,128)(2,1)S(1)}, u32[]{:S(2)}, u32[]{:S(2)}) collective-permute-start(bf16[256,128]{1,0:T(8,128)(2,1)S(1)} %get-tuple-element.102), channel_id=1, source_target_pairs={{0,12},{1,13},{2,14},{3,15},{4,0},{5,1},{6,2},{7,3},{8,4},{9,5},{1... | collective-permute-start | bytes 196616 | tf_op jit(solution)/shard_map/ppermute | solution.py:52
  69.4 9.3 %collective-permute-start.21 = (bf16[256,128]{1,0:T(8,128)(2,1)S(1)}, bf16[256,128]{1,0:T(8,128)(2,1)S(1)}, u32[]{:S(2)}, u32[]{:S(2)}) collective-permute-start(bf16[256,128]{1,0:T(8,128)(2,1)S(1)} %get-tuple-element.103), channel_id=1, source_target_pairs={{0,8},{1,9},{2,10},{3,11},{4,12},{5,13},{6,14},{7,15},{8,0},{9,1},... | collective-permute-start | bytes 196616 | tf_op jit(solution)/shard_map/ppermute | solution.py:52
  69.4 20.4 %collective-permute-start.28 = (bf16[2,128,512]{2,1,0:T(8,128)(2,1)S(1)}, bf16[2,128,512]{2,1,0:T(8,128)(2,1)S(1)}, u32[]{:S(2)}, u32[]{:S(2)}) collective-permute-start(bf16[2,128,512]{2,1,0:T(8,128)(2,1)S(1)} %get-tuple-element.90), channel_id=1, source_target_pairs={{1,0},{6,1},{3,2},{8,3},{5,4},{10,5},{7,6},{12,7},{9,8},{14,9},{11... | collective-permute-start | bytes 786440 | tf_op jit(solution)/shard_map/ppermute | solution.py:52
  72.2 19.3 %collective-permute-start.29 = (bf16[2,128,512]{2,1,0:T(8,128)(2,1)S(1)}, bf16[2,128,512]{2,1,0:T(8,128)(2,1)S(1)}, u32[]{:S(2)}, u32[]{:S(2)}) collective-permute-start(bf16[2,128,512]{2,1,0:T(8,128)(2,1)S(1)} %get-tuple-element.97), channel_id=1, source_target_pairs={{0,1},{1,0},{2,3},{3,2},{4,5},{5,4},{6,7},{7,6},{8,9},{9,8},{10,11... | collective-permute-start | bytes 786440 | tf_op jit(solution)/shard_map/ppermute | solution.py:52
  72.3 17.6 %collective-permute-start.27 = (bf16[2,128,512]{2,1,0:T(8,128)(2,1)S(1)}, bf16[2,128,512]{2,1,0:T(8,128)(2,1)S(1)}, u32[]{:S(2)}, u32[]{:S(2)}) collective-permute-start(bf16[2,128,512]{2,1,0:T(8,128)(2,1)S(1)} %add_convert_fusion.1), channel_id=1, source_target_pairs={{0,2},{1,3},{2,0},{3,1},{4,6},{5,7},{6,4},{7,5},{8,10},{9,11},{10,... | collective-permute-start | bytes 786440 | tf_op jit(solution)/shard_map/ppermute | solution.py:52
  78.8 5.7 %collective-permute-start.24 = (bf16[256,128]{1,0:T(8,128)(2,1)S(1)}, bf16[256,128]{1,0:T(8,128)(2,1)S(1)}, u32[]{:S(2)}, u32[]{:S(2)}) collective-permute-start(bf16[256,128]{1,0:T(8,128)(2,1)S(1)} %fusion.2), channel_id=1, source_target_pairs={{0,8},{1,9},{2,10},{3,11},{4,12},{5,13},{6,14},{7,15},{8,0},{9,1},... | collective-permute-start | bytes 196616 | tf_op jit(solution)/shard_map/ppermute | solution.py:52
  83.8 6.1 %collective-permute-start.23 = (bf16[256,128]{1,0:T(8,128)(2,1)S(1)}, bf16[256,128]{1,0:T(8,128)(2,1)S(1)}, u32[]{:S(2)}, u32[]{:S(2)}) collective-permute-start(bf16[256,128]{1,0:T(8,128)(2,1)S(1)} %fusion.2), channel_id=1, source_target_pairs={{0,4},{1,5},{2,6},{3,7},{4,8},{5,9},{6,10},{7,11},{8,12},{9,13},{1... | collective-permute-start | bytes 196616 | tf_op jit(solution)/shard_map/ppermute | solution.py:52
  89.9 7.1 %collective-permute-start.31 = (bf16[4,256,128]{2,1,0:T(8,128)(2,1)S(1)}, bf16[4,256,128]{2,1,0:T(8,128)(2,1)S(1)}, u32[]{:S(2)}, u32[]{:S(2)}) collective-permute-start(bf16[4,256,128]{2,1,0:T(8,128)(2,1)S(1)} %pad_maximum_fusion.1.rest_3_), channel_id=1, source_target_pairs={{0,2},{1,3},{2,0},{3,1},{4,6},{5,7},{6,4},{7,5},{8,10},{9,11},{10,... | collective-permute-start | bytes 786440 | tf_op jit(solution)/shard_map/ppermute | solution.py:52
  91.5 9.0 %collective-permute-start.32 = (bf16[4,256,128]{2,1,0:T(8,128)(2,1)S(1)}, bf16[4,256,128]{2,1,0:T(8,128)(2,1)S(1)}, u32[]{:S(2)}, u32[]{:S(2)}) collective-permute-start(bf16[4,256,128]{2,1,0:T(8,128)(2,1)S(1)} %pad_maximum_fusion.1.rest_3_), channel_id=1, source_target_pairs={{0,1},{1,0},{2,3},{3,2},{4,5},{5,4},{6,7},{7,6},{8,9},{9,8},{10,11... | collective-permute-start | bytes 786440 | tf_op jit(solution)/shard_map/ppermute | solution.py:52
  91.7 9.0 %collective-permute-start.30 = (bf16[2,128,512]{2,1,0:T(8,128)(2,1)S(1)}, bf16[2,128,512]{2,1,0:T(8,128)(2,1)S(1)}, u32[]{:S(2)}, u32[]{:S(2)}) collective-permute-start(bf16[2,128,512]{2,1,0:T(8,128)(2,1)S(1)} %add_convert_fusion), channel_id=1, source_target_pairs={{4,0},{5,1},{6,2},{7,3},{8,4},{9,5},{10,6},{11,7},{12,8},{13,9},{1... | collective-permute-start | bytes 786440 | tf_op jit(solution)/shard_map/ppermute | solution.py:52
  (18 other events, 182.2 us)

commit v15 on v14

--- a/solution.py
+++ b/solution.py
@@ -730,14 +730,15 @@
     own, send4, mixed, mine, to_near, to_core, to_both = pack(
         slab_index, verticals, context_keys, context_values, lines
     )
-    recv4 = move(send4, lines.shift_pairs(4))
     to_near = core_sum(lines, to_near, to_both)
+    recv4 = move(after(send4, to_near), lines.shift_pairs(4))
     quarter = near_sum(lines, mine, move(to_near, lines.near_pairs()), to_core)
     bases = (jnp.stack([near, 1 - near]) * (heads // 2)).astype(jnp.int32)
     prepared = prepare(
         bases, after(queries, to_near), output_cotangent, forward_output, heads, head_dim
     )
-    quarter = after(quarter, recv4, *prepared[0], *prepared[1])
+    recv4 = after(recv4, *prepared[0], *prepared[1])
+    quarter = after(quarter, recv4)
     share = far_sum(lines, quarter)
     recv_mixed = move(after(mixed, quarter), lines.mixed_pairs())
     recv2 = move(jnp.where(near == 1, recv4, own), lines.near_pairs())
@@ -768,15 +769,17 @@
     share = far_sum(lines, quarter)
     arrived_mixed = move(mixed, back(lines.mixed_pairs()))
     sum2 = (part2 + move(give2, lines.core_pairs()).astype(F32)).astype(BF16)
-    sum4 = part4 + move(give4, lines.core_pairs()).astype(F32)
+    given4 = move(give4, lines.core_pairs())
+    share = after(share, given4)
+    sum4 = part4 + given4.astype(F32)
     from_near = move(sum2, lines.near_pairs())
-    totals = after(far_gather(lines, share), from_near, arrived_mixed)
+    query_grad = query_gradients(after(bases, share), lows)
+    totals = after(far_gather(lines, share), from_near, arrived_mixed, query_grad)
     sum4 = (sum4 + jnp.where(near == 1, from_near.astype(F32), 0.0)).astype(BF16)
     arrived4 = move(after(sum4, totals), back(lines.shift_pairs(4)))
-    query_grad = query_gradients(after(bases, totals), lows)
     totals = plane_gather(lines, totals)
     key_gradient, value_gradient = assemble(
-        slab_index, verticals, after(home, query_grad), from_near, (arrived4, arrived_mixed),
+        slab_index, verticals, home, from_near, (arrived4, arrived_mixed),
         totals, blank, lines,
     )
     return query_grad, key_gradient, value_gradient

time: 105 us -> 105 us (level)
  starting transfers between devices: 31.9 us -> 33.6 us
    ppermute x34, starting transfers between devices: 31.9 us -> 33.6 us  [move(): return lax.ppermute(array, 'ctx', pairs)]
  transfers between devices with their start and end apart: 34 -> 34, of which waited for: 12 -> 15; matrix products, arithmetic and copies ran while one was open for 4% -> 1% of each run, Pallas kernels for 23% -> 23%
where the time goes in v15:
time: 105 us
  starting transfers between devices  33.6 us (32%)
  Pallas kernels  33.1 us (32%)
  waiting for transfers between devices  32.9 us (31%)
  other arithmetic  3.59 us (3%)
  between operations  1.74 us (2%)
    ppermute x34, starting transfers between devices, move(): return lax.ppermute(array, 'ctx', pairs)  33.6 us
    ppermute x34, waiting for transfers between devices, move(): return lax.ppermute(array, 'ctx', pairs)  32.9 us
    pallas_call x2, Pallas kernels, attend(): pl.pallas_call(functools.partial(attend_kernel, lines=lines, nv=nv, ns=ns...  13.4 us
    pallas_call x1, Pallas kernels, assemble(): pl.pallas_call(functools.partial(assemble_kernel, lines=lines, heads=head...  4.45 us
    pallas_call x1, Pallas kernels, pack(): pl.pallas_call(functools.partial(pack_kernel, lines=lines, heads=heads, n...  4.32 us
    pallas_call x1, Pallas kernels, query_gradients(): pl.pallas_call(query_kernel, grid_spec=pltpu.PrefetchScalarGridSpec(num_s...  3.56 us
    pallas_call x1, Pallas kernels, window_gradients(): pl.pallas_call(functools.partial(window_kernel, lines=lines, half=half, n...  3.09 us
    pallas_call x1, Pallas kernels, zeros(): pl.pallas_call(zeros_kernel, in_specs=[pl.BlockSpec(memory_space=pl.ANY)]...  2.27 us
  transfers between devices with their start and end apart: 34, of which 15 were waited for; matrix products, arithmetic and copies ran while one was open for 1% of the time, Pallas kernels for 23%

profile of v15, /device:TPU:0, one launch (start us, length us, event | category | flops | bytes accessed | tf_op | source)
XLA Modules:
  0.0 105.0 jit_solution(9981951225684231369)
XLA Ops:
  1.3 4.3 %shard_map.103 = (bf16[2,128,512]{2,1,0:T(8,128)(2,1)}, bf16[2,128,512]{2,1,0:T(8,128)(2,1)}, bf16[2,128,512]{2,1,0:T(8,128)(2,1)}, bf16[4,256,128]{2,1,0:T(8,12...) custom-call(s32[1]{0:T(128)S(6)} %copy.15.slab_index, ...), custom_call_target="tpu_custom_call" | custom-call | tf_op jit(solution)/shard_map/pallas_call | solution.py:168
  7.5 1.7 %add_convert_fusion.3 = bf16[4,256,128]{2,1,0:T(8,128)(2,1)} fusion(bf16[4,256,128]{2,1,0:T(8,128)(2,1)S(1)} %collective-permute-done, bf16[4,256,128]{2,1,0:T(8,128)(2,1)} %get-tuple-element.54), kind=kLoop, calls=%fused_computation.5 | loop fusion | flops 524288 | bytes 786432 | tf_op jit(solution)/shard_map/convert_element_type | solution.py:60
  9.3 2.9 %collective-permute-start.3 = (bf16[2,128,512]{2,1,0:T(8,128)(2,1)}, bf16[2,128,512]{2,1,0:T(8,128)(2,1)S(1)}, u32[]{:S(2)}, u32[]{:S(2)}) collective-permute-start(bf16[2,128,512]{2,1,0:T(8,128)(2,1)} %get-tuple-element.65), channel_id=1, source_target_pairs={{0,4},{1,5},{2,6},{3,7},{4,8},{5,9},{6,10},{7,11},{8,12},{9,13},{1... | collective-permute-start | bytes 786440 | tf_op jit(solution)/shard_map/ppermute | solution.py:52
  13.8 2.1 %shard_map.104 = (bf16[2,2,512,128]{3,2,1,0:T(8,128)(2,1)S(1)}, bf16[2,2,512,128]{3,2,1,0:T(8,128)(2,1)S(1)}, bf16[2,2,128,512]{3,2,1,0:T(8,128)(2,1)S(1)}, bf16...) custom-call(s32[2]{0:T(128)S(1)} %add_multiply_fusion.bases, ...), custom_call_target="tpu_custom_call" | custom-call | bytes 7340032 | tf_op jit(solution)/shard_map/pallas_call | solution.py:262
  15.9 5.2 %collective-permute-done.3.rest_4_ = bf16[2,128,512]{2,1,0:T(8,128)(2,1)S(1)} collective-permute-done((bf16[2,128,512]{2,1,0:T(8,128)(2,1)}, bf16[2,128,512]{2,1,0:T(8,128)(2,1)S(1)}, u32[]{:S(2)}, u32[]{:S(2)}) %collective-permute-start.3) | collective-permute-done | bytes 262176 | tf_op jit(solution)/shard_map/ppermute | solution.py:52
  25.8 2.2 %collective-permute-start.6 = (bf16[256,128]{1,0:T(8,128)(2,1)S(1)}, bf16[256,128]{1,0:T(8,128)(2,1)S(1)}, u32[]{:S(2)}, u32[]{:S(2)}) collective-permute-start(bf16[256,128]{1,0:T(8,128)(2,1)S(1)} %get-tuple-element.109), channel_id=1, source_target_pairs={{0,12},{1,13},{2,14},{3,15},{4,0},{5,1},{6,2},{7,3},{8,4},{9,5},{1... | collective-permute-start | bytes 196616 | tf_op jit(solution)/shard_map/ppermute | solution.py:52
  28.8 2.1 %collective-permute-done.4 = bf16[256,128]{1,0:T(8,128)(2,1)S(1)} collective-permute-done((bf16[256,128]{1,0:T(8,128)(2,1)S(1)}, bf16[256,128]{1,0:T(8,128)(2,1)S(1)}, u32[]{:S(2)}, u32[]{:S(2)}) %collective-permute-start.4) | collective-permute-done | bytes 65568 | tf_op jit(solution)/shard_map/ppermute | solution.py:52
  33.8 2.3 %collective-permute-start.10 = (bf16[256,128]{1,0:T(8,128)(2,1)S(1)}, bf16[256,128]{1,0:T(8,128)(2,1)S(1)}, u32[]{:S(2)}, u32[]{:S(2)}) collective-permute-start(bf16[256,128]{1,0:T(8,128)(2,1)S(1)} %fusion.5._), channel_id=1, source_target_pairs={{0,12},{1,13},{2,14},{3,15},{4,0},{5,1},{6,2},{7,3},{8,4},{9,5},{1... | collective-permute-start | bytes 196616 | tf_op jit(solution)/shard_map/ppermute | solution.py:52
  36.7 2.3 %shard_map.105 = (bf16[16,128,512]{2,1,0:T(8,128)(2,1)}, bf16[16,128,512]{2,1,0:T(8,128)(2,1)}) custom-call(bf16[256,128]{1,0:T(8,128)(2,1)S(1)} %fusion.5._), custom_call_target="tpu_custom_call" | custom-call | bytes 5242880 | tf_op jit(solution)/shard_map/pallas_call | solution.py:598
  39.9 4.1 %collective-permute-done.9 = bf16[256,128]{1,0:T(8,128)(2,1)S(1)} collective-permute-done((bf16[256,128]{1,0:T(8,128)(2,1)S(1)}, bf16[256,128]{1,0:T(8,128)(2,1)S(1)}, u32[]{:S(2)}, u32[]{:S(2)}) %collective-permute-start.9) | collective-permute-done | bytes 65568 | tf_op jit(solution)/shard_map/ppermute | solution.py:52
  45.5 1.9 %collective-permute-start.14 = (bf16[4,256,128]{2,1,0:T(8,128)(2,1)S(1)}, bf16[4,256,128]{2,1,0:T(8,128)(2,1)S(1)}, u32[]{:S(2)}, u32[]{:S(2)}) collective-permute-start(bf16[4,256,128]{2,1,0:T(8,128)(2,1)S(1)} %pad_maximum_fusion.rest_0_), channel_id=1, source_target_pairs={{0,2},{1,3},{2,0},{3,1},{4,6},{5,7},{6,4},{7,5},{8,10},{9,11},{10,... | collective-permute-start | bytes 786440 | tf_op jit(solution)/shard_map/ppermute | solution.py:52
  47.4 6.7 %shard_map.106 = (bf16[4,256,128]{2,1,0:T(8,128)(2,1)S(1)}, bf16[4,256,128]{2,1,0:T(8,128)(2,1)S(1)}, bf16[2,2,256,512]{3,2,1,0:T(8,128)(2,1)S(1)}, bf16[2,2,768...) custom-call(s32[2]{0:T(128)S(1)} %add_multiply_fusion.bases, ...), custom_call_target="tpu_custom_call" | custom-call | flops 2013265920 | bytes 12582912 | tf_op jit(solution)/shard_map/pallas_call | solution.py:439
  57.0 6.6 %shard_map.107 = (f32[4,256,128]{2,1,0:T(8,128)S(1)}, bf16[4,256,128]{2,1,0:T(8,128)(2,1)S(1)}, bf16[2,2,256,512]{3,2,1,0:T(8,128)(2,1)S(1)}, bf16[2,2,768,512]{...) custom-call(s32[2]{0:T(128)S(1)} %add_multiply_fusion.bases, s32[1]{0:T(128)S(6)} %copy.15.slab_index, ...), custom_call_target="tpu_custom_call" | custom-call | flops 2013265920 | bytes 12582912 | tf_op jit(solution)/shard_map/pallas_call | solution.py:439
  64.2 3.1 %shard_map.108 = (f32[2,128,512]{2,1,0:T(8,128)S(1)}, f32[2,128,512]{2,1,0:T(8,128)S(1)}, f32[2,128,512]{2,1,0:T(8,128)S(1)}, bf16[2,128,512]{2,1,0:T(8,128)(2,1...) custom-call(s32[2]{0:T(128)S(1)} %add_multiply_fusion.bases, s32[4,3]{1,0:T(4,128)S(1)} %copy-done.5, ...), custom_call_target="tpu_custom_call" | custom-call | bytes 9437184 | tf_op jit(solution)/shard_map/pallas_call | solution.py:521
  67.6 3.8 %collective-permute-start.22 = (bf16[256,128]{1,0:T(8,128)(2,1)S(1)}, bf16[256,128]{1,0:T(8,128)(2,1)S(1)}, u32[]{:S(2)}, u32[]{:S(2)}) collective-permute-start(bf16[256,128]{1,0:T(8,128)(2,1)S(1)} %get-tuple-element.106), channel_id=1, source_target_pairs={{0,12},{1,13},{2,14},{3,15},{4,0},{5,1},{6,2},{7,3},{8,4},{9,5},{1... | collective-permute-start | bytes 196616 | tf_op jit(solution)/shard_map/ppermute | solution.py:52
  71.5 3.8 %collective-permute-start.29 = (bf16[2,128,512]{2,1,0:T(8,128)(2,1)S(1)}, bf16[2,128,512]{2,1,0:T(8,128)(2,1)S(1)}, u32[]{:S(2)}, u32[]{:S(2)}) collective-permute-start(bf16[2,128,512]{2,1,0:T(8,128)(2,1)S(1)} %get-tuple-element.100), channel_id=1, source_target_pairs={{1,0},{6,1},{3,2},{8,3},{5,4},{10,5},{7,6},{12,7},{9,8},{14,9},{11... | collective-permute-start | bytes 786440 | tf_op jit(solution)/shard_map/ppermute | solution.py:52
  75.7 5.3 %collective-permute-done.21 = bf16[256,128]{1,0:T(8,128)(2,1)S(1)} collective-permute-done((bf16[256,128]{1,0:T(8,128)(2,1)S(1)}, bf16[256,128]{1,0:T(8,128)(2,1)S(1)}, u32[]{:S(2)}, u32[]{:S(2)}) %collective-permute-start.21) | collective-permute-done | bytes 65568 | tf_op jit(solution)/shard_map/ppermute | solution.py:52
  81.3 1.9 %collective-permute-start.26 = (bf16[256,128]{1,0:T(8,128)(2,1)S(1)}, bf16[256,128]{1,0:T(8,128)(2,1)S(1)}, u32[]{:S(2)}, u32[]{:S(2)}) collective-permute-start(bf16[256,128]{1,0:T(8,128)(2,1)S(1)} %fusion.2), channel_id=1, source_target_pairs={{0,4},{1,5},{2,6},{3,7},{4,8},{5,9},{6,10},{7,11},{8,12},{9,13},{1... | collective-permute-start | bytes 196616 | tf_op jit(solution)/shard_map/ppermute | solution.py:52
  83.2 3.6 %shard_map.109 = bf16[128,4096]{1,0:T(8,128)(2,1)} custom-call(s32[2]{0:T(128)S(1)} %add_multiply_fusion.bases, bf16[2,2,768,128]{3,2,1,0:T(8,128)(2,1)S(1)} %get-tuple-element.95.rest_0_, bf16[2,2,768,512]{3,2,1,0:T(8,128)(2,1)S(1)} %get-tuple-element.87.rest_3_.rest_1_, bf16[2,2,768,128]{3,2,1,0:T(8,128)(2,1)S(1)} %get-tuple-element.96.rest_2_, ...), custom_call_target="tpu_custom_call" | custom-call | bytes 10485760 | tf_op jit(solution)/shard_map/pallas_call | solution.py:567
  86.9 2.1 %collective-permute-done.27 = bf16[256,128]{1,0:T(8,128)(2,1)S(1)} collective-permute-done((bf16[256,128]{1,0:T(8,128)(2,1)S(1)}, bf16[256,128]{1,0:T(8,128)(2,1)S(1)}, u32[]{:S(2)}, u32[]{:S(2)}) %collective-permute-start.27) | collective-permute-done | bytes 65568 | tf_op jit(solution)/shard_map/ppermute | solution.py:52
  89.1 2.4 %collective-permute-start.31 = (bf16[4,256,128]{2,1,0:T(8,128)(2,1)S(1)}, bf16[4,256,128]{2,1,0:T(8,128)(2,1)S(1)}, u32[]{:S(2)}, u32[]{:S(2)}) collective-permute-start(bf16[4,256,128]{2,1,0:T(8,128)(2,1)S(1)} %pad_maximum_fusion.1.rest_3_), channel_id=1, source_target_pairs={{0,2},{1,3},{2,0},{3,1},{4,6},{5,7},{6,4},{7,5},{8,10},{9,11},{10,... | collective-permute-start | bytes 786440 | tf_op jit(solution)/shard_map/ppermute | solution.py:52
  93.0 2.8 %collective-permute-done.31.rest_4_ = bf16[4,256,128]{2,1,0:T(8,128)(2,1)S(1)} collective-permute-done((bf16[4,256,128]{2,1,0:T(8,128)(2,1)S(1)}, bf16[4,256,128]{2,1,0:T(8,128)(2,1)S(1)}, u32[]{:S(2)}, u32[]{:S(2)}) %collective-permute-start.31) | collective-permute-done | bytes 262176 | tf_op jit(solution)/shard_map/ppermute | solution.py:52
  95.9 4.6 %collective-permute-done.30.rest_1_ = bf16[2,128,512]{2,1,0:T(8,128)(2,1)S(1)} collective-permute-done((bf16[2,128,512]{2,1,0:T(8,128)(2,1)S(1)}, bf16[2,128,512]{2,1,0:T(8,128)(2,1)S(1)}, u32[]{:S(2)}, u32[]{:S(2)}) %collective-permute-start.30) | collective-permute-done | bytes 262176 | tf_op jit(solution)/shard_map/ppermute | solution.py:52
  100.4 4.5 %shard_map.110 = (bf16[16,128,512]{2,1,0:T(8,128)(2,1)}, bf16[16,128,512]{2,1,0:T(8,128)(2,1)}) custom-call(s32[1]{0:T(128)S(6)} %copy.15.slab_index, s32[4,8]{1,0:T(4,128)S(1)} %copy-done.4, f32[2,128,512]{2,1,0:T(8,128)S(1)} %get-tuple-element.90.home, ...), custom_call_target="tpu_custom_call", output_to_operand_aliasing={{0}: (10, {}), {1}: (11, {})} | custom-call | tf_op jit(solution)/shard_map/pallas_call | solution.py:695
  (84 shorter events, 20.9 us)
Async XLA Ops:
  9.3 11.8 %collective-permute-start.3 = (bf16[2,128,512]{2,1,0:T(8,128)(2,1)}, bf16[2,128,512]{2,1,0:T(8,128)(2,1)S(1)}, u32[]{:S(2)}, u32[]{:S(2)}) collective-permute-start(bf16[2,128,512]{2,1,0:T(8,128)(2,1)} %get-tuple-element.65), channel_id=1, source_target_pairs={{0,4},{1,5},{2,6},{3,7},{4,8},{5,9},{6,10},{7,11},{8,12},{9,13},{1... | collective-permute-start | bytes 786440 | tf_op jit(solution)/shard_map/ppermute | solution.py:52
  12.2 8.9 %collective-permute-start.1 = (bf16[4,256,128]{2,1,0:T(8,128)(2,1)}, bf16[4,256,128]{2,1,0:T(8,128)(2,1)}, u32[]{:S(2)}, u32[]{:S(2)}) collective-permute-start(bf16[4,256,128]{2,1,0:T(8,128)(2,1)} %get-tuple-element.63), channel_id=1, source_target_pairs={{0,1},{1,0},{2,3},{3,2},{4,5},{5,4},{6,7},{7,6},{8,9},{9,8},{10,11... | collective-permute-start | bytes 786440 | tf_op jit(solution)/shard_map/ppermute | solution.py:52
  12.2 9.0 %collective-permute-start.2 = (bf16[4,256,128]{2,1,0:T(8,128)(2,1)}, bf16[4,256,128]{2,1,0:T(8,128)(2,1)}, u32[]{:S(2)}, u32[]{:S(2)}) collective-permute-start(bf16[4,256,128]{2,1,0:T(8,128)(2,1)} %add_convert_fusion.3), channel_id=1, source_target_pairs={{0,2},{1,3},{2,0},{3,1},{4,6},{5,7},{6,4},{7,5},{8,10},{9,11},{10,... | collective-permute-start | bytes 786440 | tf_op jit(solution)/shard_map/ppermute | solution.py:52
  22.5 8.3 %collective-permute-start.11 = (bf16[2,128,512]{2,1,0:T(8,128)(2,1)S(1)}, bf16[2,128,512]{2,1,0:T(8,128)(2,1)S(1)}, u32[]{:S(2)}, u32[]{:S(2)}) collective-permute-start(bf16[2,128,512]{2,1,0:T(8,128)(2,1)S(1)} %broadcast_select_fusion), channel_id=1, source_target_pairs={{0,2},{1,3},{2,0},{3,1},{4,6},{5,7},{6,4},{7,5},{8,10},{9,11},{10,... | collective-permute-start | bytes 786440 | tf_op jit(solution)/shard_map/ppermute | solution.py:52
  24.1 6.7 %collective-permute-start.4 = (bf16[256,128]{1,0:T(8,128)(2,1)S(1)}, bf16[256,128]{1,0:T(8,128)(2,1)S(1)}, u32[]{:S(2)}, u32[]{:S(2)}) collective-permute-start(bf16[256,128]{1,0:T(8,128)(2,1)S(1)} %get-tuple-element.108), channel_id=1, source_target_pairs={{0,4},{1,5},{2,6},{3,7},{4,8},{5,9},{6,10},{7,11},{8,12},{9,13},{1... | collective-permute-start | bytes 196616 | tf_op jit(solution)/shard_map/ppermute | solution.py:52
  25.8 6.7 %collective-permute-start.6 = (bf16[256,128]{1,0:T(8,128)(2,1)S(1)}, bf16[256,128]{1,0:T(8,128)(2,1)S(1)}, u32[]{:S(2)}, u32[]{:S(2)}) collective-permute-start(bf16[256,128]{1,0:T(8,128)(2,1)S(1)} %get-tuple-element.109), channel_id=1, source_target_pairs={{0,12},{1,13},{2,14},{3,15},{4,0},{5,1},{6,2},{7,3},{8,4},{9,5},{1... | collective-permute-start | bytes 196616 | tf_op jit(solution)/shard_map/ppermute | solution.py:52
  30.8 14.6 %collective-permute-start.13 = (bf16[2,128,512]{2,1,0:T(8,128)(2,1)S(1)}, bf16[2,128,512]{2,1,0:T(8,128)(2,1)S(1)}, u32[]{:S(2)}, u32[]{:S(2)}) collective-permute-start(bf16[2,128,512]{2,1,0:T(8,128)(2,1)S(1)} %copy-done.7), channel_id=1, source_target_pairs={{0,1},{1,6},{2,3},{3,8},{4,5},{5,10},{6,7},{7,12},{8,9},{9,14},{10... | collective-permute-start | bytes 786440 | tf_op jit(solution)/shard_map/ppermute | solution.py:52
  30.8 14.6 %collective-permute-start.12 = (bf16[2,128,512]{2,1,0:T(8,128)(2,1)S(1)}, bf16[2,128,512]{2,1,0:T(8,128)(2,1)S(1)}, u32[]{:S(2)}, u32[]{:S(2)}) collective-permute-start(bf16[2,128,512]{2,1,0:T(8,128)(2,1)S(1)} %collective-permute-done.11.rest_3_), channel_id=1, source_target_pairs={{0,1},{1,0},{2,3},{3,2},{4,5},{5,4},{6,7},{7,6},{8,9},{9,8},{10,11... | collective-permute-start | bytes 786440 | tf_op jit(solution)/shard_map/ppermute | solution.py:52
  33.8 6.1 %collective-permute-start.10 = (bf16[256,128]{1,0:T(8,128)(2,1)S(1)}, bf16[256,128]{1,0:T(8,128)(2,1)S(1)}, u32[]{:S(2)}, u32[]{:S(2)}) collective-permute-start(bf16[256,128]{1,0:T(8,128)(2,1)S(1)} %fusion.5._), channel_id=1, source_target_pairs={{0,12},{1,13},{2,14},{3,15},{4,0},{5,1},{6,2},{7,3},{8,4},{9,5},{1... | collective-permute-start | bytes 196616 | tf_op jit(solution)/shard_map/ppermute | solution.py:52
  36.0 7.9 %collective-permute-start.9 = (bf16[256,128]{1,0:T(8,128)(2,1)S(1)}, bf16[256,128]{1,0:T(8,128)(2,1)S(1)}, u32[]{:S(2)}, u32[]{:S(2)}) collective-permute-start(bf16[256,128]{1,0:T(8,128)(2,1)S(1)} %fusion.5._), channel_id=1, source_target_pairs={{0,8},{1,9},{2,10},{3,11},{4,12},{5,13},{6,14},{7,15},{8,0},{9,1},... | collective-permute-start | bytes 196616 | tf_op jit(solution)/shard_map/ppermute | solution.py:52
  36.5 7.5 %collective-permute-start.8 = (bf16[256,128]{1,0:T(8,128)(2,1)S(1)}, bf16[256,128]{1,0:T(8,128)(2,1)S(1)}, u32[]{:S(2)}, u32[]{:S(2)}) collective-permute-start(bf16[256,128]{1,0:T(8,128)(2,1)S(1)} %fusion.5._), channel_id=1, source_target_pairs={{0,4},{1,5},{2,6},{3,7},{4,8},{5,9},{6,10},{7,11},{8,12},{9,13},{1... | collective-permute-start | bytes 196616 | tf_op jit(solution)/shard_map/ppermute | solution.py:52
  45.5 8.8 %collective-permute-start.14 = (bf16[4,256,128]{2,1,0:T(8,128)(2,1)S(1)}, bf16[4,256,128]{2,1,0:T(8,128)(2,1)S(1)}, u32[]{:S(2)}, u32[]{:S(2)}) collective-permute-start(bf16[4,256,128]{2,1,0:T(8,128)(2,1)S(1)} %pad_maximum_fusion.rest_0_), channel_id=1, source_target_pairs={{0,2},{1,3},{2,0},{3,1},{4,6},{5,7},{6,4},{7,5},{8,10},{9,11},{10,... | collective-permute-start | bytes 786440 | tf_op jit(solution)/shard_map/ppermute | solution.py:52
  55.8 8.4 %collective-permute-start.19 = (bf16[4,256,128]{2,1,0:T(8,128)(2,1)S(1)}, bf16[4,256,128]{2,1,0:T(8,128)(2,1)S(1)}, u32[]{:S(2)}, u32[]{:S(2)}) collective-permute-start(bf16[4,256,128]{2,1,0:T(8,128)(2,1)S(1)} %add_convert_fusion.2), channel_id=1, source_target_pairs={{0,2},{1,3},{2,0},{3,1},{4,6},{5,7},{6,4},{7,5},{8,10},{9,11},{10,... | collective-permute-start | bytes 786440 | tf_op jit(solution)/shard_map/ppermute | solution.py:52
  67.6 7.8 %collective-permute-start.20 = (bf16[256,128]{1,0:T(8,128)(2,1)S(1)}, bf16[256,128]{1,0:T(8,128)(2,1)S(1)}, u32[]{:S(2)}, u32[]{:S(2)}) collective-permute-start(bf16[256,128]{1,0:T(8,128)(2,1)S(1)} %get-tuple-element.105), channel_id=1, source_target_pairs={{0,4},{1,5},{2,6},{3,7},{4,8},{5,9},{6,10},{7,11},{8,12},{9,13},{1... | collective-permute-start | bytes 196616 | tf_op jit(solution)/shard_map/ppermute | solution.py:52
  67.6 8.1 %collective-permute-start.22 = (bf16[256,128]{1,0:T(8,128)(2,1)S(1)}, bf16[256,128]{1,0:T(8,128)(2,1)S(1)}, u32[]{:S(2)}, u32[]{:S(2)}) collective-permute-start(bf16[256,128]{1,0:T(8,128)(2,1)S(1)} %get-tuple-element.106), channel_id=1, source_target_pairs={{0,12},{1,13},{2,14},{3,15},{4,0},{5,1},{6,2},{7,3},{8,4},{9,5},{1... | collective-permute-start | bytes 196616 | tf_op jit(solution)/shard_map/ppermute | solution.py:52
  71.5 9.6 %collective-permute-start.21 = (bf16[256,128]{1,0:T(8,128)(2,1)S(1)}, bf16[256,128]{1,0:T(8,128)(2,1)S(1)}, u32[]{:S(2)}, u32[]{:S(2)}) collective-permute-start(bf16[256,128]{1,0:T(8,128)(2,1)S(1)} %get-tuple-element.107), channel_id=1, source_target_pairs={{0,8},{1,9},{2,10},{3,11},{4,12},{5,13},{6,14},{7,15},{8,0},{9,1},... | collective-permute-start | bytes 196616 | tf_op jit(solution)/shard_map/ppermute | solution.py:52
  71.5 9.7 %collective-permute-start.23 = (bf16[2,128,512]{2,1,0:T(8,128)(2,1)S(1)}, bf16[2,128,512]{2,1,0:T(8,128)(2,1)S(1)}, u32[]{:S(2)}, u32[]{:S(2)}) collective-permute-start(bf16[2,128,512]{2,1,0:T(8,128)(2,1)S(1)} %get-tuple-element.92), channel_id=1, source_target_pairs={{0,1},{1,0},{2,3},{3,2},{4,5},{5,4},{6,7},{7,6},{8,9},{9,8},{10,11... | collective-permute-start | bytes 786440 | tf_op jit(solution)/shard_map/ppermute | solution.py:52
  71.5 17.6 %collective-permute-start.29 = (bf16[2,128,512]{2,1,0:T(8,128)(2,1)S(1)}, bf16[2,128,512]{2,1,0:T(8,128)(2,1)S(1)}, u32[]{:S(2)}, u32[]{:S(2)}) collective-permute-start(bf16[2,128,512]{2,1,0:T(8,128)(2,1)S(1)} %get-tuple-element.100), channel_id=1, source_target_pairs={{1,0},{6,1},{3,2},{8,3},{5,4},{10,5},{7,6},{12,7},{9,8},{14,9},{11... | collective-permute-start | bytes 786440 | tf_op jit(solution)/shard_map/ppermute | solution.py:52
  75.4 13.7 %collective-permute-start.25 = (bf16[2,128,512]{2,1,0:T(8,128)(2,1)S(1)}, bf16[2,128,512]{2,1,0:T(8,128)(2,1)S(1)}, u32[]{:S(2)}, u32[]{:S(2)}) collective-permute-start(bf16[2,128,512]{2,1,0:T(8,128)(2,1)S(1)} %add_convert_fusion.1), channel_id=1, source_target_pairs={{0,2},{1,3},{2,0},{3,1},{4,6},{5,7},{6,4},{7,5},{8,10},{9,11},{10,... | collective-permute-start | bytes 786440 | tf_op jit(solution)/shard_map/ppermute | solution.py:52
  81.2 7.8 %collective-permute-start.27 = (bf16[256,128]{1,0:T(8,128)(2,1)S(1)}, bf16[256,128]{1,0:T(8,128)(2,1)S(1)}, u32[]{:S(2)}, u32[]{:S(2)}) collective-permute-start(bf16[256,128]{1,0:T(8,128)(2,1)S(1)} %fusion.2), channel_id=1, source_target_pairs={{0,8},{1,9},{2,10},{3,11},{4,12},{5,13},{6,14},{7,15},{8,0},{9,1},... | collective-permute-start | bytes 196616 | tf_op jit(solution)/shard_map/ppermute | solution.py:52
  81.3 7.7 %collective-permute-start.26 = (bf16[256,128]{1,0:T(8,128)(2,1)S(1)}, bf16[256,128]{1,0:T(8,128)(2,1)S(1)}, u32[]{:S(2)}, u32[]{:S(2)}) collective-permute-start(bf16[256,128]{1,0:T(8,128)(2,1)S(1)} %fusion.2), channel_id=1, source_target_pairs={{0,4},{1,5},{2,6},{3,7},{4,8},{5,9},{6,10},{7,11},{8,12},{9,13},{1... | collective-permute-start | bytes 196616 | tf_op jit(solution)/shard_map/ppermute | solution.py:52
  89.1 6.8 %collective-permute-start.31 = (bf16[4,256,128]{2,1,0:T(8,128)(2,1)S(1)}, bf16[4,256,128]{2,1,0:T(8,128)(2,1)S(1)}, u32[]{:S(2)}, u32[]{:S(2)}) collective-permute-start(bf16[4,256,128]{2,1,0:T(8,128)(2,1)S(1)} %pad_maximum_fusion.1.rest_3_), channel_id=1, source_target_pairs={{0,2},{1,3},{2,0},{3,1},{4,6},{5,7},{6,4},{7,5},{8,10},{9,11},{10,... | collective-permute-start | bytes 786440 | tf_op jit(solution)/shard_map/ppermute | solution.py:52
  91.5 8.9 %collective-permute-start.32 = (bf16[4,256,128]{2,1,0:T(8,128)(2,1)S(1)}, bf16[4,256,128]{2,1,0:T(8,128)(2,1)S(1)}, u32[]{:S(2)}, u32[]{:S(2)}) collective-permute-start(bf16[4,256,128]{2,1,0:T(8,128)(2,1)S(1)} %pad_maximum_fusion.1.rest_3_), channel_id=1, source_target_pairs={{0,1},{1,0},{2,3},{3,2},{4,5},{5,4},{6,7},{7,6},{8,9},{9,8},{10,11... | collective-permute-start | bytes 786440 | tf_op jit(solution)/shard_map/ppermute | solution.py:52
  91.7 8.8 %collective-permute-start.30 = (bf16[2,128,512]{2,1,0:T(8,128)(2,1)S(1)}, bf16[2,128,512]{2,1,0:T(8,128)(2,1)S(1)}, u32[]{:S(2)}, u32[]{:S(2)}) collective-permute-start(bf16[2,128,512]{2,1,0:T(8,128)(2,1)S(1)} %add_convert_fusion), channel_id=1, source_target_pairs={{4,0},{5,1},{6,2},{7,3},{8,4},{9,5},{10,6},{11,7},{12,8},{13,9},{1... | collective-permute-start | bytes 786440 | tf_op jit(solution)/shard_map/ppermute | solution.py:52
  (18 other events, 158.1 us)

commit v16 on v15

--- a/solution.py
+++ b/solution.py
@@ -731,7 +731,7 @@
         slab_index, verticals, context_keys, context_values, lines
     )
     to_near = core_sum(lines, to_near, to_both)
-    recv4 = move(after(send4, to_near), lines.shift_pairs(4))
+    recv4 = move(send4, lines.shift_pairs(4))
     quarter = near_sum(lines, mine, move(to_near, lines.near_pairs()), to_core)
     bases = (jnp.stack([near, 1 - near]) * (heads // 2)).astype(jnp.int32)
     prepared = prepare(

time: 105 us -> 101 us (0.962)
  waiting for transfers between devices: 32.9 us -> 28.3 us
    ppermute x34, waiting for transfers between devices: 32.9 us -> 28.3 us  [move(): return lax.ppermute(array, 'ctx', pairs)]
  transfers between devices with their start and end apart: 34 -> 34, of which waited for: 15 -> 13; matrix products, arithmetic and copies ran while one was open for 1% -> 4% of each run, Pallas kernels for 23% -> 24%
where the time goes in v16:
time: 101 us
  starting transfers between devices  34.2 us (34%)
  Pallas kernels  33.1 us (33%)
  waiting for transfers between devices  28.3 us (28%)
  other arithmetic  3.65 us (4%)
  between operations  1.76 us (2%)
    ppermute x34, starting transfers between devices, move(): return lax.ppermute(array, 'ctx', pairs)  34.2 us
    ppermute x34, waiting for transfers between devices, move(): return lax.ppermute(array, 'ctx', pairs)  28.3 us
    pallas_call x2, Pallas kernels, attend(): pl.pallas_call(functools.partial(attend_kernel, lines=lines, nv=nv, ns=ns...  13.3 us
    pallas_call x1, Pallas kernels, assemble(): pl.pallas_call(functools.partial(assemble_kernel, lines=lines, heads=head...  4.39 us
    pallas_call x1, Pallas kernels, pack(): pl.pallas_call(functools.partial(pack_kernel, lines=lines, heads=heads, n...  4.36 us
    pallas_call x1, Pallas kernels, query_gradients(): pl.pallas_call(query_kernel, grid_spec=pltpu.PrefetchScalarGridSpec(num_s...  3.53 us
    pallas_call x1, Pallas kernels, window_gradients(): pl.pallas_call(functools.partial(window_kernel, lines=lines, half=half, n...  3.07 us
    pallas_call x1, Pallas kernels, zeros(): pl.pallas_call(zeros_kernel, in_specs=[pl.BlockSpec(memory_space=pl.ANY)]...  2.27 us
  transfers between devices with their start and end apart: 34, of which 13 were waited for; matrix products, arithmetic and copies ran while one was open for 4% of the time, Pallas kernels for 24%

profile of v16, /device:TPU:0, one launch (start us, length us, event | category | flops | bytes accessed | tf_op | source)
XLA Modules:
  0.0 101.0 jit_solution(2461708143603301988)
XLA Ops:
  1.3 4.4 %shard_map.103 = (bf16[2,128,512]{2,1,0:T(8,128)(2,1)}, bf16[2,128,512]{2,1,0:T(8,128)(2,1)}, bf16[2,128,512]{2,1,0:T(8,128)(2,1)}, bf16[4,256,128]{2,1,0:T(8,12...) custom-call(s32[1]{0:T(128)S(6)} %copy.15.slab_index, ...), custom_call_target="tpu_custom_call" | custom-call | tf_op jit(solution)/shard_map/pallas_call | solution.py:168
  6.3 2.9 %collective-permute-start.3 = (bf16[2,128,512]{2,1,0:T(8,128)(2,1)}, bf16[2,128,512]{2,1,0:T(8,128)(2,1)}, u32[]{:S(2)}, u32[]{:S(2)}) collective-permute-start(bf16[2,128,512]{2,1,0:T(8,128)(2,1)} %get-tuple-element.63), channel_id=1, source_target_pairs={{0,4},{1,5},{2,6},{3,7},{4,8},{5,9},{6,10},{7,11},{8,12},{9,13},{1... | collective-permute-start | bytes 786440 | tf_op jit(solution)/shard_map/ppermute | solution.py:52
  12.7 2.1 %shard_map.104 = (bf16[2,2,512,128]{3,2,1,0:T(8,128)(2,1)S(1)}, bf16[2,2,512,128]{3,2,1,0:T(8,128)(2,1)S(1)}, bf16[2,2,128,512]{3,2,1,0:T(8,128)(2,1)S(1)}, bf16...) custom-call(s32[2]{0:T(128)S(1)} %add_multiply_fusion.bases, ...), custom_call_target="tpu_custom_call" | custom-call | bytes 7340032 | tf_op jit(solution)/shard_map/pallas_call | solution.py:262
  14.8 3.3 %collective-permute-done.3.rest_4_ = bf16[2,128,512]{2,1,0:T(8,128)(2,1)} collective-permute-done((bf16[2,128,512]{2,1,0:T(8,128)(2,1)}, bf16[2,128,512]{2,1,0:T(8,128)(2,1)}, u32[]{:S(2)}, u32[]{:S(2)}) %collective-permute-start.3) | collective-permute-done | bytes 262176 | tf_op jit(solution)/shard_map/ppermute | solution.py:52
  18.2 2.5 %collective-permute-start.11 = (bf16[2,128,512]{2,1,0:T(8,128)(2,1)S(1)}, bf16[2,128,512]{2,1,0:T(8,128)(2,1)S(1)}, u32[]{:S(2)}, u32[]{:S(2)}) collective-permute-start(bf16[2,128,512]{2,1,0:T(8,128)(2,1)S(1)} %broadcast_select_fusion), channel_id=1, source_target_pairs={{0,2},{1,3},{2,0},{3,1},{4,6},{5,7},{6,4},{7,5},{8,10},{9,11},{10,... | collective-permute-start | bytes 786440 | tf_op jit(solution)/shard_map/ppermute | solution.py:52
  22.7 3.1 %collective-permute-start.6 = (bf16[256,128]{1,0:T(8,128)(2,1)S(1)}, bf16[256,128]{1,0:T(8,128)(2,1)S(1)}, u32[]{:S(2)}, u32[]{:S(2)}) collective-permute-start(bf16[256,128]{1,0:T(8,128)(2,1)S(1)} %get-tuple-element.107), channel_id=1, source_target_pairs={{0,12},{1,13},{2,14},{3,15},{4,0},{5,1},{6,2},{7,3},{8,4},{9,5},{1... | collective-permute-start | bytes 196616 | tf_op jit(solution)/shard_map/ppermute | solution.py:52
  28.3 2.7 %collective-permute-done.5 = bf16[256,128]{1,0:T(8,128)(2,1)S(1)} collective-permute-done((bf16[256,128]{1,0:T(8,128)(2,1)S(1)}, bf16[256,128]{1,0:T(8,128)(2,1)S(1)}, u32[]{:S(2)}, u32[]{:S(2)}) %collective-permute-start.5) | collective-permute-done | bytes 65568 | tf_op jit(solution)/shard_map/ppermute | solution.py:52
  31.1 2.9 %collective-permute-start.10 = (bf16[256,128]{1,0:T(8,128)(2,1)S(1)}, bf16[256,128]{1,0:T(8,128)(2,1)S(1)}, u32[]{:S(2)}, u32[]{:S(2)}) collective-permute-start(bf16[256,128]{1,0:T(8,128)(2,1)S(1)} %fusion.5._), channel_id=1, source_target_pairs={{0,12},{1,13},{2,14},{3,15},{4,0},{5,1},{6,2},{7,3},{8,4},{9,5},{1... | collective-permute-start | bytes 196616 | tf_op jit(solution)/shard_map/ppermute | solution.py:52
  34.6 2.3 %shard_map.105 = (bf16[16,128,512]{2,1,0:T(8,128)(2,1)}, bf16[16,128,512]{2,1,0:T(8,128)(2,1)}) custom-call(bf16[256,128]{1,0:T(8,128)(2,1)S(1)} %fusion.5._), custom_call_target="tpu_custom_call" | custom-call | bytes 5242880 | tf_op jit(solution)/shard_map/pallas_call | solution.py:598
  37.4 2.8 %collective-permute-done.9 = bf16[256,128]{1,0:T(8,128)(2,1)S(1)} collective-permute-done((bf16[256,128]{1,0:T(8,128)(2,1)S(1)}, bf16[256,128]{1,0:T(8,128)(2,1)S(1)}, u32[]{:S(2)}, u32[]{:S(2)}) %collective-permute-start.9) | collective-permute-done | bytes 65568 | tf_op jit(solution)/shard_map/ppermute | solution.py:52
  40.4 3.1 %collective-permute-start.14 = (bf16[4,256,128]{2,1,0:T(8,128)(2,1)S(1)}, bf16[4,256,128]{2,1,0:T(8,128)(2,1)S(1)}, u32[]{:S(2)}, u32[]{:S(2)}) collective-permute-start(bf16[4,256,128]{2,1,0:T(8,128)(2,1)S(1)} %pad_maximum_fusion.rest_0_), channel_id=1, source_target_pairs={{0,2},{1,3},{2,0},{3,1},{4,6},{5,7},{6,4},{7,5},{8,10},{9,11},{10,... | collective-permute-start | bytes 786440 | tf_op jit(solution)/shard_map/ppermute | solution.py:52
  43.5 6.7 %shard_map.106 = (bf16[4,256,128]{2,1,0:T(8,128)(2,1)S(1)}, bf16[4,256,128]{2,1,0:T(8,128)(2,1)S(1)}, bf16[2,2,256,512]{3,2,1,0:T(8,128)(2,1)S(1)}, bf16[2,2,768...) custom-call(s32[2]{0:T(128)S(1)} %add_multiply_fusion.bases, ...), custom_call_target="tpu_custom_call" | custom-call | flops 2013265920 | bytes 12582912 | tf_op jit(solution)/shard_map/pallas_call | solution.py:439
  53.1 6.6 %shard_map.107 = (f32[4,256,128]{2,1,0:T(8,128)S(1)}, bf16[4,256,128]{2,1,0:T(8,128)(2,1)S(1)}, bf16[2,2,256,512]{3,2,1,0:T(8,128)(2,1)S(1)}, bf16[2,2,768,512]{...) custom-call(s32[2]{0:T(128)S(1)} %add_multiply_fusion.bases, s32[1]{0:T(128)S(6)} %copy.15.slab_index, ...), custom_call_target="tpu_custom_call" | custom-call | flops 2013265920 | bytes 12582912 | tf_op jit(solution)/shard_map/pallas_call | solution.py:439
  60.3 3.1 %shard_map.108 = (f32[2,128,512]{2,1,0:T(8,128)S(1)}, f32[2,128,512]{2,1,0:T(8,128)S(1)}, f32[2,128,512]{2,1,0:T(8,128)S(1)}, bf16[2,128,512]{2,1,0:T(8,128)(2,1...) custom-call(s32[2]{0:T(128)S(1)} %add_multiply_fusion.bases, s32[4,3]{1,0:T(4,128)S(1)} %copy-done.5, ...), custom_call_target="tpu_custom_call" | custom-call | bytes 9437184 | tf_op jit(solution)/shard_map/pallas_call | solution.py:521
  63.7 3.8 %collective-permute-start.22 = (bf16[256,128]{1,0:T(8,128)(2,1)S(1)}, bf16[256,128]{1,0:T(8,128)(2,1)S(1)}, u32[]{:S(2)}, u32[]{:S(2)}) collective-permute-start(bf16[256,128]{1,0:T(8,128)(2,1)S(1)} %get-tuple-element.104), channel_id=1, source_target_pairs={{0,12},{1,13},{2,14},{3,15},{4,0},{5,1},{6,2},{7,3},{8,4},{9,5},{1... | collective-permute-start | bytes 196616 | tf_op jit(solution)/shard_map/ppermute | solution.py:52
  67.5 3.8 %collective-permute-start.29 = (bf16[2,128,512]{2,1,0:T(8,128)(2,1)S(1)}, bf16[2,128,512]{2,1,0:T(8,128)(2,1)S(1)}, u32[]{:S(2)}, u32[]{:S(2)}) collective-permute-start(bf16[2,128,512]{2,1,0:T(8,128)(2,1)S(1)} %get-tuple-element.98), channel_id=1, source_target_pairs={{1,0},{6,1},{3,2},{8,3},{5,4},{10,5},{7,6},{12,7},{9,8},{14,9},{11... | collective-permute-start | bytes 786440 | tf_op jit(solution)/shard_map/ppermute | solution.py:52
  71.8 5.3 %collective-permute-done.21 = bf16[256,128]{1,0:T(8,128)(2,1)S(1)} collective-permute-done((bf16[256,128]{1,0:T(8,128)(2,1)S(1)}, bf16[256,128]{1,0:T(8,128)(2,1)S(1)}, u32[]{:S(2)}, u32[]{:S(2)}) %collective-permute-start.21) | collective-permute-done | bytes 65568 | tf_op jit(solution)/shard_map/ppermute | solution.py:52
  77.3 1.9 %collective-permute-start.26 = (bf16[256,128]{1,0:T(8,128)(2,1)S(1)}, bf16[256,128]{1,0:T(8,128)(2,1)S(1)}, u32[]{:S(2)}, u32[]{:S(2)}) collective-permute-start(bf16[256,128]{1,0:T(8,128)(2,1)S(1)} %fusion.2), channel_id=1, source_target_pairs={{0,4},{1,5},{2,6},{3,7},{4,8},{5,9},{6,10},{7,11},{8,12},{9,13},{1... | collective-permute-start | bytes 196616 | tf_op jit(solution)/shard_map/ppermute | solution.py:52
  79.2 3.5 %shard_map.109 = bf16[128,4096]{1,0:T(8,128)(2,1)} custom-call(s32[2]{0:T(128)S(1)} %add_multiply_fusion.bases, bf16[2,2,768,128]{3,2,1,0:T(8,128)(2,1)S(1)} %get-tuple-element.93.rest_0_, bf16[2,2,768,512]{3,2,1,0:T(8,128)(2,1)S(1)} %get-tuple-element.85.rest_3_.rest_1_, bf16[2,2,768,128]{3,2,1,0:T(8,128)(2,1)S(1)} %get-tuple-element.94.rest_2_, ...), custom_call_target="tpu_custom_call" | custom-call | bytes 10485760 | tf_op jit(solution)/shard_map/pallas_call | solution.py:567
  82.9 2.1 %collective-permute-done.27 = bf16[256,128]{1,0:T(8,128)(2,1)S(1)} collective-permute-done((bf16[256,128]{1,0:T(8,128)(2,1)S(1)}, bf16[256,128]{1,0:T(8,128)(2,1)S(1)}, u32[]{:S(2)}, u32[]{:S(2)}) %collective-permute-start.27) | collective-permute-done | bytes 65568 | tf_op jit(solution)/shard_map/ppermute | solution.py:52
  85.1 2.5 %collective-permute-start.31 = (bf16[4,256,128]{2,1,0:T(8,128)(2,1)S(1)}, bf16[4,256,128]{2,1,0:T(8,128)(2,1)S(1)}, u32[]{:S(2)}, u32[]{:S(2)}) collective-permute-start(bf16[4,256,128]{2,1,0:T(8,128)(2,1)S(1)} %pad_maximum_fusion.1.rest_3_), channel_id=1, source_target_pairs={{0,2},{1,3},{2,0},{3,1},{4,6},{5,7},{6,4},{7,5},{8,10},{9,11},{10,... | collective-permute-start | bytes 786440 | tf_op jit(solution)/shard_map/ppermute | solution.py:52
  89.0 2.8 %collective-permute-done.31.rest_4_ = bf16[4,256,128]{2,1,0:T(8,128)(2,1)S(1)} collective-permute-done((bf16[4,256,128]{2,1,0:T(8,128)(2,1)S(1)}, bf16[4,256,128]{2,1,0:T(8,128)(2,1)S(1)}, u32[]{:S(2)}, u32[]{:S(2)}) %collective-permute-start.31) | collective-permute-done | bytes 262176 | tf_op jit(solution)/shard_map/ppermute | solution.py:52
  91.9 4.6 %collective-permute-done.30.rest_1_ = bf16[2,128,512]{2,1,0:T(8,128)(2,1)S(1)} collective-permute-done((bf16[2,128,512]{2,1,0:T(8,128)(2,1)S(1)}, bf16[2,128,512]{2,1,0:T(8,128)(2,1)S(1)}, u32[]{:S(2)}, u32[]{:S(2)}) %collective-permute-start.30) | collective-permute-done | bytes 262176 | tf_op jit(solution)/shard_map/ppermute | solution.py:52
  96.5 4.4 %shard_map.110 = (bf16[16,128,512]{2,1,0:T(8,128)(2,1)}, bf16[16,128,512]{2,1,0:T(8,128)(2,1)}) custom-call(s32[1]{0:T(128)S(6)} %copy.15.slab_index, s32[4,8]{1,0:T(4,128)S(1)} %copy-done.4, f32[2,128,512]{2,1,0:T(8,128)S(1)} %get-tuple-element.88.home, ...), custom_call_target="tpu_custom_call", output_to_operand_aliasing={{0}: (10, {}), {1}: (11, {})} | custom-call | tf_op jit(solution)/shard_map/pallas_call | solution.py:695
  (84 shorter events, 15.9 us)
Async XLA Ops:
  6.2 14.5 %collective-permute-start.1 = (bf16[4,256,128]{2,1,0:T(8,128)(2,1)}, bf16[4,256,128]{2,1,0:T(8,128)(2,1)}, u32[]{:S(2)}, u32[]{:S(2)}) collective-permute-start(bf16[4,256,128]{2,1,0:T(8,128)(2,1)} %get-tuple-element.62), channel_id=1, source_target_pairs={{0,1},{1,0},{2,3},{3,2},{4,5},{5,4},{6,7},{7,6},{8,9},{9,8},{10,11... | collective-permute-start | bytes 786440 | tf_op jit(solution)/shard_map/ppermute | solution.py:52
  6.3 11.9 %collective-permute-start.3 = (bf16[2,128,512]{2,1,0:T(8,128)(2,1)}, bf16[2,128,512]{2,1,0:T(8,128)(2,1)}, u32[]{:S(2)}, u32[]{:S(2)}) collective-permute-start(bf16[2,128,512]{2,1,0:T(8,128)(2,1)} %get-tuple-element.63), channel_id=1, source_target_pairs={{0,4},{1,5},{2,6},{3,7},{4,8},{5,9},{6,10},{7,11},{8,12},{9,13},{1... | collective-permute-start | bytes 786440 | tf_op jit(solution)/shard_map/ppermute | solution.py:52
  11.1 9.7 %collective-permute-start.2 = (bf16[4,256,128]{2,1,0:T(8,128)(2,1)}, bf16[4,256,128]{2,1,0:T(8,128)(2,1)}, u32[]{:S(2)}, u32[]{:S(2)}) collective-permute-start(bf16[4,256,128]{2,1,0:T(8,128)(2,1)} %add_convert_fusion.3), channel_id=1, source_target_pairs={{0,2},{1,3},{2,0},{3,1},{4,6},{5,7},{6,4},{7,5},{8,10},{9,11},{10,... | collective-permute-start | bytes 786440 | tf_op jit(solution)/shard_map/ppermute | solution.py:52
  18.2 8.3 %collective-permute-start.11 = (bf16[2,128,512]{2,1,0:T(8,128)(2,1)S(1)}, bf16[2,128,512]{2,1,0:T(8,128)(2,1)S(1)}, u32[]{:S(2)}, u32[]{:S(2)}) collective-permute-start(bf16[2,128,512]{2,1,0:T(8,128)(2,1)S(1)} %broadcast_select_fusion), channel_id=1, source_target_pairs={{0,2},{1,3},{2,0},{3,1},{4,6},{5,7},{6,4},{7,5},{8,10},{9,11},{10,... | collective-permute-start | bytes 786440 | tf_op jit(solution)/shard_map/ppermute | solution.py:52
  21.9 6.4 %collective-permute-start.4 = (bf16[256,128]{1,0:T(8,128)(2,1)S(1)}, bf16[256,128]{1,0:T(8,128)(2,1)S(1)}, u32[]{:S(2)}, u32[]{:S(2)}) collective-permute-start(bf16[256,128]{1,0:T(8,128)(2,1)S(1)} %get-tuple-element.106), channel_id=1, source_target_pairs={{0,4},{1,5},{2,6},{3,7},{4,8},{5,9},{6,10},{7,11},{8,12},{9,13},{1... | collective-permute-start | bytes 196616 | tf_op jit(solution)/shard_map/ppermute | solution.py:52
  26.5 13.7 %collective-permute-start.13 = (bf16[2,128,512]{2,1,0:T(8,128)(2,1)S(1)}, bf16[2,128,512]{2,1,0:T(8,128)(2,1)S(1)}, u32[]{:S(2)}, u32[]{:S(2)}) collective-permute-start(bf16[2,128,512]{2,1,0:T(8,128)(2,1)S(1)} %copy-done.7), channel_id=1, source_target_pairs={{0,1},{1,6},{2,3},{3,8},{4,5},{5,10},{6,7},{7,12},{8,9},{9,14},{10... | collective-permute-start | bytes 786440 | tf_op jit(solution)/shard_map/ppermute | solution.py:52
  28.3 11.9 %collective-permute-start.12 = (bf16[2,128,512]{2,1,0:T(8,128)(2,1)S(1)}, bf16[2,128,512]{2,1,0:T(8,128)(2,1)S(1)}, u32[]{:S(2)}, u32[]{:S(2)}) collective-permute-start(bf16[2,128,512]{2,1,0:T(8,128)(2,1)S(1)} %collective-permute-done.11.rest_3_), channel_id=1, source_target_pairs={{0,1},{1,0},{2,3},{3,2},{4,5},{5,4},{6,7},{7,6},{8,9},{9,8},{10,11... | collective-permute-start | bytes 786440 | tf_op jit(solution)/shard_map/ppermute | solution.py:52
  31.1 6.3 %collective-permute-start.10 = (bf16[256,128]{1,0:T(8,128)(2,1)S(1)}, bf16[256,128]{1,0:T(8,128)(2,1)S(1)}, u32[]{:S(2)}, u32[]{:S(2)}) collective-permute-start(bf16[256,128]{1,0:T(8,128)(2,1)S(1)} %fusion.5._), channel_id=1, source_target_pairs={{0,12},{1,13},{2,14},{3,15},{4,0},{5,1},{6,2},{7,3},{8,4},{9,5},{1... | collective-permute-start | bytes 196616 | tf_op jit(solution)/shard_map/ppermute | solution.py:52
  34.0 6.2 %collective-permute-start.9 = (bf16[256,128]{1,0:T(8,128)(2,1)S(1)}, bf16[256,128]{1,0:T(8,128)(2,1)S(1)}, u32[]{:S(2)}, u32[]{:S(2)}) collective-permute-start(bf16[256,128]{1,0:T(8,128)(2,1)S(1)} %fusion.5._), channel_id=1, source_target_pairs={{0,8},{1,9},{2,10},{3,11},{4,12},{5,13},{6,14},{7,15},{8,0},{9,1},... | collective-permute-start | bytes 196616 | tf_op jit(solution)/shard_map/ppermute | solution.py:52
  34.0 6.2 %collective-permute-start.8 = (bf16[256,128]{1,0:T(8,128)(2,1)S(1)}, bf16[256,128]{1,0:T(8,128)(2,1)S(1)}, u32[]{:S(2)}, u32[]{:S(2)}) collective-permute-start(bf16[256,128]{1,0:T(8,128)(2,1)S(1)} %fusion.5._), channel_id=1, source_target_pairs={{0,4},{1,5},{2,6},{3,7},{4,8},{5,9},{6,10},{7,11},{8,12},{9,13},{1... | collective-permute-start | bytes 196616 | tf_op jit(solution)/shard_map/ppermute | solution.py:52
  40.4 9.9 %collective-permute-start.14 = (bf16[4,256,128]{2,1,0:T(8,128)(2,1)S(1)}, bf16[4,256,128]{2,1,0:T(8,128)(2,1)S(1)}, u32[]{:S(2)}, u32[]{:S(2)}) collective-permute-start(bf16[4,256,128]{2,1,0:T(8,128)(2,1)S(1)} %pad_maximum_fusion.rest_0_), channel_id=1, source_target_pairs={{0,2},{1,3},{2,0},{3,1},{4,6},{5,7},{6,4},{7,5},{8,10},{9,11},{10,... | collective-permute-start | bytes 786440 | tf_op jit(solution)/shard_map/ppermute | solution.py:52
  51.9 8.4 %collective-permute-start.19 = (bf16[4,256,128]{2,1,0:T(8,128)(2,1)S(1)}, bf16[4,256,128]{2,1,0:T(8,128)(2,1)S(1)}, u32[]{:S(2)}, u32[]{:S(2)}) collective-permute-start(bf16[4,256,128]{2,1,0:T(8,128)(2,1)S(1)} %add_convert_fusion.2), channel_id=1, source_target_pairs={{0,2},{1,3},{2,0},{3,1},{4,6},{5,7},{6,4},{7,5},{8,10},{9,11},{10,... | collective-permute-start | bytes 786440 | tf_op jit(solution)/shard_map/ppermute | solution.py:52
  63.6 7.8 %collective-permute-start.20 = (bf16[256,128]{1,0:T(8,128)(2,1)S(1)}, bf16[256,128]{1,0:T(8,128)(2,1)S(1)}, u32[]{:S(2)}, u32[]{:S(2)}) collective-permute-start(bf16[256,128]{1,0:T(8,128)(2,1)S(1)} %get-tuple-element.103), channel_id=1, source_target_pairs={{0,4},{1,5},{2,6},{3,7},{4,8},{5,9},{6,10},{7,11},{8,12},{9,13},{1... | collective-permute-start | bytes 196616 | tf_op jit(solution)/shard_map/ppermute | solution.py:52
  63.7 8.1 %collective-permute-start.22 = (bf16[256,128]{1,0:T(8,128)(2,1)S(1)}, bf16[256,128]{1,0:T(8,128)(2,1)S(1)}, u32[]{:S(2)}, u32[]{:S(2)}) collective-permute-start(bf16[256,128]{1,0:T(8,128)(2,1)S(1)} %get-tuple-element.104), channel_id=1, source_target_pairs={{0,12},{1,13},{2,14},{3,15},{4,0},{5,1},{6,2},{7,3},{8,4},{9,5},{1... | collective-permute-start | bytes 196616 | tf_op jit(solution)/shard_map/ppermute | solution.py:52
  67.5 9.6 %collective-permute-start.21 = (bf16[256,128]{1,0:T(8,128)(2,1)S(1)}, bf16[256,128]{1,0:T(8,128)(2,1)S(1)}, u32[]{:S(2)}, u32[]{:S(2)}) collective-permute-start(bf16[256,128]{1,0:T(8,128)(2,1)S(1)} %get-tuple-element.105), channel_id=1, source_target_pairs={{0,8},{1,9},{2,10},{3,11},{4,12},{5,13},{6,14},{7,15},{8,0},{9,1},... | collective-permute-start | bytes 196616 | tf_op jit(solution)/shard_map/ppermute | solution.py:52
  67.5 9.6 %collective-permute-start.23 = (bf16[2,128,512]{2,1,0:T(8,128)(2,1)S(1)}, bf16[2,128,512]{2,1,0:T(8,128)(2,1)S(1)}, u32[]{:S(2)}, u32[]{:S(2)}) collective-permute-start(bf16[2,128,512]{2,1,0:T(8,128)(2,1)S(1)} %get-tuple-element.90), channel_id=1, source_target_pairs={{0,1},{1,0},{2,3},{3,2},{4,5},{5,4},{6,7},{7,6},{8,9},{9,8},{10,11... | collective-permute-start | bytes 786440 | tf_op jit(solution)/shard_map/ppermute | solution.py:52
  67.5 17.6 %collective-permute-start.29 = (bf16[2,128,512]{2,1,0:T(8,128)(2,1)S(1)}, bf16[2,128,512]{2,1,0:T(8,128)(2,1)S(1)}, u32[]{:S(2)}, u32[]{:S(2)}) collective-permute-start(bf16[2,128,512]{2,1,0:T(8,128)(2,1)S(1)} %get-tuple-element.98), channel_id=1, source_target_pairs={{1,0},{6,1},{3,2},{8,3},{5,4},{10,5},{7,6},{12,7},{9,8},{14,9},{11... | collective-permute-start | bytes 786440 | tf_op jit(solution)/shard_map/ppermute | solution.py:52
  71.4 13.6 %collective-permute-start.25 = (bf16[2,128,512]{2,1,0:T(8,128)(2,1)S(1)}, bf16[2,128,512]{2,1,0:T(8,128)(2,1)S(1)}, u32[]{:S(2)}, u32[]{:S(2)}) collective-permute-start(bf16[2,128,512]{2,1,0:T(8,128)(2,1)S(1)} %add_convert_fusion.1), channel_id=1, source_target_pairs={{0,2},{1,3},{2,0},{3,1},{4,6},{5,7},{6,4},{7,5},{8,10},{9,11},{10,... | collective-permute-start | bytes 786440 | tf_op jit(solution)/shard_map/ppermute | solution.py:52
  77.1 5.8 %collective-permute-start.28 = (bf16[256,128]{1,0:T(8,128)(2,1)S(1)}, bf16[256,128]{1,0:T(8,128)(2,1)S(1)}, u32[]{:S(2)}, u32[]{:S(2)}) collective-permute-start(bf16[256,128]{1,0:T(8,128)(2,1)S(1)} %fusion.2), channel_id=1, source_target_pairs={{0,12},{1,13},{2,14},{3,15},{4,0},{5,1},{6,2},{7,3},{8,4},{9,5},{1... | collective-permute-start | bytes 196616 | tf_op jit(solution)/shard_map/ppermute | solution.py:52
  77.2 7.8 %collective-permute-start.27 = (bf16[256,128]{1,0:T(8,128)(2,1)S(1)}, bf16[256,128]{1,0:T(8,128)(2,1)S(1)}, u32[]{:S(2)}, u32[]{:S(2)}) collective-permute-start(bf16[256,128]{1,0:T(8,128)(2,1)S(1)} %fusion.2), channel_id=1, source_target_pairs={{0,8},{1,9},{2,10},{3,11},{4,12},{5,13},{6,14},{7,15},{8,0},{9,1},... | collective-permute-start | bytes 196616 | tf_op jit(solution)/shard_map/ppermute | solution.py:52
  77.3 7.7 %collective-permute-start.26 = (bf16[256,128]{1,0:T(8,128)(2,1)S(1)}, bf16[256,128]{1,0:T(8,128)(2,1)S(1)}, u32[]{:S(2)}, u32[]{:S(2)}) collective-permute-start(bf16[256,128]{1,0:T(8,128)(2,1)S(1)} %fusion.2), channel_id=1, source_target_pairs={{0,4},{1,5},{2,6},{3,7},{4,8},{5,9},{6,10},{7,11},{8,12},{9,13},{1... | collective-permute-start | bytes 196616 | tf_op jit(solution)/shard_map/ppermute | solution.py:52
  85.1 6.8 %collective-permute-start.31 = (bf16[4,256,128]{2,1,0:T(8,128)(2,1)S(1)}, bf16[4,256,128]{2,1,0:T(8,128)(2,1)S(1)}, u32[]{:S(2)}, u32[]{:S(2)}) collective-permute-start(bf16[4,256,128]{2,1,0:T(8,128)(2,1)S(1)} %pad_maximum_fusion.1.rest_3_), channel_id=1, source_target_pairs={{0,2},{1,3},{2,0},{3,1},{4,6},{5,7},{6,4},{7,5},{8,10},{9,11},{10,... | collective-permute-start | bytes 786440 | tf_op jit(solution)/shard_map/ppermute | solution.py:52
  87.5 8.9 %collective-permute-start.32 = (bf16[4,256,128]{2,1,0:T(8,128)(2,1)S(1)}, bf16[4,256,128]{2,1,0:T(8,128)(2,1)S(1)}, u32[]{:S(2)}, u32[]{:S(2)}) collective-permute-start(bf16[4,256,128]{2,1,0:T(8,128)(2,1)S(1)} %pad_maximum_fusion.1.rest_3_), channel_id=1, source_target_pairs={{0,1},{1,0},{2,3},{3,2},{4,5},{5,4},{6,7},{7,6},{8,9},{9,8},{10,11... | collective-permute-start | bytes 786440 | tf_op jit(solution)/shard_map/ppermute | solution.py:52
  87.7 8.8 %collective-permute-start.30 = (bf16[2,128,512]{2,1,0:T(8,128)(2,1)S(1)}, bf16[2,128,512]{2,1,0:T(8,128)(2,1)S(1)}, u32[]{:S(2)}, u32[]{:S(2)}) collective-permute-start(bf16[2,128,512]{2,1,0:T(8,128)(2,1)S(1)} %add_convert_fusion), channel_id=1, source_target_pairs={{4,0},{5,1},{6,2},{7,3},{8,4},{9,5},{10,6},{11,7},{12,8},{13,9},{1... | collective-permute-start | bytes 786440 | tf_op jit(solution)/shard_map/ppermute | solution.py:52
  (18 other events, 156.7 us)
